TPU v7x, 512 devices: a whole 4x8x8 slice. The times are simulated.
512 devices in a mesh: dp: 32 (over z_hi, x, core), tensor: 16 (over z_lo, y).
Axes of the slice: x: 4, y: 8, z: 8 (z_hi: 4, z_lo: 2; z = z_hi * 2 + z_lo), core: 2. Of those that a mesh axis runs over, the one named last changes fastest.
Arguments:
- inputs: bfloat16 [4096, 8192], P(('dp', 'tensor')), may hold values from -24 to 24
- cotangent: bfloat16 [4096, 8192], P('dp', 'tensor'), may hold values from -6 to 6
- weight: bfloat16 [8192, 8192], P('dp', 'tensor'), may hold values from -0.0625 to 0.0625
- left_factor: bfloat16 [8192, 16], replicated, may hold values from -0.0625 to 0.0625
- right_factor: bfloat16 [16, 8192], P(None, 'tensor'), may hold values from -0.0625 to 0.0625
- singular: float32 [16], replicated, may hold values from -6 to 6
- keep_mask: int32 [16], replicated, may hold values 0 or 1
Outputs:
- grad_inputs: bfloat16 [4096, 8192], P(('dp', 'tensor'))
- grad_left: float32 [8192, 16], P(('dp', 'tensor'))
- grad_right: float32 [16, 8192], P(None, 'tensor')
- grad_singular: float32 [16], replicated
Inputs may be any that keep to these rules, and one draw needn't show every extreme that they name: `keep_mask`: 1 keeps a singular value, 0 prunes it.
All inputs are finite; a program needn't handle non-finite values.
Results may differ from a plain program's by a relative error of at most 0.0034.
Values may be sent and summed in bfloat16 or wider, within the bound.
No kernel may reach another device: no remote copies, remote signals or barrier semaphores. Data moves between devices by JAX's collectives and lax.ppermute only.
A program may use at most 64 MiB of HBM per device.

v0:
```python
import jax
import jax.numpy as jnp
from jax import lax
from jax.sharding import PartitionSpec as P

adapter_scale = 2.0


def body(inputs, cotangent, weight, left_factor, right_factor, singular, keep_mask):
    data_count = lax.axis_size("dp")
    head_count = lax.axis_size("tensor")
    head_index = lax.axis_index("tensor")
    tok_rows = cotangent.shape[0]
    own_rows = inputs.shape[0]
    model_width = inputs.shape[1]
    keep_float = keep_mask.astype(jnp.float32)
    coeff = adapter_scale * singular * keep_float
    back_part = lax.dot_general(
        cotangent, right_factor, (((1,), (1,)), ((), ())), preferred_element_type=jnp.float32
    )
    whole = lax.all_gather(inputs, "tensor", axis=0, tiled=True)
    back_rank = lax.psum(back_part, "tensor")
    projected = jnp.dot(whole, left_factor, preferred_element_type=jnp.float32)
    scaled_back = (back_rank * coeff).astype(jnp.bfloat16)
    own_back = lax.dynamic_slice_in_dim(scaled_back, head_index * own_rows, own_rows, 0)
    slab_width = model_width // (data_count * head_count)
    strided = whole.reshape(tok_rows, data_count, head_count, slab_width)
    picked = lax.dynamic_index_in_dim(strided, head_index, 2, keepdims=False)
    left_terms = jnp.einsum("tip,tr->ipr", picked, scaled_back, preferred_element_type=jnp.float32)
    grad_left = lax.psum_scatter(left_terms, "dp", scatter_dimension=0, tiled=True)[0] / data_count
    singular_part = jnp.sum(projected * back_rank, axis=0)
    scaled_fwd = (projected * coeff).astype(jnp.bfloat16)
    right_part = lax.dot_general(
        scaled_fwd, cotangent, (((0,), (0,)), ((), ())), preferred_element_type=jnp.float32
    )
    right_sum, singular_sum = lax.psum((right_part, singular_part), "dp")
    terms = lax.dot_general(
        cotangent,
        lax.all_gather(weight, "dp", axis=0, tiled=True),
        (((1,), (1,)), ((), ())),
        preferred_element_type=jnp.float32,
    )
    base_grad = lax.psum_scatter(terms, "tensor", scatter_dimension=0, tiled=True)
    adapter_term = lax.dot_general(
        own_back, left_factor, (((1,), (1,)), ((), ())), preferred_element_type=jnp.float32
    )
    grad_inputs = (base_grad + adapter_term).astype(jnp.bfloat16)
    grad_right = right_sum / data_count
    grad_singular = adapter_scale * keep_float * singular_sum / data_count
    return (grad_inputs, grad_left, grad_right, grad_singular)


def solution(mesh):
    in_specs = (
        P(("dp", "tensor"), None),
        P("dp", "tensor"),
        P("dp", "tensor"),
        P(),
        P(None, "tensor"),
        P(),
        P(),
    )
    out_specs = (P(("dp", "tensor"), None), P(("dp", "tensor"), None), P(None, "tensor"), P())
    return jax.shard_map(body, mesh=mesh, in_specs=in_specs, out_specs=out_specs, check_vma=False)
```

profile of v0, /device:TPU:6, one launch (start us, length us, event | category | flops | bytes accessed | tf_op | source)
XLA Modules:
  0.0 364.8 jit_solution(13162151406143727812)
XLA Ops:
  7.2 0.0 copy-start
  7.2 0.0 all-gather.5.cloned.1.call-start
  7.2 0.7 all-gather.5.cloned.1.call-update
  7.9 0.0 all-gather.3.cloned.1.call-start
  8.0 0.7 all-gather.3.cloned.1.call-update
  8.7 0.0 reduce-scatter.5.cloned.1.call-start
  8.7 1.0 fusion.11
  9.8 36.5 %psum.21 = f32[128,16]{0,1:T(8,128)S(1)} all-reduce(f32[128,16]{0,1:T(8,128)S(1)} %fusion.11), channel_id=1, replica_groups=mesh['dp'=32,'tensor'=16] {'tensor'}, use_global_device_ids=true, to_apply=%region_1.2 | all-reduce | flops 2048 | bytes 16384 | tf_op jit(solution)/shard_map/psum | solution.py:22
  46.3 0.7 convert_multiply_fusion
  47.0 41.9 %all-gather.5.cloned.1.call-done = bf16[128,8192]{1,0:T(8,128)(2,1)} async-done(((bf16[8,8192]{1,0:T(8,128)(2,1)}), bf16[128,8192]{1,0:T(8,128)(2,1)}) %all-gather.5.cloned.1.call-update) | async-done | bytes 2097168 | tf_op jit(solution)/shard_map/all_gather | solution.py:21
  88.9 0.0 copy-start.1
  88.9 4.2 %copy.13 = bf16[128,8192]{0,1:T(8,128)(2,1)} copy(bf16[128,8192]{1,0:T(8,128)(2,1)} %all-gather.5.cloned.1.call-done) | data formatting | bytes 4194304 | tf_op jit(solution)/shard_map/all_gather | solution.py:21
  93.1 0.0 copy-done
  93.1 0.0 copy-done.1
  93.1 0.0 copy-start.2
  93.1 0.8 multiply_reduce_fusion
  93.9 1.8 fusion.1
  95.7 0.0 reduce-scatter.5.cloned.1.call-update
  95.7 0.0 reduce-scatter.3.cloned.1.call-start
  95.8 78.8 %all-gather.3.cloned.1.call-done = bf16[8192,512]{1,0:T(8,128)(2,1)} async-done(((bf16[256,512]{1,0:T(8,128)(2,1)}), bf16[8192,512]{1,0:T(8,128)(2,1)}) %all-gather.3.cloned.1.call-update) | async-done | bytes 8388624 | tf_op jit(solution)/shard_map/all_gather | solution.py:39
  174.6 0.0 copy-done.2
  174.6 8.2 %fusion.10 = f32[128,8192]{1,0:T(8,128)} fusion(bf16[128,512]{1,0:T(8,128)(2,1)S(1)} %copy-done.2, bf16[8192,512]{1,0:T(8,128)(2,1)} %all-gather.3.cloned.1.call-done), kind=kOutput, calls=%fused_computation.18 | convolution fusion | flops 1073741824 | bytes 12713984 | tf_op jit(solution)/shard_map/dot_general | solution.py:37
  182.7 0.0 copy-start.3
  182.7 0.0 reduce-scatter.3.cloned.1.call-update
  182.8 0.2 fusion.4
  182.9 124.9 %all-reduce = (f32[16,512]{1,0:T(8,128)S(1)}, f32[16]{0:T(128)S(1)}) all-reduce(f32[16,512]{1,0:T(8,128)S(1)} %fusion.4, f32[16]{0:T(128)S(1)} %get-tuple-element.6), channel_id=1, replica_groups=mesh['dp'=32,'tensor'=16] {'dp'}, use_global_device_ids=true, to_apply=%region_3.4 | all-reduce | flops 8208 | bytes 65664 | tf_op jit(solution)/shard_map/psum | solution.py:36
  307.8 0.0 copy-done.3
  307.8 0.5 multiply_multiply_fusion
  308.4 0.6 broadcast_multiply_fusion
  309.0 0.0 reduce-scatter.5.cloned.1.call-done
  309.0 1.3 multiply_bitcast_fusion
  310.3 46.1 %reduce-scatter.3.cloned.1.call-done = f32[8,8192]{1,0:T(8,128)} async-done(((f32[128,8192]{1,0:T(8,128)}), f32[8,8192]{1,0:T(8,128)}) %reduce-scatter.3.cloned.1.call-update) | async-done | bytes 262160 | tf_op jit(solution)/shard_map/reduce_scatter | solution.py:43
  356.3 1.9 fusion
Async XLA Ops:
  7.2 86.0 %copy-start = (bf16[8192,16]{0,1:T(8,128)(2,1)S(1)}, bf16[8192,16]{0,1:T(8,128)(2,1)}, u32[]{:S(2)}) copy-start(bf16[8192,16]{0,1:T(8,128)(2,1)} %param.10) | copy-start | bytes 786436
  7.2 81.7 %all-gather.5.cloned.1.call-start = ((), (), s32[]{:S(2)}) async-start(), calls=%async_computation.4 | async-start | bytes 2228224 | tf_op jit(solution)/shard_map/all_gather | solution.py:21
  7.9 166.6 %all-gather.3.cloned.1.call-start = ((), (), s32[]{:S(2)}) async-start(), calls=%async_computation.2 | async-start | bytes 8650752 | tf_op jit(solution)/shard_map/all_gather | solution.py:39
  8.7 300.3 %reduce-scatter.5.cloned.1.call-start = ((), (), s32[]{:S(2)}) async-start(), calls=%async_computation.5 | async-start | bytes 270336 | tf_op jit(solution)/shard_map/reduce_scatter | solution.py:30
  88.9 4.2 %copy-start.1 = (bf16[128,8192]{1,0:T(8,128)(2,1)S(1)}, bf16[128,8192]{1,0:T(8,128)(2,1)}, u32[]{:S(2)}) copy-start(bf16[128,8192]{1,0:T(8,128)(2,1)} %all-gather.5.cloned.1.call-done) | copy-start | bytes 6291460
  93.1 81.4 %copy-start.2 = (bf16[128,512]{1,0:T(8,128)(2,1)S(1)}, bf16[128,512]{1,0:T(8,128)(2,1)}, u32[]{:S(2)}) copy-start(bf16[128,512]{1,0:T(8,128)(2,1)} %param.8) | copy-start | bytes 393220
  95.7 260.6 %reduce-scatter.3.cloned.1.call-start = ((), (), s32[]{:S(2)}) async-start(), calls=%async_computation.3 | async-start | bytes 4456448 | tf_op jit(solution)/shard_map/reduce_scatter | solution.py:43
  182.7 125.1 %copy-start.3 = (s32[16]{0:T(128)S(1)}, s32[16]{0:T(128)}, u32[]{:S(2)}) copy-start(s32[16]{0:T(128)} %param.13) | copy-start | bytes 196
Sparse Core Ops, SparseCore 0:
  10.1 78.7 all-gather.4
  92.0 82.4 all-gather.2
  178.9 93.8 reduce-scatter.4
  275.4 80.8 reduce-scatter.2
where the time goes:
time: 365 us
  waiting for transfers between devices  168 us (46%)
  blocking collectives  161 us (44%)
  matrix products  13.8 us (4%)
  between operations  13.8 us (4%)
  local copies, waits for them, and re-layouts  4.24 us (1%)
    psum x1, blocking collectives, body(): right_sum, singular_sum = lax.psum((right_part, singular_part), 'dp')  125 us
    all_gather x1, waiting for transfers between devices, body(): lax.all_gather(weight, 'dp', axis=0, tiled=True)  78.8 us
    reduce_scatter x1, waiting for transfers between devices, body(): lax.psum_scatter(terms, 'tensor', scatter_dimension=0, tiled=True)  46.1 us
    all_gather x1, waiting for transfers between devices, body(): whole = lax.all_gather(inputs, 'tensor', axis=0, tiled=True)  41.9 us
    psum x1, blocking collectives, body(): back_rank = lax.psum(back_part, 'tensor')  36.5 us
    dot_general x1, matrix products, body(): lax.dot_general(cotangent, lax.all_gather(weight, 'dp', axis=0, tiled=Tru...  8.16 us
  transfers between devices with their start and end apart: 4, of which 3 were waited for; matrix products, arithmetic and copies ran while one was open for 5% of the time, Pallas kernels for 0%

commit v1 on v0

v1 whole, which is shorter than its diff:
```python
import jax
import jax.numpy as jnp
from jax import lax
from jax.experimental import pallas as pl
from jax.experimental.pallas import tpu as pltpu
from jax.sharding import Mesh
from jax.sharding import PartitionSpec as P

adapter_scale = 2.0
n_dp = 32
f32 = jnp.float32
bf16 = jnp.bfloat16
in_vmem = pl.BlockSpec(memory_space=pltpu.VMEM)
in_smem = pl.BlockSpec(memory_space=pltpu.SMEM)
unread = pl.BlockSpec(memory_space=pl.ANY)


def dot_t(a, b):
    return lax.dot_general(a, b, (((1,), (1,)), ((), ())), preferred_element_type=f32)


def t_dot(a, b):
    return lax.dot_general(a, b, (((0,), (0,)), ((), ())), preferred_element_type=f32)


def swap(a, axis, count, mask):
    return lax.ppermute(a, axis, [(i, i ^ mask) for i in range(count)])


def call(kernel, out_shape, in_specs, flops, moved):
    return pl.pallas_call(
        kernel,
        out_shape=out_shape,
        in_specs=in_specs,
        out_specs=jax.tree.map(lambda _: in_vmem, out_shape),
        compiler_params=pltpu.CompilerParams(vmem_limit_bytes=32 << 20),
        cost_estimate=pl.CostEstimate(flops=flops, bytes_accessed=moved, transcendentals=0),
    )


def rank_kernel(cot_ref, right_ref, inputs_ref, left_ref, after_ref, out_ref):
    back = dot_t(cot_ref[...], right_ref[...])
    projected = jnp.dot(inputs_ref[...], left_ref[...], preferred_element_type=f32)
    out_ref[...] = jnp.zeros((16, 8, 128), f32)
    out_ref[:, :, 0:16] = back.reshape(16, 8, 16)
    out_ref[:, :, 16:32] = jnp.broadcast_to(projected[None], (16, 8, 16))


def pack_kernel(
    place_ref, sent_ref, rank_ref, coeff_ref, cot_ref, weight_ref, got_ref, inputs_ref, after1, after3,
    x_ref, back_ref, right_ref,
):
    lane = lax.broadcasted_iota(jnp.int32, (1, 128), 1)
    rank = rank_ref[...]
    coeff = coeff_ref[...]
    own = jnp.where(lane < 16, jnp.sum(rank, axis=0), 0.0)
    back = (own * coeff).astype(bf16)
    back_ref[...] = back
    fwd = (jnp.where((lane >= 16) & (lane < 32), rank, 0.0) * coeff).astype(bf16)
    right_ref[...] = t_dot(fwd.reshape(128, 128), cot_ref[...])[16:32]
    projected = pltpu.roll(sent_ref[0], 112, 1)
    singular = jnp.sum(projected * own, axis=0, keepdims=True)
    high = singular.astype(bf16).astype(f32)
    low = singular - high
    wide = lambda a: jnp.broadcast_to(a, (32, 128))
    back32 = back.astype(f32)
    small = jnp.concatenate(
        [
            jnp.concatenate([back32] * 4, axis=0),
            jnp.concatenate([pltpu.roll(back32, 16, 1)] * 4, axis=0),
            wide(pltpu.roll(jnp.broadcast_to(high, (8, 128)), 32, 1)[0:1]),
            wide(pltpu.roll(jnp.broadcast_to(low, (8, 128)), 32, 1)[0:1]),
        ],
        axis=1,
    ).astype(bf16)
    inputs = inputs_ref[...].astype(f32)
    kept = weight_ref[pl.ds(pl.multiple_of(place_ref[1] * 128, 128), 128), :]
    got = got_ref[...]
    for x in range(4):
        x_ref[x, 0:128, :] = kept
        x_ref[x, 128:256, :] = got
        rows = [inputs[:, (h * 4 + x) * 512 : (h * 4 + x + 1) * 512] for h in range(4)]
        x_ref[x, 256:288, :] = jnp.concatenate(rows, axis=0).astype(bf16)
        x_ref[x, 288:320, :] = small


def terms_kernel(place_ref, own_ref, other_ref, c0_ref, c1_ref, c2_ref, c3_ref, right_ref, out_ref, right_out_ref):
    core, z_high = place_ref[0], place_ref[2]
    right_out_ref[...] = right_ref[...]
    cots = (c0_ref, c1_ref, c2_ref, c3_ref)
    parts = [jnp.concatenate([c[half] for c in cots], axis=0) for half in (0, 1)]
    for s, ref in enumerate((own_ref, other_ref)):
        total = dot_t(parts[0], ref[:, 0:128, :].reshape(512, 512))
        total += dot_t(parts[1], ref[:, 128:256, :].reshape(512, 512))
        total = total.astype(bf16).reshape(4, 128, 512)
        for k in range(4):
            out_ref[z_high ^ k, :, s * 512 : (s + 1) * 512] = total[k]
    tok, back, singular = [], [], jnp.zeros((1, 128), f32)
    for ref in (own_ref, other_ref):
        for x in range(4):
            rows = ref[x, 256:288, :]
            tok.append(jnp.where(core == 0, rows[:, :256], rows[:, 256:]))
            back.append(ref[x, 288:320, 0:256])
            line = ref[x, 288:320, 256:512].astype(f32)[0:1]
            singular += line[:, :128] + line[:, 128:]
    tok = jnp.concatenate(tok, axis=0)
    back = jnp.concatenate(back, axis=0)
    group = lax.rem(lax.broadcasted_iota(jnp.int32, (256, 1), 0), 32) // 8
    for h in range(4):
        both = t_dot(tok, jnp.where(group == h, back, jnp.zeros_like(back)))
        a = both[:, :128].reshape(16, 2, 8, 128)[:, 0]
        b = both[:, 128:].reshape(16, 2, 8, 128)[:, 1]
        z = (a + b + singular).reshape(128, 128)
        high = z.astype(bf16).astype(f32)
        out_ref[h, :, 1024:1152] = (high + pltpu.roll(z - high, 64, 1)).astype(bf16)


def body(inputs, cotangent, weight, left_factor, right_factor, singular, keep_mask):
    core = lax.axis_index("c")
    z_low = lax.axis_index("zl")
    z_high = lax.axis_index("zh")
    place = jnp.stack([core, z_low, z_high]).astype(jnp.int32)
    shape = jax.ShapeDtypeStruct
    keep_float = keep_mask.astype(f32)
    coeff = adapter_scale * singular * keep_float

    given = lax.dynamic_index_in_dim(weight.reshape(2, 128, 512), 1 - z_low, 0, keepdims=False)
    got = swap(given, "zl", 2, 1)

    cot_other = swap(cotangent, "zl", 2, 1)
    cot_pair = jnp.stack([cotangent, cot_other])
    cots = [cot_pair] + [swap(cot_pair, "zh", 4, k) for k in (1, 2, 3)]

    rank_out = call(
        rank_kernel, shape((16, 8, 128), f32), [in_vmem] * 4 + [unread], 6 << 20, 1 << 20
    )(cotangent, right_factor, inputs, left_factor, cot_other)
    rank_in = lax.all_to_all(rank_out, ("zl", "y"), 0, 0)

    coeff_lanes = jnp.pad(jnp.concatenate([coeff, coeff]), (0, 96)).reshape(1, 128)
    x_out, scaled_back, right_part = call(
        pack_kernel,
        (shape((4, 320, 512), bf16), shape((8, 128), bf16), shape((16, 512), f32)),
        [in_smem] + [in_vmem] * 7 + [unread] * 2,
        16 << 20,
        3 << 20,
    )(place, rank_out, rank_in, coeff_lanes, cotangent, weight, got, inputs, cots[1], cots[3])
    x_in = lax.all_to_all(x_out, "x", 0, 0)
    right_part = right_part + swap(right_part, "zh", 4, 1)
    right_part = right_part + swap(right_part, "zh", 4, 2)

    out, right_part = call(
        terms_kernel,
        (shape((4, 128, 1152), bf16), shape((16, 512), f32)),
        [in_smem] + [in_vmem] * 7,
        1 << 30,
        5 << 20,
    )(place, x_in, swap(x_in, "c", 2, 1), *cots, right_part)
    back = lax.all_to_all(out.reshape(64, 8, 1152), ("zh", "zl", "y"), 0, 0)
    right_part = right_part + swap(right_part, "c", 2, 1)
    right_part = right_part + swap(right_part, "x", 4, 1)
    right_sum = right_part + swap(right_part, "x", 4, 2)

    summed = jnp.sum(back[:, :, :1024].reshape(4, 2, 8, 8, 1024).astype(f32), axis=2)
    summed = summed.reshape(4, 2, 8, 2, 4, 128)
    summed = jnp.where(core == 0, summed, summed[:, :, :, ::-1])
    base_grad = summed.transpose(2, 0, 4, 3, 1, 5).reshape(8, 8192)
    grad_inputs = (base_grad + dot_t(scaled_back[:, :16], left_factor)).astype(bf16)
    tail = jnp.sum(back[:, :, 1024:].astype(f32), axis=0)
    tail = tail[:, :64] + tail[:, 64:]
    grad_left = jnp.concatenate([tail[:, :16], tail[:, 16:32]], axis=0) / n_dp
    grad_right = right_sum / n_dp
    grad_singular = adapter_scale * keep_float * tail[0, 32:48] / n_dp
    return (grad_inputs, grad_left, grad_right, grad_singular)


def solution(mesh):
    fine = Mesh(mesh.devices.reshape(4, 4, 2, 2, 8), ("zh", "x", "c", "zl", "y"))
    dp = ("zh", "x", "c")
    tensor = ("zl", "y")
    in_specs = (
        P(dp + tensor, None),
        P(dp, tensor),
        P(dp, tensor),
        P(),
        P(None, tensor),
        P(),
        P(),
    )
    out_specs = (P(dp + tensor, None), P(dp + tensor, None), P(None, tensor), P())
    return jax.shard_map(body, mesh=fine, in_specs=in_specs, out_specs=out_specs, check_vma=False)
```

time: 365 us -> 141 us (0.39)
  blocking collectives: 161 us -> 18 us
  waiting for transfers between devices: 168 us -> 42.9 us
  starting transfers between devices: 0.16 us -> 62 us
  matrix products: 13.8 us -> 0.82 us
  between operations: 13.8 us -> 0.88 us
  Pallas kernels: 0 us -> 5.41 us
    psum x2 -> x0, blocking collectives: 161 us -> none  [the longest x1 125 us: body(): right_sum, singular_sum = lax.psum((right_part, singular_part), 'dp')]
    all_gather x2 -> x0, waiting for transfers between devices: 121 us -> none  [the longest x1 78.8 us: body(): lax.all_gather(weight, 'dp', axis=0, tiled=True)]
    reduce_scatter x2 -> x0, waiting for transfers between devices: 46.1 us -> none  [the longest x1 46.1 us: body(): lax.psum_scatter(terms, 'tensor', scatter_dimension=0, tiled=True)]
    ppermute x0 -> x11, starting transfers between devices: none -> 44.7 us  [swap(): return lax.ppermute(a, axis, [(i, i ^ mask) for i in range(count)])]
    all_to_all x0 -> x2, waiting for transfers between devices: none -> 22.5 us  [the longest x1 14.9 us: body(): back = lax.all_to_all(out.reshape(64, 8, 1152), ('zh', 'zl', 'y'), 0, 0)]
    ppermute x0 -> x11, waiting for transfers between devices: none -> 20.4 us  [swap(): return lax.ppermute(a, axis, [(i, i ^ mask) for i in range(count)])]
    all_to_all x0 -> x1, blocking collectives: none -> 18 us  [body(): x_in = lax.all_to_all(x_out, 'x', 0, 0)]
    all_to_all x0 -> x2, starting transfers between devices: none -> 17.3 us  [the longest x1 9.22 us: body(): back = lax.all_to_all(out.reshape(64, 8, 1152), ('zh', 'zl', 'y'), 0, 0)]
  transfers between devices with their start and end apart: 4 -> 13, of which waited for: 3 -> 8; matrix products, arithmetic and copies ran while one was open for 5% -> 5% of each run, Pallas kernels for 0% -> 1%
where the time goes in v1:
time: 141 us; the launch traced here: 139 us
  starting transfers between devices  62 us (44%)
  waiting for transfers between devices  42.9 us (30%)
  blocking collectives  18 us (13%)
  Pallas kernels  5.41 us (4%)
  other arithmetic  5.14 us (4%)
  local copies, waits for them, and re-layouts  3.58 us (3%)
    ppermute x11, starting transfers between devices, swap(): return lax.ppermute(a, axis, [(i, i ^ mask) for i in range(count)])  44.7 us
    ppermute x11, waiting for transfers between devices, swap(): return lax.ppermute(a, axis, [(i, i ^ mask) for i in range(count)])  20.4 us
    all_to_all x1, blocking collectives, body(): x_in = lax.all_to_all(x_out, 'x', 0, 0)  18 us
    all_to_all x1, waiting for transfers between devices, body(): back = lax.all_to_all(out.reshape(64, 8, 1152), ('zh', 'zl', 'y'), 0, 0)  14.9 us
    all_to_all x1, starting transfers between devices, body(): back = lax.all_to_all(out.reshape(64, 8, 1152), ('zh', 'zl', 'y'), 0, 0)  9.22 us
    all_to_all x1, starting transfers between devices, body(): rank_in = lax.all_to_all(rank_out, ('zl', 'y'), 0, 0)  8.11 us
    all_to_all x1, waiting for transfers between devices, body(): rank_in = lax.all_to_all(rank_out, ('zl', 'y'), 0, 0)  7.64 us
    pallas_call x1, Pallas kernels, body(): call(terms_kernel, (shape((4, 128, 1152), bf16), shape((16, 512), f32)),...  3.12 us
  transfers between devices with their start and end apart: 13, of which 8 were waited for; matrix products, arithmetic and copies ran while one was open for 5% of the time, Pallas kernels for 1%

profile of v1, /device:TPU:6, one launch (start us, length us, event | category | flops | bytes accessed | tf_op | source)
XLA Modules:
  0.0 138.7 jit_solution(12989275202853823426)
XLA Ops:
  0.6 4.3 %collective-permute-start = (bf16[128,512]{1,0:T(8,128)(2,1)}, bf16[128,512]{1,0:T(8,128)(2,1)S(1)}, u32[]{:S(2)}, u32[]{:S(2)}) collective-permute-start(bf16[128,512]{1,0:T(8,128)(2,1)} %cot_ref.3), channel_id=1, source_target_pairs={{0,8},{8,0},{1,9},{9,1},{2,10},{10,2},{3,11},{11,3},{4,12},{12,4},... | collective-permute-start | bytes 393224 | tf_op jit(solution)/shard_map/ppermute | solution.py:27
  4.9 1.6 %dynamic-slice_bitcast_fusion = bf16[128,512]{1,0:T(8,128)(2,1)} fusion(bf16[2,128,512]{2,1,0:T(8,128)(2,1)} %bitcast.24, s32[]{:T(128)S(6)} %select_n.13), kind=kLoop, calls=%fused_computation.7 | loop fusion | bytes 262148 | tf_op jit(solution)/shard_map/jit(dynamic_index_in_dim)/squeeze | solution.py:127
  6.5 1.9 %collective-permute-start.1 = (bf16[128,512]{1,0:T(8,128)(2,1)}, bf16[128,512]{1,0:T(8,128)(2,1)}, u32[]{:S(2)}, u32[]{:S(2)}) collective-permute-start(bf16[128,512]{1,0:T(8,128)(2,1)} %dynamic-slice_bitcast_fusion), channel_id=1, source_target_pairs={{0,8},{8,0},{1,9},{9,1},{2,10},{10,2},{3,11},{11,3},{4,12},{12,4},... | collective-permute-start | bytes 393224 | tf_op jit(solution)/shard_map/ppermute | solution.py:27
  8.4 0.2 collective-permute-done.after_ref
  8.6 0.9 pad_maximum_fusion.c0_ref
  9.5 0.0 copy-start
  9.6 0.0 copy-start.2
  9.6 0.0 copy-start.3
  9.6 10.5 %collective-permute-start.3 = (bf16[2,128,512]{2,1,0:T(8,128)(2,1)S(1)}, bf16[2,128,512]{2,1,0:T(8,128)(2,1)S(1)}, u32[]{:S(2)}, u32[]{:S(2)}) collective-permute-start(bf16[2,128,512]{2,1,0:T(8,128)(2,1)S(1)} %pad_maximum_fusion.c0_ref), channel_id=1, source_target_pairs={{0,384},{128,256},{256,128},{384,0},{1,385},{129,257},{257,129},{3... | collective-permute-start | bytes 786440 | tf_op jit(solution)/shard_map/ppermute | solution.py:27
  20.1 2.5 %collective-permute-start.2 = (bf16[2,128,512]{2,1,0:T(8,128)(2,1)S(1)}, bf16[2,128,512]{2,1,0:T(8,128)(2,1)S(1)}, u32[]{:S(2)}, u32[]{:S(2)}) collective-permute-start(bf16[2,128,512]{2,1,0:T(8,128)(2,1)S(1)} %pad_maximum_fusion.c0_ref), channel_id=1, source_target_pairs={{0,128},{128,0},{256,384},{384,256},{1,129},{129,1},{257,385},{385... | collective-permute-start | bytes 786440 | tf_op jit(solution)/shard_map/ppermute | solution.py:27
  22.6 1.2 convert_multiply_fusion
  23.8 1.9 %copy.12.left_ref = bf16[8192,16]{1,0:T(8,128)(2,1)S(1)} copy(bf16[8192,16]{0,1:T(8,128)(2,1)} %param.10) | data formatting | bytes 524288 | tf_op args[3]
  25.7 0.0 copy-start.1
  25.7 1.1 shard_map.102.sent_ref
  26.8 8.1 %all-to-all-start = ((f32[16,8,128]{2,1,0:T(8,128)}), f32[16,8,128]{2,1,0:T(8,128)S(1)}, u32[]{:S(2)}, u32[]{:S(2)}) async-start(f32[16,8,128]{2,1,0:T(8,128)} %shard_map.102.sent_ref), calls=%async_computation | async-start | bytes 131072 | tf_op jit(solution)/shard_map/all_to_all | solution.py:137
  35.0 0.8 fusion.4.coeff_ref
  35.8 0.1 pad_add_fusion.place_ref
  35.8 0.0 collective-permute-done.1.got_ref
  35.8 7.6 %all-to-all-done.rank_ref = f32[16,8,128]{2,1,0:T(8,128)S(1)} async-done(((f32[16,8,128]{2,1,0:T(8,128)}), f32[16,8,128]{2,1,0:T(8,128)S(1)}, u32[]{:S(2)}, u32[]{:S(2)}) %all-to-all-start) | async-done | bytes 65568 | tf_op jit(solution)/shard_map/all_to_all | solution.py:137
  43.5 0.0 collective-permute-done.2.after1.c1_ref
  43.5 1.2 shard_map.103
  44.7 18.0 %all_to_all.15.own_ref = bf16[4,320,512]{2,1,0:T(8,128)(2,1)S(1)} all-to-all(bf16[4,320,512]{2,1,0:T(8,128)(2,1)S(1)} %get-tuple-element.9), channel_id=1, replica_groups=mesh['zh'=4,'x'=4,'c'=2,'zl'=2,'y'=8] {'x'}, dimensions={0} | all-to-all | bytes 2621440 | tf_op jit(solution)/shard_map/all_to_all | solution.py:147
  62.6 1.9 %collective-permute-start.4 = (bf16[4,320,512]{2,1,0:T(8,128)(2,1)S(1)}, bf16[4,320,512]{2,1,0:T(8,128)(2,1)S(1)}, u32[]{:S(2)}, u32[]{:S(2)}) collective-permute-start(bf16[4,320,512]{2,1,0:T(8,128)(2,1)S(1)} %all_to_all.15.own_ref), channel_id=1, source_target_pairs={{0,16},{16,0},{1,17},{17,1},{2,18},{18,2},{3,19},{19,3},{4,20},{20... | collective-permute-start | bytes 3932168 | tf_op jit(solution)/shard_map/ppermute | solution.py:27
  64.5 3.9 %collective-permute-start.5 = (bf16[2,128,512]{2,1,0:T(8,128)(2,1)S(1)}, bf16[2,128,512]{2,1,0:T(8,128)(2,1)S(1)}, u32[]{:S(2)}, u32[]{:S(2)}) collective-permute-start(bf16[2,128,512]{2,1,0:T(8,128)(2,1)S(1)} %pad_maximum_fusion.c0_ref), channel_id=1, source_target_pairs={{0,256},{128,384},{256,0},{384,128},{1,257},{129,385},{257,1},{385... | collective-permute-start | bytes 786440 | tf_op jit(solution)/shard_map/ppermute | solution.py:27
  68.5 2.5 %collective-permute-start.6 = (f32[16,512]{1,0:T(8,128)S(1)}, f32[16,512]{1,0:T(8,128)S(1)}, u32[]{:S(2)}, u32[]{:S(2)}) collective-permute-start(f32[16,512]{1,0:T(8,128)S(1)} %get-tuple-element.10), channel_id=1, source_target_pairs={{0,128},{128,0},{256,384},{384,256},{1,129},{129,1},{257,385},{385... | collective-permute-start | bytes 98312 | tf_op jit(solution)/shard_map/ppermute | solution.py:27
  70.9 10.2 %collective-permute-done.6 = f32[16,512]{1,0:T(8,128)S(1)} collective-permute-done((f32[16,512]{1,0:T(8,128)S(1)}, f32[16,512]{1,0:T(8,128)S(1)}, u32[]{:S(2)}, u32[]{:S(2)}) %collective-permute-start.6) | collective-permute-done | bytes 32800 | tf_op jit(solution)/shard_map/ppermute | solution.py:27
  81.1 9.2 %collective-permute-start.7 = (f32[16,512]{1,0:T(8,128)S(1)}, f32[16,512]{1,0:T(8,128)S(1)}, u32[]{:S(2)}, u32[]{:S(2)}) collective-permute-start(f32[16,512]{1,0:T(8,128)S(1)} %add.29), channel_id=1, source_target_pairs={{0,256},{128,384},{256,0},{384,128},{1,257},{129,385},{257,1},{385... | collective-permute-start | bytes 98312 | tf_op jit(solution)/shard_map/ppermute | solution.py:27
  90.4 1.9 %collective-permute-done.7 = f32[16,512]{1,0:T(8,128)S(1)} collective-permute-done((f32[16,512]{1,0:T(8,128)S(1)}, f32[16,512]{1,0:T(8,128)S(1)}, u32[]{:S(2)}, u32[]{:S(2)}) %collective-permute-start.7) | collective-permute-done | bytes 32800 | tf_op jit(solution)/shard_map/ppermute | solution.py:27
  92.2 0.0 collective-permute-done.5.c2_ref
  92.2 0.0 collective-permute-done.4.other_ref
  92.3 3.1 %shard_map.104 = (bf16[4,128,1152]{2,1,0:T(8,128)(2,1)}, f32[16,512]{1,0:T(8,128)S(1)}) custom-call(s32[3]{0:T(128)S(1)} %pad_add_fusion.place_ref, bf16[4,320,512]{2,1,0:T(8,128)(2,1)S(1)} %all_to_all.15.own_ref, bf16[4,320,512]{2,1,0:T(8,128)(2,1)S(1)} %collective-permute-done.4.other_ref, bf16[2,128,512]{2,1,0:T(8,128)(2,1)S(1)} %pad_maximum_fusion.c0_ref, ...), custom_call_target="tpu_custom_call" | custom-call | flops 1073741824 | bytes 5242880 | tf_op jit(solution)/shard_map/pallas_call | solution.py:151
  95.4 9.2 %all-to-all-start.2 = ((bf16[64,8,1152]{2,1,0:T(8,128)(2,1)}), bf16[64,8,1152]{2,1,0:T(8,128)(2,1)S(1)}, u32[]{:S(2)}, u32[]{:S(2)}) async-start(bf16[64,8,1152]{2,1,0:T(8,128)(2,1)} %bitcast.8), calls=%async_computation.2 | async-start | bytes 2359296 | tf_op jit(solution)/shard_map/all_to_all | solution.py:158
  104.6 1.9 %collective-permute-start.8 = (f32[16,512]{1,0:T(8,128)S(1)}, f32[16,512]{1,0:T(8,128)S(1)}, u32[]{:S(2)}, u32[]{:S(2)}) collective-permute-start(f32[16,512]{1,0:T(8,128)S(1)} %get-tuple-element.13), channel_id=1, source_target_pairs={{0,16},{16,0},{1,17},{17,1},{2,18},{18,2},{3,19},{19,3},{4,20},{20... | collective-permute-start | bytes 98312 | tf_op jit(solution)/shard_map/ppermute | solution.py:27
  106.5 1.2 collective-permute-done.8
  107.7 2.1 %collective-permute-start.9 = (f32[16,512]{1,0:T(8,128)S(1)}, f32[16,512]{1,0:T(8,128)S(1)}, u32[]{:S(2)}, u32[]{:S(2)}) collective-permute-start(f32[16,512]{1,0:T(8,128)S(1)} %add.33), channel_id=1, source_target_pairs={{0,32},{32,0},{64,96},{96,64},{1,33},{33,1},{65,97},{97,65},{2,34}... | collective-permute-start | bytes 98312 | tf_op jit(solution)/shard_map/ppermute | solution.py:27
  109.8 3.7 %collective-permute-done.9 = f32[16,512]{1,0:T(8,128)S(1)} collective-permute-done((f32[16,512]{1,0:T(8,128)S(1)}, f32[16,512]{1,0:T(8,128)S(1)}, u32[]{:S(2)}, u32[]{:S(2)}) %collective-permute-start.9) | collective-permute-done | bytes 32800 | tf_op jit(solution)/shard_map/ppermute | solution.py:27
  113.5 4.0 %collective-permute-start.10 = (f32[16,512]{1,0:T(8,128)S(1)}, f32[16,512]{1,0:T(8,128)S(1)}, u32[]{:S(2)}, u32[]{:S(2)}) collective-permute-start(f32[16,512]{1,0:T(8,128)S(1)} %add.34), channel_id=1, source_target_pairs={{0,64},{32,96},{64,0},{96,32},{1,65},{33,97},{65,1},{97,33},{2,66}... | collective-permute-start | bytes 98312 | tf_op jit(solution)/shard_map/ppermute | solution.py:27
  117.5 0.0 copy-start.4
  117.5 3.3 %collective-permute-done.10 = f32[16,512]{1,0:T(8,128)S(1)} collective-permute-done((f32[16,512]{1,0:T(8,128)S(1)}, f32[16,512]{1,0:T(8,128)S(1)}, u32[]{:S(2)}, u32[]{:S(2)}) %collective-permute-start.10) | collective-permute-done | bytes 32800 | tf_op jit(solution)/shard_map/ppermute | solution.py:27
  120.8 0.6 add_multiply_fusion
  121.4 14.9 %all-to-all-done.2 = bf16[64,8,1152]{2,1,0:T(8,128)(2,1)S(1)} async-done(((bf16[64,8,1152]{2,1,0:T(8,128)(2,1)}), bf16[64,8,1152]{2,1,0:T(8,128)(2,1)S(1)}, u32[]{:S(2)}, u32[]{:S(2)}) %all-to-all-start.2) | async-done | bytes 1179680 | tf_op jit(solution)/shard_map/all_to_all | solution.py:158
  136.3 0.1 convert_reduce_fusion.1
  136.4 0.1 slice_add_fusion
  136.5 0.6 fusion.5
  137.0 0.1 fusion.6
  137.1 0.1 convert_reduce_fusion
  137.3 0.8 fusion
  138.1 0.6 maximum_multiply_fusion
  (14 shorter events, 0.1 us)
Async XLA Ops:
  0.6 8.0 %collective-permute-start = (bf16[128,512]{1,0:T(8,128)(2,1)}, bf16[128,512]{1,0:T(8,128)(2,1)S(1)}, u32[]{:S(2)}, u32[]{:S(2)}) collective-permute-start(bf16[128,512]{1,0:T(8,128)(2,1)} %cot_ref.3), channel_id=1, source_target_pairs={{0,8},{8,0},{1,9},{9,1},{2,10},{10,2},{3,11},{11,3},{4,12},{12,4},... | collective-permute-start | bytes 393224 | tf_op jit(solution)/shard_map/ppermute | solution.py:27
  6.5 29.3 %collective-permute-start.1 = (bf16[128,512]{1,0:T(8,128)(2,1)}, bf16[128,512]{1,0:T(8,128)(2,1)}, u32[]{:S(2)}, u32[]{:S(2)}) collective-permute-start(bf16[128,512]{1,0:T(8,128)(2,1)} %dynamic-slice_bitcast_fusion), channel_id=1, source_target_pairs={{0,8},{8,0},{1,9},{9,1},{2,10},{10,2},{3,11},{11,3},{4,12},{12,4},... | collective-permute-start | bytes 393224 | tf_op jit(solution)/shard_map/ppermute | solution.py:27
  9.5 16.1 %copy-start = (bf16[128,512]{1,0:T(8,128)(2,1)S(1)}, bf16[128,512]{1,0:T(8,128)(2,1)}, u32[]{:S(2)}) copy-start(bf16[128,512]{1,0:T(8,128)(2,1)} %cot_ref.3) | copy-start | bytes 393220
  9.6 16.1 %copy-start.2 = (bf16[8,8192]{1,0:T(8,128)(2,1)S(1)}, bf16[8,8192]{1,0:T(8,128)(2,1)}, u32[]{:S(2)}) copy-start(bf16[8,8192]{1,0:T(8,128)(2,1)} %inputs_ref.3) | copy-start | bytes 393220
  9.6 16.1 %copy-start.3 = (bf16[16,512]{1,0:T(8,128)(2,1)S(1)}, bf16[16,512]{1,0:T(8,128)(2,1)}, u32[]{:S(2)}) copy-start(bf16[16,512]{1,0:T(8,128)(2,1)} %right_ref.1) | copy-start | bytes 49156
  9.6 33.9 %collective-permute-start.3 = (bf16[2,128,512]{2,1,0:T(8,128)(2,1)S(1)}, bf16[2,128,512]{2,1,0:T(8,128)(2,1)S(1)}, u32[]{:S(2)}, u32[]{:S(2)}) collective-permute-start(bf16[2,128,512]{2,1,0:T(8,128)(2,1)S(1)} %pad_maximum_fusion.c0_ref), channel_id=1, source_target_pairs={{0,384},{128,256},{256,128},{384,0},{1,385},{129,257},{257,129},{3... | collective-permute-start | bytes 786440 | tf_op jit(solution)/shard_map/ppermute | solution.py:27
  20.1 23.4 %collective-permute-start.2 = (bf16[2,128,512]{2,1,0:T(8,128)(2,1)S(1)}, bf16[2,128,512]{2,1,0:T(8,128)(2,1)S(1)}, u32[]{:S(2)}, u32[]{:S(2)}) collective-permute-start(bf16[2,128,512]{2,1,0:T(8,128)(2,1)S(1)} %pad_maximum_fusion.c0_ref), channel_id=1, source_target_pairs={{0,128},{128,0},{256,384},{384,256},{1,129},{129,1},{257,385},{385... | collective-permute-start | bytes 786440 | tf_op jit(solution)/shard_map/ppermute | solution.py:27
  25.7 17.8 %copy-start.1 = (bf16[256,512]{1,0:T(8,128)(2,1)S(1)}, bf16[256,512]{1,0:T(8,128)(2,1)}, u32[]{:S(2)}) copy-start(bf16[256,512]{1,0:T(8,128)(2,1)} %weight_ref.1) | copy-start | bytes 786436
  26.8 16.6 %all-to-all-start = ((f32[16,8,128]{2,1,0:T(8,128)}), f32[16,8,128]{2,1,0:T(8,128)S(1)}, u32[]{:S(2)}, u32[]{:S(2)}) async-start(f32[16,8,128]{2,1,0:T(8,128)} %shard_map.102.sent_ref), calls=%async_computation | async-start | bytes 131072 | tf_op jit(solution)/shard_map/all_to_all | solution.py:137
  62.6 29.6 %collective-permute-start.4 = (bf16[4,320,512]{2,1,0:T(8,128)(2,1)S(1)}, bf16[4,320,512]{2,1,0:T(8,128)(2,1)S(1)}, u32[]{:S(2)}, u32[]{:S(2)}) collective-permute-start(bf16[4,320,512]{2,1,0:T(8,128)(2,1)S(1)} %all_to_all.15.own_ref), channel_id=1, source_target_pairs={{0,16},{16,0},{1,17},{17,1},{2,18},{18,2},{3,19},{19,3},{4,20},{20... | collective-permute-start | bytes 3932168 | tf_op jit(solution)/shard_map/ppermute | solution.py:27
  64.5 27.7 %collective-permute-start.5 = (bf16[2,128,512]{2,1,0:T(8,128)(2,1)S(1)}, bf16[2,128,512]{2,1,0:T(8,128)(2,1)S(1)}, u32[]{:S(2)}, u32[]{:S(2)}) collective-permute-start(bf16[2,128,512]{2,1,0:T(8,128)(2,1)S(1)} %pad_maximum_fusion.c0_ref), channel_id=1, source_target_pairs={{0,256},{128,384},{256,0},{384,128},{1,257},{129,385},{257,1},{385... | collective-permute-start | bytes 786440 | tf_op jit(solution)/shard_map/ppermute | solution.py:27
  68.5 12.6 %collective-permute-start.6 = (f32[16,512]{1,0:T(8,128)S(1)}, f32[16,512]{1,0:T(8,128)S(1)}, u32[]{:S(2)}, u32[]{:S(2)}) collective-permute-start(f32[16,512]{1,0:T(8,128)S(1)} %get-tuple-element.10), channel_id=1, source_target_pairs={{0,128},{128,0},{256,384},{384,256},{1,129},{129,1},{257,385},{385... | collective-permute-start | bytes 98312 | tf_op jit(solution)/shard_map/ppermute | solution.py:27
  81.1 11.1 %collective-permute-start.7 = (f32[16,512]{1,0:T(8,128)S(1)}, f32[16,512]{1,0:T(8,128)S(1)}, u32[]{:S(2)}, u32[]{:S(2)}) collective-permute-start(f32[16,512]{1,0:T(8,128)S(1)} %add.29), channel_id=1, source_target_pairs={{0,256},{128,384},{256,0},{384,128},{1,257},{129,385},{257,1},{385... | collective-permute-start | bytes 98312 | tf_op jit(solution)/shard_map/ppermute | solution.py:27
  95.4 41.1 %copy-start.5 = (s32[16]{0:T(128)S(1)}, s32[16]{0:T(128)}, u32[]{:S(2)}) copy-start(s32[16]{0:T(128)} %param.13) | copy-start | bytes 196
  95.4 40.9 %all-to-all-start.2 = ((bf16[64,8,1152]{2,1,0:T(8,128)(2,1)}), bf16[64,8,1152]{2,1,0:T(8,128)(2,1)S(1)}, u32[]{:S(2)}, u32[]{:S(2)}) async-start(bf16[64,8,1152]{2,1,0:T(8,128)(2,1)} %bitcast.8), calls=%async_computation.2 | async-start | bytes 2359296 | tf_op jit(solution)/shard_map/all_to_all | solution.py:158
  104.6 3.1 %collective-permute-start.8 = (f32[16,512]{1,0:T(8,128)S(1)}, f32[16,512]{1,0:T(8,128)S(1)}, u32[]{:S(2)}, u32[]{:S(2)}) collective-permute-start(f32[16,512]{1,0:T(8,128)S(1)} %get-tuple-element.13), channel_id=1, source_target_pairs={{0,16},{16,0},{1,17},{17,1},{2,18},{18,2},{3,19},{19,3},{4,20},{20... | collective-permute-start | bytes 98312 | tf_op jit(solution)/shard_map/ppermute | solution.py:27
  107.7 5.8 %collective-permute-start.9 = (f32[16,512]{1,0:T(8,128)S(1)}, f32[16,512]{1,0:T(8,128)S(1)}, u32[]{:S(2)}, u32[]{:S(2)}) collective-permute-start(f32[16,512]{1,0:T(8,128)S(1)} %add.33), channel_id=1, source_target_pairs={{0,32},{32,0},{64,96},{96,64},{1,33},{33,1},{65,97},{97,65},{2,34}... | collective-permute-start | bytes 98312 | tf_op jit(solution)/shard_map/ppermute | solution.py:27
  113.5 7.3 %collective-permute-start.10 = (f32[16,512]{1,0:T(8,128)S(1)}, f32[16,512]{1,0:T(8,128)S(1)}, u32[]{:S(2)}, u32[]{:S(2)}) collective-permute-start(f32[16,512]{1,0:T(8,128)S(1)} %add.34), channel_id=1, source_target_pairs={{0,64},{32,96},{64,0},{96,32},{1,65},{33,97},{65,1},{97,33},{2,66}... | collective-permute-start | bytes 98312 | tf_op jit(solution)/shard_map/ppermute | solution.py:27
  117.5 19.8 %copy-start.4 = (bf16[8192,16]{0,1:T(8,128)(2,1)S(1)}, bf16[8192,16]{0,1:T(8,128)(2,1)}, u32[]{:S(2)}) copy-start(bf16[8192,16]{0,1:T(8,128)(2,1)} %param.10) | copy-start | bytes 786436

commit v2 on v1

--- a/solution.py
+++ b/solution.py
@@ -38,9 +38,19 @@
     )
 
 
-def rank_kernel(cot_ref, right_ref, inputs_ref, left_ref, after_ref, out_ref):
+def after(a, *others):
+    return pl.pallas_call(
+        lambda *refs: None,
+        out_shape=jax.ShapeDtypeStruct(a.shape, a.dtype),
+        in_specs=[unread] * (1 + len(others)),
+        out_specs=unread,
+        input_output_aliases={0: 0},
+    )(a, *others)
+
+
+def rank_kernel(cot_ref, right_ref, projected_ref, after_ref, out_ref):
     back = dot_t(cot_ref[...], right_ref[...])
-    projected = jnp.dot(inputs_ref[...], left_ref[...], preferred_element_type=f32)
+    projected = projected_ref[...]
     out_ref[...] = jnp.zeros((16, 8, 128), f32)
     out_ref[:, :, 0:16] = back.reshape(16, 8, 16)
     out_ref[:, :, 16:32] = jnp.broadcast_to(projected[None], (16, 8, 16))
@@ -131,9 +141,10 @@
     cot_pair = jnp.stack([cotangent, cot_other])
     cots = [cot_pair] + [swap(cot_pair, "zh", 4, k) for k in (1, 2, 3)]
 
+    own_projected = jnp.dot(inputs, left_factor, preferred_element_type=f32)
     rank_out = call(
-        rank_kernel, shape((16, 8, 128), f32), [in_vmem] * 4 + [unread], 6 << 20, 1 << 20
-    )(cotangent, right_factor, inputs, left_factor, cot_other)
+        rank_kernel, shape((16, 8, 128), f32), [in_vmem] * 3 + [unread], 6 << 20, 1 << 20
+    )(cotangent, right_factor, own_projected, cot_other)
     rank_in = lax.all_to_all(rank_out, ("zl", "y"), 0, 0)
 
     coeff_lanes = jnp.pad(jnp.concatenate([coeff, coeff]), (0, 96)).reshape(1, 128)
@@ -147,6 +158,7 @@
     x_in = lax.all_to_all(x_out, "x", 0, 0)
     right_part = right_part + swap(right_part, "zh", 4, 1)
     right_part = right_part + swap(right_part, "zh", 4, 2)
+    x_in = after(x_in, cots[2], right_part)
 
     out, right_part = call(
         terms_kernel,

time: 141 us -> 135 us (0.957)
  blocking collectives: 18 us -> 0 us
  waiting for transfers between devices: 42.9 us -> 50.4 us
  local copies, waits for them, and re-layouts: 3.58 us -> 6.77 us
  starting transfers between devices: 62 us -> 63.6 us
    all_to_all x1 -> x0, blocking collectives: 18 us -> none  [body(): x_in = lax.all_to_all(x_out, 'x', 0, 0)]
    ppermute x11, waiting for transfers between devices: 20.4 us -> 25.7 us  [swap(): return lax.ppermute(a, axis, [(i, i ^ mask) for i in range(count)])]
    all_to_all x0 -> x1, starting transfers between devices: none -> 4.77 us  [body(): x_in = lax.all_to_all(x_out, 'x', 0, 0)]
    unnamed x13 -> x24, local copies, waits for them, and re-layouts: 1.92 us -> 5.69 us
    ppermute x11, starting transfers between devices: 44.7 us -> 42.3 us  [swap(): return lax.ppermute(a, axis, [(i, i ^ mask) for i in range(count)])]
  transfers between devices with their start and end apart: 13 -> 14, of which waited for: 8 -> 9; matrix products, arithmetic and copies ran while one was open for 5% -> 3% of each run, Pallas kernels for 1% -> 1%
where the time goes in v2:
time: 135 us; the launch traced here: 134 us
  starting transfers between devices  63.6 us (47%)
  waiting for transfers between devices  50.4 us (37%)
  local copies, waits for them, and re-layouts  6.77 us (5%)
  Pallas kernels  5.98 us (4%)
  other arithmetic  4.51 us (3%)
  matrix products  1.92 us (1%)
    ppermute x11, starting transfers between devices, swap(): return lax.ppermute(a, axis, [(i, i ^ mask) for i in range(count)])  42.3 us
    ppermute x11, waiting for transfers between devices, swap(): return lax.ppermute(a, axis, [(i, i ^ mask) for i in range(count)])  25.7 us
    all_to_all x1, waiting for transfers between devices, body(): back = lax.all_to_all(out.reshape(64, 8, 1152), ('zh', 'zl', 'y'), 0, 0)  16.3 us
    all_to_all x1, starting transfers between devices, body(): back = lax.all_to_all(out.reshape(64, 8, 1152), ('zh', 'zl', 'y'), 0, 0)  8.92 us
    all_to_all x1, waiting for transfers between devices, body(): rank_in = lax.all_to_all(rank_out, ('zl', 'y'), 0, 0)  8.37 us
    all_to_all x1, starting transfers between devices, body(): rank_in = lax.all_to_all(rank_out, ('zl', 'y'), 0, 0)  7.59 us
    unnamed x24, local copies, waits for them, and re-layouts  5.69 us
    all_to_all x1, starting transfers between devices, body(): x_in = lax.all_to_all(x_out, 'x', 0, 0)  4.77 us
  transfers between devices with their start and end apart: 14, of which 9 were waited for; matrix products, arithmetic and copies ran while one was open for 3% of the time, Pallas kernels for 1%

profile of v2, /device:TPU:6, one launch (start us, length us, event | category | flops | bytes accessed | tf_op | source)
XLA Modules:
  0.0 134.0 jit_solution(17617850896700141159)
XLA Ops:
  0.6 0.0 copy-start
  0.7 1.0 dynamic-slice_bitcast_fusion
  1.7 4.3 %collective-permute-start.1 = (bf16[128,512]{1,0:T(8,128)(2,1)S(1)}, bf16[128,512]{1,0:T(8,128)(2,1)S(1)}, u32[]{:S(2)}, u32[]{:S(2)}) collective-permute-start(bf16[128,512]{1,0:T(8,128)(2,1)S(1)} %dynamic-slice_bitcast_fusion), channel_id=1, source_target_pairs={{0,8},{8,0},{1,9},{9,1},{2,10},{10,2},{3,11},{11,3},{4,12},{12,4},... | collective-permute-start | bytes 393224 | tf_op jit(solution)/shard_map/ppermute | solution.py:27
  6.0 1.9 %collective-permute-start = (bf16[128,512]{1,0:T(8,128)(2,1)}, bf16[128,512]{1,0:T(8,128)(2,1)S(1)}, u32[]{:S(2)}, u32[]{:S(2)}) collective-permute-start(bf16[128,512]{1,0:T(8,128)(2,1)} %cot_ref.3), channel_id=1, source_target_pairs={{0,8},{8,0},{1,9},{9,1},{2,10},{10,2},{3,11},{11,3},{4,12},{12,4},... | collective-permute-start | bytes 393224 | tf_op jit(solution)/shard_map/ppermute | solution.py:27
  7.9 1.1 fusion.7.projected_ref
  9.0 4.0 %collective-permute-done.after_ref = bf16[128,512]{1,0:T(8,128)(2,1)S(1)} collective-permute-done((bf16[128,512]{1,0:T(8,128)(2,1)}, bf16[128,512]{1,0:T(8,128)(2,1)S(1)}, u32[]{:S(2)}, u32[]{:S(2)}) %collective-permute-start) | collective-permute-done | bytes 131104 | tf_op jit(solution)/shard_map/ppermute | solution.py:27
  13.0 0.9 pad_maximum_fusion.c0_ref
  14.0 10.0 %collective-permute-start.3 = (bf16[2,128,512]{2,1,0:T(8,128)(2,1)S(1)}, bf16[2,128,512]{2,1,0:T(8,128)(2,1)S(1)}, u32[]{:S(2)}, u32[]{:S(2)}) collective-permute-start(bf16[2,128,512]{2,1,0:T(8,128)(2,1)S(1)} %pad_maximum_fusion.c0_ref), channel_id=1, source_target_pairs={{0,384},{128,256},{256,128},{384,0},{1,385},{129,257},{257,129},{3... | collective-permute-start | bytes 786440 | tf_op jit(solution)/shard_map/ppermute | solution.py:27
  24.0 2.5 %collective-permute-start.2 = (bf16[2,128,512]{2,1,0:T(8,128)(2,1)S(1)}, bf16[2,128,512]{2,1,0:T(8,128)(2,1)S(1)}, u32[]{:S(2)}, u32[]{:S(2)}) collective-permute-start(bf16[2,128,512]{2,1,0:T(8,128)(2,1)S(1)} %pad_maximum_fusion.c0_ref), channel_id=1, source_target_pairs={{0,128},{128,0},{256,384},{384,256},{1,129},{129,1},{257,385},{385... | collective-permute-start | bytes 786440 | tf_op jit(solution)/shard_map/ppermute | solution.py:27
  26.5 0.7 convert_multiply_fusion
  27.2 0.9 copy-done.3
  28.1 0.7 copy-done.10
  28.8 0.8 shard_map.102.sent_ref
  29.6 7.6 %all-to-all-start = ((f32[16,8,128]{2,1,0:T(8,128)}), f32[16,8,128]{2,1,0:T(8,128)S(1)}, u32[]{:S(2)}, u32[]{:S(2)}) async-start(f32[16,8,128]{2,1,0:T(8,128)} %shard_map.102.sent_ref), calls=%async_computation | async-start | bytes 131072 | tf_op jit(solution)/shard_map/all_to_all | solution.py:148
  37.2 0.1 fusion.4.coeff_ref
  37.2 0.1 pad_add_fusion.place_ref
  37.3 8.4 %all-to-all-done.rank_ref = f32[16,8,128]{2,1,0:T(8,128)S(1)} async-done(((f32[16,8,128]{2,1,0:T(8,128)}), f32[16,8,128]{2,1,0:T(8,128)S(1)}, u32[]{:S(2)}, u32[]{:S(2)}) %all-to-all-start) | async-done | bytes 65568 | tf_op jit(solution)/shard_map/all_to_all | solution.py:148
  45.7 2.1 %shard_map.103 = (bf16[4,320,512]{2,1,0:T(8,128)(2,1)}, bf16[8,128]{1,0:T(8,128)(2,1)S(1)}, f32[16,512]{1,0:T(8,128)S(1)}) custom-call(s32[3]{0:T(128)S(1)} %pad_add_fusion.place_ref, f32[16,8,128]{2,1,0:T(8,128)} %shard_map.102.sent_ref, f32[16,8,128]{2,1,0:T(8,128)S(1)} %all-to-all-done.rank_ref, f32[1,128]{1,0:T(1,128)S(1)} %fusion.4.coeff_ref, ...), custom_call_target="tpu_custom_call" | custom-call | flops 16777216 | bytes 3145728 | tf_op jit(solution)/shard_map/pallas_call | solution.py:151
  47.8 4.8 %all-to-all-start.1 = ((bf16[4,320,512]{2,1,0:T(8,128)(2,1)}), bf16[4,320,512]{2,1,0:T(8,128)(2,1)S(1)}, u32[]{:S(2)}, u32[]{:S(2)}) async-start(bf16[4,320,512]{2,1,0:T(8,128)(2,1)} %get-tuple-element.9), calls=%async_computation.1 | async-start | bytes 2621440 | tf_op jit(solution)/shard_map/all_to_all | solution.py:158
  52.6 3.7 %collective-permute-start.4 = (bf16[2,128,512]{2,1,0:T(8,128)(2,1)S(1)}, bf16[2,128,512]{2,1,0:T(8,128)(2,1)S(1)}, u32[]{:S(2)}, u32[]{:S(2)}) collective-permute-start(bf16[2,128,512]{2,1,0:T(8,128)(2,1)S(1)} %pad_maximum_fusion.c0_ref), channel_id=1, source_target_pairs={{0,256},{128,384},{256,0},{384,128},{1,257},{129,385},{257,1},{385... | collective-permute-start | bytes 786440 | tf_op jit(solution)/shard_map/ppermute | solution.py:27
  56.3 2.5 %collective-permute-start.5 = (f32[16,512]{1,0:T(8,128)S(1)}, f32[16,512]{1,0:T(8,128)S(1)}, u32[]{:S(2)}, u32[]{:S(2)}) collective-permute-start(f32[16,512]{1,0:T(8,128)S(1)} %get-tuple-element.10), channel_id=1, source_target_pairs={{0,128},{128,0},{256,384},{384,256},{1,129},{129,1},{257,385},{385... | collective-permute-start | bytes 98312 | tf_op jit(solution)/shard_map/ppermute | solution.py:27
  58.8 8.2 %collective-permute-done.5 = f32[16,512]{1,0:T(8,128)S(1)} collective-permute-done((f32[16,512]{1,0:T(8,128)S(1)}, f32[16,512]{1,0:T(8,128)S(1)}, u32[]{:S(2)}, u32[]{:S(2)}) %collective-permute-start.5) | collective-permute-done | bytes 32800 | tf_op jit(solution)/shard_map/ppermute | solution.py:27
  67.0 7.5 %collective-permute-start.6 = (f32[16,512]{1,0:T(8,128)S(1)}, f32[16,512]{1,0:T(8,128)S(1)}, u32[]{:S(2)}, u32[]{:S(2)}) collective-permute-start(f32[16,512]{1,0:T(8,128)S(1)} %add.29), channel_id=1, source_target_pairs={{0,256},{128,384},{256,0},{384,128},{1,257},{129,385},{257,1},{385... | collective-permute-start | bytes 98312 | tf_op jit(solution)/shard_map/ppermute | solution.py:27
  74.5 2.2 %collective-permute-done.6 = f32[16,512]{1,0:T(8,128)S(1)} collective-permute-done((f32[16,512]{1,0:T(8,128)S(1)}, f32[16,512]{1,0:T(8,128)S(1)}, u32[]{:S(2)}, u32[]{:S(2)}) %collective-permute-start.6) | collective-permute-done | bytes 32800 | tf_op jit(solution)/shard_map/ppermute | solution.py:27
  76.7 0.6 add.30.refs_2_.right_ref
  77.3 0.7 copy-done.7
  78.0 1.1 copy-done.1
  79.1 1.9 %collective-permute-start.7 = (bf16[4,320,512]{2,1,0:T(8,128)(2,1)}, bf16[4,320,512]{2,1,0:T(8,128)(2,1)S(1)}, u32[]{:S(2)}, u32[]{:S(2)}) collective-permute-start(bf16[4,320,512]{2,1,0:T(8,128)(2,1)} %shard_map.104.own_ref), channel_id=1, source_target_pairs={{0,16},{16,0},{1,17},{17,1},{2,18},{18,2},{3,19},{19,3},{4,20},{20... | collective-permute-start | bytes 3932168 | tf_op jit(solution)/shard_map/ppermute | solution.py:27
  81.0 3.2 %collective-permute-done.7.other_ref = bf16[4,320,512]{2,1,0:T(8,128)(2,1)S(1)} collective-permute-done((bf16[4,320,512]{2,1,0:T(8,128)(2,1)}, bf16[4,320,512]{2,1,0:T(8,128)(2,1)S(1)}, u32[]{:S(2)}, u32[]{:S(2)}) %collective-permute-start.7) | collective-permute-done | bytes 1310752 | tf_op jit(solution)/shard_map/ppermute | solution.py:27
  84.2 1.3 copy-done.2
  85.5 0.9 copy-done.8
  86.5 3.1 %shard_map.105 = (bf16[4,128,1152]{2,1,0:T(8,128)(2,1)}, f32[16,512]{1,0:T(8,128)S(1)}) custom-call(s32[3]{0:T(128)S(1)} %pad_add_fusion.place_ref, bf16[4,320,512]{2,1,0:T(8,128)(2,1)S(1)} %copy-done.2, bf16[4,320,512]{2,1,0:T(8,128)(2,1)S(1)} %collective-permute-done.7.other_ref, bf16[2,128,512]{2,1,0:T(8,128)(2,1)S(1)} %pad_maximum_fusion.c0_ref, ...), custom_call_target="tpu_custom_call" | custom-call | flops 1073741824 | bytes 5242880 | tf_op jit(solution)/shard_map/pallas_call | solution.py:163
  89.6 8.9 %all-to-all-start.2 = ((bf16[64,8,1152]{2,1,0:T(8,128)(2,1)}), bf16[64,8,1152]{2,1,0:T(8,128)(2,1)S(1)}, u32[]{:S(2)}, u32[]{:S(2)}) async-start(bf16[64,8,1152]{2,1,0:T(8,128)(2,1)} %bitcast.8), calls=%async_computation.2 | async-start | bytes 2359296 | tf_op jit(solution)/shard_map/all_to_all | solution.py:170
  98.5 1.9 %collective-permute-start.8 = (f32[16,512]{1,0:T(8,128)S(1)}, f32[16,512]{1,0:T(8,128)S(1)}, u32[]{:S(2)}, u32[]{:S(2)}) collective-permute-start(f32[16,512]{1,0:T(8,128)S(1)} %get-tuple-element.13), channel_id=1, source_target_pairs={{0,16},{16,0},{1,17},{17,1},{2,18},{18,2},{3,19},{19,3},{4,20},{20... | collective-permute-start | bytes 98312 | tf_op jit(solution)/shard_map/ppermute | solution.py:27
  100.4 1.2 collective-permute-done.8
  101.6 2.8 %collective-permute-start.9 = (f32[16,512]{1,0:T(8,128)S(1)}, f32[16,512]{1,0:T(8,128)S(1)}, u32[]{:S(2)}, u32[]{:S(2)}) collective-permute-start(f32[16,512]{1,0:T(8,128)S(1)} %add.33), channel_id=1, source_target_pairs={{0,32},{32,0},{64,96},{96,64},{1,33},{33,1},{65,97},{97,65},{2,34}... | collective-permute-start | bytes 98312 | tf_op jit(solution)/shard_map/ppermute | solution.py:27
  104.4 3.0 %collective-permute-done.9 = f32[16,512]{1,0:T(8,128)S(1)} collective-permute-done((f32[16,512]{1,0:T(8,128)S(1)}, f32[16,512]{1,0:T(8,128)S(1)}, u32[]{:S(2)}, u32[]{:S(2)}) %collective-permute-start.9) | collective-permute-done | bytes 32800 | tf_op jit(solution)/shard_map/ppermute | solution.py:27
  107.4 3.4 %collective-permute-start.10 = (f32[16,512]{1,0:T(8,128)S(1)}, f32[16,512]{1,0:T(8,128)S(1)}, u32[]{:S(2)}, u32[]{:S(2)}) collective-permute-start(f32[16,512]{1,0:T(8,128)S(1)} %add.34), channel_id=1, source_target_pairs={{0,64},{32,96},{64,0},{96,32},{1,65},{33,97},{65,1},{97,33},{2,66}... | collective-permute-start | bytes 98312 | tf_op jit(solution)/shard_map/ppermute | solution.py:27
  110.8 3.9 %collective-permute-done.10 = f32[16,512]{1,0:T(8,128)S(1)} collective-permute-done((f32[16,512]{1,0:T(8,128)S(1)}, f32[16,512]{1,0:T(8,128)S(1)}, u32[]{:S(2)}, u32[]{:S(2)}) %collective-permute-start.10) | collective-permute-done | bytes 32800 | tf_op jit(solution)/shard_map/ppermute | solution.py:27
  114.7 0.6 add_multiply_fusion
  115.3 16.3 %all-to-all-done.2 = bf16[64,8,1152]{2,1,0:T(8,128)(2,1)S(1)} async-done(((bf16[64,8,1152]{2,1,0:T(8,128)(2,1)}), bf16[64,8,1152]{2,1,0:T(8,128)(2,1)S(1)}, u32[]{:S(2)}, u32[]{:S(2)}) %all-to-all-start.2) | async-done | bytes 1179680 | tf_op jit(solution)/shard_map/all_to_all | solution.py:170
  131.6 0.1 convert_reduce_fusion.1
  131.7 0.1 slice_add_fusion
  131.8 0.6 fusion.5
  132.3 0.1 fusion.6
  132.4 0.1 convert_reduce_fusion
  132.6 0.8 fusion
  133.4 0.6 maximum_multiply_fusion
  (28 shorter events, 0.1 us)
Async XLA Ops:
  0.6 7.3 %copy-start = (bf16[8192,16]{0,1:T(8,128)(2,1)S(1)}, bf16[8192,16]{0,1:T(8,128)(2,1)}, u32[]{:S(2)}) copy-start(bf16[8192,16]{0,1:T(8,128)(2,1)} %param.10) | copy-start | bytes 786436
  0.6 45.0 %copy-start.5 = (bf16[256,512]{1,0:T(8,128)(2,1)S(1)}, bf16[256,512]{1,0:T(8,128)(2,1)}, u32[]{:S(2)}) copy-start(bf16[256,512]{1,0:T(8,128)(2,1)} %weight_ref.1) | copy-start | bytes 786436
  0.7 45.0 %copy-start.4 = (bf16[128,512]{1,0:T(8,128)(2,1)S(1)}, bf16[128,512]{1,0:T(8,128)(2,1)}, u32[]{:S(2)}) copy-start(bf16[128,512]{1,0:T(8,128)(2,1)} %cot_ref.3) | copy-start | bytes 393220
  0.7 45.0 %copy-start.6 = (bf16[8,8192]{1,0:T(8,128)(2,1)S(1)}, bf16[8,8192]{1,0:T(8,128)(2,1)}, u32[]{:S(2)}) copy-start(bf16[8,8192]{1,0:T(8,128)(2,1)} %inputs_ref.1) | copy-start | bytes 393220
  1.7 35.6 %collective-permute-start.1 = (bf16[128,512]{1,0:T(8,128)(2,1)S(1)}, bf16[128,512]{1,0:T(8,128)(2,1)S(1)}, u32[]{:S(2)}, u32[]{:S(2)}) collective-permute-start(bf16[128,512]{1,0:T(8,128)(2,1)S(1)} %dynamic-slice_bitcast_fusion), channel_id=1, source_target_pairs={{0,8},{8,0},{1,9},{9,1},{2,10},{10,2},{3,11},{11,3},{4,12},{12,4},... | collective-permute-start | bytes 393224 | tf_op jit(solution)/shard_map/ppermute | solution.py:27
  6.0 7.1 %collective-permute-start = (bf16[128,512]{1,0:T(8,128)(2,1)}, bf16[128,512]{1,0:T(8,128)(2,1)S(1)}, u32[]{:S(2)}, u32[]{:S(2)}) collective-permute-start(bf16[128,512]{1,0:T(8,128)(2,1)} %cot_ref.3), channel_id=1, source_target_pairs={{0,8},{8,0},{1,9},{9,1},{2,10},{10,2},{3,11},{11,3},{4,12},{12,4},... | collective-permute-start | bytes 393224 | tf_op jit(solution)/shard_map/ppermute | solution.py:27
  14.0 31.7 %collective-permute-start.3 = (bf16[2,128,512]{2,1,0:T(8,128)(2,1)S(1)}, bf16[2,128,512]{2,1,0:T(8,128)(2,1)S(1)}, u32[]{:S(2)}, u32[]{:S(2)}) collective-permute-start(bf16[2,128,512]{2,1,0:T(8,128)(2,1)S(1)} %pad_maximum_fusion.c0_ref), channel_id=1, source_target_pairs={{0,384},{128,256},{256,128},{384,0},{1,385},{129,257},{257,129},{3... | collective-permute-start | bytes 786440 | tf_op jit(solution)/shard_map/ppermute | solution.py:27
  24.0 21.7 %collective-permute-start.2 = (bf16[2,128,512]{2,1,0:T(8,128)(2,1)S(1)}, bf16[2,128,512]{2,1,0:T(8,128)(2,1)S(1)}, u32[]{:S(2)}, u32[]{:S(2)}) collective-permute-start(bf16[2,128,512]{2,1,0:T(8,128)(2,1)S(1)} %pad_maximum_fusion.c0_ref), channel_id=1, source_target_pairs={{0,128},{128,0},{256,384},{384,256},{1,129},{129,1},{257,385},{385... | collective-permute-start | bytes 786440 | tf_op jit(solution)/shard_map/ppermute | solution.py:27
  27.1 0.9 copy-start.3
  28.1 0.7 copy-start.10
  29.6 16.1 %all-to-all-start = ((f32[16,8,128]{2,1,0:T(8,128)}), f32[16,8,128]{2,1,0:T(8,128)S(1)}, u32[]{:S(2)}, u32[]{:S(2)}) async-start(f32[16,8,128]{2,1,0:T(8,128)} %shard_map.102.sent_ref), calls=%async_computation | async-start | bytes 131072 | tf_op jit(solution)/shard_map/all_to_all | solution.py:148
  47.8 29.5 %all-to-all-start.1 = ((bf16[4,320,512]{2,1,0:T(8,128)(2,1)}), bf16[4,320,512]{2,1,0:T(8,128)(2,1)S(1)}, u32[]{:S(2)}, u32[]{:S(2)}) async-start(bf16[4,320,512]{2,1,0:T(8,128)(2,1)} %get-tuple-element.9), calls=%async_computation.1 | async-start | bytes 2621440 | tf_op jit(solution)/shard_map/all_to_all | solution.py:158
  52.6 24.7 %collective-permute-start.4 = (bf16[2,128,512]{2,1,0:T(8,128)(2,1)S(1)}, bf16[2,128,512]{2,1,0:T(8,128)(2,1)S(1)}, u32[]{:S(2)}, u32[]{:S(2)}) collective-permute-start(bf16[2,128,512]{2,1,0:T(8,128)(2,1)S(1)} %pad_maximum_fusion.c0_ref), channel_id=1, source_target_pairs={{0,256},{128,384},{256,0},{384,128},{1,257},{129,385},{257,1},{385... | collective-permute-start | bytes 786440 | tf_op jit(solution)/shard_map/ppermute | solution.py:27
  56.3 10.6 %collective-permute-start.5 = (f32[16,512]{1,0:T(8,128)S(1)}, f32[16,512]{1,0:T(8,128)S(1)}, u32[]{:S(2)}, u32[]{:S(2)}) collective-permute-start(f32[16,512]{1,0:T(8,128)S(1)} %get-tuple-element.10), channel_id=1, source_target_pairs={{0,128},{128,0},{256,384},{384,256},{1,129},{129,1},{257,385},{385... | collective-permute-start | bytes 98312 | tf_op jit(solution)/shard_map/ppermute | solution.py:27
  67.0 9.7 %collective-permute-start.6 = (f32[16,512]{1,0:T(8,128)S(1)}, f32[16,512]{1,0:T(8,128)S(1)}, u32[]{:S(2)}, u32[]{:S(2)}) collective-permute-start(f32[16,512]{1,0:T(8,128)S(1)} %add.29), channel_id=1, source_target_pairs={{0,256},{128,384},{256,0},{384,128},{1,257},{129,385},{257,1},{385... | collective-permute-start | bytes 98312 | tf_op jit(solution)/shard_map/ppermute | solution.py:27
  77.3 6.9 %copy-start.9 = (f32[16,512]{1,0:T(8,128)S(1)}, f32[16,512]{1,0:T(8,128)}, u32[]{:S(2)}) copy-start(f32[16,512]{1,0:T(8,128)} %add.30.refs_2_.right_ref) | copy-start | bytes 98308
  77.3 0.7 copy-start.7
  78.0 1.1 copy-start.1
  79.1 5.1 %collective-permute-start.7 = (bf16[4,320,512]{2,1,0:T(8,128)(2,1)}, bf16[4,320,512]{2,1,0:T(8,128)(2,1)S(1)}, u32[]{:S(2)}, u32[]{:S(2)}) collective-permute-start(bf16[4,320,512]{2,1,0:T(8,128)(2,1)} %shard_map.104.own_ref), channel_id=1, source_target_pairs={{0,16},{16,0},{1,17},{17,1},{2,18},{18,2},{3,19},{19,3},{4,20},{20... | collective-permute-start | bytes 3932168 | tf_op jit(solution)/shard_map/ppermute | solution.py:27
  84.2 1.3 copy-start.2
  85.5 0.9 copy-start.8
  89.6 42.2 %copy-start.11 = (s32[16]{0:T(128)S(1)}, s32[16]{0:T(128)}, u32[]{:S(2)}) copy-start(s32[16]{0:T(128)} %param.13) | copy-start | bytes 196
  89.6 42.0 %all-to-all-start.2 = ((bf16[64,8,1152]{2,1,0:T(8,128)(2,1)}), bf16[64,8,1152]{2,1,0:T(8,128)(2,1)S(1)}, u32[]{:S(2)}, u32[]{:S(2)}) async-start(bf16[64,8,1152]{2,1,0:T(8,128)(2,1)} %bitcast.8), calls=%async_computation.2 | async-start | bytes 2359296 | tf_op jit(solution)/shard_map/all_to_all | solution.py:170
  98.5 3.1 %collective-permute-start.8 = (f32[16,512]{1,0:T(8,128)S(1)}, f32[16,512]{1,0:T(8,128)S(1)}, u32[]{:S(2)}, u32[]{:S(2)}) collective-permute-start(f32[16,512]{1,0:T(8,128)S(1)} %get-tuple-element.13), channel_id=1, source_target_pairs={{0,16},{16,0},{1,17},{17,1},{2,18},{18,2},{3,19},{19,3},{4,20},{20... | collective-permute-start | bytes 98312 | tf_op jit(solution)/shard_map/ppermute | solution.py:27
  101.6 5.8 %collective-permute-start.9 = (f32[16,512]{1,0:T(8,128)S(1)}, f32[16,512]{1,0:T(8,128)S(1)}, u32[]{:S(2)}, u32[]{:S(2)}) collective-permute-start(f32[16,512]{1,0:T(8,128)S(1)} %add.33), channel_id=1, source_target_pairs={{0,32},{32,0},{64,96},{96,64},{1,33},{33,1},{65,97},{97,65},{2,34}... | collective-permute-start | bytes 98312 | tf_op jit(solution)/shard_map/ppermute | solution.py:27
  107.4 7.3 %collective-permute-start.10 = (f32[16,512]{1,0:T(8,128)S(1)}, f32[16,512]{1,0:T(8,128)S(1)}, u32[]{:S(2)}, u32[]{:S(2)}) collective-permute-start(f32[16,512]{1,0:T(8,128)S(1)} %add.34), channel_id=1, source_target_pairs={{0,64},{32,96},{64,0},{96,32},{1,65},{33,97},{65,1},{97,33},{2,66}... | collective-permute-start | bytes 98312 | tf_op jit(solution)/shard_map/ppermute | solution.py:27

commit v3 on v2

--- a/solution.py
+++ b/solution.py
@@ -48,7 +48,7 @@
     )(a, *others)
 
 
-def rank_kernel(cot_ref, right_ref, projected_ref, after_ref, out_ref):
+def rank_kernel(cot_ref, right_ref, projected_ref, out_ref):
     back = dot_t(cot_ref[...], right_ref[...])
     projected = projected_ref[...]
     out_ref[...] = jnp.zeros((16, 8, 128), f32)
@@ -58,7 +58,7 @@
 
 def pack_kernel(
     place_ref, sent_ref, rank_ref, coeff_ref, cot_ref, weight_ref, got_ref, inputs_ref, after1, after3,
-    x_ref, back_ref, right_ref,
+    x_ref, back_ref,
 ):
     lane = lax.broadcasted_iota(jnp.int32, (1, 128), 1)
     rank = rank_ref[...]
@@ -67,7 +67,9 @@
     back = (own * coeff).astype(bf16)
     back_ref[...] = back
     fwd = (jnp.where((lane >= 16) & (lane < 32), rank, 0.0) * coeff).astype(bf16)
-    right_ref[...] = t_dot(fwd.reshape(128, 128), cot_ref[...])[16:32]
+    right = t_dot(fwd.reshape(128, 128), cot_ref[...])[16:32]
+    right_high = right.astype(bf16)
+    right_low = (right - right_high.astype(f32)).astype(bf16)
     projected = pltpu.roll(sent_ref[0], 112, 1)
     singular = jnp.sum(projected * own, axis=0, keepdims=True)
     high = singular.astype(bf16).astype(f32)
@@ -92,19 +94,37 @@
         rows = [inputs[:, (h * 4 + x) * 512 : (h * 4 + x + 1) * 512] for h in range(4)]
         x_ref[x, 256:288, :] = jnp.concatenate(rows, axis=0).astype(bf16)
         x_ref[x, 288:320, :] = small
-
-
-def terms_kernel(place_ref, own_ref, other_ref, c0_ref, c1_ref, c2_ref, c3_ref, right_ref, out_ref, right_out_ref):
+        x_ref[x, 320:336, :] = right_high
+        x_ref[x, 336:352, :] = right_low
+
+
+def products(parts, ref):
+    total = dot_t(parts[0], ref[:, 0:128, :].reshape(512, 512))
+    total += dot_t(parts[1], ref[:, 128:256, :].reshape(512, 512))
+    return total.astype(bf16).reshape(4, 128, 512)
+
+
+def stacked(cots):
+    return [jnp.concatenate([c[half] for c in cots], axis=0) for half in (0, 1)]
+
+
+def own_kernel(own_ref, c0_ref, c1_ref, c2_ref, c3_ref, out_ref):
+    out_ref[...] = products(stacked((c0_ref, c1_ref, c2_ref, c3_ref)), own_ref)
+
+
+def other_kernel(
+    place_ref, done_ref, own_ref, other_ref, c0_ref, c1_ref, c2_ref, c3_ref, out_ref, right_ref
+):
     core, z_high = place_ref[0], place_ref[2]
-    right_out_ref[...] = right_ref[...]
-    cots = (c0_ref, c1_ref, c2_ref, c3_ref)
-    parts = [jnp.concatenate([c[half] for c in cots], axis=0) for half in (0, 1)]
-    for s, ref in enumerate((own_ref, other_ref)):
-        total = dot_t(parts[0], ref[:, 0:128, :].reshape(512, 512))
-        total += dot_t(parts[1], ref[:, 128:256, :].reshape(512, 512))
-        total = total.astype(bf16).reshape(4, 128, 512)
-        for k in range(4):
-            out_ref[z_high ^ k, :, s * 512 : (s + 1) * 512] = total[k]
+    total = products(stacked((c0_ref, c1_ref, c2_ref, c3_ref)), other_ref)
+    for k in range(4):
+        out_ref[z_high ^ k, :, 0:512] = done_ref[k]
+        out_ref[z_high ^ k, :, 512:1024] = total[k]
+    right = jnp.zeros((16, 512), f32)
+    for ref in (own_ref, other_ref):
+        for x in range(4):
+            right += ref[x, 320:336, :].astype(f32) + ref[x, 336:352, :].astype(f32)
+    right_ref[...] = right
     tok, back, singular = [], [], jnp.zeros((1, 128), f32)
     for ref in (own_ref, other_ref):
         for x in range(4):
@@ -143,34 +163,32 @@
 
     own_projected = jnp.dot(inputs, left_factor, preferred_element_type=f32)
     rank_out = call(
-        rank_kernel, shape((16, 8, 128), f32), [in_vmem] * 3 + [unread], 6 << 20, 1 << 20
-    )(cotangent, right_factor, own_projected, cot_other)
+        rank_kernel, shape((16, 8, 128), f32), [in_vmem] * 3, 6 << 20, 1 << 20
+    )(cotangent, right_factor, own_projected)
     rank_in = lax.all_to_all(rank_out, ("zl", "y"), 0, 0)
 
     coeff_lanes = jnp.pad(jnp.concatenate([coeff, coeff]), (0, 96)).reshape(1, 128)
-    x_out, scaled_back, right_part = call(
+    x_out, scaled_back = call(
         pack_kernel,
-        (shape((4, 320, 512), bf16), shape((8, 128), bf16), shape((16, 512), f32)),
+        (shape((4, 352, 512), bf16), shape((8, 128), bf16)),
         [in_smem] + [in_vmem] * 7 + [unread] * 2,
         16 << 20,
         3 << 20,
     )(place, rank_out, rank_in, coeff_lanes, cotangent, weight, got, inputs, cots[1], cots[3])
     x_in = lax.all_to_all(x_out, "x", 0, 0)
-    right_part = right_part + swap(right_part, "zh", 4, 1)
-    right_part = right_part + swap(right_part, "zh", 4, 2)
-    x_in = after(x_in, cots[2], right_part)
-
+    x_in = after(x_in, cots[2])
+    x_other = swap(x_in, "c", 2, 1)
+
+    done = call(own_kernel, shape((4, 128, 512), bf16), [in_vmem] * 5, 1 << 29, 3 << 20)(x_in, *cots)
     out, right_part = call(
-        terms_kernel,
+        other_kernel,
         (shape((4, 128, 1152), bf16), shape((16, 512), f32)),
         [in_smem] + [in_vmem] * 7,
-        1 << 30,
+        1 << 29,
         5 << 20,
-    )(place, x_in, swap(x_in, "c", 2, 1), *cots, right_part)
+    )(place, done, x_in, x_other, *cots)
     back = lax.all_to_all(out.reshape(64, 8, 1152), ("zh", "zl", "y"), 0, 0)
-    right_part = right_part + swap(right_part, "c", 2, 1)
-    right_part = right_part + swap(right_part, "x", 4, 1)
-    right_sum = right_part + swap(right_part, "x", 4, 2)
+    right_sum = right_part + sum(swap(right_part, "zh", 4, k) for k in (1, 2, 3))
 
     summed = jnp.sum(back[:, :, :1024].reshape(4, 2, 8, 8, 1024).astype(f32), axis=2)
     summed = summed.reshape(4, 2, 8, 2, 4, 128)

time: 135 us -> 127 us (0.941)
  starting transfers between devices: 63.6 us -> 59.5 us
  waiting for transfers between devices: 50.4 us -> 46.3 us
  local copies, waits for them, and re-layouts: 6.77 us -> 9.11 us
    ppermute x11 -> x9, waiting for transfers between devices: 25.7 us -> 44.3 us  [swap(): return lax.ppermute(a, axis, [(i, i ^ mask) for i in range(count)])]
    all_to_all x1, waiting for transfers between devices: 16.3 us -> 2.06 us  [body(): back = lax.all_to_all(out.reshape(64, 8, 1152), ('zh', 'zl', 'y'), 0, 0)]
    all_to_all x1, waiting for transfers between devices: 8.37 us -> 0.01 us  [body(): rank_in = lax.all_to_all(rank_out, ('zl', 'y'), 0, 0)]
    ppermute x11 -> x9, starting transfers between devices: 42.3 us -> 37 us  [swap(): return lax.ppermute(a, axis, [(i, i ^ mask) for i in range(count)])]
    unnamed x24 -> x28, local copies, waits for them, and re-layouts: 5.69 us -> 8.1 us
    all_to_all x1, starting transfers between devices: 8.92 us -> 10.5 us  [body(): back = lax.all_to_all(out.reshape(64, 8, 1152), ('zh', 'zl', 'y'), 0, 0)]
    pallas_call x3 -> x4, Pallas kernels: 5.97 us -> 5.12 us  [the longest x1 2.54 us: body(): call(other_kernel, (shape((4, 128, 1152), bf16), shape((16, 512), f32)),...]
  transfers between devices with their start and end apart: 14 -> 12, of which waited for: 9 -> 7; matrix products, arithmetic and copies ran while one was open for 3% -> 3% of each run, Pallas kernels for 1% -> 1%
where the time goes in v3:
time: 127 us; the launch traced here: 126 us
  starting transfers between devices  59.5 us (47%)
  waiting for transfers between devices  46.3 us (36%)
  local copies, waits for them, and re-layouts  9.11 us (7%)
  Pallas kernels  5.12 us (4%)
  other arithmetic  3.21 us (3%)
  matrix products  1.92 us (2%)
    ppermute x9, waiting for transfers between devices, swap(): return lax.ppermute(a, axis, [(i, i ^ mask) for i in range(count)])  44.3 us
    ppermute x9, starting transfers between devices, swap(): return lax.ppermute(a, axis, [(i, i ^ mask) for i in range(count)])  37 us
    all_to_all x1, starting transfers between devices, body(): back = lax.all_to_all(out.reshape(64, 8, 1152), ('zh', 'zl', 'y'), 0, 0)  10.5 us
    unnamed x28, local copies, waits for them, and re-layouts  8.1 us
    all_to_all x1, starting transfers between devices, body(): rank_in = lax.all_to_all(rank_out, ('zl', 'y'), 0, 0)  7.2 us
    all_to_all x1, starting transfers between devices, body(): x_in = lax.all_to_all(x_out, 'x', 0, 0)  4.77 us
    pallas_call x1, Pallas kernels, body(): call(other_kernel, (shape((4, 128, 1152), bf16), shape((16, 512), f32)),...  2.54 us
  transfers between devices with their start and end apart: 12, of which 7 were waited for; matrix products, arithmetic and copies ran while one was open for 3% of the time, Pallas kernels for 1%

profile of v3, /device:TPU:6, one launch (start us, length us, event | category | flops | bytes accessed | tf_op | source)
XLA Modules:
  0.0 126.1 jit_solution(10459456813880098376)
XLA Ops:
  0.6 0.0 copy-start
  0.6 0.0 copy-start.8
  0.7 0.0 copy-start.9
  0.7 4.4 %collective-permute-start.1 = (bf16[128,512]{1,0:T(8,128)(2,1)}, bf16[128,512]{1,0:T(8,128)(2,1)S(1)}, u32[]{:S(2)}, u32[]{:S(2)}) collective-permute-start(bf16[128,512]{1,0:T(8,128)(2,1)} %cot_ref.3), channel_id=1, source_target_pairs={{0,8},{8,0},{1,9},{9,1},{2,10},{10,2},{3,11},{11,3},{4,12},{12,4},... | collective-permute-start | bytes 393224 | tf_op jit(solution)/shard_map/ppermute | solution.py:27
  5.1 1.1 fusion.7.projected_ref
  6.2 0.9 copy-done.7
  7.1 0.7 copy-done.11
  7.9 0.8 shard_map.102.sent_ref
  8.7 7.2 %all-to-all-start = ((f32[16,8,128]{2,1,0:T(8,128)}), f32[16,8,128]{2,1,0:T(8,128)S(1)}, u32[]{:S(2)}, u32[]{:S(2)}) async-start(f32[16,8,128]{2,1,0:T(8,128)} %shard_map.102.sent_ref), calls=%async_computation | async-start | bytes 131072 | tf_op jit(solution)/shard_map/all_to_all | solution.py:168
  15.9 0.9 dynamic-slice_bitcast_fusion
  16.8 3.8 %collective-permute-start = (bf16[128,512]{1,0:T(8,128)(2,1)S(1)}, bf16[128,512]{1,0:T(8,128)(2,1)S(1)}, u32[]{:S(2)}, u32[]{:S(2)}) collective-permute-start(bf16[128,512]{1,0:T(8,128)(2,1)S(1)} %dynamic-slice_bitcast_fusion), channel_id=1, source_target_pairs={{0,8},{8,0},{1,9},{9,1},{2,10},{10,2},{3,11},{11,3},{4,12},{12,4},... | collective-permute-start | bytes 393224 | tf_op jit(solution)/shard_map/ppermute | solution.py:27
  20.6 0.9 pad_maximum_fusion.c0_ref
  21.6 10.0 %collective-permute-start.3 = (bf16[2,128,512]{2,1,0:T(8,128)(2,1)S(1)}, bf16[2,128,512]{2,1,0:T(8,128)(2,1)S(1)}, u32[]{:S(2)}, u32[]{:S(2)}) collective-permute-start(bf16[2,128,512]{2,1,0:T(8,128)(2,1)S(1)} %pad_maximum_fusion.c0_ref), channel_id=1, source_target_pairs={{0,384},{128,256},{256,128},{384,0},{1,385},{129,257},{257,129},{3... | collective-permute-start | bytes 786440 | tf_op jit(solution)/shard_map/ppermute | solution.py:27
  31.6 2.5 %collective-permute-start.2 = (bf16[2,128,512]{2,1,0:T(8,128)(2,1)S(1)}, bf16[2,128,512]{2,1,0:T(8,128)(2,1)S(1)}, u32[]{:S(2)}, u32[]{:S(2)}) collective-permute-start(bf16[2,128,512]{2,1,0:T(8,128)(2,1)S(1)} %pad_maximum_fusion.c0_ref), channel_id=1, source_target_pairs={{0,128},{128,0},{256,384},{384,256},{1,129},{129,1},{257,385},{385... | collective-permute-start | bytes 786440 | tf_op jit(solution)/shard_map/ppermute | solution.py:27
  34.1 0.1 fusion.4.coeff_ref
  34.2 0.1 pad_add_fusion.place_ref
  34.3 7.2 %collective-permute-done.3.after3.c3_ref = bf16[2,128,512]{2,1,0:T(8,128)(2,1)S(1)} collective-permute-done((bf16[2,128,512]{2,1,0:T(8,128)(2,1)S(1)}, bf16[2,128,512]{2,1,0:T(8,128)(2,1)S(1)}, u32[]{:S(2)}, u32[]{:S(2)}) %collective-permute-start.3) | collective-permute-done | bytes 262176 | tf_op jit(solution)/shard_map/ppermute | solution.py:27
  41.5 5.0 %collective-permute-done.2.after1.c1_ref = bf16[2,128,512]{2,1,0:T(8,128)(2,1)S(1)} collective-permute-done((bf16[2,128,512]{2,1,0:T(8,128)(2,1)S(1)}, bf16[2,128,512]{2,1,0:T(8,128)(2,1)S(1)}, u32[]{:S(2)}, u32[]{:S(2)}) %collective-permute-start.2) | collective-permute-done | bytes 262176 | tf_op jit(solution)/shard_map/ppermute | solution.py:27
  46.5 0.9 copy-done.10
  47.4 1.1 shard_map.103
  48.5 1.1 copy-done.6
  49.6 4.8 %all-to-all-start.1 = ((bf16[4,352,512]{2,1,0:T(8,128)(2,1)}), bf16[4,352,512]{2,1,0:T(8,128)(2,1)S(1)}, u32[]{:S(2)}, u32[]{:S(2)}) async-start(bf16[4,352,512]{2,1,0:T(8,128)(2,1)} %copy-done.6), calls=%async_computation.1 | async-start | bytes 2883584 | tf_op jit(solution)/shard_map/all_to_all | solution.py:178
  54.4 2.2 %collective-permute-start.4 = (bf16[2,128,512]{2,1,0:T(8,128)(2,1)S(1)}, bf16[2,128,512]{2,1,0:T(8,128)(2,1)S(1)}, u32[]{:S(2)}, u32[]{:S(2)}) collective-permute-start(bf16[2,128,512]{2,1,0:T(8,128)(2,1)S(1)} %pad_maximum_fusion.c0_ref), channel_id=1, source_target_pairs={{0,256},{128,384},{256,0},{384,128},{1,257},{129,385},{257,1},{385... | collective-permute-start | bytes 786440 | tf_op jit(solution)/shard_map/ppermute | solution.py:27
  56.5 13.3 %collective-permute-done.4.refs_1_.c2_ref = bf16[2,128,512]{2,1,0:T(8,128)(2,1)S(1)} collective-permute-done((bf16[2,128,512]{2,1,0:T(8,128)(2,1)S(1)}, bf16[2,128,512]{2,1,0:T(8,128)(2,1)S(1)}, u32[]{:S(2)}, u32[]{:S(2)}) %collective-permute-start.4) | collective-permute-done | bytes 262176 | tf_op jit(solution)/shard_map/ppermute | solution.py:27
  69.8 0.7 copy-done.4
  70.5 1.1 copy-done.1
  71.6 1.9 %collective-permute-start.5 = (bf16[4,352,512]{2,1,0:T(8,128)(2,1)}, bf16[4,352,512]{2,1,0:T(8,128)(2,1)S(1)}, u32[]{:S(2)}, u32[]{:S(2)}) collective-permute-start(bf16[4,352,512]{2,1,0:T(8,128)(2,1)} %shard_map.104.own_ref), channel_id=1, source_target_pairs={{0,16},{16,0},{1,17},{17,1},{2,18},{18,2},{3,19},{19,3},{4,20},{20... | collective-permute-start | bytes 4325384 | tf_op jit(solution)/shard_map/ppermute | solution.py:27
  73.6 1.4 %copy-done.2 = bf16[4,352,512]{2,1,0:T(8,128)(2,1)S(1)} copy-done((bf16[4,352,512]{2,1,0:T(8,128)(2,1)S(1)}, bf16[4,352,512]{2,1,0:T(8,128)(2,1)}, u32[]{:S(2)}) %copy-start.2) | copy-done | bytes 1441816
  74.9 0.9 copy-done.5
  75.9 0.7 shard_map.105.done_ref
  76.6 0.3 collective-permute-done.5.other_ref
  77.0 0.3 copy-done.3
  77.2 2.5 %shard_map.106 = (bf16[4,128,1152]{2,1,0:T(8,128)(2,1)}, f32[16,512]{1,0:T(8,128)S(1)}) custom-call(s32[3]{0:T(128)S(1)} %pad_add_fusion.place_ref, bf16[4,128,512]{2,1,0:T(8,128)(2,1)S(1)} %shard_map.105.done_ref, bf16[4,352,512]{2,1,0:T(8,128)(2,1)S(1)} %copy-done.3, bf16[4,352,512]{2,1,0:T(8,128)(2,1)S(1)} %collective-permute-done.5.other_ref, ...), custom_call_target="tpu_custom_call" | custom-call | flops 536870912 | bytes 5242880 | tf_op jit(solution)/shard_map/pallas_call | solution.py:183
  79.8 10.5 %all-to-all-start.2 = ((bf16[64,8,1152]{2,1,0:T(8,128)(2,1)}), bf16[64,8,1152]{2,1,0:T(8,128)(2,1)S(1)}, u32[]{:S(2)}, u32[]{:S(2)}) async-start(bf16[64,8,1152]{2,1,0:T(8,128)(2,1)} %bitcast.8), calls=%async_computation.2 | async-start | bytes 2359296 | tf_op jit(solution)/shard_map/all_to_all | solution.py:190
  90.3 5.8 %collective-permute-start.8 = (f32[16,512]{1,0:T(8,128)S(1)}, f32[16,512]{1,0:T(8,128)S(1)}, u32[]{:S(2)}, u32[]{:S(2)}) collective-permute-start(f32[16,512]{1,0:T(8,128)S(1)} %get-tuple-element.11), channel_id=1, source_target_pairs={{0,384},{128,256},{256,128},{384,0},{1,385},{129,257},{257,129},{3... | collective-permute-start | bytes 98312 | tf_op jit(solution)/shard_map/ppermute | solution.py:27
  96.1 4.1 %collective-permute-start.7 = (f32[16,512]{1,0:T(8,128)S(1)}, f32[16,512]{1,0:T(8,128)S(1)}, u32[]{:S(2)}, u32[]{:S(2)}) collective-permute-start(f32[16,512]{1,0:T(8,128)S(1)} %get-tuple-element.11), channel_id=1, source_target_pairs={{0,256},{128,384},{256,0},{384,128},{1,257},{129,385},{257,1},{385... | collective-permute-start | bytes 98312 | tf_op jit(solution)/shard_map/ppermute | solution.py:27
  100.2 2.4 %collective-permute-start.6 = (f32[16,512]{1,0:T(8,128)S(1)}, f32[16,512]{1,0:T(8,128)S(1)}, u32[]{:S(2)}, u32[]{:S(2)}) collective-permute-start(f32[16,512]{1,0:T(8,128)S(1)} %get-tuple-element.11), channel_id=1, source_target_pairs={{0,128},{128,0},{256,384},{384,256},{1,129},{129,1},{257,385},{385... | collective-permute-start | bytes 98312 | tf_op jit(solution)/shard_map/ppermute | solution.py:27
  102.6 6.0 %collective-permute-done.7 = f32[16,512]{1,0:T(8,128)S(1)} collective-permute-done((f32[16,512]{1,0:T(8,128)S(1)}, f32[16,512]{1,0:T(8,128)S(1)}, u32[]{:S(2)}, u32[]{:S(2)}) %collective-permute-start.7) | collective-permute-done | bytes 32800 | tf_op jit(solution)/shard_map/ppermute | solution.py:27
  108.6 12.4 %collective-permute-done.6 = f32[16,512]{1,0:T(8,128)S(1)} collective-permute-done((f32[16,512]{1,0:T(8,128)S(1)}, f32[16,512]{1,0:T(8,128)S(1)}, u32[]{:S(2)}, u32[]{:S(2)}) %collective-permute-start.6) | collective-permute-done | bytes 32800 | tf_op jit(solution)/shard_map/ppermute | solution.py:27
  121.0 0.6 add_multiply_fusion
  121.6 2.1 %all-to-all-done.2 = bf16[64,8,1152]{2,1,0:T(8,128)(2,1)S(1)} async-done(((bf16[64,8,1152]{2,1,0:T(8,128)(2,1)}), bf16[64,8,1152]{2,1,0:T(8,128)(2,1)S(1)}, u32[]{:S(2)}, u32[]{:S(2)}) %all-to-all-start.2) | async-done | bytes 1179680 | tf_op jit(solution)/shard_map/all_to_all | solution.py:190
  123.7 0.1 convert_reduce_fusion.1
  123.7 0.1 slice_add_fusion
  123.8 0.6 fusion.5
  124.4 0.1 fusion.6
  124.5 0.1 convert_reduce_fusion
  124.7 0.8 fusion
  125.5 0.6 maximum_multiply_fusion
  (25 shorter events, 0.1 us)
Async XLA Ops:
  0.6 4.5 %copy-start = (bf16[8192,16]{0,1:T(8,128)(2,1)S(1)}, bf16[8192,16]{0,1:T(8,128)(2,1)}, u32[]{:S(2)}) copy-start(bf16[8192,16]{0,1:T(8,128)(2,1)} %param.10) | copy-start | bytes 786436
  0.6 45.9 %copy-start.8 = (bf16[128,512]{1,0:T(8,128)(2,1)S(1)}, bf16[128,512]{1,0:T(8,128)(2,1)}, u32[]{:S(2)}) copy-start(bf16[128,512]{1,0:T(8,128)(2,1)} %cot_ref.3) | copy-start | bytes 393220
  0.7 45.8 %copy-start.9 = (bf16[256,512]{1,0:T(8,128)(2,1)S(1)}, bf16[256,512]{1,0:T(8,128)(2,1)}, u32[]{:S(2)}) copy-start(bf16[256,512]{1,0:T(8,128)(2,1)} %weight_ref.1) | copy-start | bytes 786436
  0.7 33.4 %copy-start.13 = (s32[16]{0:T(128)S(1)}, s32[16]{0:T(128)}, u32[]{:S(2)}) copy-start(s32[16]{0:T(128)} %param.13) | copy-start | bytes 196
  0.7 33.4 %copy-start.12 = (f32[16]{0:T(128)S(1)}, f32[16]{0:T(128)}, u32[]{:S(2)}) copy-start(f32[16]{0:T(128)} %param.12) | copy-start | bytes 196
  0.7 19.9 %collective-permute-start.1 = (bf16[128,512]{1,0:T(8,128)(2,1)}, bf16[128,512]{1,0:T(8,128)(2,1)S(1)}, u32[]{:S(2)}, u32[]{:S(2)}) collective-permute-start(bf16[128,512]{1,0:T(8,128)(2,1)} %cot_ref.3), channel_id=1, source_target_pairs={{0,8},{8,0},{1,9},{9,1},{2,10},{10,2},{3,11},{11,3},{4,12},{12,4},... | collective-permute-start | bytes 393224 | tf_op jit(solution)/shard_map/ppermute | solution.py:27
  6.2 0.9 copy-start.7
  7.1 0.7 copy-start.11
  8.7 25.6 %all-to-all-start = ((f32[16,8,128]{2,1,0:T(8,128)}), f32[16,8,128]{2,1,0:T(8,128)S(1)}, u32[]{:S(2)}, u32[]{:S(2)}) async-start(f32[16,8,128]{2,1,0:T(8,128)} %shard_map.102.sent_ref), calls=%async_computation | async-start | bytes 131072 | tf_op jit(solution)/shard_map/all_to_all | solution.py:168
  16.8 17.5 %collective-permute-start = (bf16[128,512]{1,0:T(8,128)(2,1)S(1)}, bf16[128,512]{1,0:T(8,128)(2,1)S(1)}, u32[]{:S(2)}, u32[]{:S(2)}) collective-permute-start(bf16[128,512]{1,0:T(8,128)(2,1)S(1)} %dynamic-slice_bitcast_fusion), channel_id=1, source_target_pairs={{0,8},{8,0},{1,9},{9,1},{2,10},{10,2},{3,11},{11,3},{4,12},{12,4},... | collective-permute-start | bytes 393224 | tf_op jit(solution)/shard_map/ppermute | solution.py:27
  21.6 19.9 %collective-permute-start.3 = (bf16[2,128,512]{2,1,0:T(8,128)(2,1)S(1)}, bf16[2,128,512]{2,1,0:T(8,128)(2,1)S(1)}, u32[]{:S(2)}, u32[]{:S(2)}) collective-permute-start(bf16[2,128,512]{2,1,0:T(8,128)(2,1)S(1)} %pad_maximum_fusion.c0_ref), channel_id=1, source_target_pairs={{0,384},{128,256},{256,128},{384,0},{1,385},{129,257},{257,129},{3... | collective-permute-start | bytes 786440 | tf_op jit(solution)/shard_map/ppermute | solution.py:27
  31.6 14.9 %collective-permute-start.2 = (bf16[2,128,512]{2,1,0:T(8,128)(2,1)S(1)}, bf16[2,128,512]{2,1,0:T(8,128)(2,1)S(1)}, u32[]{:S(2)}, u32[]{:S(2)}) collective-permute-start(bf16[2,128,512]{2,1,0:T(8,128)(2,1)S(1)} %pad_maximum_fusion.c0_ref), channel_id=1, source_target_pairs={{0,128},{128,0},{256,384},{384,256},{1,129},{129,1},{257,385},{385... | collective-permute-start | bytes 786440 | tf_op jit(solution)/shard_map/ppermute | solution.py:27
  46.5 0.9 copy-start.10
  48.5 1.1 copy-start.6
  49.6 20.2 %all-to-all-start.1 = ((bf16[4,352,512]{2,1,0:T(8,128)(2,1)}), bf16[4,352,512]{2,1,0:T(8,128)(2,1)S(1)}, u32[]{:S(2)}, u32[]{:S(2)}) async-start(bf16[4,352,512]{2,1,0:T(8,128)(2,1)} %copy-done.6), calls=%async_computation.1 | async-start | bytes 2883584 | tf_op jit(solution)/shard_map/all_to_all | solution.py:178
  54.4 15.5 %collective-permute-start.4 = (bf16[2,128,512]{2,1,0:T(8,128)(2,1)S(1)}, bf16[2,128,512]{2,1,0:T(8,128)(2,1)S(1)}, u32[]{:S(2)}, u32[]{:S(2)}) collective-permute-start(bf16[2,128,512]{2,1,0:T(8,128)(2,1)S(1)} %pad_maximum_fusion.c0_ref), channel_id=1, source_target_pairs={{0,256},{128,384},{256,0},{384,128},{1,257},{129,385},{257,1},{385... | collective-permute-start | bytes 786440 | tf_op jit(solution)/shard_map/ppermute | solution.py:27
  69.8 0.7 copy-start.4
  70.5 1.1 copy-start.1
  71.6 5.3 %collective-permute-start.5 = (bf16[4,352,512]{2,1,0:T(8,128)(2,1)}, bf16[4,352,512]{2,1,0:T(8,128)(2,1)S(1)}, u32[]{:S(2)}, u32[]{:S(2)}) collective-permute-start(bf16[4,352,512]{2,1,0:T(8,128)(2,1)} %shard_map.104.own_ref), channel_id=1, source_target_pairs={{0,16},{16,0},{1,17},{17,1},{2,18},{18,2},{3,19},{19,3},{4,20},{20... | collective-permute-start | bytes 4325384 | tf_op jit(solution)/shard_map/ppermute | solution.py:27
  73.6 1.4 %copy-start.2 = (bf16[4,352,512]{2,1,0:T(8,128)(2,1)S(1)}, bf16[4,352,512]{2,1,0:T(8,128)(2,1)}, u32[]{:S(2)}) copy-start(bf16[4,352,512]{2,1,0:T(8,128)(2,1)} %shard_map.104.own_ref) | copy-start | bytes 4325380
  74.9 0.9 copy-start.5
  75.9 1.4 %copy-start.3 = (bf16[4,352,512]{2,1,0:T(8,128)(2,1)S(1)}, bf16[4,352,512]{2,1,0:T(8,128)(2,1)}, u32[]{:S(2)}) copy-start(bf16[4,352,512]{2,1,0:T(8,128)(2,1)} %shard_map.104.own_ref) | copy-start | bytes 4325380
  79.8 43.9 %all-to-all-start.2 = ((bf16[64,8,1152]{2,1,0:T(8,128)(2,1)}), bf16[64,8,1152]{2,1,0:T(8,128)(2,1)S(1)}, u32[]{:S(2)}, u32[]{:S(2)}) async-start(bf16[64,8,1152]{2,1,0:T(8,128)(2,1)} %bitcast.8), calls=%async_computation.2 | async-start | bytes 2359296 | tf_op jit(solution)/shard_map/all_to_all | solution.py:190
  90.3 12.3 %collective-permute-start.8 = (f32[16,512]{1,0:T(8,128)S(1)}, f32[16,512]{1,0:T(8,128)S(1)}, u32[]{:S(2)}, u32[]{:S(2)}) collective-permute-start(f32[16,512]{1,0:T(8,128)S(1)} %get-tuple-element.11), channel_id=1, source_target_pairs={{0,384},{128,256},{256,128},{384,0},{1,385},{129,257},{257,129},{3... | collective-permute-start | bytes 98312 | tf_op jit(solution)/shard_map/ppermute | solution.py:27
  96.1 12.5 %collective-permute-start.7 = (f32[16,512]{1,0:T(8,128)S(1)}, f32[16,512]{1,0:T(8,128)S(1)}, u32[]{:S(2)}, u32[]{:S(2)}) collective-permute-start(f32[16,512]{1,0:T(8,128)S(1)} %get-tuple-element.11), channel_id=1, source_target_pairs={{0,256},{128,384},{256,0},{384,128},{1,257},{129,385},{257,1},{385... | collective-permute-start | bytes 98312 | tf_op jit(solution)/shard_map/ppermute | solution.py:27
  100.2 20.8 %collective-permute-start.6 = (f32[16,512]{1,0:T(8,128)S(1)}, f32[16,512]{1,0:T(8,128)S(1)}, u32[]{:S(2)}, u32[]{:S(2)}) collective-permute-start(f32[16,512]{1,0:T(8,128)S(1)} %get-tuple-element.11), channel_id=1, source_target_pairs={{0,128},{128,0},{256,384},{384,256},{1,129},{129,1},{257,385},{385... | collective-permute-start | bytes 98312 | tf_op jit(solution)/shard_map/ppermute | solution.py:27

commit v4 on v3

--- a/solution.py
+++ b/solution.py
@@ -12,7 +12,7 @@
 bf16 = jnp.bfloat16
 in_vmem = pl.BlockSpec(memory_space=pltpu.VMEM)
 in_smem = pl.BlockSpec(memory_space=pltpu.SMEM)
-unread = pl.BlockSpec(memory_space=pl.ANY)
+anywhere = pl.BlockSpec(memory_space=pl.ANY)
 
 
 def dot_t(a, b):
@@ -27,12 +27,13 @@
     return lax.ppermute(a, axis, [(i, i ^ mask) for i in range(count)])
 
 
-def call(kernel, out_shape, in_specs, flops, moved):
+def call(kernel, out_shape, in_specs, flops, moved, out_specs=None, scratch=()):
     return pl.pallas_call(
         kernel,
         out_shape=out_shape,
         in_specs=in_specs,
-        out_specs=jax.tree.map(lambda _: in_vmem, out_shape),
+        out_specs=out_specs or jax.tree.map(lambda _: in_vmem, out_shape),
+        scratch_shapes=scratch,
         compiler_params=pltpu.CompilerParams(vmem_limit_bytes=32 << 20),
         cost_estimate=pl.CostEstimate(flops=flops, bytes_accessed=moved, transcendentals=0),
     )
@@ -42,13 +43,20 @@
     return pl.pallas_call(
         lambda *refs: None,
         out_shape=jax.ShapeDtypeStruct(a.shape, a.dtype),
-        in_specs=[unread] * (1 + len(others)),
-        out_specs=unread,
+        in_specs=[in_vmem] * (1 + len(others)),
+        out_specs=in_vmem,
         input_output_aliases={0: 0},
+        compiler_params=pltpu.CompilerParams(vmem_limit_bytes=32 << 20),
     )(a, *others)
 
 
-def rank_kernel(cot_ref, right_ref, projected_ref, out_ref):
+def rank_kernel(cot_any, right_any, projected_ref, out_ref, cot_ref, right_ref, sems):
+    first = pltpu.make_async_copy(cot_any, cot_ref, sems.at[0])
+    second = pltpu.make_async_copy(right_any, right_ref, sems.at[1])
+    first.start()
+    second.start()
+    first.wait()
+    second.wait()
     back = dot_t(cot_ref[...], right_ref[...])
     projected = projected_ref[...]
     out_ref[...] = jnp.zeros((16, 8, 128), f32)
@@ -57,8 +65,8 @@
 
 
 def pack_kernel(
-    place_ref, sent_ref, rank_ref, coeff_ref, cot_ref, weight_ref, got_ref, inputs_ref, after1, after3,
-    x_ref, back_ref,
+    place_ref, sent_ref, rank_ref, coeff_ref, cot_ref, weight_ref, got_ref, inputs_ref, after1, after2, after3,
+    x_any, back_ref, x_ref, sems,
 ):
     lane = lax.broadcasted_iota(jnp.int32, (1, 128), 1)
     rank = rank_ref[...]
@@ -96,6 +104,9 @@
         x_ref[x, 288:320, :] = small
         x_ref[x, 320:336, :] = right_high
         x_ref[x, 336:352, :] = right_low
+        pltpu.make_async_copy(x_ref.at[x], x_any.at[x], sems.at[x]).start()
+    for x in range(4):
+        pltpu.make_async_copy(x_ref.at[x], x_any.at[x], sems.at[x]).wait()
 
 
 def products(parts, ref):
@@ -104,19 +115,13 @@
     return total.astype(bf16).reshape(4, 128, 512)
 
 
-def stacked(cots):
-    return [jnp.concatenate([c[half] for c in cots], axis=0) for half in (0, 1)]
-
-
-def own_kernel(own_ref, c0_ref, c1_ref, c2_ref, c3_ref, out_ref):
-    out_ref[...] = products(stacked((c0_ref, c1_ref, c2_ref, c3_ref)), own_ref)
-
-
-def other_kernel(
-    place_ref, done_ref, own_ref, other_ref, c0_ref, c1_ref, c2_ref, c3_ref, out_ref, right_ref
-):
+def own_kernel(own_ref, near_ref, far_ref, out_ref):
+    out_ref[...] = products((near_ref[...].reshape(512, 512), far_ref[...].reshape(512, 512)), own_ref)
+
+
+def other_kernel(place_ref, done_ref, own_ref, other_ref, near_ref, far_ref, out_ref, right_ref):
     core, z_high = place_ref[0], place_ref[2]
-    total = products(stacked((c0_ref, c1_ref, c2_ref, c3_ref)), other_ref)
+    total = products((near_ref[...].reshape(512, 512), far_ref[...].reshape(512, 512)), other_ref)
     for k in range(4):
         out_ref[z_high ^ k, :, 0:512] = done_ref[k]
         out_ref[z_high ^ k, :, 512:1024] = total[k]
@@ -157,13 +162,14 @@
     given = lax.dynamic_index_in_dim(weight.reshape(2, 128, 512), 1 - z_low, 0, keepdims=False)
     got = swap(given, "zl", 2, 1)
 
-    cot_other = swap(cotangent, "zl", 2, 1)
-    cot_pair = jnp.stack([cotangent, cot_other])
-    cots = [cot_pair] + [swap(cot_pair, "zh", 4, k) for k in (1, 2, 3)]
+    cots = [cotangent] + [swap(cotangent, "zh", 4, k) for k in (1, 2, 3)]
+    near = jnp.stack(cots)
+    far = swap(near, "zl", 2, 1)
 
     own_projected = jnp.dot(inputs, left_factor, preferred_element_type=f32)
     rank_out = call(
-        rank_kernel, shape((16, 8, 128), f32), [in_vmem] * 3, 6 << 20, 1 << 20
+        rank_kernel, shape((16, 8, 128), f32), [anywhere] * 2 + [in_vmem], 6 << 20, 1 << 20,
+        scratch=[pltpu.VMEM((128, 512), bf16), pltpu.VMEM((16, 512), bf16), pltpu.SemaphoreType.DMA((2,))],
     )(cotangent, right_factor, own_projected)
     rank_in = lax.all_to_all(rank_out, ("zl", "y"), 0, 0)
 
@@ -171,22 +177,24 @@
     x_out, scaled_back = call(
         pack_kernel,
         (shape((4, 352, 512), bf16), shape((8, 128), bf16)),
-        [in_smem] + [in_vmem] * 7 + [unread] * 2,
+        [in_smem] + [in_vmem] * 7 + [anywhere] * 3,
         16 << 20,
         3 << 20,
-    )(place, rank_out, rank_in, coeff_lanes, cotangent, weight, got, inputs, cots[1], cots[3])
+        out_specs=(anywhere, in_vmem),
+        scratch=[pltpu.VMEM((4, 352, 512), bf16), pltpu.SemaphoreType.DMA((4,))],
+    )(place, rank_out, rank_in, coeff_lanes, cotangent, weight, got, inputs, *cots[1:])
     x_in = lax.all_to_all(x_out, "x", 0, 0)
-    x_in = after(x_in, cots[2])
+    x_in = after(x_in, far)
     x_other = swap(x_in, "c", 2, 1)
 
-    done = call(own_kernel, shape((4, 128, 512), bf16), [in_vmem] * 5, 1 << 29, 3 << 20)(x_in, *cots)
+    done = call(own_kernel, shape((4, 128, 512), bf16), [in_vmem] * 3, 1 << 29, 3 << 20)(x_in, near, far)
     out, right_part = call(
         other_kernel,
         (shape((4, 128, 1152), bf16), shape((16, 512), f32)),
-        [in_smem] + [in_vmem] * 7,
+        [in_smem] + [in_vmem] * 5,
         1 << 29,
         5 << 20,
-    )(place, done, x_in, x_other, *cots)
+    )(place, done, x_in, x_other, near, far)
     back = lax.all_to_all(out.reshape(64, 8, 1152), ("zh", "zl", "y"), 0, 0)
     right_sum = right_part + sum(swap(right_part, "zh", 4, k) for k in (1, 2, 3))
 

time: 127 us -> 119 us (0.937)
  waiting for transfers between devices: 46.3 us -> 38.1 us
  local copies, waits for them, and re-layouts: 9.11 us -> 6.46 us
  starting transfers between devices: 59.5 us -> 61.8 us
    ppermute x9, waiting for transfers between devices: 44.3 us -> 28.5 us  [swap(): return lax.ppermute(a, axis, [(i, i ^ mask) for i in range(count)])]
    all_to_all x1, waiting for transfers between devices: 0.01 us -> 2.93 us  [body(): rank_in = lax.all_to_all(rank_out, ('zl', 'y'), 0, 0)]
    unnamed x28 -> x18, local copies, waits for them, and re-layouts: 8.1 us -> 5.45 us
    all_to_all x1, waiting for transfers between devices: 2.06 us -> 4.51 us  [body(): back = lax.all_to_all(out.reshape(64, 8, 1152), ('zh', 'zl', 'y'), 0, 0)]
    all_to_all x1, waiting for transfers between devices: 0.01 us -> 2.17 us  [body(): x_in = lax.all_to_all(x_out, 'x', 0, 0)]
    ppermute x9, starting transfers between devices: 37 us -> 38.3 us  [swap(): return lax.ppermute(a, axis, [(i, i ^ mask) for i in range(count)])]
where the time goes in v4:
time: 119 us; the launch traced here: 118 us
  starting transfers between devices  61.8 us (52%)
  waiting for transfers between devices  38.1 us (32%)
  local copies, waits for them, and re-layouts  6.46 us (5%)
  Pallas kernels  5.37 us (5%)
  other arithmetic  3.01 us (3%)
  matrix products  1.92 us (2%)
    ppermute x9, starting transfers between devices, swap(): return lax.ppermute(a, axis, [(i, i ^ mask) for i in range(count)])  38.3 us
    ppermute x9, waiting for transfers between devices, swap(): return lax.ppermute(a, axis, [(i, i ^ mask) for i in range(count)])  28.5 us
    all_to_all x1, starting transfers between devices, body(): back = lax.all_to_all(out.reshape(64, 8, 1152), ('zh', 'zl', 'y'), 0, 0)  10.4 us
    all_to_all x1, starting transfers between devices, body(): rank_in = lax.all_to_all(rank_out, ('zl', 'y'), 0, 0)  8.13 us
    unnamed x18, local copies, waits for them, and re-layouts  5.45 us
    all_to_all x1, starting transfers between devices, body(): x_in = lax.all_to_all(x_out, 'x', 0, 0)  4.92 us
    all_to_all x1, waiting for transfers between devices, body(): back = lax.all_to_all(out.reshape(64, 8, 1152), ('zh', 'zl', 'y'), 0, 0)  4.51 us
    all_to_all x1, waiting for transfers between devices, body(): rank_in = lax.all_to_all(rank_out, ('zl', 'y'), 0, 0)  2.93 us
  transfers between devices with their start and end apart: 12, of which 7 were waited for; matrix products, arithmetic and copies ran while one was open for 3% of the time, Pallas kernels for 1%

profile of v4, /device:TPU:6, one launch (start us, length us, event | category | flops | bytes accessed | tf_op | source)
XLA Modules:
  0.0 117.6 jit_solution(3659934077868299456)
XLA Ops:
  0.6 0.0 copy-start
  0.6 11.1 %collective-permute-start.3 = (bf16[128,512]{1,0:T(8,128)(2,1)}, bf16[128,512]{1,0:T(8,128)(2,1)S(1)}, u32[]{:S(2)}, u32[]{:S(2)}) collective-permute-start(bf16[128,512]{1,0:T(8,128)(2,1)} %cot_ref.1), channel_id=1, source_target_pairs={{0,384},{128,256},{256,128},{384,0},{1,385},{129,257},{257,129},{3... | collective-permute-start | bytes 393224 | tf_op jit(solution)/shard_map/ppermute | solution.py:27
  11.7 1.9 %collective-permute-start.2 = (bf16[128,512]{1,0:T(8,128)(2,1)}, bf16[128,512]{1,0:T(8,128)(2,1)S(1)}, u32[]{:S(2)}, u32[]{:S(2)}) collective-permute-start(bf16[128,512]{1,0:T(8,128)(2,1)} %cot_ref.1), channel_id=1, source_target_pairs={{0,256},{128,384},{256,0},{384,128},{1,257},{129,385},{257,1},{385... | collective-permute-start | bytes 393224 | tf_op jit(solution)/shard_map/ppermute | solution.py:27
  13.7 4.3 %collective-permute-start.1 = (bf16[128,512]{1,0:T(8,128)(2,1)}, bf16[128,512]{1,0:T(8,128)(2,1)S(1)}, u32[]{:S(2)}, u32[]{:S(2)}) collective-permute-start(bf16[128,512]{1,0:T(8,128)(2,1)} %cot_ref.1), channel_id=1, source_target_pairs={{0,128},{128,0},{256,384},{384,256},{1,129},{129,1},{257,385},{385... | collective-permute-start | bytes 393224 | tf_op jit(solution)/shard_map/ppermute | solution.py:27
  17.9 1.1 fusion.7.projected_ref
  19.0 0.9 copy-done.2
  20.0 0.7 copy-done.7
  20.7 1.0 shard_map.102.sent_ref
  21.7 8.1 %all-to-all-start = ((f32[16,8,128]{2,1,0:T(8,128)}), f32[16,8,128]{2,1,0:T(8,128)S(1)}, u32[]{:S(2)}, u32[]{:S(2)}) async-start(f32[16,8,128]{2,1,0:T(8,128)} %shard_map.102.sent_ref), calls=%async_computation | async-start | bytes 131072 | tf_op jit(solution)/shard_map/all_to_all | solution.py:174
  29.8 0.9 dynamic-slice_bitcast_fusion
  30.7 3.8 %collective-permute-start = (bf16[128,512]{1,0:T(8,128)(2,1)S(1)}, bf16[128,512]{1,0:T(8,128)(2,1)S(1)}, u32[]{:S(2)}, u32[]{:S(2)}) collective-permute-start(bf16[128,512]{1,0:T(8,128)(2,1)S(1)} %dynamic-slice_bitcast_fusion), channel_id=1, source_target_pairs={{0,8},{8,0},{1,9},{9,1},{2,10},{10,2},{3,11},{11,3},{4,12},{12,4},... | collective-permute-start | bytes 393224 | tf_op jit(solution)/shard_map/ppermute | solution.py:27
  34.6 0.7 convert_multiply_fusion
  35.2 0.1 fusion.4.coeff_ref
  35.3 0.1 pad_add_fusion.place_ref
  35.4 2.9 %all-to-all-done.rank_ref = f32[16,8,128]{2,1,0:T(8,128)S(1)} async-done(((f32[16,8,128]{2,1,0:T(8,128)}), f32[16,8,128]{2,1,0:T(8,128)S(1)}, u32[]{:S(2)}, u32[]{:S(2)}) %all-to-all-start) | async-done | bytes 65568 | tf_op jit(solution)/shard_map/all_to_all | solution.py:174
  38.3 0.0 collective-permute-done.got_ref
  38.3 0.0 collective-permute-done.3.after3
  38.3 0.0 copy-start.3
  38.3 0.9 copy-done.3
  39.2 0.9 copy-done.5
  40.2 0.9 copy-done.6
  41.1 2.2 %shard_map.103 = (bf16[4,352,512]{2,1,0:T(8,128)(2,1)}, bf16[8,128]{1,0:T(8,128)(2,1)S(1)}) custom-call(s32[3]{0:T(128)S(1)} %pad_add_fusion.place_ref, f32[16,8,128]{2,1,0:T(8,128)} %shard_map.102.sent_ref, f32[16,8,128]{2,1,0:T(8,128)S(1)} %all-to-all-done.rank_ref, f32[1,128]{1,0:T(1,128)S(1)} %fusion.4.coeff_ref, bf16[128,512]{1,0:T(8,128)(2,1)S(1)} %copy-done.3, ...), custom_call_target="tpu_custom_call" | custom-call | flops 16777216 | bytes 3145728 | tf_op jit(solution)/shard_map/pallas_call | solution.py:177
  43.3 0.0 copy-start.4
  43.3 4.9 %all-to-all-start.1 = ((bf16[4,352,512]{2,1,0:T(8,128)(2,1)}), bf16[4,352,512]{2,1,0:T(8,128)(2,1)S(1)}, u32[]{:S(2)}, u32[]{:S(2)}) async-start(bf16[4,352,512]{2,1,0:T(8,128)(2,1)} %get-tuple-element.8), calls=%async_computation.1 | async-start | bytes 2883584 | tf_op jit(solution)/shard_map/all_to_all | solution.py:186
  48.2 0.1 pad_maximum_fusion.near_ref
  48.3 3.1 %collective-permute-start.4 = (bf16[4,128,512]{2,1,0:T(8,128)(2,1)S(1)}, bf16[4,128,512]{2,1,0:T(8,128)(2,1)S(1)}, u32[]{:S(2)}, u32[]{:S(2)}) collective-permute-start(bf16[4,128,512]{2,1,0:T(8,128)(2,1)S(1)} %pad_maximum_fusion.near_ref), channel_id=1, source_target_pairs={{0,8},{8,0},{1,9},{9,1},{2,10},{10,2},{3,11},{11,3},{4,12},{12,4},... | collective-permute-start | bytes 1572872 | tf_op jit(solution)/shard_map/ppermute | solution.py:27
  51.4 10.0 %collective-permute-done.4.refs_1_.far_ref = bf16[4,128,512]{2,1,0:T(8,128)(2,1)S(1)} collective-permute-done((bf16[4,128,512]{2,1,0:T(8,128)(2,1)S(1)}, bf16[4,128,512]{2,1,0:T(8,128)(2,1)S(1)}, u32[]{:S(2)}, u32[]{:S(2)}) %collective-permute-start.4) | collective-permute-done | bytes 524320 | tf_op jit(solution)/shard_map/ppermute | solution.py:27
  61.4 2.2 %all-to-all-done.1.refs_0_ = bf16[4,352,512]{2,1,0:T(8,128)(2,1)S(1)} async-done(((bf16[4,352,512]{2,1,0:T(8,128)(2,1)}), bf16[4,352,512]{2,1,0:T(8,128)(2,1)S(1)}, u32[]{:S(2)}, u32[]{:S(2)}) %all-to-all-start.1) | async-done | bytes 1441824 | tf_op jit(solution)/shard_map/all_to_all | solution.py:186
  63.6 1.9 %collective-permute-start.5 = (bf16[4,352,512]{2,1,0:T(8,128)(2,1)S(1)}, bf16[4,352,512]{2,1,0:T(8,128)(2,1)S(1)}, u32[]{:S(2)}, u32[]{:S(2)}) collective-permute-start(bf16[4,352,512]{2,1,0:T(8,128)(2,1)S(1)} %shard_map.104.own_ref), channel_id=1, source_target_pairs={{0,16},{16,0},{1,17},{17,1},{2,18},{18,2},{3,19},{19,3},{4,20},{20... | collective-permute-start | bytes 4325384 | tf_op jit(solution)/shard_map/ppermute | solution.py:27
  65.5 0.7 shard_map.105.done_ref
  66.2 2.4 %collective-permute-done.5.other_ref = bf16[4,352,512]{2,1,0:T(8,128)(2,1)S(1)} collective-permute-done((bf16[4,352,512]{2,1,0:T(8,128)(2,1)S(1)}, bf16[4,352,512]{2,1,0:T(8,128)(2,1)S(1)}, u32[]{:S(2)}, u32[]{:S(2)}) %collective-permute-start.5) | collective-permute-done | bytes 1441824 | tf_op jit(solution)/shard_map/ppermute | solution.py:27
  68.7 1.5 %shard_map.106 = (bf16[4,128,1152]{2,1,0:T(8,128)(2,1)S(1)}, f32[16,512]{1,0:T(8,128)S(1)}) custom-call(s32[3]{0:T(128)S(1)} %pad_add_fusion.place_ref, bf16[4,128,512]{2,1,0:T(8,128)(2,1)S(1)} %shard_map.105.done_ref, bf16[4,352,512]{2,1,0:T(8,128)(2,1)S(1)} %shard_map.104.own_ref, bf16[4,352,512]{2,1,0:T(8,128)(2,1)S(1)} %collective-permute-done.5.other_ref, ...), custom_call_target="tpu_custom_call" | custom-call | flops 536870912 | bytes 5242880 | tf_op jit(solution)/shard_map/pallas_call | solution.py:191
  70.2 1.0 copy-done.1
  71.2 10.4 %all-to-all-start.2 = ((bf16[64,8,1152]{2,1,0:T(8,128)(2,1)}), bf16[64,8,1152]{2,1,0:T(8,128)(2,1)S(1)}, u32[]{:S(2)}, u32[]{:S(2)}) async-start(bf16[64,8,1152]{2,1,0:T(8,128)(2,1)} %bitcast.27), calls=%async_computation.2 | async-start | bytes 2359296 | tf_op jit(solution)/shard_map/all_to_all | solution.py:198
  81.6 5.8 %collective-permute-start.8 = (f32[16,512]{1,0:T(8,128)S(1)}, f32[16,512]{1,0:T(8,128)S(1)}, u32[]{:S(2)}, u32[]{:S(2)}) collective-permute-start(f32[16,512]{1,0:T(8,128)S(1)} %get-tuple-element.11), channel_id=1, source_target_pairs={{0,384},{128,256},{256,128},{384,0},{1,385},{129,257},{257,129},{3... | collective-permute-start | bytes 98312 | tf_op jit(solution)/shard_map/ppermute | solution.py:27
  87.4 4.1 %collective-permute-start.7 = (f32[16,512]{1,0:T(8,128)S(1)}, f32[16,512]{1,0:T(8,128)S(1)}, u32[]{:S(2)}, u32[]{:S(2)}) collective-permute-start(f32[16,512]{1,0:T(8,128)S(1)} %get-tuple-element.11), channel_id=1, source_target_pairs={{0,256},{128,384},{256,0},{384,128},{1,257},{129,385},{257,1},{385... | collective-permute-start | bytes 98312 | tf_op jit(solution)/shard_map/ppermute | solution.py:27
  91.5 2.4 %collective-permute-start.6 = (f32[16,512]{1,0:T(8,128)S(1)}, f32[16,512]{1,0:T(8,128)S(1)}, u32[]{:S(2)}, u32[]{:S(2)}) collective-permute-start(f32[16,512]{1,0:T(8,128)S(1)} %get-tuple-element.11), channel_id=1, source_target_pairs={{0,128},{128,0},{256,384},{384,256},{1,129},{129,1},{257,385},{385... | collective-permute-start | bytes 98312 | tf_op jit(solution)/shard_map/ppermute | solution.py:27
  93.9 9.5 %collective-permute-done.8 = f32[16,512]{1,0:T(8,128)S(1)} collective-permute-done((f32[16,512]{1,0:T(8,128)S(1)}, f32[16,512]{1,0:T(8,128)S(1)}, u32[]{:S(2)}, u32[]{:S(2)}) %collective-permute-start.8) | collective-permute-done | bytes 32800 | tf_op jit(solution)/shard_map/ppermute | solution.py:27
  103.4 6.6 %collective-permute-done.6 = f32[16,512]{1,0:T(8,128)S(1)} collective-permute-done((f32[16,512]{1,0:T(8,128)S(1)}, f32[16,512]{1,0:T(8,128)S(1)}, u32[]{:S(2)}, u32[]{:S(2)}) %collective-permute-start.6) | collective-permute-done | bytes 32800 | tf_op jit(solution)/shard_map/ppermute | solution.py:27
  110.0 0.6 add_multiply_fusion
  110.6 4.5 %all-to-all-done.2 = bf16[64,8,1152]{2,1,0:T(8,128)(2,1)S(1)} async-done(((bf16[64,8,1152]{2,1,0:T(8,128)(2,1)}), bf16[64,8,1152]{2,1,0:T(8,128)(2,1)S(1)}, u32[]{:S(2)}, u32[]{:S(2)}) %all-to-all-start.2) | async-done | bytes 1179680 | tf_op jit(solution)/shard_map/all_to_all | solution.py:198
  115.1 0.1 convert_reduce_fusion.1
  115.2 0.1 slice_add_fusion
  115.3 0.6 fusion.5
  115.9 0.1 fusion.6
  115.9 0.1 convert_reduce_fusion
  116.1 0.8 fusion
  116.9 0.6 maximum_multiply_fusion
  (15 shorter events, 0.1 us)
Async XLA Ops:
  0.6 17.3 %copy-start = (bf16[8192,16]{0,1:T(8,128)(2,1)S(1)}, bf16[8192,16]{0,1:T(8,128)(2,1)}, u32[]{:S(2)}) copy-start(bf16[8192,16]{0,1:T(8,128)(2,1)} %param.10) | copy-start | bytes 786436
  0.6 37.7 %collective-permute-start.3 = (bf16[128,512]{1,0:T(8,128)(2,1)}, bf16[128,512]{1,0:T(8,128)(2,1)S(1)}, u32[]{:S(2)}, u32[]{:S(2)}) collective-permute-start(bf16[128,512]{1,0:T(8,128)(2,1)} %cot_ref.1), channel_id=1, source_target_pairs={{0,384},{128,256},{256,128},{384,0},{1,385},{129,257},{257,129},{3... | collective-permute-start | bytes 393224 | tf_op jit(solution)/shard_map/ppermute | solution.py:27
  11.7 26.6 %collective-permute-start.2 = (bf16[128,512]{1,0:T(8,128)(2,1)}, bf16[128,512]{1,0:T(8,128)(2,1)S(1)}, u32[]{:S(2)}, u32[]{:S(2)}) collective-permute-start(bf16[128,512]{1,0:T(8,128)(2,1)} %cot_ref.1), channel_id=1, source_target_pairs={{0,256},{128,384},{256,0},{384,128},{1,257},{129,385},{257,1},{385... | collective-permute-start | bytes 393224 | tf_op jit(solution)/shard_map/ppermute | solution.py:27
  13.7 24.7 %collective-permute-start.1 = (bf16[128,512]{1,0:T(8,128)(2,1)}, bf16[128,512]{1,0:T(8,128)(2,1)S(1)}, u32[]{:S(2)}, u32[]{:S(2)}) collective-permute-start(bf16[128,512]{1,0:T(8,128)(2,1)} %cot_ref.1), channel_id=1, source_target_pairs={{0,128},{128,0},{256,384},{384,256},{1,129},{129,1},{257,385},{385... | collective-permute-start | bytes 393224 | tf_op jit(solution)/shard_map/ppermute | solution.py:27
  19.0 0.9 copy-start.2
  20.0 0.7 copy-start.7
  21.7 16.7 %all-to-all-start = ((f32[16,8,128]{2,1,0:T(8,128)}), f32[16,8,128]{2,1,0:T(8,128)S(1)}, u32[]{:S(2)}, u32[]{:S(2)}) async-start(f32[16,8,128]{2,1,0:T(8,128)} %shard_map.102.sent_ref), calls=%async_computation | async-start | bytes 131072 | tf_op jit(solution)/shard_map/all_to_all | solution.py:174
  30.7 7.6 %collective-permute-start = (bf16[128,512]{1,0:T(8,128)(2,1)S(1)}, bf16[128,512]{1,0:T(8,128)(2,1)S(1)}, u32[]{:S(2)}, u32[]{:S(2)}) collective-permute-start(bf16[128,512]{1,0:T(8,128)(2,1)S(1)} %dynamic-slice_bitcast_fusion), channel_id=1, source_target_pairs={{0,8},{8,0},{1,9},{9,1},{2,10},{10,2},{3,11},{11,3},{4,12},{12,4},... | collective-permute-start | bytes 393224 | tf_op jit(solution)/shard_map/ppermute | solution.py:27
  38.3 0.9 copy-start.3
  39.2 0.9 copy-start.5
  40.2 0.9 copy-start.6
  43.3 4.9 %copy-start.4 = (bf16[128,512]{1,0:T(8,128)(2,1)S(1)}, bf16[128,512]{1,0:T(8,128)(2,1)}, u32[]{:S(2)}) copy-start(bf16[128,512]{1,0:T(8,128)(2,1)} %cot_ref.1) | copy-start | bytes 393220
  43.3 20.3 %all-to-all-start.1 = ((bf16[4,352,512]{2,1,0:T(8,128)(2,1)}), bf16[4,352,512]{2,1,0:T(8,128)(2,1)S(1)}, u32[]{:S(2)}, u32[]{:S(2)}) async-start(bf16[4,352,512]{2,1,0:T(8,128)(2,1)} %get-tuple-element.8), calls=%async_computation.1 | async-start | bytes 2883584 | tf_op jit(solution)/shard_map/all_to_all | solution.py:186
  48.3 13.1 %collective-permute-start.4 = (bf16[4,128,512]{2,1,0:T(8,128)(2,1)S(1)}, bf16[4,128,512]{2,1,0:T(8,128)(2,1)S(1)}, u32[]{:S(2)}, u32[]{:S(2)}) collective-permute-start(bf16[4,128,512]{2,1,0:T(8,128)(2,1)S(1)} %pad_maximum_fusion.near_ref), channel_id=1, source_target_pairs={{0,8},{8,0},{1,9},{9,1},{2,10},{10,2},{3,11},{11,3},{4,12},{12,4},... | collective-permute-start | bytes 1572872 | tf_op jit(solution)/shard_map/ppermute | solution.py:27
  63.6 5.1 %collective-permute-start.5 = (bf16[4,352,512]{2,1,0:T(8,128)(2,1)S(1)}, bf16[4,352,512]{2,1,0:T(8,128)(2,1)S(1)}, u32[]{:S(2)}, u32[]{:S(2)}) collective-permute-start(bf16[4,352,512]{2,1,0:T(8,128)(2,1)S(1)} %shard_map.104.own_ref), channel_id=1, source_target_pairs={{0,16},{16,0},{1,17},{17,1},{2,18},{18,2},{3,19},{19,3},{4,20},{20... | collective-permute-start | bytes 4325384 | tf_op jit(solution)/shard_map/ppermute | solution.py:27
  70.2 1.0 copy-start.1
  71.2 44.1 %copy-start.8 = (s32[16]{0:T(128)S(1)}, s32[16]{0:T(128)}, u32[]{:S(2)}) copy-start(s32[16]{0:T(128)} %param.13) | copy-start | bytes 196
  71.2 43.9 %all-to-all-start.2 = ((bf16[64,8,1152]{2,1,0:T(8,128)(2,1)}), bf16[64,8,1152]{2,1,0:T(8,128)(2,1)S(1)}, u32[]{:S(2)}, u32[]{:S(2)}) async-start(bf16[64,8,1152]{2,1,0:T(8,128)(2,1)} %bitcast.27), calls=%async_computation.2 | async-start | bytes 2359296 | tf_op jit(solution)/shard_map/all_to_all | solution.py:198
  81.6 21.8 %collective-permute-start.8 = (f32[16,512]{1,0:T(8,128)S(1)}, f32[16,512]{1,0:T(8,128)S(1)}, u32[]{:S(2)}, u32[]{:S(2)}) collective-permute-start(f32[16,512]{1,0:T(8,128)S(1)} %get-tuple-element.11), channel_id=1, source_target_pairs={{0,384},{128,256},{256,128},{384,0},{1,385},{129,257},{257,129},{3... | collective-permute-start | bytes 98312 | tf_op jit(solution)/shard_map/ppermute | solution.py:27
  87.4 16.0 %collective-permute-start.7 = (f32[16,512]{1,0:T(8,128)S(1)}, f32[16,512]{1,0:T(8,128)S(1)}, u32[]{:S(2)}, u32[]{:S(2)}) collective-permute-start(f32[16,512]{1,0:T(8,128)S(1)} %get-tuple-element.11), channel_id=1, source_target_pairs={{0,256},{128,384},{256,0},{384,128},{1,257},{129,385},{257,1},{385... | collective-permute-start | bytes 98312 | tf_op jit(solution)/shard_map/ppermute | solution.py:27
  91.5 18.5 %collective-permute-start.6 = (f32[16,512]{1,0:T(8,128)S(1)}, f32[16,512]{1,0:T(8,128)S(1)}, u32[]{:S(2)}, u32[]{:S(2)}) collective-permute-start(f32[16,512]{1,0:T(8,128)S(1)} %get-tuple-element.11), channel_id=1, source_target_pairs={{0,128},{128,0},{256,384},{384,256},{1,129},{129,1},{257,385},{385... | collective-permute-start | bytes 98312 | tf_op jit(solution)/shard_map/ppermute | solution.py:27

commit v5 on v4

v5 whole, which is shorter than its diff:
```python
import jax
import jax.numpy as jnp
from jax import lax
from jax.experimental import pallas as pl
from jax.experimental.pallas import tpu as pltpu
from jax.sharding import Mesh
from jax.sharding import PartitionSpec as P

adapter_scale = 2.0
n_dp = 32
f32 = jnp.float32
bf16 = jnp.bfloat16
in_vmem = pl.BlockSpec(memory_space=pltpu.VMEM)
in_smem = pl.BlockSpec(memory_space=pltpu.SMEM)
anywhere = pl.BlockSpec(memory_space=pl.ANY)
in_hbm = pl.BlockSpec(memory_space=pltpu.HBM)
dma = pltpu.SemaphoreType.DMA


def dot_t(a, b):
    return lax.dot_general(a, b, (((1,), (1,)), ((), ())), preferred_element_type=f32)


def t_dot(a, b):
    return lax.dot_general(a, b, (((0,), (0,)), ((), ())), preferred_element_type=f32)


def swap(a, axis, count, mask):
    return lax.ppermute(a, axis, [(i, i ^ mask) for i in range(count)])


def call(kernel, out_shape, in_specs, flops, moved, out_specs=None, scratch=()):
    return pl.pallas_call(
        kernel,
        out_shape=out_shape,
        in_specs=in_specs,
        out_specs=out_specs or jax.tree.map(lambda _: in_vmem, out_shape),
        scratch_shapes=scratch,
        compiler_params=pltpu.CompilerParams(vmem_limit_bytes=32 << 20),
        cost_estimate=pl.CostEstimate(flops=flops, bytes_accessed=moved, transcendentals=0),
    )


def after(a, *others):
    return pl.pallas_call(
        lambda *refs: None,
        out_shape=jax.ShapeDtypeStruct(a.shape, a.dtype),
        in_specs=[in_vmem] * (1 + len(others)),
        out_specs=in_vmem,
        input_output_aliases={0: 0},
        compiler_params=pltpu.CompilerParams(vmem_limit_bytes=32 << 20),
    )(a, *others)


def rank_kernel(place_ref, cot_any, right_any, weight_any, projected_ref, out_ref, cot_ref, given_ref, right_ref, sems):
    given_rows = pl.ds(pl.multiple_of((1 - place_ref[1]) * 128, 128), 128)
    copies = [
        pltpu.make_async_copy(cot_any, cot_ref, sems.at[0]),
        pltpu.make_async_copy(right_any, right_ref, sems.at[1]),
        pltpu.make_async_copy(weight_any.at[given_rows], given_ref, sems.at[2]),
    ]
    for copy in copies:
        copy.start()
    out_ref[...] = jnp.zeros((16, 8, 128), f32)
    out_ref[:, :, 16:32] = jnp.broadcast_to(projected_ref[...][None], (16, 8, 16))
    for copy in copies:
        copy.wait()
    out_ref[:, :, 0:16] = dot_t(cot_ref[...], right_ref[...]).reshape(16, 8, 16)


def pack_kernel(
    place_ref, sent_ref, rank_ref, coeff_ref, cot_ref, weight_any, got_ref, inputs_any, after1, after2, after3,
    x_any, back_ref, kept_ref, inputs_ref, x_ref, in_sems, out_sems,
):
    kept_rows = pl.ds(pl.multiple_of(place_ref[1] * 128, 128), 128)
    inputs_in = pltpu.make_async_copy(inputs_any, inputs_ref, in_sems.at[0])
    kept_in = pltpu.make_async_copy(weight_any.at[kept_rows], kept_ref, in_sems.at[1])
    inputs_in.start()
    kept_in.start()
    outs = [pltpu.make_async_copy(got_ref, x_any.at[x, 128:256], out_sems.at[x]) for x in range(4)]
    for copy in outs:
        copy.start()
    lane = lax.broadcasted_iota(jnp.int32, (1, 128), 1)
    rank = rank_ref[...]
    coeff = coeff_ref[...]
    own = jnp.where(lane < 16, jnp.sum(rank, axis=0), 0.0)
    back = (own * coeff).astype(bf16)
    back_ref[...] = back
    fwd = (jnp.where((lane >= 16) & (lane < 32), rank, 0.0) * coeff).astype(bf16)
    right = t_dot(fwd.reshape(128, 128), cot_ref[...])[16:32]
    right_high = right.astype(bf16)
    right_low = (right - right_high.astype(f32)).astype(bf16)
    projected = pltpu.roll(sent_ref[0], 112, 1)
    singular = jnp.broadcast_to(jnp.sum(projected * own, axis=0, keepdims=True), (8, 128))
    high = singular.astype(bf16).astype(f32)
    back8 = back.astype(f32)
    none = jnp.zeros((8, 128), f32)
    small = jnp.concatenate(
        [
            jnp.concatenate([back8, pltpu.roll(back8, 16, 1), none, none], axis=1),
            jnp.concatenate([none, none, pltpu.roll(high, 32, 1), pltpu.roll(singular - high, 32, 1)], axis=1),
        ],
        axis=0,
    ).astype(bf16)
    kept_in.wait()
    for x in range(4):
        outs.append(pltpu.make_async_copy(kept_ref, x_any.at[x, 0:128], out_sems.at[4 + x]))
        outs[-1].start()
    inputs_in.wait()
    inputs = inputs_ref[...].astype(f32)
    for x in range(4):
        rows = [inputs[:, (h * 4 + x) * 512 : (h * 4 + x + 1) * 512] for h in range(4)]
        x_ref[x, 0:32, :] = jnp.concatenate(rows, axis=0).astype(bf16)
        x_ref[x, 32:48, :] = small
        x_ref[x, 48:64, :] = right_high
        x_ref[x, 64:80, :] = right_low
        outs.append(pltpu.make_async_copy(x_ref.at[x], x_any.at[x, 256:336], out_sems.at[8 + x]))
        outs[-1].start()
    for copy in outs:
        copy.wait()


def products(parts, ref):
    total = dot_t(parts[0], ref[:, 0:128, :].reshape(512, 512))
    total += dot_t(parts[1], ref[:, 128:256, :].reshape(512, 512))
    return total.astype(bf16).reshape(4, 128, 512)


def own_kernel(own_ref, near_ref, far_ref, out_ref):
    out_ref[...] = products((near_ref[...].reshape(512, 512), far_ref[...].reshape(512, 512)), own_ref)


def other_kernel(
    place_ref, done_ref, own_ref, other_ref, near_ref, far_ref, out_any, right_ref, out_ref, sems
):
    core, z_high = place_ref[0], place_ref[2]
    total = products((near_ref[...].reshape(512, 512), far_ref[...].reshape(512, 512)), other_ref)
    for k in range(4):
        out_ref[z_high ^ k, :, 0:512] = done_ref[k]
        out_ref[z_high ^ k, :, 512:1024] = total[k]
    tok, back, singular = [], [], jnp.zeros((1, 128), f32)
    for ref in (own_ref, other_ref):
        for x in range(4):
            rows = ref[x, 256:288, :]
            tok.append(jnp.where(core == 0, rows[:, :256], rows[:, 256:]))
            small = ref[x, 288:304, :].astype(f32)
            back.extend([small[0:8, :256]] * 4)
            singular += small[8:9, 256:384] + small[8:9, 384:512]
    tok = jnp.concatenate(tok, axis=0)
    back = jnp.concatenate(back, axis=0)
    group = lax.rem(lax.broadcasted_iota(jnp.int32, (256, 1), 0), 32) // 8
    copies = []
    for h in range(4):
        both = t_dot(tok, jnp.where(group == h, back, 0.0).astype(bf16))
        a = both[:, :128].reshape(16, 2, 8, 128)[:, 0]
        b = both[:, 128:].reshape(16, 2, 8, 128)[:, 1]
        z = (a + b + singular).reshape(128, 128)
        high = z.astype(bf16).astype(f32)
        out_ref[h, :, 1024:1152] = (high + pltpu.roll(z - high, 64, 1)).astype(bf16)
        copies.append(pltpu.make_async_copy(out_ref.at[h], out_any.at[h], sems.at[h]))
        copies[-1].start()
    right = jnp.zeros((16, 512), f32)
    for ref in (own_ref, other_ref):
        for x in range(4):
            right += ref[x, 304:320, :].astype(f32) + ref[x, 320:336, :].astype(f32)
    right_ref[...] = right
    for copy in copies:
        copy.wait()


def final_kernel(
    place_ref, back_ref, scaled_ref, left_any, keep_ref, inputs_any, grad_left_any, singular_any,
    left_ref, inputs_ref, grad_left_ref, singular_ref, sems,
):
    left_in = pltpu.make_async_copy(left_any, left_ref, sems.at[0])
    left_in.start()
    core = place_ref[0]
    tail = jnp.sum(back_ref[:, :, 1024:].astype(f32), axis=0)
    tail = (tail + pltpu.roll(tail, 64, 1)) / n_dp
    grad_left_ref[0:8, :] = tail[:, 0:16]
    grad_left_ref[8:16, :] = pltpu.roll(tail, 112, 1)[:, 0:16]
    singular_ref[...] = adapter_scale * keep_ref[...] * pltpu.roll(tail, 96, 1)[0:1, 0:16]
    outs = [
        pltpu.make_async_copy(grad_left_ref, grad_left_any, sems.at[1]),
        pltpu.make_async_copy(singular_ref, singular_any, sems.at[2]),
    ]
    outs[0].start()
    outs[1].start()
    left_in.wait()
    scaled = scaled_ref[:, 0:16]
    for h in range(4):
        for low in range(2):
            first = (h * 2 + low) * 8
            total = jnp.sum(back_ref[first : first + 8, :, 0:1024].astype(f32), axis=0)
            own, other = total[:, :512], total[:, 512:]
            for c, part in enumerate((jnp.where(core == 0, own, other), jnp.where(core == 0, other, own))):
                for x in range(4):
                    at = h * 2048 + x * 512 + c * 256 + low * 128
                    term = jnp.dot(scaled, left_ref[:, at : at + 128], preferred_element_type=f32)
                    inputs_ref[:, at : at + 128] = (part[:, x * 128 : x * 128 + 128] + term).astype(bf16)
    outs.append(pltpu.make_async_copy(inputs_ref, inputs_any, sems.at[3]))
    outs[2].start()
    for copy in outs:
        copy.wait()


def body(inputs, cotangent, weight, left_factor, right_factor, singular, keep_mask):
    core = lax.axis_index("c")
    z_low = lax.axis_index("zl")
    z_high = lax.axis_index("zh")
    place = jnp.stack([core, z_low, z_high]).astype(jnp.int32)
    shape = jax.ShapeDtypeStruct
    keep_float = keep_mask.astype(f32)
    coeff = adapter_scale * singular * keep_float

    own_projected = jnp.dot(inputs, left_factor, preferred_element_type=f32)
    rank_out, cot, given = call(
        rank_kernel,
        (shape((16, 8, 128), f32), shape((128, 512), bf16), shape((128, 512), bf16)),
        [in_smem] + [in_hbm] * 3 + [in_vmem],
        2 << 20,
        1 << 20,
        scratch=[pltpu.VMEM((16, 512), bf16), dma((3,))],
    )(place, cotangent, right_factor, weight, own_projected)
    rank_in = lax.all_to_all(rank_out, ("zl", "y"), 0, 0)

    got = swap(given, "zl", 2, 1)

    cots = [cot] + [swap(cot, "zh", 4, k) for k in (1, 2, 3)]
    near = jnp.stack(cots)
    far = swap(near, "zl", 2, 1)

    coeff_lanes = jnp.pad(jnp.concatenate([coeff, coeff]), (0, 96)).reshape(1, 128)
    x_out, scaled_back = call(
        pack_kernel,
        (shape((4, 336, 512), bf16), shape((8, 128), bf16)),
        [in_smem] + [in_vmem] * 4 + [in_hbm, in_vmem, in_hbm] + [anywhere] * 3,
        16 << 20,
        3 << 20,
        out_specs=(in_hbm, in_vmem),
        scratch=[
            pltpu.VMEM((128, 512), bf16),
            pltpu.VMEM((8, 8192), bf16),
            pltpu.VMEM((4, 80, 512), bf16),
            dma((2,)),
            dma((12,)),
        ],
    )(place, rank_out, rank_in, coeff_lanes, cot, weight, got, inputs, *cots[1:])
    x_in = after(lax.all_to_all(x_out, "x", 0, 0), far)
    x_other = swap(x_in, "c", 2, 1)

    done = call(own_kernel, shape((4, 128, 512), bf16), [in_vmem] * 3, 1 << 29, 3 << 20)(x_in, near, far)
    out, right_part = call(
        other_kernel,
        (shape((4, 128, 1152), bf16), shape((16, 512), f32)),
        [in_smem] + [in_vmem] * 5,
        1 << 29,
        5 << 20,
        out_specs=(in_hbm, in_vmem),
        scratch=[pltpu.VMEM((4, 128, 1152), bf16), dma((4,))],
    )(place, done, x_in, x_other, near, far)
    back = lax.all_to_all(out.reshape(64, 8, 1152), ("zh", "zl", "y"), 0, 0)
    right_sum = right_part + sum(swap(right_part, "zh", 4, k) for k in (1, 2, 3))

    grad_inputs, grad_left, grad_singular = call(
        final_kernel,
        (shape((8, 8192), bf16), shape((16, 16), f32), shape((1, 16), f32)),
        [in_smem, in_vmem, in_vmem, in_hbm, in_vmem],
        2 << 20,
        2 << 20,
        out_specs=(in_hbm, in_hbm, in_hbm),
        scratch=[
            pltpu.VMEM((16, 8192), bf16),
            pltpu.VMEM((8, 8192), bf16),
            pltpu.VMEM((16, 16), f32),
            pltpu.VMEM((1, 16), f32),
            dma((4,)),
        ],
    )(place, back, scaled_back, left_factor.T, keep_float.reshape(1, 16))
    grad_right = right_sum / n_dp
    return (grad_inputs, grad_left, grad_right, grad_singular.reshape(16))


def solution(mesh):
    fine = Mesh(mesh.devices.reshape(4, 4, 2, 2, 8), ("zh", "x", "c", "zl", "y"))
    dp = ("zh", "x", "c")
    tensor = ("zl", "y")
    in_specs = (
        P(dp + tensor, None),
        P(dp, tensor),
        P(dp, tensor),
        P(),
        P(None, tensor),
        P(),
        P(),
    )
    out_specs = (P(dp + tensor, None), P(dp + tensor, None), P(None, tensor), P())
    return jax.shard_map(body, mesh=fine, in_specs=in_specs, out_specs=out_specs, check_vma=False)
```

time: 119 us -> 121 us (1.017)
  the two profiles are of different devices: /device:TPU:6 before, /device:TPU:9 now
where the time goes in v5:
time: 121 us; the launch traced here: 120 us
  starting transfers between devices  60.8 us (50%)
  waiting for transfers between devices  41 us (34%)
  Pallas kernels  9.31 us (8%)
  local copies, waits for them, and re-layouts  5.48 us (5%)
  other arithmetic  1.54 us (1%)
  matrix products  1.21 us (1%)
    ppermute x9, starting transfers between devices, swap(): return lax.ppermute(a, axis, [(i, i ^ mask) for i in range(count)])  39.1 us
    ppermute x9, waiting for transfers between devices, swap(): return lax.ppermute(a, axis, [(i, i ^ mask) for i in range(count)])  34.8 us
    all_to_all x1, starting transfers between devices, body(): back = lax.all_to_all(out.reshape(64, 8, 1152), ('zh', 'zl', 'y'), 0, 0)  9.78 us
    all_to_all x1, starting transfers between devices, body(): rank_in = lax.all_to_all(rank_out, ('zl', 'y'), 0, 0)  7.92 us
    unnamed x16, local copies, waits for them, and re-layouts  5.48 us
    all_to_all x1, starting transfers between devices, body(): x_in = after(lax.all_to_all(x_out, 'x', 0, 0), far)  4.02 us
    all_to_all x1, waiting for transfers between devices, body(): x_in = after(lax.all_to_all(x_out, 'x', 0, 0), far)  3.26 us
    all_to_all x1, waiting for transfers between devices, body(): rank_in = lax.all_to_all(rank_out, ('zl', 'y'), 0, 0)  3.01 us
  transfers between devices with their start and end apart: 12, of which 6 were waited for; matrix products, arithmetic and copies ran while one was open for 1% of the time, Pallas kernels for 1%

profile of v5, /device:TPU:9, one launch (start us, length us, event | category | flops | bytes accessed | tf_op | source)
XLA Modules:
  0.0 120.2 jit_solution(662291565425929982)
XLA Ops:
  0.6 1.2 %fusion.2.projected_ref = f32[8,16]{1,0:T(8,128)S(1)} fusion(bf16[8,8192]{1,0:T(8,128)(2,1)} %inputs_any.1, bf16[8192,16]{0,1:T(8,128)(2,1)} %param.10), kind=kOutput, calls=%fused_computation.9 | convolution fusion | flops 2097152 | bytes 393728 | tf_op jit(solution)/shard_map/dot_general | solution.py:216
  1.8 0.1 pad_add_fusion.place_ref
  1.9 0.0 copy-start.2
  1.9 1.0 copy-done.2
  2.9 0.0 copy-start.5
  2.9 0.9 copy-done.5
  3.8 0.0 copy-start.6
  3.8 0.7 copy-done.6
  4.5 1.8 %shard_map.102 = (f32[16,8,128]{2,1,0:T(8,128)}, bf16[128,512]{1,0:T(8,128)(2,1)S(1)}, bf16[128,512]{1,0:T(8,128)(2,1)S(1)}) custom-call(s32[3]{0:T(128)S(1)} %pad_add_fusion.place_ref, bf16[128,512]{1,0:T(8,128)(2,1)S(1)} %copy-done.5, bf16[16,512]{1,0:T(8,128)(2,1)S(1)} %copy-done.6, bf16[256,512]{1,0:T(8,128)(2,1)S(1)} %copy-done.2, ...), custom_call_target="tpu_custom_call" | custom-call | flops 2097152 | bytes 1048576 | tf_op jit(solution)/shard_map/pallas_call | solution.py:217
  6.3 5.8 %collective-permute-start.1 = (bf16[128,512]{1,0:T(8,128)(2,1)S(1)}, bf16[128,512]{1,0:T(8,128)(2,1)S(1)}, u32[]{:S(2)}, u32[]{:S(2)}) collective-permute-start(bf16[128,512]{1,0:T(8,128)(2,1)S(1)} %get-tuple-element.15.cot_ref), channel_id=1, source_target_pairs={{0,128},{128,0},{256,384},{384,256},{1,129},{129,1},{257,385},{385... | collective-permute-start | bytes 393224 | tf_op jit(solution)/shard_map/ppermute | solution.py:29
  12.1 8.8 %collective-permute-start.2 = (bf16[128,512]{1,0:T(8,128)(2,1)S(1)}, bf16[128,512]{1,0:T(8,128)(2,1)S(1)}, u32[]{:S(2)}, u32[]{:S(2)}) collective-permute-start(bf16[128,512]{1,0:T(8,128)(2,1)S(1)} %get-tuple-element.15.cot_ref), channel_id=1, source_target_pairs={{0,256},{128,384},{256,0},{384,128},{1,257},{129,385},{257,1},{385... | collective-permute-start | bytes 393224 | tf_op jit(solution)/shard_map/ppermute | solution.py:29
  21.0 1.9 %collective-permute-start.3 = (bf16[128,512]{1,0:T(8,128)(2,1)S(1)}, bf16[128,512]{1,0:T(8,128)(2,1)S(1)}, u32[]{:S(2)}, u32[]{:S(2)}) collective-permute-start(bf16[128,512]{1,0:T(8,128)(2,1)S(1)} %get-tuple-element.15.cot_ref), channel_id=1, source_target_pairs={{0,384},{128,256},{256,128},{384,0},{1,385},{129,257},{257,129},{3... | collective-permute-start | bytes 393224 | tf_op jit(solution)/shard_map/ppermute | solution.py:29
  22.9 7.9 %all-to-all-start = ((f32[16,8,128]{2,1,0:T(8,128)}), f32[16,8,128]{2,1,0:T(8,128)S(1)}, u32[]{:S(2)}, u32[]{:S(2)}) async-start(f32[16,8,128]{2,1,0:T(8,128)} %get-tuple-element.14.sent_ref), calls=%async_computation | async-start | bytes 131072 | tf_op jit(solution)/shard_map/all_to_all | solution.py:225
  30.8 3.1 %collective-permute-start = (bf16[128,512]{1,0:T(8,128)(2,1)S(1)}, bf16[128,512]{1,0:T(8,128)(2,1)S(1)}, u32[]{:S(2)}, u32[]{:S(2)}) collective-permute-start(bf16[128,512]{1,0:T(8,128)(2,1)S(1)} %get-tuple-element.16), channel_id=1, source_target_pairs={{0,8},{8,0},{1,9},{9,1},{2,10},{10,2},{3,11},{11,3},{4,12},{12,4},... | collective-permute-start | bytes 393224 | tf_op jit(solution)/shard_map/ppermute | solution.py:29
  33.9 0.7 convert_multiply_fusion
  34.6 0.1 fusion.1.coeff_ref
  34.7 3.0 %all-to-all-done.rank_ref = f32[16,8,128]{2,1,0:T(8,128)S(1)} async-done(((f32[16,8,128]{2,1,0:T(8,128)}), f32[16,8,128]{2,1,0:T(8,128)S(1)}, u32[]{:S(2)}, u32[]{:S(2)}) %all-to-all-start) | async-done | bytes 65568 | tf_op jit(solution)/shard_map/all_to_all | solution.py:225
  37.7 0.0 collective-permute-done.1.after1
  37.7 0.0 collective-permute-done.2.after2
  37.7 0.0 collective-permute-done.3.after3
  37.7 0.0 collective-permute-done.got_ref
  37.7 0.0 copy-start.3
  37.7 0.9 copy-done.3
  38.7 0.9 copy-done.4
  39.6 2.5 %shard_map.103 = (bf16[4,336,512]{2,1,0:T(8,128)(2,1)}, bf16[8,128]{1,0:T(8,128)(2,1)S(1)}) custom-call(s32[3]{0:T(128)S(1)} %pad_add_fusion.place_ref, f32[16,8,128]{2,1,0:T(8,128)} %get-tuple-element.14.sent_ref, f32[16,8,128]{2,1,0:T(8,128)S(1)} %all-to-all-done.rank_ref, f32[1,128]{1,0:T(1,128)S(1)} %fusion.1.coeff_ref, ...), custom_call_target="tpu_custom_call" | custom-call | flops 16777216 | bytes 3145728 | tf_op jit(solution)/shard_map/pallas_call | solution.py:234
  42.1 4.0 %all-to-all-start.1 = ((bf16[4,336,512]{2,1,0:T(8,128)(2,1)}), bf16[4,336,512]{2,1,0:T(8,128)(2,1)S(1)}, u32[]{:S(2)}, u32[]{:S(2)}) async-start(bf16[4,336,512]{2,1,0:T(8,128)(2,1)} %get-tuple-element.17), calls=%async_computation.1 | async-start | bytes 2752512 | tf_op jit(solution)/shard_map/all_to_all | solution.py:249
  46.1 0.1 pad_maximum_fusion.near_ref
  46.2 2.5 %collective-permute-start.4 = (bf16[4,128,512]{2,1,0:T(8,128)(2,1)S(1)}, bf16[4,128,512]{2,1,0:T(8,128)(2,1)S(1)}, u32[]{:S(2)}, u32[]{:S(2)}) collective-permute-start(bf16[4,128,512]{2,1,0:T(8,128)(2,1)S(1)} %pad_maximum_fusion.near_ref), channel_id=1, source_target_pairs={{0,8},{8,0},{1,9},{9,1},{2,10},{10,2},{3,11},{11,3},{4,12},{12,4},... | collective-permute-start | bytes 1572872 | tf_op jit(solution)/shard_map/ppermute | solution.py:29
  48.6 10.1 %collective-permute-done.4.refs_1_.far_ref = bf16[4,128,512]{2,1,0:T(8,128)(2,1)S(1)} collective-permute-done((bf16[4,128,512]{2,1,0:T(8,128)(2,1)S(1)}, bf16[4,128,512]{2,1,0:T(8,128)(2,1)S(1)}, u32[]{:S(2)}, u32[]{:S(2)}) %collective-permute-start.4) | collective-permute-done | bytes 524320 | tf_op jit(solution)/shard_map/ppermute | solution.py:29
  58.7 3.3 %all-to-all-done.1.refs_0_ = bf16[4,336,512]{2,1,0:T(8,128)(2,1)S(1)} async-done(((bf16[4,336,512]{2,1,0:T(8,128)(2,1)}), bf16[4,336,512]{2,1,0:T(8,128)(2,1)S(1)}, u32[]{:S(2)}, u32[]{:S(2)}) %all-to-all-start.1) | async-done | bytes 1376288 | tf_op jit(solution)/shard_map/all_to_all | solution.py:249
  62.0 5.6 %collective-permute-start.5 = (bf16[4,336,512]{2,1,0:T(8,128)(2,1)S(1)}, bf16[4,336,512]{2,1,0:T(8,128)(2,1)S(1)}, u32[]{:S(2)}, u32[]{:S(2)}) collective-permute-start(bf16[4,336,512]{2,1,0:T(8,128)(2,1)S(1)} %shard_map.104.own_ref), channel_id=1, source_target_pairs={{0,16},{16,0},{1,17},{17,1},{2,18},{18,2},{3,19},{19,3},{4,20},{20... | collective-permute-start | bytes 4128776 | tf_op jit(solution)/shard_map/ppermute | solution.py:29
  67.5 0.7 shard_map.105.done_ref
  68.3 2.0 %collective-permute-done.5.other_ref = bf16[4,336,512]{2,1,0:T(8,128)(2,1)S(1)} collective-permute-done((bf16[4,336,512]{2,1,0:T(8,128)(2,1)S(1)}, bf16[4,336,512]{2,1,0:T(8,128)(2,1)S(1)}, u32[]{:S(2)}, u32[]{:S(2)}) %collective-permute-start.5) | collective-permute-done | bytes 1376288 | tf_op jit(solution)/shard_map/ppermute | solution.py:29
  70.3 2.6 %shard_map.106 = (bf16[4,128,1152]{2,1,0:T(8,128)(2,1)S(1)}, f32[16,512]{1,0:T(8,128)S(1)}) custom-call(s32[3]{0:T(128)S(1)} %pad_add_fusion.place_ref, bf16[4,128,512]{2,1,0:T(8,128)(2,1)S(1)} %shard_map.105.done_ref, bf16[4,336,512]{2,1,0:T(8,128)(2,1)S(1)} %shard_map.104.own_ref, bf16[4,336,512]{2,1,0:T(8,128)(2,1)S(1)} %collective-permute-done.5.other_ref, ...), custom_call_target="tpu_custom_call" | custom-call | flops 536870912 | bytes 5242880 | tf_op jit(solution)/shard_map/pallas_call | solution.py:253
  72.9 0.0 copy-start
  72.9 1.0 copy-done
  73.9 9.8 %all-to-all-start.2 = ((bf16[64,8,1152]{2,1,0:T(8,128)(2,1)}), bf16[64,8,1152]{2,1,0:T(8,128)(2,1)S(1)}, u32[]{:S(2)}, u32[]{:S(2)}) async-start(bf16[64,8,1152]{2,1,0:T(8,128)(2,1)} %bitcast.16), calls=%async_computation.2 | async-start | bytes 2359296 | tf_op jit(solution)/shard_map/all_to_all | solution.py:262
  83.7 4.0 %collective-permute-start.6 = (f32[16,512]{1,0:T(8,128)S(1)}, f32[16,512]{1,0:T(8,128)S(1)}, u32[]{:S(2)}, u32[]{:S(2)}) collective-permute-start(f32[16,512]{1,0:T(8,128)S(1)} %get-tuple-element.22), channel_id=1, source_target_pairs={{0,128},{128,0},{256,384},{384,256},{1,129},{129,1},{257,385},{385... | collective-permute-start | bytes 98312 | tf_op jit(solution)/shard_map/ppermute | solution.py:29
  87.7 5.4 %collective-permute-start.7 = (f32[16,512]{1,0:T(8,128)S(1)}, f32[16,512]{1,0:T(8,128)S(1)}, u32[]{:S(2)}, u32[]{:S(2)}) collective-permute-start(f32[16,512]{1,0:T(8,128)S(1)} %get-tuple-element.22), channel_id=1, source_target_pairs={{0,256},{128,384},{256,0},{384,128},{1,257},{129,385},{257,1},{385... | collective-permute-start | bytes 98312 | tf_op jit(solution)/shard_map/ppermute | solution.py:29
  93.2 2.0 %collective-permute-start.8 = (f32[16,512]{1,0:T(8,128)S(1)}, f32[16,512]{1,0:T(8,128)S(1)}, u32[]{:S(2)}, u32[]{:S(2)}) collective-permute-start(f32[16,512]{1,0:T(8,128)S(1)} %get-tuple-element.22), channel_id=1, source_target_pairs={{0,384},{128,256},{256,128},{384,0},{1,385},{129,257},{257,129},{3... | collective-permute-start | bytes 98312 | tf_op jit(solution)/shard_map/ppermute | solution.py:29
  95.1 0.0 copy-done.7
  95.2 14.0 %collective-permute-done.6 = f32[16,512]{1,0:T(8,128)S(1)} collective-permute-done((f32[16,512]{1,0:T(8,128)S(1)}, f32[16,512]{1,0:T(8,128)S(1)}, u32[]{:S(2)}, u32[]{:S(2)}) %collective-permute-start.6) | collective-permute-done | bytes 32800 | tf_op jit(solution)/shard_map/ppermute | solution.py:29
  109.2 8.7 %collective-permute-done.7 = f32[16,512]{1,0:T(8,128)S(1)} collective-permute-done((f32[16,512]{1,0:T(8,128)S(1)}, f32[16,512]{1,0:T(8,128)S(1)}, u32[]{:S(2)}, u32[]{:S(2)}) %collective-permute-start.7) | collective-permute-done | bytes 32800 | tf_op jit(solution)/shard_map/ppermute | solution.py:29
  117.8 0.0 collective-permute-done.8
  117.8 0.6 add_multiply_fusion
  118.5 0.0 all-to-all-done.2.back_ref
  118.5 0.0 copy-done.1
  118.5 1.7 %shard_map.107 = (bf16[8,8192]{1,0:T(8,128)(2,1)}, f32[16,16]{1,0:T(8,128)}, f32[1,16]{1,0:T(1,128)}) custom-call(s32[3]{0:T(128)S(1)} %pad_add_fusion.place_ref, bf16[64,8,1152]{2,1,0:T(8,128)(2,1)S(1)} %all-to-all-done.2.back_ref, bf16[8,128]{1,0:T(8,128)(2,1)S(1)} %get-tuple-element.19.scaled_ref, bf16[16,8192]{1,0:T(8,128)(2,1)S(1)} %bitcast.17, ...), custom_call_target="tpu_custom_call" | custom-call | flops 2097152 | bytes 2097152 | tf_op jit(solution)/shard_map/pallas_call | solution.py:265
  (5 shorter events, 0.0 us)
Async XLA Ops:
  1.9 1.0 copy-start.2
  2.9 0.9 copy-start.5
  3.8 0.7 copy-start.6
  6.3 31.4 %collective-permute-start.1 = (bf16[128,512]{1,0:T(8,128)(2,1)S(1)}, bf16[128,512]{1,0:T(8,128)(2,1)S(1)}, u32[]{:S(2)}, u32[]{:S(2)}) collective-permute-start(bf16[128,512]{1,0:T(8,128)(2,1)S(1)} %get-tuple-element.15.cot_ref), channel_id=1, source_target_pairs={{0,128},{128,0},{256,384},{384,256},{1,129},{129,1},{257,385},{385... | collective-permute-start | bytes 393224 | tf_op jit(solution)/shard_map/ppermute | solution.py:29
  12.1 25.6 %collective-permute-start.2 = (bf16[128,512]{1,0:T(8,128)(2,1)S(1)}, bf16[128,512]{1,0:T(8,128)(2,1)S(1)}, u32[]{:S(2)}, u32[]{:S(2)}) collective-permute-start(bf16[128,512]{1,0:T(8,128)(2,1)S(1)} %get-tuple-element.15.cot_ref), channel_id=1, source_target_pairs={{0,256},{128,384},{256,0},{384,128},{1,257},{129,385},{257,1},{385... | collective-permute-start | bytes 393224 | tf_op jit(solution)/shard_map/ppermute | solution.py:29
  21.0 16.7 %collective-permute-start.3 = (bf16[128,512]{1,0:T(8,128)(2,1)S(1)}, bf16[128,512]{1,0:T(8,128)(2,1)S(1)}, u32[]{:S(2)}, u32[]{:S(2)}) collective-permute-start(bf16[128,512]{1,0:T(8,128)(2,1)S(1)} %get-tuple-element.15.cot_ref), channel_id=1, source_target_pairs={{0,384},{128,256},{256,128},{384,0},{1,385},{129,257},{257,129},{3... | collective-permute-start | bytes 393224 | tf_op jit(solution)/shard_map/ppermute | solution.py:29
  22.9 14.8 %all-to-all-start = ((f32[16,8,128]{2,1,0:T(8,128)}), f32[16,8,128]{2,1,0:T(8,128)S(1)}, u32[]{:S(2)}, u32[]{:S(2)}) async-start(f32[16,8,128]{2,1,0:T(8,128)} %get-tuple-element.14.sent_ref), calls=%async_computation | async-start | bytes 131072 | tf_op jit(solution)/shard_map/all_to_all | solution.py:225
  30.8 6.9 %collective-permute-start = (bf16[128,512]{1,0:T(8,128)(2,1)S(1)}, bf16[128,512]{1,0:T(8,128)(2,1)S(1)}, u32[]{:S(2)}, u32[]{:S(2)}) collective-permute-start(bf16[128,512]{1,0:T(8,128)(2,1)S(1)} %get-tuple-element.16), channel_id=1, source_target_pairs={{0,8},{8,0},{1,9},{9,1},{2,10},{10,2},{3,11},{11,3},{4,12},{12,4},... | collective-permute-start | bytes 393224 | tf_op jit(solution)/shard_map/ppermute | solution.py:29
  37.7 1.0 copy-start.3
  38.7 0.9 copy-start.4
  42.1 19.9 %all-to-all-start.1 = ((bf16[4,336,512]{2,1,0:T(8,128)(2,1)}), bf16[4,336,512]{2,1,0:T(8,128)(2,1)S(1)}, u32[]{:S(2)}, u32[]{:S(2)}) async-start(bf16[4,336,512]{2,1,0:T(8,128)(2,1)} %get-tuple-element.17), calls=%async_computation.1 | async-start | bytes 2752512 | tf_op jit(solution)/shard_map/all_to_all | solution.py:249
  46.2 12.6 %collective-permute-start.4 = (bf16[4,128,512]{2,1,0:T(8,128)(2,1)S(1)}, bf16[4,128,512]{2,1,0:T(8,128)(2,1)S(1)}, u32[]{:S(2)}, u32[]{:S(2)}) collective-permute-start(bf16[4,128,512]{2,1,0:T(8,128)(2,1)S(1)} %pad_maximum_fusion.near_ref), channel_id=1, source_target_pairs={{0,8},{8,0},{1,9},{9,1},{2,10},{10,2},{3,11},{11,3},{4,12},{12,4},... | collective-permute-start | bytes 1572872 | tf_op jit(solution)/shard_map/ppermute | solution.py:29
  62.0 8.3 %collective-permute-start.5 = (bf16[4,336,512]{2,1,0:T(8,128)(2,1)S(1)}, bf16[4,336,512]{2,1,0:T(8,128)(2,1)S(1)}, u32[]{:S(2)}, u32[]{:S(2)}) collective-permute-start(bf16[4,336,512]{2,1,0:T(8,128)(2,1)S(1)} %shard_map.104.own_ref), channel_id=1, source_target_pairs={{0,16},{16,0},{1,17},{17,1},{2,18},{18,2},{3,19},{19,3},{4,20},{20... | collective-permute-start | bytes 4128776 | tf_op jit(solution)/shard_map/ppermute | solution.py:29
  72.9 1.1 copy-start
  73.9 21.2 %copy-start.7 = (s32[16]{0:T(128)S(1)}, s32[16]{0:T(128)}, u32[]{:S(2)}) copy-start(s32[16]{0:T(128)} %param.13) | copy-start | bytes 196
  73.9 44.5 %copy-start.1 = (bf16[8192,16]{0,1:T(8,128)(2,1)S(1)}, bf16[8192,16]{0,1:T(8,128)(2,1)}, u32[]{:S(2)}) copy-start(bf16[8192,16]{0,1:T(8,128)(2,1)} %param.10) | copy-start | bytes 786436
  73.9 44.5 %all-to-all-start.2 = ((bf16[64,8,1152]{2,1,0:T(8,128)(2,1)}), bf16[64,8,1152]{2,1,0:T(8,128)(2,1)S(1)}, u32[]{:S(2)}, u32[]{:S(2)}) async-start(bf16[64,8,1152]{2,1,0:T(8,128)(2,1)} %bitcast.16), calls=%async_computation.2 | async-start | bytes 2359296 | tf_op jit(solution)/shard_map/all_to_all | solution.py:262
  83.7 25.4 %collective-permute-start.6 = (f32[16,512]{1,0:T(8,128)S(1)}, f32[16,512]{1,0:T(8,128)S(1)}, u32[]{:S(2)}, u32[]{:S(2)}) collective-permute-start(f32[16,512]{1,0:T(8,128)S(1)} %get-tuple-element.22), channel_id=1, source_target_pairs={{0,128},{128,0},{256,384},{384,256},{1,129},{129,1},{257,385},{385... | collective-permute-start | bytes 98312 | tf_op jit(solution)/shard_map/ppermute | solution.py:29
  87.7 30.1 %collective-permute-start.7 = (f32[16,512]{1,0:T(8,128)S(1)}, f32[16,512]{1,0:T(8,128)S(1)}, u32[]{:S(2)}, u32[]{:S(2)}) collective-permute-start(f32[16,512]{1,0:T(8,128)S(1)} %get-tuple-element.22), channel_id=1, source_target_pairs={{0,256},{128,384},{256,0},{384,128},{1,257},{129,385},{257,1},{385... | collective-permute-start | bytes 98312 | tf_op jit(solution)/shard_map/ppermute | solution.py:29
  93.2 24.7 %collective-permute-start.8 = (f32[16,512]{1,0:T(8,128)S(1)}, f32[16,512]{1,0:T(8,128)S(1)}, u32[]{:S(2)}, u32[]{:S(2)}) collective-permute-start(f32[16,512]{1,0:T(8,128)S(1)} %get-tuple-element.22), channel_id=1, source_target_pairs={{0,384},{128,256},{256,128},{384,0},{1,385},{129,257},{257,129},{3... | collective-permute-start | bytes 98312 | tf_op jit(solution)/shard_map/ppermute | solution.py:29

commit v6 on v5

--- a/solution.py
+++ b/solution.py
@@ -52,32 +52,15 @@
     )(a, *others)
 
 
-def rank_kernel(place_ref, cot_any, right_any, weight_any, projected_ref, out_ref, cot_ref, given_ref, right_ref, sems):
-    given_rows = pl.ds(pl.multiple_of((1 - place_ref[1]) * 128, 128), 128)
-    copies = [
-        pltpu.make_async_copy(cot_any, cot_ref, sems.at[0]),
-        pltpu.make_async_copy(right_any, right_ref, sems.at[1]),
-        pltpu.make_async_copy(weight_any.at[given_rows], given_ref, sems.at[2]),
-    ]
-    for copy in copies:
-        copy.start()
-    out_ref[...] = jnp.zeros((16, 8, 128), f32)
-    out_ref[:, :, 16:32] = jnp.broadcast_to(projected_ref[...][None], (16, 8, 16))
-    for copy in copies:
-        copy.wait()
-    out_ref[:, :, 0:16] = dot_t(cot_ref[...], right_ref[...]).reshape(16, 8, 16)
-
-
 def pack_kernel(
-    place_ref, sent_ref, rank_ref, coeff_ref, cot_ref, weight_any, got_ref, inputs_any, after1, after2, after3,
-    x_any, back_ref, kept_ref, inputs_ref, x_ref, in_sems, out_sems,
+    place_ref, sent_ref, rank_ref, coeff_ref, cot_ref, weight_any, got_any, slices_ref, after1, after2, after3,
+    x_any, back_ref, kept_ref, rest_ref, kept_sem, out_sems,
 ):
-    kept_rows = pl.ds(pl.multiple_of(place_ref[1] * 128, 128), 128)
-    inputs_in = pltpu.make_async_copy(inputs_any, inputs_ref, in_sems.at[0])
-    kept_in = pltpu.make_async_copy(weight_any.at[kept_rows], kept_ref, in_sems.at[1])
-    inputs_in.start()
+    rows = pl.ds(pl.multiple_of(place_ref[1] * 128, 128), 128)
+    kept_in = pltpu.make_async_copy(weight_any.at[rows], kept_ref, kept_sem)
     kept_in.start()
-    outs = [pltpu.make_async_copy(got_ref, x_any.at[x, 128:256], out_sems.at[x]) for x in range(4)]
+    outs = [pltpu.make_async_copy(got_any.at[rows], x_any.at[x, 128:256], out_sems.at[x]) for x in range(4)]
+    outs += [pltpu.make_async_copy(slices_ref.at[x], x_any.at[x, 256:288], out_sems.at[4 + x]) for x in range(4)]
     for copy in outs:
         copy.start()
     lane = lax.broadcasted_iota(jnp.int32, (1, 128), 1)
@@ -102,19 +85,14 @@
         ],
         axis=0,
     ).astype(bf16)
+    rest_ref[0:16, :] = small
+    rest_ref[16:32, :] = right_high
+    rest_ref[32:48, :] = right_low
     kept_in.wait()
     for x in range(4):
-        outs.append(pltpu.make_async_copy(kept_ref, x_any.at[x, 0:128], out_sems.at[4 + x]))
-        outs[-1].start()
-    inputs_in.wait()
-    inputs = inputs_ref[...].astype(f32)
-    for x in range(4):
-        rows = [inputs[:, (h * 4 + x) * 512 : (h * 4 + x + 1) * 512] for h in range(4)]
-        x_ref[x, 0:32, :] = jnp.concatenate(rows, axis=0).astype(bf16)
-        x_ref[x, 32:48, :] = small
-        x_ref[x, 48:64, :] = right_high
-        x_ref[x, 64:80, :] = right_low
-        outs.append(pltpu.make_async_copy(x_ref.at[x], x_any.at[x, 256:336], out_sems.at[8 + x]))
+        outs.append(pltpu.make_async_copy(kept_ref, x_any.at[x, 0:128], out_sems.at[8 + x]))
+        outs.append(pltpu.make_async_copy(rest_ref, x_any.at[x, 288:336], out_sems.at[12 + x]))
+        outs[-2].start()
         outs[-1].start()
     for copy in outs:
         copy.wait()
@@ -131,7 +109,7 @@
 
 
 def other_kernel(
-    place_ref, done_ref, own_ref, other_ref, near_ref, far_ref, out_any, right_ref, out_ref, sems
+    place_ref, done_ref, own_ref, other_ref, near_ref, far_ref, out_ref, right_ref
 ):
     core, z_high = place_ref[0], place_ref[2]
     total = products((near_ref[...].reshape(512, 512), far_ref[...].reshape(512, 512)), other_ref)
@@ -149,7 +127,6 @@
     tok = jnp.concatenate(tok, axis=0)
     back = jnp.concatenate(back, axis=0)
     group = lax.rem(lax.broadcasted_iota(jnp.int32, (256, 1), 0), 32) // 8
-    copies = []
     for h in range(4):
         both = t_dot(tok, jnp.where(group == h, back, 0.0).astype(bf16))
         a = both[:, :128].reshape(16, 2, 8, 128)[:, 0]
@@ -157,15 +134,11 @@
         z = (a + b + singular).reshape(128, 128)
         high = z.astype(bf16).astype(f32)
         out_ref[h, :, 1024:1152] = (high + pltpu.roll(z - high, 64, 1)).astype(bf16)
-        copies.append(pltpu.make_async_copy(out_ref.at[h], out_any.at[h], sems.at[h]))
-        copies[-1].start()
     right = jnp.zeros((16, 512), f32)
     for ref in (own_ref, other_ref):
         for x in range(4):
             right += ref[x, 304:320, :].astype(f32) + ref[x, 320:336, :].astype(f32)
     right_ref[...] = right
-    for copy in copies:
-        copy.wait()
 
 
 def final_kernel(
@@ -213,39 +186,29 @@
     keep_float = keep_mask.astype(f32)
     coeff = adapter_scale * singular * keep_float
 
+    got = swap(weight, "zl", 2, 1)
+
+    back_part = dot_t(cotangent, right_factor).reshape(16, 8, 16)
     own_projected = jnp.dot(inputs, left_factor, preferred_element_type=f32)
-    rank_out, cot, given = call(
-        rank_kernel,
-        (shape((16, 8, 128), f32), shape((128, 512), bf16), shape((128, 512), bf16)),
-        [in_smem] + [in_hbm] * 3 + [in_vmem],
-        2 << 20,
-        1 << 20,
-        scratch=[pltpu.VMEM((16, 512), bf16), dma((3,))],
-    )(place, cotangent, right_factor, weight, own_projected)
+    rank_out = jnp.pad(back_part, ((0, 0), (0, 0), (0, 112))) + jnp.pad(own_projected, ((0, 0), (16, 96)))
     rank_in = lax.all_to_all(rank_out, ("zl", "y"), 0, 0)
 
-    got = swap(given, "zl", 2, 1)
-
+    cot = after(cotangent, got)
     cots = [cot] + [swap(cot, "zh", 4, k) for k in (1, 2, 3)]
     near = jnp.stack(cots)
     far = swap(near, "zl", 2, 1)
 
     coeff_lanes = jnp.pad(jnp.concatenate([coeff, coeff]), (0, 96)).reshape(1, 128)
+    slices = inputs.reshape(8, 4, 4, 512).transpose(2, 1, 0, 3).reshape(4, 32, 512)
     x_out, scaled_back = call(
         pack_kernel,
         (shape((4, 336, 512), bf16), shape((8, 128), bf16)),
-        [in_smem] + [in_vmem] * 4 + [in_hbm, in_vmem, in_hbm] + [anywhere] * 3,
+        [in_smem] + [in_vmem] * 4 + [anywhere] * 2 + [in_vmem] + [anywhere] * 3,
         16 << 20,
         3 << 20,
         out_specs=(in_hbm, in_vmem),
-        scratch=[
-            pltpu.VMEM((128, 512), bf16),
-            pltpu.VMEM((8, 8192), bf16),
-            pltpu.VMEM((4, 80, 512), bf16),
-            dma((2,)),
-            dma((12,)),
-        ],
-    )(place, rank_out, rank_in, coeff_lanes, cot, weight, got, inputs, *cots[1:])
+        scratch=[pltpu.VMEM((128, 512), bf16), pltpu.VMEM((48, 512), bf16), dma, dma((16,))],
+    )(place, rank_out, rank_in, coeff_lanes, cot, weight, got, slices, *cots[1:])
     x_in = after(lax.all_to_all(x_out, "x", 0, 0), far)
     x_other = swap(x_in, "c", 2, 1)
 
@@ -256,8 +219,6 @@
         [in_smem] + [in_vmem] * 5,
         1 << 29,
         5 << 20,
-        out_specs=(in_hbm, in_vmem),
-        scratch=[pltpu.VMEM((4, 128, 1152), bf16), dma((4,))],
     )(place, done, x_in, x_other, near, far)
     back = lax.all_to_all(out.reshape(64, 8, 1152), ("zh", "zl", "y"), 0, 0)
     right_sum = right_part + sum(swap(right_part, "zh", 4, k) for k in (1, 2, 3))

time: 121 us -> 123 us (1.017)
  waiting for transfers between devices: 41 us -> 51 us
  local copies, waits for them, and re-layouts: 5.48 us -> 2.1 us
  Pallas kernels: 9.31 us -> 6.23 us
  starting transfers between devices: 60.8 us -> 58.9 us
    ppermute x9, waiting for transfers between devices: 34.8 us -> 47.7 us  [swap(): return lax.ppermute(a, axis, [(i, i ^ mask) for i in range(count)])]
    unnamed x16 -> x13, local copies, waits for them, and re-layouts: 5.48 us -> 2.02 us
    all_to_all x1, waiting for transfers between devices: 3.01 us -> 0.01 us  [body(): rank_in = lax.all_to_all(rank_out, ('zl', 'y'), 0, 0)]
    ppermute x9, starting transfers between devices: 39.1 us -> 36.5 us  [swap(): return lax.ppermute(a, axis, [(i, i ^ mask) for i in range(count)])]
    pallas_call x1 -> x0, Pallas kernels: 1.79 us -> none  [body(): call(rank_kernel, (shape((16, 8, 128), f32), shape((128, 512), bf16), sha...]
    all_to_all x1, starting transfers between devices: 9.78 us -> 11.4 us  [body(): back = lax.all_to_all(out.reshape(64, 8, 1152), ('zh', 'zl', 'y'), 0, 0)]
  transfers between devices with their start and end apart: 12 -> 12, of which waited for: 6 -> 7; matrix products, arithmetic and copies ran while one was open for 1% -> 3% of each run, Pallas kernels for 1% -> 1%
where the time goes in v6:
time: 123 us
  starting transfers between devices  58.9 us (48%)
  waiting for transfers between devices  51 us (41%)
  Pallas kernels  6.23 us (5%)
  other arithmetic  2.19 us (2%)
  local copies, waits for them, and re-layouts  2.1 us (2%)
  matrix products  1.37 us (1%)
    ppermute x9, waiting for transfers between devices, swap(): return lax.ppermute(a, axis, [(i, i ^ mask) for i in range(count)])  47.7 us
    ppermute x9, starting transfers between devices, swap(): return lax.ppermute(a, axis, [(i, i ^ mask) for i in range(count)])  36.5 us
    all_to_all x1, starting transfers between devices, body(): back = lax.all_to_all(out.reshape(64, 8, 1152), ('zh', 'zl', 'y'), 0, 0)  11.4 us
    all_to_all x1, starting transfers between devices, body(): rank_in = lax.all_to_all(rank_out, ('zl', 'y'), 0, 0)  7 us
    all_to_all x1, starting transfers between devices, body(): x_in = after(lax.all_to_all(x_out, 'x', 0, 0), far)  4.03 us
    all_to_all x1, waiting for transfers between devices, body(): x_in = after(lax.all_to_all(x_out, 'x', 0, 0), far)  3.26 us
  transfers between devices with their start and end apart: 12, of which 7 were waited for; matrix products, arithmetic and copies ran while one was open for 3% of the time, Pallas kernels for 1%

profile of v6, /device:TPU:9, one launch (start us, length us, event | category | flops | bytes accessed | tf_op | source)
XLA Modules:
  0.0 122.6 jit_solution(10752088370789731910)
XLA Ops:
  0.6 0.0 copy-start
  0.6 0.0 copy-start.4
  0.7 0.0 copy-start.3
  0.7 1.0 copy.21.refs_0_
  1.6 4.0 %collective-permute-start = (bf16[256,512]{1,0:T(8,128)(2,1)}, bf16[256,512]{1,0:T(8,128)(2,1)S(1)}, u32[]{:S(2)}, u32[]{:S(2)}) collective-permute-start(bf16[256,512]{1,0:T(8,128)(2,1)} %weight_any.1), channel_id=1, source_target_pairs={{0,8},{8,0},{1,9},{9,1},{2,10},{10,2},{3,11},{11,3},{4,12},{12,4},... | collective-permute-start | bytes 786440 | tf_op jit(solution)/shard_map/ppermute | solution.py:29
  5.6 0.0 copy-done
  5.6 0.2 convolution_bitcast_fusion
  5.8 1.2 fusion.2
  7.0 0.1 pad.13
  7.1 0.7 pad_add_fusion.sent_ref
  7.7 7.0 %all-to-all-start = ((f32[16,8,128]{2,1,0:T(8,128)}), f32[16,8,128]{2,1,0:T(8,128)S(1)}, u32[]{:S(2)}, u32[]{:S(2)}) async-start(f32[16,8,128]{2,1,0:T(8,128)} %pad_add_fusion.sent_ref), calls=%async_computation | async-start | bytes 131072 | tf_op jit(solution)/shard_map/all_to_all | solution.py:194
  14.7 0.7 convert_multiply_fusion
  15.4 0.0 collective-permute-done.refs_1_.got_any
  15.4 5.8 %collective-permute-start.1 = (bf16[128,512]{1,0:T(8,128)(2,1)S(1)}, bf16[128,512]{1,0:T(8,128)(2,1)S(1)}, u32[]{:S(2)}, u32[]{:S(2)}) collective-permute-start(bf16[128,512]{1,0:T(8,128)(2,1)S(1)} %shard_map.102.cot_ref), channel_id=1, source_target_pairs={{0,128},{128,0},{256,384},{384,256},{1,129},{129,1},{257,385},{385... | collective-permute-start | bytes 393224 | tf_op jit(solution)/shard_map/ppermute | solution.py:29
  21.2 7.9 %collective-permute-start.2 = (bf16[128,512]{1,0:T(8,128)(2,1)S(1)}, bf16[128,512]{1,0:T(8,128)(2,1)S(1)}, u32[]{:S(2)}, u32[]{:S(2)}) collective-permute-start(bf16[128,512]{1,0:T(8,128)(2,1)S(1)} %shard_map.102.cot_ref), channel_id=1, source_target_pairs={{0,256},{128,384},{256,0},{384,128},{1,257},{129,385},{257,1},{385... | collective-permute-start | bytes 393224 | tf_op jit(solution)/shard_map/ppermute | solution.py:29
  29.2 1.9 %collective-permute-start.3 = (bf16[128,512]{1,0:T(8,128)(2,1)S(1)}, bf16[128,512]{1,0:T(8,128)(2,1)S(1)}, u32[]{:S(2)}, u32[]{:S(2)}) collective-permute-start(bf16[128,512]{1,0:T(8,128)(2,1)S(1)} %shard_map.102.cot_ref), channel_id=1, source_target_pairs={{0,384},{128,256},{256,128},{384,0},{1,385},{129,257},{257,129},{3... | collective-permute-start | bytes 393224 | tf_op jit(solution)/shard_map/ppermute | solution.py:29
  31.1 0.1 fusion.1.coeff_ref
  31.2 0.0 copy-done.4
  31.2 0.1 pad_add_fusion.1.place_ref
  31.3 0.0 all-to-all-done.rank_ref
  31.3 0.0 collective-permute-done.1.after1
  31.3 1.6 %collective-permute-done.2.after2 = bf16[128,512]{1,0:T(8,128)(2,1)S(1)} collective-permute-done((bf16[128,512]{1,0:T(8,128)(2,1)S(1)}, bf16[128,512]{1,0:T(8,128)(2,1)S(1)}, u32[]{:S(2)}, u32[]{:S(2)}) %collective-permute-start.2) | collective-permute-done | bytes 131104 | tf_op jit(solution)/shard_map/ppermute | solution.py:29
  32.9 8.8 %collective-permute-done.3.after3 = bf16[128,512]{1,0:T(8,128)(2,1)S(1)} collective-permute-done((bf16[128,512]{1,0:T(8,128)(2,1)S(1)}, bf16[128,512]{1,0:T(8,128)(2,1)S(1)}, u32[]{:S(2)}, u32[]{:S(2)}) %collective-permute-start.3) | collective-permute-done | bytes 131104 | tf_op jit(solution)/shard_map/ppermute | solution.py:29
  41.7 0.0 copy-done.3
  41.7 2.3 %shard_map.103 = (bf16[4,336,512]{2,1,0:T(8,128)(2,1)}, bf16[8,128]{1,0:T(8,128)(2,1)S(1)}) custom-call(s32[3]{0:T(128)S(1)} %pad_add_fusion.1.place_ref, f32[16,8,128]{2,1,0:T(8,128)} %pad_add_fusion.sent_ref, f32[16,8,128]{2,1,0:T(8,128)S(1)} %all-to-all-done.rank_ref, f32[1,128]{1,0:T(1,128)S(1)} %fusion.1.coeff_ref, ...), custom_call_target="tpu_custom_call" | custom-call | flops 16777216 | bytes 3145728 | tf_op jit(solution)/shard_map/pallas_call | solution.py:203
  44.0 4.0 %all-to-all-start.1 = ((bf16[4,336,512]{2,1,0:T(8,128)(2,1)}), bf16[4,336,512]{2,1,0:T(8,128)(2,1)S(1)}, u32[]{:S(2)}, u32[]{:S(2)}) async-start(bf16[4,336,512]{2,1,0:T(8,128)(2,1)} %get-tuple-element.11), calls=%async_computation.1 | async-start | bytes 2752512 | tf_op jit(solution)/shard_map/all_to_all | solution.py:212
  48.0 0.1 pad_maximum_fusion.near_ref
  48.1 1.9 %collective-permute-start.4 = (bf16[4,128,512]{2,1,0:T(8,128)(2,1)S(1)}, bf16[4,128,512]{2,1,0:T(8,128)(2,1)S(1)}, u32[]{:S(2)}, u32[]{:S(2)}) collective-permute-start(bf16[4,128,512]{2,1,0:T(8,128)(2,1)S(1)} %pad_maximum_fusion.near_ref), channel_id=1, source_target_pairs={{0,8},{8,0},{1,9},{9,1},{2,10},{10,2},{3,11},{11,3},{4,12},{12,4},... | collective-permute-start | bytes 1572872 | tf_op jit(solution)/shard_map/ppermute | solution.py:29
  50.0 12.6 %collective-permute-done.4.refs_1_.far_ref = bf16[4,128,512]{2,1,0:T(8,128)(2,1)S(1)} collective-permute-done((bf16[4,128,512]{2,1,0:T(8,128)(2,1)S(1)}, bf16[4,128,512]{2,1,0:T(8,128)(2,1)S(1)}, u32[]{:S(2)}, u32[]{:S(2)}) %collective-permute-start.4) | collective-permute-done | bytes 524320 | tf_op jit(solution)/shard_map/ppermute | solution.py:29
  62.7 3.3 %all-to-all-done.1.refs_0_ = bf16[4,336,512]{2,1,0:T(8,128)(2,1)S(1)} async-done(((bf16[4,336,512]{2,1,0:T(8,128)(2,1)}), bf16[4,336,512]{2,1,0:T(8,128)(2,1)S(1)}, u32[]{:S(2)}, u32[]{:S(2)}) %all-to-all-start.1) | async-done | bytes 1376288 | tf_op jit(solution)/shard_map/all_to_all | solution.py:212
  65.9 3.6 %collective-permute-start.5 = (bf16[4,336,512]{2,1,0:T(8,128)(2,1)S(1)}, bf16[4,336,512]{2,1,0:T(8,128)(2,1)S(1)}, u32[]{:S(2)}, u32[]{:S(2)}) collective-permute-start(bf16[4,336,512]{2,1,0:T(8,128)(2,1)S(1)} %shard_map.104.own_ref), channel_id=1, source_target_pairs={{0,16},{16,0},{1,17},{17,1},{2,18},{18,2},{3,19},{19,3},{4,20},{20... | collective-permute-start | bytes 4128776 | tf_op jit(solution)/shard_map/ppermute | solution.py:29
  69.5 0.7 shard_map.105.done_ref
  70.2 2.0 %collective-permute-done.5.other_ref = bf16[4,336,512]{2,1,0:T(8,128)(2,1)S(1)} collective-permute-done((bf16[4,336,512]{2,1,0:T(8,128)(2,1)S(1)}, bf16[4,336,512]{2,1,0:T(8,128)(2,1)S(1)}, u32[]{:S(2)}, u32[]{:S(2)}) %collective-permute-start.5) | collective-permute-done | bytes 1376288 | tf_op jit(solution)/shard_map/ppermute | solution.py:29
  72.2 1.5 %shard_map.106 = (bf16[4,128,1152]{2,1,0:T(8,128)(2,1)S(1)}, f32[16,512]{1,0:T(8,128)S(1)}) custom-call(s32[3]{0:T(128)S(1)} %pad_add_fusion.1.place_ref, bf16[4,128,512]{2,1,0:T(8,128)(2,1)S(1)} %shard_map.105.done_ref, bf16[4,336,512]{2,1,0:T(8,128)(2,1)S(1)} %shard_map.104.own_ref, bf16[4,336,512]{2,1,0:T(8,128)(2,1)S(1)} %collective-permute-done.5.other_ref, ...), custom_call_target="tpu_custom_call" | custom-call | flops 536870912 | bytes 5242880 | tf_op jit(solution)/shard_map/pallas_call | solution.py:216
  73.7 0.0 copy-start.1
  73.7 1.0 copy-done.1
  74.7 11.4 %all-to-all-start.2 = ((bf16[64,8,1152]{2,1,0:T(8,128)(2,1)}), bf16[64,8,1152]{2,1,0:T(8,128)(2,1)S(1)}, u32[]{:S(2)}, u32[]{:S(2)}) async-start(bf16[64,8,1152]{2,1,0:T(8,128)(2,1)} %bitcast.27), calls=%async_computation.2 | async-start | bytes 2359296 | tf_op jit(solution)/shard_map/all_to_all | solution.py:223
  86.1 4.0 %collective-permute-start.6 = (f32[16,512]{1,0:T(8,128)S(1)}, f32[16,512]{1,0:T(8,128)S(1)}, u32[]{:S(2)}, u32[]{:S(2)}) collective-permute-start(f32[16,512]{1,0:T(8,128)S(1)} %get-tuple-element.16), channel_id=1, source_target_pairs={{0,128},{128,0},{256,384},{384,256},{1,129},{129,1},{257,385},{385... | collective-permute-start | bytes 98312 | tf_op jit(solution)/shard_map/ppermute | solution.py:29
  90.1 5.4 %collective-permute-start.7 = (f32[16,512]{1,0:T(8,128)S(1)}, f32[16,512]{1,0:T(8,128)S(1)}, u32[]{:S(2)}, u32[]{:S(2)}) collective-permute-start(f32[16,512]{1,0:T(8,128)S(1)} %get-tuple-element.16), channel_id=1, source_target_pairs={{0,256},{128,384},{256,0},{384,128},{1,257},{129,385},{257,1},{385... | collective-permute-start | bytes 98312 | tf_op jit(solution)/shard_map/ppermute | solution.py:29
  95.5 2.0 %collective-permute-start.8 = (f32[16,512]{1,0:T(8,128)S(1)}, f32[16,512]{1,0:T(8,128)S(1)}, u32[]{:S(2)}, u32[]{:S(2)}) collective-permute-start(f32[16,512]{1,0:T(8,128)S(1)} %get-tuple-element.16), channel_id=1, source_target_pairs={{0,384},{128,256},{256,128},{384,0},{1,385},{129,257},{257,129},{3... | collective-permute-start | bytes 98312 | tf_op jit(solution)/shard_map/ppermute | solution.py:29
  97.5 0.0 copy-done.5
  97.5 14.0 %collective-permute-done.6 = f32[16,512]{1,0:T(8,128)S(1)} collective-permute-done((f32[16,512]{1,0:T(8,128)S(1)}, f32[16,512]{1,0:T(8,128)S(1)}, u32[]{:S(2)}, u32[]{:S(2)}) %collective-permute-start.6) | collective-permute-done | bytes 32800 | tf_op jit(solution)/shard_map/ppermute | solution.py:29
  111.6 8.6 %collective-permute-done.7 = f32[16,512]{1,0:T(8,128)S(1)} collective-permute-done((f32[16,512]{1,0:T(8,128)S(1)}, f32[16,512]{1,0:T(8,128)S(1)}, u32[]{:S(2)}, u32[]{:S(2)}) %collective-permute-start.7) | collective-permute-done | bytes 32800 | tf_op jit(solution)/shard_map/ppermute | solution.py:29
  120.2 0.0 collective-permute-done.8
  120.2 0.6 add_multiply_fusion
  120.8 0.0 all-to-all-done.2.back_ref
  120.8 0.0 copy-done.2
  120.9 1.7 %shard_map.107 = (bf16[8,8192]{1,0:T(8,128)(2,1)}, f32[16,16]{1,0:T(8,128)}, f32[1,16]{1,0:T(1,128)}) custom-call(s32[3]{0:T(128)S(1)} %pad_add_fusion.1.place_ref, bf16[64,8,1152]{2,1,0:T(8,128)(2,1)S(1)} %all-to-all-done.2.back_ref, bf16[8,128]{1,0:T(8,128)(2,1)S(1)} %get-tuple-element.13.scaled_ref, bf16[16,8192]{1,0:T(8,128)(2,1)S(1)} %bitcast.28, ...), custom_call_target="tpu_custom_call" | custom-call | flops 2097152 | bytes 2097152 | tf_op jit(solution)/shard_map/pallas_call | solution.py:226
  (6 shorter events, 0.0 us)
Async XLA Ops:
  0.6 5.0 %copy-start = (bf16[16,512]{1,0:T(8,128)(2,1)S(1)}, bf16[16,512]{1,0:T(8,128)(2,1)}, u32[]{:S(2)}) copy-start(bf16[16,512]{1,0:T(8,128)(2,1)} %param.11) | copy-start | bytes 49156
  0.6 30.5 %copy-start.4 = (bf16[8,8192]{1,0:T(8,128)(2,1)S(1)}, bf16[8,8192]{1,0:T(8,128)(2,1)}, u32[]{:S(2)}) copy-start(bf16[8,8192]{1,0:T(8,128)(2,1)} %param.7) | copy-start | bytes 393220
  0.7 41.0 %copy-start.3 = (bf16[256,512]{1,0:T(8,128)(2,1)S(1)}, bf16[256,512]{1,0:T(8,128)(2,1)}, u32[]{:S(2)}) copy-start(bf16[256,512]{1,0:T(8,128)(2,1)} %weight_any.1) | copy-start | bytes 786436
  1.6 13.8 %collective-permute-start = (bf16[256,512]{1,0:T(8,128)(2,1)}, bf16[256,512]{1,0:T(8,128)(2,1)S(1)}, u32[]{:S(2)}, u32[]{:S(2)}) collective-permute-start(bf16[256,512]{1,0:T(8,128)(2,1)} %weight_any.1), channel_id=1, source_target_pairs={{0,8},{8,0},{1,9},{9,1},{2,10},{10,2},{3,11},{11,3},{4,12},{12,4},... | collective-permute-start | bytes 786440 | tf_op jit(solution)/shard_map/ppermute | solution.py:29
  7.7 23.5 %all-to-all-start = ((f32[16,8,128]{2,1,0:T(8,128)}), f32[16,8,128]{2,1,0:T(8,128)S(1)}, u32[]{:S(2)}, u32[]{:S(2)}) async-start(f32[16,8,128]{2,1,0:T(8,128)} %pad_add_fusion.sent_ref), calls=%async_computation | async-start | bytes 131072 | tf_op jit(solution)/shard_map/all_to_all | solution.py:194
  15.4 15.9 %collective-permute-start.1 = (bf16[128,512]{1,0:T(8,128)(2,1)S(1)}, bf16[128,512]{1,0:T(8,128)(2,1)S(1)}, u32[]{:S(2)}, u32[]{:S(2)}) collective-permute-start(bf16[128,512]{1,0:T(8,128)(2,1)S(1)} %shard_map.102.cot_ref), channel_id=1, source_target_pairs={{0,128},{128,0},{256,384},{384,256},{1,129},{129,1},{257,385},{385... | collective-permute-start | bytes 393224 | tf_op jit(solution)/shard_map/ppermute | solution.py:29
  21.2 11.6 %collective-permute-start.2 = (bf16[128,512]{1,0:T(8,128)(2,1)S(1)}, bf16[128,512]{1,0:T(8,128)(2,1)S(1)}, u32[]{:S(2)}, u32[]{:S(2)}) collective-permute-start(bf16[128,512]{1,0:T(8,128)(2,1)S(1)} %shard_map.102.cot_ref), channel_id=1, source_target_pairs={{0,256},{128,384},{256,0},{384,128},{1,257},{129,385},{257,1},{385... | collective-permute-start | bytes 393224 | tf_op jit(solution)/shard_map/ppermute | solution.py:29
  29.2 12.5 %collective-permute-start.3 = (bf16[128,512]{1,0:T(8,128)(2,1)S(1)}, bf16[128,512]{1,0:T(8,128)(2,1)S(1)}, u32[]{:S(2)}, u32[]{:S(2)}) collective-permute-start(bf16[128,512]{1,0:T(8,128)(2,1)S(1)} %shard_map.102.cot_ref), channel_id=1, source_target_pairs={{0,384},{128,256},{256,128},{384,0},{1,385},{129,257},{257,129},{3... | collective-permute-start | bytes 393224 | tf_op jit(solution)/shard_map/ppermute | solution.py:29
  44.0 21.9 %all-to-all-start.1 = ((bf16[4,336,512]{2,1,0:T(8,128)(2,1)}), bf16[4,336,512]{2,1,0:T(8,128)(2,1)S(1)}, u32[]{:S(2)}, u32[]{:S(2)}) async-start(bf16[4,336,512]{2,1,0:T(8,128)(2,1)} %get-tuple-element.11), calls=%async_computation.1 | async-start | bytes 2752512 | tf_op jit(solution)/shard_map/all_to_all | solution.py:212
  48.1 14.6 %collective-permute-start.4 = (bf16[4,128,512]{2,1,0:T(8,128)(2,1)S(1)}, bf16[4,128,512]{2,1,0:T(8,128)(2,1)S(1)}, u32[]{:S(2)}, u32[]{:S(2)}) collective-permute-start(bf16[4,128,512]{2,1,0:T(8,128)(2,1)S(1)} %pad_maximum_fusion.near_ref), channel_id=1, source_target_pairs={{0,8},{8,0},{1,9},{9,1},{2,10},{10,2},{3,11},{11,3},{4,12},{12,4},... | collective-permute-start | bytes 1572872 | tf_op jit(solution)/shard_map/ppermute | solution.py:29
  65.9 6.3 %collective-permute-start.5 = (bf16[4,336,512]{2,1,0:T(8,128)(2,1)S(1)}, bf16[4,336,512]{2,1,0:T(8,128)(2,1)S(1)}, u32[]{:S(2)}, u32[]{:S(2)}) collective-permute-start(bf16[4,336,512]{2,1,0:T(8,128)(2,1)S(1)} %shard_map.104.own_ref), channel_id=1, source_target_pairs={{0,16},{16,0},{1,17},{17,1},{2,18},{18,2},{3,19},{19,3},{4,20},{20... | collective-permute-start | bytes 4128776 | tf_op jit(solution)/shard_map/ppermute | solution.py:29
  73.7 1.0 copy-start.1
  74.7 22.8 %copy-start.5 = (s32[16]{0:T(128)S(1)}, s32[16]{0:T(128)}, u32[]{:S(2)}) copy-start(s32[16]{0:T(128)} %param.13) | copy-start | bytes 196
  74.7 46.1 %copy-start.2 = (bf16[8192,16]{0,1:T(8,128)(2,1)S(1)}, bf16[8192,16]{0,1:T(8,128)(2,1)}, u32[]{:S(2)}) copy-start(bf16[8192,16]{0,1:T(8,128)(2,1)} %param.10) | copy-start | bytes 786436
  74.7 46.1 %all-to-all-start.2 = ((bf16[64,8,1152]{2,1,0:T(8,128)(2,1)}), bf16[64,8,1152]{2,1,0:T(8,128)(2,1)S(1)}, u32[]{:S(2)}, u32[]{:S(2)}) async-start(bf16[64,8,1152]{2,1,0:T(8,128)(2,1)} %bitcast.27), calls=%async_computation.2 | async-start | bytes 2359296 | tf_op jit(solution)/shard_map/all_to_all | solution.py:223
  86.1 25.5 %collective-permute-start.6 = (f32[16,512]{1,0:T(8,128)S(1)}, f32[16,512]{1,0:T(8,128)S(1)}, u32[]{:S(2)}, u32[]{:S(2)}) collective-permute-start(f32[16,512]{1,0:T(8,128)S(1)} %get-tuple-element.16), channel_id=1, source_target_pairs={{0,128},{128,0},{256,384},{384,256},{1,129},{129,1},{257,385},{385... | collective-permute-start | bytes 98312 | tf_op jit(solution)/shard_map/ppermute | solution.py:29
  90.1 30.1 %collective-permute-start.7 = (f32[16,512]{1,0:T(8,128)S(1)}, f32[16,512]{1,0:T(8,128)S(1)}, u32[]{:S(2)}, u32[]{:S(2)}) collective-permute-start(f32[16,512]{1,0:T(8,128)S(1)} %get-tuple-element.16), channel_id=1, source_target_pairs={{0,256},{128,384},{256,0},{384,128},{1,257},{129,385},{257,1},{385... | collective-permute-start | bytes 98312 | tf_op jit(solution)/shard_map/ppermute | solution.py:29
  95.5 24.7 %collective-permute-start.8 = (f32[16,512]{1,0:T(8,128)S(1)}, f32[16,512]{1,0:T(8,128)S(1)}, u32[]{:S(2)}, u32[]{:S(2)}) collective-permute-start(f32[16,512]{1,0:T(8,128)S(1)} %get-tuple-element.16), channel_id=1, source_target_pairs={{0,384},{128,256},{256,128},{384,0},{1,385},{129,257},{257,129},{3... | collective-permute-start | bytes 98312 | tf_op jit(solution)/shard_map/ppermute | solution.py:29

commit v7 on v6

--- a/solution.py
+++ b/solution.py
@@ -53,7 +53,7 @@
 
 
 def pack_kernel(
-    place_ref, sent_ref, rank_ref, coeff_ref, cot_ref, weight_any, got_any, slices_ref, after1, after2, after3,
+    place_ref, sent_ref, rank_ref, coeff_ref, cot_ref, weight_any, got_any, slices_ref, after1, after3,
     x_any, back_ref, kept_ref, rest_ref, kept_sem, out_sems,
 ):
     rows = pl.ds(pl.multiple_of(place_ref[1] * 128, 128), 128)
@@ -71,8 +71,6 @@
     back_ref[...] = back
     fwd = (jnp.where((lane >= 16) & (lane < 32), rank, 0.0) * coeff).astype(bf16)
     right = t_dot(fwd.reshape(128, 128), cot_ref[...])[16:32]
-    right_high = right.astype(bf16)
-    right_low = (right - right_high.astype(f32)).astype(bf16)
     projected = pltpu.roll(sent_ref[0], 112, 1)
     singular = jnp.broadcast_to(jnp.sum(projected * own, axis=0, keepdims=True), (8, 128))
     high = singular.astype(bf16).astype(f32)
@@ -86,12 +84,11 @@
         axis=0,
     ).astype(bf16)
     rest_ref[0:16, :] = small
-    rest_ref[16:32, :] = right_high
-    rest_ref[32:48, :] = right_low
+    rest_ref[16:32, :] = right.astype(bf16)
     kept_in.wait()
     for x in range(4):
         outs.append(pltpu.make_async_copy(kept_ref, x_any.at[x, 0:128], out_sems.at[8 + x]))
-        outs.append(pltpu.make_async_copy(rest_ref, x_any.at[x, 288:336], out_sems.at[12 + x]))
+        outs.append(pltpu.make_async_copy(rest_ref, x_any.at[x, 288:320], out_sems.at[12 + x]))
         outs[-2].start()
         outs[-1].start()
     for copy in outs:
@@ -104,18 +101,22 @@
     return total.astype(bf16).reshape(4, 128, 512)
 
 
-def own_kernel(own_ref, near_ref, far_ref, out_ref):
-    out_ref[...] = products((near_ref[...].reshape(512, 512), far_ref[...].reshape(512, 512)), own_ref)
+def rows_of(three_ref, last_ref):
+    return jnp.concatenate([three_ref[...].reshape(384, 512), last_ref[...]], axis=0)
+
+
+def own_kernel(own_ref, near_ref, last_ref, far_ref, far_last_ref, out_ref):
+    out_ref[...] = products((rows_of(near_ref, last_ref), rows_of(far_ref, far_last_ref)), own_ref)
 
 
 def other_kernel(
-    place_ref, done_ref, own_ref, other_ref, near_ref, far_ref, out_ref, right_ref
+    place_ref, done_ref, own_ref, other_ref, near_ref, last_ref, far_ref, far_last_ref, out_ref, right_ref
 ):
     core, z_high = place_ref[0], place_ref[2]
-    total = products((near_ref[...].reshape(512, 512), far_ref[...].reshape(512, 512)), other_ref)
-    for k in range(4):
-        out_ref[z_high ^ k, :, 0:512] = done_ref[k]
-        out_ref[z_high ^ k, :, 512:1024] = total[k]
+    total = products((rows_of(near_ref, last_ref), rows_of(far_ref, far_last_ref)), other_ref)
+    for i, k in enumerate((0, 1, 3, 2)):
+        out_ref[z_high ^ k, :, 0:512] = done_ref[i]
+        out_ref[z_high ^ k, :, 512:1024] = total[i]
     tok, back, singular = [], [], jnp.zeros((1, 128), f32)
     for ref in (own_ref, other_ref):
         for x in range(4):
@@ -137,7 +138,7 @@
     right = jnp.zeros((16, 512), f32)
     for ref in (own_ref, other_ref):
         for x in range(4):
-            right += ref[x, 304:320, :].astype(f32) + ref[x, 320:336, :].astype(f32)
+            right += ref[x, 304:320, :].astype(f32)
     right_ref[...] = right
 
 
@@ -195,33 +196,38 @@
 
     cot = after(cotangent, got)
     cots = [cot] + [swap(cot, "zh", 4, k) for k in (1, 2, 3)]
-    near = jnp.stack(cots)
+    near = jnp.stack([cots[0], cots[1], cots[3]])
     far = swap(near, "zl", 2, 1)
+    last = cots[2]
+    far_last = swap(last, "zl", 2, 1)
 
     coeff_lanes = jnp.pad(jnp.concatenate([coeff, coeff]), (0, 96)).reshape(1, 128)
     slices = inputs.reshape(8, 4, 4, 512).transpose(2, 1, 0, 3).reshape(4, 32, 512)
     x_out, scaled_back = call(
         pack_kernel,
-        (shape((4, 336, 512), bf16), shape((8, 128), bf16)),
-        [in_smem] + [in_vmem] * 4 + [anywhere] * 2 + [in_vmem] + [anywhere] * 3,
+        (shape((4, 320, 512), bf16), shape((8, 128), bf16)),
+        [in_smem] + [in_vmem] * 4 + [anywhere] * 2 + [in_vmem] + [anywhere] * 2,
         16 << 20,
         3 << 20,
         out_specs=(in_hbm, in_vmem),
-        scratch=[pltpu.VMEM((128, 512), bf16), pltpu.VMEM((48, 512), bf16), dma, dma((16,))],
-    )(place, rank_out, rank_in, coeff_lanes, cot, weight, got, slices, *cots[1:])
-    x_in = after(lax.all_to_all(x_out, "x", 0, 0), far)
+        scratch=[pltpu.VMEM((128, 512), bf16), pltpu.VMEM((32, 512), bf16), dma, dma((16,))],
+    )(place, rank_out, rank_in, coeff_lanes, cot, weight, got, slices, cots[1], cots[3])
+    x_in = after(lax.all_to_all(x_out, "x", 0, 0), far, far_last)
     x_other = swap(x_in, "c", 2, 1)
 
-    done = call(own_kernel, shape((4, 128, 512), bf16), [in_vmem] * 3, 1 << 29, 3 << 20)(x_in, near, far)
+    done = call(own_kernel, shape((4, 128, 512), bf16), [in_vmem] * 5, 1 << 29, 3 << 20)(
+        x_in, near, last, far, far_last
+    )
     out, right_part = call(
         other_kernel,
         (shape((4, 128, 1152), bf16), shape((16, 512), f32)),
-        [in_smem] + [in_vmem] * 5,
+        [in_smem] + [in_vmem] * 7,
         1 << 29,
         5 << 20,
-    )(place, done, x_in, x_other, near, far)
+    )(place, done, x_in, x_other, near, last, far, far_last)
     back = lax.all_to_all(out.reshape(64, 8, 1152), ("zh", "zl", "y"), 0, 0)
-    right_sum = right_part + sum(swap(right_part, "zh", 4, k) for k in (1, 2, 3))
+    right_sent = right_part.astype(bf16)
+    right_sum = right_part + sum(swap(right_sent, "zh", 4, k).astype(f32) for k in (1, 2, 3))
 
     grad_inputs, grad_left, grad_singular = call(
         final_kernel,

time: 123 us -> 121 us (0.984)
  the two profiles are of different devices: /device:TPU:9 before, /device:TPU:6 now
where the time goes in v7:
time: 121 us; the launch traced here: 120 us
  starting transfers between devices  63.3 us (52%)
  waiting for transfers between devices  44.4 us (37%)
  Pallas kernels  7.26 us (6%)
  other arithmetic  2.18 us (2%)
  matrix products  1.36 us (1%)
    ppermute x10, starting transfers between devices, swap(): return lax.ppermute(a, axis, [(i, i ^ mask) for i in range(count)])  43.7 us
    ppermute x10, waiting for transfers between devices, swap(): return lax.ppermute(a, axis, [(i, i ^ mask) for i in range(count)])  33.6 us
    all_to_all x1, waiting for transfers between devices, body(): back = lax.all_to_all(out.reshape(64, 8, 1152), ('zh', 'zl', 'y'), 0, 0)  10.8 us
    all_to_all x1, starting transfers between devices, body(): back = lax.all_to_all(out.reshape(64, 8, 1152), ('zh', 'zl', 'y'), 0, 0)  7.67 us
    all_to_all x1, starting transfers between devices, body(): rank_in = lax.all_to_all(rank_out, ('zl', 'y'), 0, 0)  7.21 us
    all_to_all x1, starting transfers between devices, body(): x_in = after(lax.all_to_all(x_out, 'x', 0, 0), far, far_last)  4.78 us
    pallas_call x1, Pallas kernels, body(): call(other_kernel, (shape((4, 128, 1152), bf16), shape((16, 512), f32)),...  2.53 us
  transfers between devices with their start and end apart: 13, of which 6 were waited for; matrix products, arithmetic and copies ran while one was open for 3% of the time, Pallas kernels for 1%

profile of v7, /device:TPU:6, one launch (start us, length us, event | category | flops | bytes accessed | tf_op | source)
XLA Modules:
  0.0 120.5 jit_solution(14085786986073560773)
XLA Ops:
  0.6 0.0 copy-start
  0.6 0.0 copy-start.3
  0.7 0.0 copy-start.2
  0.7 1.0 copy.21.refs_0_
  1.6 4.3 %collective-permute-start = (bf16[256,512]{1,0:T(8,128)(2,1)}, bf16[256,512]{1,0:T(8,128)(2,1)S(1)}, u32[]{:S(2)}, u32[]{:S(2)}) collective-permute-start(bf16[256,512]{1,0:T(8,128)(2,1)} %weight_any.1), channel_id=1, source_target_pairs={{0,8},{8,0},{1,9},{9,1},{2,10},{10,2},{3,11},{11,3},{4,12},{12,4},... | collective-permute-start | bytes 786440 | tf_op jit(solution)/shard_map/ppermute | solution.py:29
  5.9 0.0 copy-done
  5.9 0.2 convolution_bitcast_fusion
  6.1 1.2 %fusion.2 = f32[8,16]{1,0:T(8,128)S(1)} fusion(bf16[8,8192]{1,0:T(8,128)(2,1)} %param.7, bf16[8192,16]{0,1:T(8,128)(2,1)} %param.10), kind=kOutput, calls=%fused_computation.12 | convolution fusion | flops 2097152 | bytes 393728 | tf_op jit(solution)/shard_map/dot_general | solution.py:193
  7.3 0.1 pad.13
  7.4 0.7 pad_add_fusion.sent_ref
  8.0 7.2 %all-to-all-start = ((f32[16,8,128]{2,1,0:T(8,128)}), f32[16,8,128]{2,1,0:T(8,128)S(1)}, u32[]{:S(2)}, u32[]{:S(2)}) async-start(f32[16,8,128]{2,1,0:T(8,128)} %pad_add_fusion.sent_ref), calls=%async_computation | async-start | bytes 131072 | tf_op jit(solution)/shard_map/all_to_all | solution.py:195
  15.2 0.7 convert_multiply_fusion
  15.9 0.0 collective-permute-done.refs_1_.got_any
  15.9 6.1 %collective-permute-start.1 = (bf16[128,512]{1,0:T(8,128)(2,1)S(1)}, bf16[128,512]{1,0:T(8,128)(2,1)S(1)}, u32[]{:S(2)}, u32[]{:S(2)}) collective-permute-start(bf16[128,512]{1,0:T(8,128)(2,1)S(1)} %shard_map.102.cot_ref), channel_id=1, source_target_pairs={{0,128},{128,0},{256,384},{384,256},{1,129},{129,1},{257,385},{385... | collective-permute-start | bytes 393224 | tf_op jit(solution)/shard_map/ppermute | solution.py:29
  22.0 6.4 %collective-permute-start.2 = (bf16[128,512]{1,0:T(8,128)(2,1)S(1)}, bf16[128,512]{1,0:T(8,128)(2,1)S(1)}, u32[]{:S(2)}, u32[]{:S(2)}) collective-permute-start(bf16[128,512]{1,0:T(8,128)(2,1)S(1)} %shard_map.102.cot_ref), channel_id=1, source_target_pairs={{0,384},{128,256},{256,128},{384,0},{1,385},{129,257},{257,129},{3... | collective-permute-start | bytes 393224 | tf_op jit(solution)/shard_map/ppermute | solution.py:29
  28.4 0.1 fusion.1.coeff_ref
  28.5 0.0 copy-done.3
  28.5 0.1 pad_add_fusion.1.place_ref
  28.6 0.0 all-to-all-done.rank_ref
  28.6 0.0 collective-permute-done.1.after1
  28.6 5.5 %collective-permute-done.2.after3 = bf16[128,512]{1,0:T(8,128)(2,1)S(1)} collective-permute-done((bf16[128,512]{1,0:T(8,128)(2,1)S(1)}, bf16[128,512]{1,0:T(8,128)(2,1)S(1)}, u32[]{:S(2)}, u32[]{:S(2)}) %collective-permute-start.2) | collective-permute-done | bytes 131104 | tf_op jit(solution)/shard_map/ppermute | solution.py:29
  34.1 0.0 copy-done.2
  34.1 2.3 %shard_map.103 = (bf16[4,320,512]{2,1,0:T(8,128)(2,1)}, bf16[8,128]{1,0:T(8,128)(2,1)S(1)}) custom-call(s32[3]{0:T(128)S(1)} %pad_add_fusion.1.place_ref, f32[16,8,128]{2,1,0:T(8,128)} %pad_add_fusion.sent_ref, f32[16,8,128]{2,1,0:T(8,128)S(1)} %all-to-all-done.rank_ref, f32[1,128]{1,0:T(1,128)S(1)} %fusion.1.coeff_ref, ...), custom_call_target="tpu_custom_call" | custom-call | flops 16777216 | bytes 3145728 | tf_op jit(solution)/shard_map/pallas_call | solution.py:206
  36.4 4.8 %all-to-all-start.1 = ((bf16[4,320,512]{2,1,0:T(8,128)(2,1)}), bf16[4,320,512]{2,1,0:T(8,128)(2,1)S(1)}, u32[]{:S(2)}, u32[]{:S(2)}) async-start(bf16[4,320,512]{2,1,0:T(8,128)(2,1)} %get-tuple-element.11), calls=%async_computation.1 | async-start | bytes 2621440 | tf_op jit(solution)/shard_map/all_to_all | solution.py:215
  41.2 2.9 %collective-permute-start.3 = (bf16[3,128,512]{2,1,0:T(8,128)(2,1)S(1)}, bf16[3,128,512]{2,1,0:T(8,128)(2,1)S(1)}, u32[]{:S(2)}, u32[]{:S(2)}) collective-permute-start(bf16[3,128,512]{2,1,0:T(8,128)(2,1)S(1)} %pad_maximum_fusion.near_ref), channel_id=1, source_target_pairs={{0,8},{8,0},{1,9},{9,1},{2,10},{10,2},{3,11},{11,3},{4,12},{12,4},... | collective-permute-start | bytes 1179656 | tf_op jit(solution)/shard_map/ppermute | solution.py:29
  44.1 7.8 %collective-permute-start.4 = (bf16[128,512]{1,0:T(8,128)(2,1)S(1)}, bf16[128,512]{1,0:T(8,128)(2,1)S(1)}, u32[]{:S(2)}, u32[]{:S(2)}) collective-permute-start(bf16[128,512]{1,0:T(8,128)(2,1)S(1)} %shard_map.102.cot_ref), channel_id=1, source_target_pairs={{0,256},{128,384},{256,0},{384,128},{1,257},{129,385},{257,1},{385... | collective-permute-start | bytes 393224 | tf_op jit(solution)/shard_map/ppermute | solution.py:29
  51.9 11.7 %collective-permute-done.4.last_ref = bf16[128,512]{1,0:T(8,128)(2,1)S(1)} collective-permute-done((bf16[128,512]{1,0:T(8,128)(2,1)S(1)}, bf16[128,512]{1,0:T(8,128)(2,1)S(1)}, u32[]{:S(2)}, u32[]{:S(2)}) %collective-permute-start.4) | collective-permute-done | bytes 131104 | tf_op jit(solution)/shard_map/ppermute | solution.py:29
  63.6 2.1 %collective-permute-start.5 = (bf16[128,512]{1,0:T(8,128)(2,1)S(1)}, bf16[128,512]{1,0:T(8,128)(2,1)S(1)}, u32[]{:S(2)}, u32[]{:S(2)}) collective-permute-start(bf16[128,512]{1,0:T(8,128)(2,1)S(1)} %collective-permute-done.4.last_ref), channel_id=1, source_target_pairs={{0,8},{8,0},{1,9},{9,1},{2,10},{10,2},{3,11},{11,3},{4,12},{12,4},... | collective-permute-start | bytes 393224 | tf_op jit(solution)/shard_map/ppermute | solution.py:29
  65.7 4.8 %collective-permute-done.5.refs_2_.far_last_ref = bf16[128,512]{1,0:T(8,128)(2,1)S(1)} collective-permute-done((bf16[128,512]{1,0:T(8,128)(2,1)S(1)}, bf16[128,512]{1,0:T(8,128)(2,1)S(1)}, u32[]{:S(2)}, u32[]{:S(2)}) %collective-permute-start.5) | collective-permute-done | bytes 131104 | tf_op jit(solution)/shard_map/ppermute | solution.py:29
  70.5 0.0 collective-permute-done.3.refs_1_.far_ref
  70.5 0.0 all-to-all-done.1.refs_0_
  70.5 1.9 %collective-permute-start.6 = (bf16[4,320,512]{2,1,0:T(8,128)(2,1)S(1)}, bf16[4,320,512]{2,1,0:T(8,128)(2,1)S(1)}, u32[]{:S(2)}, u32[]{:S(2)}) collective-permute-start(bf16[4,320,512]{2,1,0:T(8,128)(2,1)S(1)} %shard_map.104.own_ref), channel_id=1, source_target_pairs={{0,16},{16,0},{1,17},{17,1},{2,18},{18,2},{3,19},{19,3},{4,20},{20... | collective-permute-start | bytes 3932168 | tf_op jit(solution)/shard_map/ppermute | solution.py:29
  72.4 0.7 shard_map.105.done_ref
  73.2 2.3 %collective-permute-done.6.other_ref = bf16[4,320,512]{2,1,0:T(8,128)(2,1)S(1)} collective-permute-done((bf16[4,320,512]{2,1,0:T(8,128)(2,1)S(1)}, bf16[4,320,512]{2,1,0:T(8,128)(2,1)S(1)}, u32[]{:S(2)}, u32[]{:S(2)}) %collective-permute-start.6) | collective-permute-done | bytes 1310752 | tf_op jit(solution)/shard_map/ppermute | solution.py:29
  75.4 2.5 %shard_map.106 = (bf16[4,128,1152]{2,1,0:T(8,128)(2,1)}, f32[16,512]{1,0:T(8,128)S(1)}) custom-call(s32[3]{0:T(128)S(1)} %pad_add_fusion.1.place_ref, bf16[4,128,512]{2,1,0:T(8,128)(2,1)S(1)} %shard_map.105.done_ref, bf16[4,320,512]{2,1,0:T(8,128)(2,1)S(1)} %shard_map.104.own_ref, bf16[4,320,512]{2,1,0:T(8,128)(2,1)S(1)} %collective-permute-done.6.other_ref, ...), custom_call_target="tpu_custom_call" | custom-call | flops 536870912 | bytes 5242880 | tf_op jit(solution)/shard_map/pallas_call | solution.py:221
  77.9 0.0 copy-start.4
  77.9 7.7 %all-to-all-start.2 = ((bf16[64,8,1152]{2,1,0:T(8,128)(2,1)}), bf16[64,8,1152]{2,1,0:T(8,128)(2,1)S(1)}, u32[]{:S(2)}, u32[]{:S(2)}) async-start(bf16[64,8,1152]{2,1,0:T(8,128)(2,1)} %bitcast.11), calls=%async_computation.2 | async-start | bytes 2359296 | tf_op jit(solution)/shard_map/all_to_all | solution.py:228
  85.6 4.4 %collective-permute-start.7 = (bf16[16,512]{1,0:T(8,128)(2,1)S(1)}, bf16[16,512]{1,0:T(8,128)(2,1)S(1)}, u32[]{:S(2)}, u32[]{:S(2)}) collective-permute-start(bf16[16,512]{1,0:T(8,128)(2,1)S(1)} %convert_element_type.22), channel_id=1, source_target_pairs={{0,128},{128,0},{256,384},{384,256},{1,129},{129,1},{257,385},{385... | collective-permute-start | bytes 49160 | tf_op jit(solution)/shard_map/ppermute | solution.py:29
  90.0 5.7 %collective-permute-start.8 = (bf16[16,512]{1,0:T(8,128)(2,1)S(1)}, bf16[16,512]{1,0:T(8,128)(2,1)S(1)}, u32[]{:S(2)}, u32[]{:S(2)}) collective-permute-start(bf16[16,512]{1,0:T(8,128)(2,1)S(1)} %convert_element_type.22), channel_id=1, source_target_pairs={{0,256},{128,384},{256,0},{384,128},{1,257},{129,385},{257,1},{385... | collective-permute-start | bytes 49160 | tf_op jit(solution)/shard_map/ppermute | solution.py:29
  95.7 2.2 %collective-permute-start.9 = (bf16[16,512]{1,0:T(8,128)(2,1)S(1)}, bf16[16,512]{1,0:T(8,128)(2,1)S(1)}, u32[]{:S(2)}, u32[]{:S(2)}) collective-permute-start(bf16[16,512]{1,0:T(8,128)(2,1)S(1)} %convert_element_type.22), channel_id=1, source_target_pairs={{0,384},{128,256},{256,128},{384,0},{1,385},{129,257},{257,129},{3... | collective-permute-start | bytes 49160 | tf_op jit(solution)/shard_map/ppermute | solution.py:29
  97.9 0.0 copy-done.4
  97.9 9.3 %collective-permute-done.7 = bf16[16,512]{1,0:T(8,128)(2,1)S(1)} collective-permute-done((bf16[16,512]{1,0:T(8,128)(2,1)S(1)}, bf16[16,512]{1,0:T(8,128)(2,1)S(1)}, u32[]{:S(2)}, u32[]{:S(2)}) %collective-permute-start.7) | collective-permute-done | bytes 16416 | tf_op jit(solution)/shard_map/ppermute | solution.py:29
  107.2 0.0 collective-permute-done.8
  107.2 0.0 collective-permute-done.9
  107.3 0.6 add_multiply_fusion
  107.9 10.8 %all-to-all-done.2.back_ref = bf16[64,8,1152]{2,1,0:T(8,128)(2,1)S(1)} async-done(((bf16[64,8,1152]{2,1,0:T(8,128)(2,1)}), bf16[64,8,1152]{2,1,0:T(8,128)(2,1)S(1)}, u32[]{:S(2)}, u32[]{:S(2)}) %all-to-all-start.2) | async-done | bytes 1179680 | tf_op jit(solution)/shard_map/all_to_all | solution.py:228
  118.7 0.0 copy-done.1
  118.7 1.7 %shard_map.107 = (bf16[8,8192]{1,0:T(8,128)(2,1)}, f32[16,16]{1,0:T(8,128)}, f32[1,16]{1,0:T(1,128)}) custom-call(s32[3]{0:T(128)S(1)} %pad_add_fusion.1.place_ref, bf16[64,8,1152]{2,1,0:T(8,128)(2,1)S(1)} %all-to-all-done.2.back_ref, bf16[8,128]{1,0:T(8,128)(2,1)S(1)} %get-tuple-element.13.scaled_ref, bf16[16,8192]{1,0:T(8,128)(2,1)S(1)} %bitcast.26, ...), custom_call_target="tpu_custom_call" | custom-call | flops 2097152 | bytes 2097152 | tf_op jit(solution)/shard_map/pallas_call | solution.py:232
  (7 shorter events, 0.1 us)
Async XLA Ops:
  0.6 5.3 %copy-start = (bf16[16,512]{1,0:T(8,128)(2,1)S(1)}, bf16[16,512]{1,0:T(8,128)(2,1)}, u32[]{:S(2)}) copy-start(bf16[16,512]{1,0:T(8,128)(2,1)} %param.11) | copy-start | bytes 49156
  0.6 27.8 %copy-start.3 = (bf16[8,8192]{1,0:T(8,128)(2,1)S(1)}, bf16[8,8192]{1,0:T(8,128)(2,1)}, u32[]{:S(2)}) copy-start(bf16[8,8192]{1,0:T(8,128)(2,1)} %param.7) | copy-start | bytes 393220
  0.7 33.4 %copy-start.2 = (bf16[256,512]{1,0:T(8,128)(2,1)S(1)}, bf16[256,512]{1,0:T(8,128)(2,1)}, u32[]{:S(2)}) copy-start(bf16[256,512]{1,0:T(8,128)(2,1)} %weight_any.1) | copy-start | bytes 786436
  1.6 14.3 %collective-permute-start = (bf16[256,512]{1,0:T(8,128)(2,1)}, bf16[256,512]{1,0:T(8,128)(2,1)S(1)}, u32[]{:S(2)}, u32[]{:S(2)}) collective-permute-start(bf16[256,512]{1,0:T(8,128)(2,1)} %weight_any.1), channel_id=1, source_target_pairs={{0,8},{8,0},{1,9},{9,1},{2,10},{10,2},{3,11},{11,3},{4,12},{12,4},... | collective-permute-start | bytes 786440 | tf_op jit(solution)/shard_map/ppermute | solution.py:29
  8.0 20.6 %all-to-all-start = ((f32[16,8,128]{2,1,0:T(8,128)}), f32[16,8,128]{2,1,0:T(8,128)S(1)}, u32[]{:S(2)}, u32[]{:S(2)}) async-start(f32[16,8,128]{2,1,0:T(8,128)} %pad_add_fusion.sent_ref), calls=%async_computation | async-start | bytes 131072 | tf_op jit(solution)/shard_map/all_to_all | solution.py:195
  15.9 12.7 %collective-permute-start.1 = (bf16[128,512]{1,0:T(8,128)(2,1)S(1)}, bf16[128,512]{1,0:T(8,128)(2,1)S(1)}, u32[]{:S(2)}, u32[]{:S(2)}) collective-permute-start(bf16[128,512]{1,0:T(8,128)(2,1)S(1)} %shard_map.102.cot_ref), channel_id=1, source_target_pairs={{0,128},{128,0},{256,384},{384,256},{1,129},{129,1},{257,385},{385... | collective-permute-start | bytes 393224 | tf_op jit(solution)/shard_map/ppermute | solution.py:29
  22.0 12.1 %collective-permute-start.2 = (bf16[128,512]{1,0:T(8,128)(2,1)S(1)}, bf16[128,512]{1,0:T(8,128)(2,1)S(1)}, u32[]{:S(2)}, u32[]{:S(2)}) collective-permute-start(bf16[128,512]{1,0:T(8,128)(2,1)S(1)} %shard_map.102.cot_ref), channel_id=1, source_target_pairs={{0,384},{128,256},{256,128},{384,0},{1,385},{129,257},{257,129},{3... | collective-permute-start | bytes 393224 | tf_op jit(solution)/shard_map/ppermute | solution.py:29
  36.4 34.1 %all-to-all-start.1 = ((bf16[4,320,512]{2,1,0:T(8,128)(2,1)}), bf16[4,320,512]{2,1,0:T(8,128)(2,1)S(1)}, u32[]{:S(2)}, u32[]{:S(2)}) async-start(bf16[4,320,512]{2,1,0:T(8,128)(2,1)} %get-tuple-element.11), calls=%async_computation.1 | async-start | bytes 2621440 | tf_op jit(solution)/shard_map/all_to_all | solution.py:215
  41.2 29.3 %collective-permute-start.3 = (bf16[3,128,512]{2,1,0:T(8,128)(2,1)S(1)}, bf16[3,128,512]{2,1,0:T(8,128)(2,1)S(1)}, u32[]{:S(2)}, u32[]{:S(2)}) collective-permute-start(bf16[3,128,512]{2,1,0:T(8,128)(2,1)S(1)} %pad_maximum_fusion.near_ref), channel_id=1, source_target_pairs={{0,8},{8,0},{1,9},{9,1},{2,10},{10,2},{3,11},{11,3},{4,12},{12,4},... | collective-permute-start | bytes 1179656 | tf_op jit(solution)/shard_map/ppermute | solution.py:29
  44.1 19.5 %collective-permute-start.4 = (bf16[128,512]{1,0:T(8,128)(2,1)S(1)}, bf16[128,512]{1,0:T(8,128)(2,1)S(1)}, u32[]{:S(2)}, u32[]{:S(2)}) collective-permute-start(bf16[128,512]{1,0:T(8,128)(2,1)S(1)} %shard_map.102.cot_ref), channel_id=1, source_target_pairs={{0,256},{128,384},{256,0},{384,128},{1,257},{129,385},{257,1},{385... | collective-permute-start | bytes 393224 | tf_op jit(solution)/shard_map/ppermute | solution.py:29
  63.6 6.8 %collective-permute-start.5 = (bf16[128,512]{1,0:T(8,128)(2,1)S(1)}, bf16[128,512]{1,0:T(8,128)(2,1)S(1)}, u32[]{:S(2)}, u32[]{:S(2)}) collective-permute-start(bf16[128,512]{1,0:T(8,128)(2,1)S(1)} %collective-permute-done.4.last_ref), channel_id=1, source_target_pairs={{0,8},{8,0},{1,9},{9,1},{2,10},{10,2},{3,11},{11,3},{4,12},{12,4},... | collective-permute-start | bytes 393224 | tf_op jit(solution)/shard_map/ppermute | solution.py:29
  70.5 4.9 %collective-permute-start.6 = (bf16[4,320,512]{2,1,0:T(8,128)(2,1)S(1)}, bf16[4,320,512]{2,1,0:T(8,128)(2,1)S(1)}, u32[]{:S(2)}, u32[]{:S(2)}) collective-permute-start(bf16[4,320,512]{2,1,0:T(8,128)(2,1)S(1)} %shard_map.104.own_ref), channel_id=1, source_target_pairs={{0,16},{16,0},{1,17},{17,1},{2,18},{18,2},{3,19},{19,3},{4,20},{20... | collective-permute-start | bytes 3932168 | tf_op jit(solution)/shard_map/ppermute | solution.py:29
  77.9 19.9 %copy-start.4 = (s32[16]{0:T(128)S(1)}, s32[16]{0:T(128)}, u32[]{:S(2)}) copy-start(s32[16]{0:T(128)} %param.13) | copy-start | bytes 196
  77.9 40.8 %copy-start.1 = (bf16[8192,16]{0,1:T(8,128)(2,1)S(1)}, bf16[8192,16]{0,1:T(8,128)(2,1)}, u32[]{:S(2)}) copy-start(bf16[8192,16]{0,1:T(8,128)(2,1)} %param.10) | copy-start | bytes 786436
  77.9 40.8 %all-to-all-start.2 = ((bf16[64,8,1152]{2,1,0:T(8,128)(2,1)}), bf16[64,8,1152]{2,1,0:T(8,128)(2,1)S(1)}, u32[]{:S(2)}, u32[]{:S(2)}) async-start(bf16[64,8,1152]{2,1,0:T(8,128)(2,1)} %bitcast.11), calls=%async_computation.2 | async-start | bytes 2359296 | tf_op jit(solution)/shard_map/all_to_all | solution.py:228
  85.6 21.6 %collective-permute-start.7 = (bf16[16,512]{1,0:T(8,128)(2,1)S(1)}, bf16[16,512]{1,0:T(8,128)(2,1)S(1)}, u32[]{:S(2)}, u32[]{:S(2)}) collective-permute-start(bf16[16,512]{1,0:T(8,128)(2,1)S(1)} %convert_element_type.22), channel_id=1, source_target_pairs={{0,128},{128,0},{256,384},{384,256},{1,129},{129,1},{257,385},{385... | collective-permute-start | bytes 49160 | tf_op jit(solution)/shard_map/ppermute | solution.py:29
  90.0 17.2 %collective-permute-start.8 = (bf16[16,512]{1,0:T(8,128)(2,1)S(1)}, bf16[16,512]{1,0:T(8,128)(2,1)S(1)}, u32[]{:S(2)}, u32[]{:S(2)}) collective-permute-start(bf16[16,512]{1,0:T(8,128)(2,1)S(1)} %convert_element_type.22), channel_id=1, source_target_pairs={{0,256},{128,384},{256,0},{384,128},{1,257},{129,385},{257,1},{385... | collective-permute-start | bytes 49160 | tf_op jit(solution)/shard_map/ppermute | solution.py:29
  95.7 11.5 %collective-permute-start.9 = (bf16[16,512]{1,0:T(8,128)(2,1)S(1)}, bf16[16,512]{1,0:T(8,128)(2,1)S(1)}, u32[]{:S(2)}, u32[]{:S(2)}) collective-permute-start(bf16[16,512]{1,0:T(8,128)(2,1)S(1)} %convert_element_type.22), channel_id=1, source_target_pairs={{0,384},{128,256},{256,128},{384,0},{1,385},{129,257},{257,129},{3... | collective-permute-start | bytes 49160 | tf_op jit(solution)/shard_map/ppermute | solution.py:29

commit v8 on v7

--- a/solution.py
+++ b/solution.py
@@ -164,8 +164,7 @@
     scaled = scaled_ref[:, 0:16]
     for h in range(4):
         for low in range(2):
-            first = (h * 2 + low) * 8
-            total = jnp.sum(back_ref[first : first + 8, :, 0:1024].astype(f32), axis=0)
+            total = sum(back_ref[h * 16 + i * 2 + low, :, 0:1024].astype(f32) for i in range(8))
             own, other = total[:, :512], total[:, 512:]
             for c, part in enumerate((jnp.where(core == 0, own, other), jnp.where(core == 0, other, own))):
                 for x in range(4):
@@ -180,26 +179,26 @@
 
 def body(inputs, cotangent, weight, left_factor, right_factor, singular, keep_mask):
     core = lax.axis_index("c")
-    z_low = lax.axis_index("zl")
+    y_low = lax.axis_index("yl")
     z_high = lax.axis_index("zh")
-    place = jnp.stack([core, z_low, z_high]).astype(jnp.int32)
+    place = jnp.stack([core, y_low, z_high]).astype(jnp.int32)
     shape = jax.ShapeDtypeStruct
     keep_float = keep_mask.astype(f32)
     coeff = adapter_scale * singular * keep_float
 
-    got = swap(weight, "zl", 2, 1)
+    got = swap(weight, "yl", 2, 1)
 
     back_part = dot_t(cotangent, right_factor).reshape(16, 8, 16)
     own_projected = jnp.dot(inputs, left_factor, preferred_element_type=f32)
     rank_out = jnp.pad(back_part, ((0, 0), (0, 0), (0, 112))) + jnp.pad(own_projected, ((0, 0), (16, 96)))
-    rank_in = lax.all_to_all(rank_out, ("zl", "y"), 0, 0)
+    rank_in = lax.all_to_all(rank_out, ("zl", "yh", "yl"), 0, 0)
 
     cot = after(cotangent, got)
     cots = [cot] + [swap(cot, "zh", 4, k) for k in (1, 2, 3)]
     near = jnp.stack([cots[0], cots[1], cots[3]])
-    far = swap(near, "zl", 2, 1)
+    far = swap(near, "yl", 2, 1)
     last = cots[2]
-    far_last = swap(last, "zl", 2, 1)
+    far_last = swap(last, "yl", 2, 1)
 
     coeff_lanes = jnp.pad(jnp.concatenate([coeff, coeff]), (0, 96)).reshape(1, 128)
     slices = inputs.reshape(8, 4, 4, 512).transpose(2, 1, 0, 3).reshape(4, 32, 512)
@@ -225,7 +224,7 @@
         1 << 29,
         5 << 20,
     )(place, done, x_in, x_other, near, last, far, far_last)
-    back = lax.all_to_all(out.reshape(64, 8, 1152), ("zh", "zl", "y"), 0, 0)
+    back = lax.all_to_all(out.reshape(64, 8, 1152), ("zh", "zl", "yh", "yl"), 0, 0)
     right_sent = right_part.astype(bf16)
     right_sum = right_part + sum(swap(right_sent, "zh", 4, k).astype(f32) for k in (1, 2, 3))
 
@@ -249,9 +248,9 @@
 
 
 def solution(mesh):
-    fine = Mesh(mesh.devices.reshape(4, 4, 2, 2, 8), ("zh", "x", "c", "zl", "y"))
+    fine = Mesh(mesh.devices.reshape(4, 4, 2, 2, 4, 2), ("zh", "x", "c", "zl", "yh", "yl"))
     dp = ("zh", "x", "c")
-    tensor = ("zl", "y")
+    tensor = ("zl", "yh", "yl")
     in_specs = (
         P(dp + tensor, None),
         P(dp, tensor),

time: 121 us -> 118 us (0.975)
  waiting for transfers between devices: 44.4 us -> 39 us
  starting transfers between devices: 63.3 us -> 65.1 us
    ppermute x10, waiting for transfers between devices: 33.6 us -> 28.1 us  [swap(): return lax.ppermute(a, axis, [(i, i ^ mask) for i in range(count)])]
    all_to_all x2, starting transfers between devices: 14.9 us -> 18.9 us  [the longest x1 10.8 us: body(): lax.all_to_all(out.reshape(64, 8, 1152), ('zh', 'zl', 'yh', 'yl'), 0, 0)]
    ppermute x10, starting transfers between devices: 43.7 us -> 41.4 us  [swap(): return lax.ppermute(a, axis, [(i, i ^ mask) for i in range(count)])]
where the time goes in v8:
time: 118 us; the launch traced here: 117 us
  starting transfers between devices  65.1 us (55%)
  waiting for transfers between devices  39 us (33%)
  Pallas kernels  7.26 us (6%)
  other arithmetic  2.18 us (2%)
  matrix products  1.37 us (1%)
    ppermute x10, starting transfers between devices, swap(): return lax.ppermute(a, axis, [(i, i ^ mask) for i in range(count)])  41.4 us
    ppermute x10, waiting for transfers between devices, swap(): return lax.ppermute(a, axis, [(i, i ^ mask) for i in range(count)])  28.1 us
    all_to_all x1, waiting for transfers between devices, body(): lax.all_to_all(out.reshape(64, 8, 1152), ('zh', 'zl', 'yh', 'yl'), 0, 0)  10.9 us
    all_to_all x1, starting transfers between devices, body(): lax.all_to_all(out.reshape(64, 8, 1152), ('zh', 'zl', 'yh', 'yl'), 0, 0)  10.8 us
    all_to_all x1, starting transfers between devices, body(): rank_in = lax.all_to_all(rank_out, ('zl', 'yh', 'yl'), 0, 0)  8.11 us
    all_to_all x1, starting transfers between devices, body(): x_in = after(lax.all_to_all(x_out, 'x', 0, 0), far, far_last)  4.78 us
    pallas_call x1, Pallas kernels, body(): call(other_kernel, (shape((4, 128, 1152), bf16), shape((16, 512), f32)),...  2.53 us
  transfers between devices with their start and end apart: 13, of which 6 were waited for; matrix products, arithmetic and copies ran while one was open for 3% of the time, Pallas kernels for 1%

profile of v8, /device:TPU:6, one launch (start us, length us, event | category | flops | bytes accessed | tf_op | source)
XLA Modules:
  0.0 116.8 jit_solution(12784407546149896414)
XLA Ops:
  0.6 0.0 copy-start
  0.6 0.0 copy-start.3
  0.7 0.0 copy-start.2
  0.7 1.0 copy.21.refs_0_
  1.6 3.5 %collective-permute-start = (bf16[256,512]{1,0:T(8,128)(2,1)}, bf16[256,512]{1,0:T(8,128)(2,1)S(1)}, u32[]{:S(2)}, u32[]{:S(2)}) collective-permute-start(bf16[256,512]{1,0:T(8,128)(2,1)} %weight_any.1), channel_id=1, source_target_pairs={{0,1},{1,0},{2,3},{3,2},{4,5},{5,4},{6,7},{7,6},{8,9},{9,8},{10,11... | collective-permute-start | bytes 786440 | tf_op jit(solution)/shard_map/ppermute | solution.py:29
  5.1 0.0 copy-done
  5.1 0.2 convolution_bitcast_fusion
  5.3 1.2 %fusion.2 = f32[8,16]{1,0:T(8,128)S(1)} fusion(bf16[8,8192]{1,0:T(8,128)(2,1)} %param.7, bf16[8192,16]{0,1:T(8,128)(2,1)} %param.10), kind=kOutput, calls=%fused_computation.12 | convolution fusion | flops 2097152 | bytes 393728 | tf_op jit(solution)/shard_map/dot_general | solution.py:192
  6.5 0.1 pad.13
  6.6 0.7 pad_add_fusion.sent_ref
  7.2 8.1 %all-to-all-start = ((f32[16,8,128]{2,1,0:T(8,128)}), f32[16,8,128]{2,1,0:T(8,128)S(1)}, u32[]{:S(2)}, u32[]{:S(2)}) async-start(f32[16,8,128]{2,1,0:T(8,128)} %pad_add_fusion.sent_ref), calls=%async_computation | async-start | bytes 131072 | tf_op jit(solution)/shard_map/all_to_all | solution.py:194
  15.3 0.7 convert_multiply_fusion
  16.0 0.0 collective-permute-done.refs_1_.got_any
  16.0 6.1 %collective-permute-start.1 = (bf16[128,512]{1,0:T(8,128)(2,1)S(1)}, bf16[128,512]{1,0:T(8,128)(2,1)S(1)}, u32[]{:S(2)}, u32[]{:S(2)}) collective-permute-start(bf16[128,512]{1,0:T(8,128)(2,1)S(1)} %shard_map.102.cot_ref), channel_id=1, source_target_pairs={{0,128},{128,0},{256,384},{384,256},{1,129},{129,1},{257,385},{385... | collective-permute-start | bytes 393224 | tf_op jit(solution)/shard_map/ppermute | solution.py:29
  22.1 6.4 %collective-permute-start.2 = (bf16[128,512]{1,0:T(8,128)(2,1)S(1)}, bf16[128,512]{1,0:T(8,128)(2,1)S(1)}, u32[]{:S(2)}, u32[]{:S(2)}) collective-permute-start(bf16[128,512]{1,0:T(8,128)(2,1)S(1)} %shard_map.102.cot_ref), channel_id=1, source_target_pairs={{0,384},{128,256},{256,128},{384,0},{1,385},{129,257},{257,129},{3... | collective-permute-start | bytes 393224 | tf_op jit(solution)/shard_map/ppermute | solution.py:29
  28.5 0.1 fusion.1.coeff_ref
  28.6 0.0 copy-done.3
  28.6 0.1 pad_add_fusion.1.place_ref
  28.7 0.0 all-to-all-done.rank_ref
  28.7 0.0 collective-permute-done.1.after1
  28.7 5.5 %collective-permute-done.2.after3 = bf16[128,512]{1,0:T(8,128)(2,1)S(1)} collective-permute-done((bf16[128,512]{1,0:T(8,128)(2,1)S(1)}, bf16[128,512]{1,0:T(8,128)(2,1)S(1)}, u32[]{:S(2)}, u32[]{:S(2)}) %collective-permute-start.2) | collective-permute-done | bytes 131104 | tf_op jit(solution)/shard_map/ppermute | solution.py:29
  34.2 0.0 copy-done.2
  34.2 2.3 %shard_map.103 = (bf16[4,320,512]{2,1,0:T(8,128)(2,1)}, bf16[8,128]{1,0:T(8,128)(2,1)S(1)}) custom-call(s32[3]{0:T(128)S(1)} %pad_add_fusion.1.place_ref, f32[16,8,128]{2,1,0:T(8,128)} %pad_add_fusion.sent_ref, f32[16,8,128]{2,1,0:T(8,128)S(1)} %all-to-all-done.rank_ref, f32[1,128]{1,0:T(1,128)S(1)} %fusion.1.coeff_ref, ...), custom_call_target="tpu_custom_call" | custom-call | flops 16777216 | bytes 3145728 | tf_op jit(solution)/shard_map/pallas_call | solution.py:205
  36.5 4.8 %all-to-all-start.1 = ((bf16[4,320,512]{2,1,0:T(8,128)(2,1)}), bf16[4,320,512]{2,1,0:T(8,128)(2,1)S(1)}, u32[]{:S(2)}, u32[]{:S(2)}) async-start(bf16[4,320,512]{2,1,0:T(8,128)(2,1)} %get-tuple-element.11), calls=%async_computation.1 | async-start | bytes 2621440 | tf_op jit(solution)/shard_map/all_to_all | solution.py:214
  41.3 3.5 %collective-permute-start.3 = (bf16[3,128,512]{2,1,0:T(8,128)(2,1)S(1)}, bf16[3,128,512]{2,1,0:T(8,128)(2,1)S(1)}, u32[]{:S(2)}, u32[]{:S(2)}) collective-permute-start(bf16[3,128,512]{2,1,0:T(8,128)(2,1)S(1)} %pad_maximum_fusion.near_ref), channel_id=1, source_target_pairs={{0,1},{1,0},{2,3},{3,2},{4,5},{5,4},{6,7},{7,6},{8,9},{9,8},{10,11... | collective-permute-start | bytes 1179656 | tf_op jit(solution)/shard_map/ppermute | solution.py:29
  44.8 5.5 %collective-permute-start.4 = (bf16[128,512]{1,0:T(8,128)(2,1)S(1)}, bf16[128,512]{1,0:T(8,128)(2,1)S(1)}, u32[]{:S(2)}, u32[]{:S(2)}) collective-permute-start(bf16[128,512]{1,0:T(8,128)(2,1)S(1)} %shard_map.102.cot_ref), channel_id=1, source_target_pairs={{0,256},{128,384},{256,0},{384,128},{1,257},{129,385},{257,1},{385... | collective-permute-start | bytes 393224 | tf_op jit(solution)/shard_map/ppermute | solution.py:29
  50.3 6.6 %collective-permute-done.4.last_ref = bf16[128,512]{1,0:T(8,128)(2,1)S(1)} collective-permute-done((bf16[128,512]{1,0:T(8,128)(2,1)S(1)}, bf16[128,512]{1,0:T(8,128)(2,1)S(1)}, u32[]{:S(2)}, u32[]{:S(2)}) %collective-permute-start.4) | collective-permute-done | bytes 131104 | tf_op jit(solution)/shard_map/ppermute | solution.py:29
  56.8 2.4 %collective-permute-start.5 = (bf16[128,512]{1,0:T(8,128)(2,1)S(1)}, bf16[128,512]{1,0:T(8,128)(2,1)S(1)}, u32[]{:S(2)}, u32[]{:S(2)}) collective-permute-start(bf16[128,512]{1,0:T(8,128)(2,1)S(1)} %collective-permute-done.4.last_ref), channel_id=1, source_target_pairs={{0,1},{1,0},{2,3},{3,2},{4,5},{5,4},{6,7},{7,6},{8,9},{9,8},{10,11... | collective-permute-start | bytes 393224 | tf_op jit(solution)/shard_map/ppermute | solution.py:29
  59.2 4.5 %collective-permute-done.5.refs_2_.far_last_ref = bf16[128,512]{1,0:T(8,128)(2,1)S(1)} collective-permute-done((bf16[128,512]{1,0:T(8,128)(2,1)S(1)}, bf16[128,512]{1,0:T(8,128)(2,1)S(1)}, u32[]{:S(2)}, u32[]{:S(2)}) %collective-permute-start.5) | collective-permute-done | bytes 131104 | tf_op jit(solution)/shard_map/ppermute | solution.py:29
  63.7 0.0 collective-permute-done.3.refs_1_.far_ref
  63.7 0.0 all-to-all-done.1.refs_0_
  63.7 1.9 %collective-permute-start.6 = (bf16[4,320,512]{2,1,0:T(8,128)(2,1)S(1)}, bf16[4,320,512]{2,1,0:T(8,128)(2,1)S(1)}, u32[]{:S(2)}, u32[]{:S(2)}) collective-permute-start(bf16[4,320,512]{2,1,0:T(8,128)(2,1)S(1)} %shard_map.104.own_ref), channel_id=1, source_target_pairs={{0,16},{16,0},{1,17},{17,1},{2,18},{18,2},{3,19},{19,3},{4,20},{20... | collective-permute-start | bytes 3932168 | tf_op jit(solution)/shard_map/ppermute | solution.py:29
  65.6 0.7 shard_map.105.done_ref
  66.4 2.3 %collective-permute-done.6.other_ref = bf16[4,320,512]{2,1,0:T(8,128)(2,1)S(1)} collective-permute-done((bf16[4,320,512]{2,1,0:T(8,128)(2,1)S(1)}, bf16[4,320,512]{2,1,0:T(8,128)(2,1)S(1)}, u32[]{:S(2)}, u32[]{:S(2)}) %collective-permute-start.6) | collective-permute-done | bytes 1310752 | tf_op jit(solution)/shard_map/ppermute | solution.py:29
  68.6 2.5 %shard_map.106 = (bf16[4,128,1152]{2,1,0:T(8,128)(2,1)}, f32[16,512]{1,0:T(8,128)S(1)}) custom-call(s32[3]{0:T(128)S(1)} %pad_add_fusion.1.place_ref, bf16[4,128,512]{2,1,0:T(8,128)(2,1)S(1)} %shard_map.105.done_ref, bf16[4,320,512]{2,1,0:T(8,128)(2,1)S(1)} %shard_map.104.own_ref, bf16[4,320,512]{2,1,0:T(8,128)(2,1)S(1)} %collective-permute-done.6.other_ref, ...), custom_call_target="tpu_custom_call" | custom-call | flops 536870912 | bytes 5242880 | tf_op jit(solution)/shard_map/pallas_call | solution.py:220
  71.2 0.0 copy-start.4
  71.2 10.8 %all-to-all-start.2 = ((bf16[64,8,1152]{2,1,0:T(8,128)(2,1)}), bf16[64,8,1152]{2,1,0:T(8,128)(2,1)S(1)}, u32[]{:S(2)}, u32[]{:S(2)}) async-start(bf16[64,8,1152]{2,1,0:T(8,128)(2,1)} %bitcast.11), calls=%async_computation.2 | async-start | bytes 2359296 | tf_op jit(solution)/shard_map/all_to_all | solution.py:227
  81.9 4.4 %collective-permute-start.7 = (bf16[16,512]{1,0:T(8,128)(2,1)S(1)}, bf16[16,512]{1,0:T(8,128)(2,1)S(1)}, u32[]{:S(2)}, u32[]{:S(2)}) collective-permute-start(bf16[16,512]{1,0:T(8,128)(2,1)S(1)} %convert_element_type.22), channel_id=1, source_target_pairs={{0,128},{128,0},{256,384},{384,256},{1,129},{129,1},{257,385},{385... | collective-permute-start | bytes 49160 | tf_op jit(solution)/shard_map/ppermute | solution.py:29
  86.3 5.7 %collective-permute-start.8 = (bf16[16,512]{1,0:T(8,128)(2,1)S(1)}, bf16[16,512]{1,0:T(8,128)(2,1)S(1)}, u32[]{:S(2)}, u32[]{:S(2)}) collective-permute-start(bf16[16,512]{1,0:T(8,128)(2,1)S(1)} %convert_element_type.22), channel_id=1, source_target_pairs={{0,256},{128,384},{256,0},{384,128},{1,257},{129,385},{257,1},{385... | collective-permute-start | bytes 49160 | tf_op jit(solution)/shard_map/ppermute | solution.py:29
  92.0 2.2 %collective-permute-start.9 = (bf16[16,512]{1,0:T(8,128)(2,1)S(1)}, bf16[16,512]{1,0:T(8,128)(2,1)S(1)}, u32[]{:S(2)}, u32[]{:S(2)}) collective-permute-start(bf16[16,512]{1,0:T(8,128)(2,1)S(1)} %convert_element_type.22), channel_id=1, source_target_pairs={{0,384},{128,256},{256,128},{384,0},{1,385},{129,257},{257,129},{3... | collective-permute-start | bytes 49160 | tf_op jit(solution)/shard_map/ppermute | solution.py:29
  94.2 0.0 copy-done.4
  94.2 9.3 %collective-permute-done.7 = bf16[16,512]{1,0:T(8,128)(2,1)S(1)} collective-permute-done((bf16[16,512]{1,0:T(8,128)(2,1)S(1)}, bf16[16,512]{1,0:T(8,128)(2,1)S(1)}, u32[]{:S(2)}, u32[]{:S(2)}) %collective-permute-start.7) | collective-permute-done | bytes 16416 | tf_op jit(solution)/shard_map/ppermute | solution.py:29
  103.5 0.0 collective-permute-done.8
  103.5 0.0 collective-permute-done.9
  103.5 0.6 add_multiply_fusion
  104.2 10.9 %all-to-all-done.2.back_ref = bf16[64,8,1152]{2,1,0:T(8,128)(2,1)S(1)} async-done(((bf16[64,8,1152]{2,1,0:T(8,128)(2,1)}), bf16[64,8,1152]{2,1,0:T(8,128)(2,1)S(1)}, u32[]{:S(2)}, u32[]{:S(2)}) %all-to-all-start.2) | async-done | bytes 1179680 | tf_op jit(solution)/shard_map/all_to_all | solution.py:227
  115.0 0.0 copy-done.1
  115.0 1.7 %shard_map.107 = (bf16[8,8192]{1,0:T(8,128)(2,1)}, f32[16,16]{1,0:T(8,128)}, f32[1,16]{1,0:T(1,128)}) custom-call(s32[3]{0:T(128)S(1)} %pad_add_fusion.1.place_ref, bf16[64,8,1152]{2,1,0:T(8,128)(2,1)S(1)} %all-to-all-done.2.back_ref, bf16[8,128]{1,0:T(8,128)(2,1)S(1)} %get-tuple-element.13.scaled_ref, bf16[16,8192]{1,0:T(8,128)(2,1)S(1)} %bitcast.26, ...), custom_call_target="tpu_custom_call" | custom-call | flops 2097152 | bytes 2097152 | tf_op jit(solution)/shard_map/pallas_call | solution.py:231
  (7 shorter events, 0.1 us)
Async XLA Ops:
  0.6 4.5 %copy-start = (bf16[16,512]{1,0:T(8,128)(2,1)S(1)}, bf16[16,512]{1,0:T(8,128)(2,1)}, u32[]{:S(2)}) copy-start(bf16[16,512]{1,0:T(8,128)(2,1)} %param.11) | copy-start | bytes 49156
  0.6 28.0 %copy-start.3 = (bf16[8,8192]{1,0:T(8,128)(2,1)S(1)}, bf16[8,8192]{1,0:T(8,128)(2,1)}, u32[]{:S(2)}) copy-start(bf16[8,8192]{1,0:T(8,128)(2,1)} %param.7) | copy-start | bytes 393220
  0.7 33.5 %copy-start.2 = (bf16[256,512]{1,0:T(8,128)(2,1)S(1)}, bf16[256,512]{1,0:T(8,128)(2,1)}, u32[]{:S(2)}) copy-start(bf16[256,512]{1,0:T(8,128)(2,1)} %weight_any.1) | copy-start | bytes 786436
  1.6 14.4 %collective-permute-start = (bf16[256,512]{1,0:T(8,128)(2,1)}, bf16[256,512]{1,0:T(8,128)(2,1)S(1)}, u32[]{:S(2)}, u32[]{:S(2)}) collective-permute-start(bf16[256,512]{1,0:T(8,128)(2,1)} %weight_any.1), channel_id=1, source_target_pairs={{0,1},{1,0},{2,3},{3,2},{4,5},{5,4},{6,7},{7,6},{8,9},{9,8},{10,11... | collective-permute-start | bytes 786440 | tf_op jit(solution)/shard_map/ppermute | solution.py:29
  7.2 21.5 %all-to-all-start = ((f32[16,8,128]{2,1,0:T(8,128)}), f32[16,8,128]{2,1,0:T(8,128)S(1)}, u32[]{:S(2)}, u32[]{:S(2)}) async-start(f32[16,8,128]{2,1,0:T(8,128)} %pad_add_fusion.sent_ref), calls=%async_computation | async-start | bytes 131072 | tf_op jit(solution)/shard_map/all_to_all | solution.py:194
  16.0 12.7 %collective-permute-start.1 = (bf16[128,512]{1,0:T(8,128)(2,1)S(1)}, bf16[128,512]{1,0:T(8,128)(2,1)S(1)}, u32[]{:S(2)}, u32[]{:S(2)}) collective-permute-start(bf16[128,512]{1,0:T(8,128)(2,1)S(1)} %shard_map.102.cot_ref), channel_id=1, source_target_pairs={{0,128},{128,0},{256,384},{384,256},{1,129},{129,1},{257,385},{385... | collective-permute-start | bytes 393224 | tf_op jit(solution)/shard_map/ppermute | solution.py:29
  22.1 12.1 %collective-permute-start.2 = (bf16[128,512]{1,0:T(8,128)(2,1)S(1)}, bf16[128,512]{1,0:T(8,128)(2,1)S(1)}, u32[]{:S(2)}, u32[]{:S(2)}) collective-permute-start(bf16[128,512]{1,0:T(8,128)(2,1)S(1)} %shard_map.102.cot_ref), channel_id=1, source_target_pairs={{0,384},{128,256},{256,128},{384,0},{1,385},{129,257},{257,129},{3... | collective-permute-start | bytes 393224 | tf_op jit(solution)/shard_map/ppermute | solution.py:29
  36.5 27.2 %all-to-all-start.1 = ((bf16[4,320,512]{2,1,0:T(8,128)(2,1)}), bf16[4,320,512]{2,1,0:T(8,128)(2,1)S(1)}, u32[]{:S(2)}, u32[]{:S(2)}) async-start(bf16[4,320,512]{2,1,0:T(8,128)(2,1)} %get-tuple-element.11), calls=%async_computation.1 | async-start | bytes 2621440 | tf_op jit(solution)/shard_map/all_to_all | solution.py:214
  41.3 22.4 %collective-permute-start.3 = (bf16[3,128,512]{2,1,0:T(8,128)(2,1)S(1)}, bf16[3,128,512]{2,1,0:T(8,128)(2,1)S(1)}, u32[]{:S(2)}, u32[]{:S(2)}) collective-permute-start(bf16[3,128,512]{2,1,0:T(8,128)(2,1)S(1)} %pad_maximum_fusion.near_ref), channel_id=1, source_target_pairs={{0,1},{1,0},{2,3},{3,2},{4,5},{5,4},{6,7},{7,6},{8,9},{9,8},{10,11... | collective-permute-start | bytes 1179656 | tf_op jit(solution)/shard_map/ppermute | solution.py:29
  44.8 12.1 %collective-permute-start.4 = (bf16[128,512]{1,0:T(8,128)(2,1)S(1)}, bf16[128,512]{1,0:T(8,128)(2,1)S(1)}, u32[]{:S(2)}, u32[]{:S(2)}) collective-permute-start(bf16[128,512]{1,0:T(8,128)(2,1)S(1)} %shard_map.102.cot_ref), channel_id=1, source_target_pairs={{0,256},{128,384},{256,0},{384,128},{1,257},{129,385},{257,1},{385... | collective-permute-start | bytes 393224 | tf_op jit(solution)/shard_map/ppermute | solution.py:29
  56.8 6.8 %collective-permute-start.5 = (bf16[128,512]{1,0:T(8,128)(2,1)S(1)}, bf16[128,512]{1,0:T(8,128)(2,1)S(1)}, u32[]{:S(2)}, u32[]{:S(2)}) collective-permute-start(bf16[128,512]{1,0:T(8,128)(2,1)S(1)} %collective-permute-done.4.last_ref), channel_id=1, source_target_pairs={{0,1},{1,0},{2,3},{3,2},{4,5},{5,4},{6,7},{7,6},{8,9},{9,8},{10,11... | collective-permute-start | bytes 393224 | tf_op jit(solution)/shard_map/ppermute | solution.py:29
  63.7 4.9 %collective-permute-start.6 = (bf16[4,320,512]{2,1,0:T(8,128)(2,1)S(1)}, bf16[4,320,512]{2,1,0:T(8,128)(2,1)S(1)}, u32[]{:S(2)}, u32[]{:S(2)}) collective-permute-start(bf16[4,320,512]{2,1,0:T(8,128)(2,1)S(1)} %shard_map.104.own_ref), channel_id=1, source_target_pairs={{0,16},{16,0},{1,17},{17,1},{2,18},{18,2},{3,19},{19,3},{4,20},{20... | collective-permute-start | bytes 3932168 | tf_op jit(solution)/shard_map/ppermute | solution.py:29
  71.2 23.0 %copy-start.4 = (s32[16]{0:T(128)S(1)}, s32[16]{0:T(128)}, u32[]{:S(2)}) copy-start(s32[16]{0:T(128)} %param.13) | copy-start | bytes 196
  71.2 43.9 %copy-start.1 = (bf16[8192,16]{0,1:T(8,128)(2,1)S(1)}, bf16[8192,16]{0,1:T(8,128)(2,1)}, u32[]{:S(2)}) copy-start(bf16[8192,16]{0,1:T(8,128)(2,1)} %param.10) | copy-start | bytes 786436
  71.2 43.9 %all-to-all-start.2 = ((bf16[64,8,1152]{2,1,0:T(8,128)(2,1)}), bf16[64,8,1152]{2,1,0:T(8,128)(2,1)S(1)}, u32[]{:S(2)}, u32[]{:S(2)}) async-start(bf16[64,8,1152]{2,1,0:T(8,128)(2,1)} %bitcast.11), calls=%async_computation.2 | async-start | bytes 2359296 | tf_op jit(solution)/shard_map/all_to_all | solution.py:227
  81.9 21.6 %collective-permute-start.7 = (bf16[16,512]{1,0:T(8,128)(2,1)S(1)}, bf16[16,512]{1,0:T(8,128)(2,1)S(1)}, u32[]{:S(2)}, u32[]{:S(2)}) collective-permute-start(bf16[16,512]{1,0:T(8,128)(2,1)S(1)} %convert_element_type.22), channel_id=1, source_target_pairs={{0,128},{128,0},{256,384},{384,256},{1,129},{129,1},{257,385},{385... | collective-permute-start | bytes 49160 | tf_op jit(solution)/shard_map/ppermute | solution.py:29
  86.3 17.2 %collective-permute-start.8 = (bf16[16,512]{1,0:T(8,128)(2,1)S(1)}, bf16[16,512]{1,0:T(8,128)(2,1)S(1)}, u32[]{:S(2)}, u32[]{:S(2)}) collective-permute-start(bf16[16,512]{1,0:T(8,128)(2,1)S(1)} %convert_element_type.22), channel_id=1, source_target_pairs={{0,256},{128,384},{256,0},{384,128},{1,257},{129,385},{257,1},{385... | collective-permute-start | bytes 49160 | tf_op jit(solution)/shard_map/ppermute | solution.py:29
  92.0 11.5 %collective-permute-start.9 = (bf16[16,512]{1,0:T(8,128)(2,1)S(1)}, bf16[16,512]{1,0:T(8,128)(2,1)S(1)}, u32[]{:S(2)}, u32[]{:S(2)}) collective-permute-start(bf16[16,512]{1,0:T(8,128)(2,1)S(1)} %convert_element_type.22), channel_id=1, source_target_pairs={{0,384},{128,256},{256,128},{384,0},{1,385},{129,257},{257,129},{3... | collective-permute-start | bytes 49160 | tf_op jit(solution)/shard_map/ppermute | solution.py:29

commit v9 on v8

--- a/solution.py
+++ b/solution.py
@@ -53,7 +53,7 @@
 
 
 def pack_kernel(
-    place_ref, sent_ref, rank_ref, coeff_ref, cot_ref, weight_any, got_any, slices_ref, after1, after3,
+    place_ref, sent_ref, rank_ref, coeff_ref, cot_ref, weight_any, got_any, slices_ref, after1,
     x_any, back_ref, kept_ref, rest_ref, kept_sem, out_sems,
 ):
     rows = pl.ds(pl.multiple_of(place_ref[1] * 128, 128), 128)
@@ -101,8 +101,8 @@
     return total.astype(bf16).reshape(4, 128, 512)
 
 
-def rows_of(three_ref, last_ref):
-    return jnp.concatenate([three_ref[...].reshape(384, 512), last_ref[...]], axis=0)
+def rows_of(first_ref, last_ref):
+    return jnp.concatenate([first_ref[...].reshape(256, 512), last_ref[...].reshape(256, 512)], axis=0)
 
 
 def own_kernel(own_ref, near_ref, last_ref, far_ref, far_last_ref, out_ref):
@@ -114,9 +114,9 @@
 ):
     core, z_high = place_ref[0], place_ref[2]
     total = products((rows_of(near_ref, last_ref), rows_of(far_ref, far_last_ref)), other_ref)
-    for i, k in enumerate((0, 1, 3, 2)):
-        out_ref[z_high ^ k, :, 0:512] = done_ref[i]
-        out_ref[z_high ^ k, :, 512:1024] = total[i]
+    for k in range(4):
+        out_ref[z_high ^ k, :, 0:512] = done_ref[k]
+        out_ref[z_high ^ k, :, 512:1024] = total[k]
     tok, back, singular = [], [], jnp.zeros((1, 128), f32)
     for ref in (own_ref, other_ref):
         for x in range(4):
@@ -195,9 +195,9 @@
 
     cot = after(cotangent, got)
     cots = [cot] + [swap(cot, "zh", 4, k) for k in (1, 2, 3)]
-    near = jnp.stack([cots[0], cots[1], cots[3]])
+    near = jnp.stack(cots[:2])
     far = swap(near, "yl", 2, 1)
-    last = cots[2]
+    last = jnp.stack(cots[2:])
     far_last = swap(last, "yl", 2, 1)
 
     coeff_lanes = jnp.pad(jnp.concatenate([coeff, coeff]), (0, 96)).reshape(1, 128)
@@ -205,12 +205,12 @@
     x_out, scaled_back = call(
         pack_kernel,
         (shape((4, 320, 512), bf16), shape((8, 128), bf16)),
-        [in_smem] + [in_vmem] * 4 + [anywhere] * 2 + [in_vmem] + [anywhere] * 2,
+        [in_smem] + [in_vmem] * 4 + [anywhere] * 2 + [in_vmem] + [anywhere],
         16 << 20,
         3 << 20,
         out_specs=(in_hbm, in_vmem),
         scratch=[pltpu.VMEM((128, 512), bf16), pltpu.VMEM((32, 512), bf16), dma, dma((16,))],
-    )(place, rank_out, rank_in, coeff_lanes, cot, weight, got, slices, cots[1], cots[3])
+    )(place, rank_out, rank_in, coeff_lanes, cot, weight, got, slices, cots[1])
     x_in = after(lax.all_to_all(x_out, "x", 0, 0), far, far_last)
     x_other = swap(x_in, "c", 2, 1)
 

time: 118 us -> 119 us (level)
  starting transfers between devices: 65.1 us -> 66.7 us
    ppermute x10, waiting for transfers between devices: 28.1 us -> 26.2 us  [swap(): return lax.ppermute(a, axis, [(i, i ^ mask) for i in range(count)])]
    all_to_all x1, starting transfers between devices: 10.8 us -> 12.6 us  [body(): lax.all_to_all(out.reshape(64, 8, 1152), ('zh', 'zl', 'yh', 'yl'), 0, 0)]
    all_to_all x1, waiting for transfers between devices: 0.01 us -> 1.58 us  [body(): rank_in = lax.all_to_all(rank_out, ('zl', 'yh', 'yl'), 0, 0)]
  transfers between devices with their start and end apart: 13 -> 13, of which waited for: 6 -> 7; matrix products, arithmetic and copies ran while one was open for 3% -> 3% of each run, Pallas kernels for 1% -> 1%
where the time goes in v9:
time: 119 us; the launch traced here: 118 us
  starting transfers between devices  66.7 us (56%)
  waiting for transfers between devices  38.6 us (32%)
  Pallas kernels  6.23 us (5%)
  other arithmetic  2.18 us (2%)
  local copies, waits for them, and re-layouts  2.1 us (2%)
  matrix products  1.37 us (1%)
    ppermute x10, starting transfers between devices, swap(): return lax.ppermute(a, axis, [(i, i ^ mask) for i in range(count)])  41.3 us
    ppermute x10, waiting for transfers between devices, swap(): return lax.ppermute(a, axis, [(i, i ^ mask) for i in range(count)])  26.2 us
    all_to_all x1, starting transfers between devices, body(): lax.all_to_all(out.reshape(64, 8, 1152), ('zh', 'zl', 'yh', 'yl'), 0, 0)  12.6 us
    all_to_all x1, waiting for transfers between devices, body(): lax.all_to_all(out.reshape(64, 8, 1152), ('zh', 'zl', 'yh', 'yl'), 0, 0)  10.8 us
    all_to_all x1, starting transfers between devices, body(): rank_in = lax.all_to_all(rank_out, ('zl', 'yh', 'yl'), 0, 0)  8.11 us
    all_to_all x1, starting transfers between devices, body(): x_in = after(lax.all_to_all(x_out, 'x', 0, 0), far, far_last)  4.78 us
  transfers between devices with their start and end apart: 13, of which 7 were waited for; matrix products, arithmetic and copies ran while one was open for 3% of the time, Pallas kernels for 1%

profile of v9, /device:TPU:6, one launch (start us, length us, event | category | flops | bytes accessed | tf_op | source)
XLA Modules:
  0.0 118.0 jit_solution(17511786951384825675)
XLA Ops:
  0.6 0.0 copy-start
  0.6 0.0 copy-start.4
  0.7 0.0 copy-start.3
  0.7 1.0 copy.21.refs_0_
  1.6 3.5 %collective-permute-start = (bf16[256,512]{1,0:T(8,128)(2,1)}, bf16[256,512]{1,0:T(8,128)(2,1)S(1)}, u32[]{:S(2)}, u32[]{:S(2)}) collective-permute-start(bf16[256,512]{1,0:T(8,128)(2,1)} %weight_any.1), channel_id=1, source_target_pairs={{0,1},{1,0},{2,3},{3,2},{4,5},{5,4},{6,7},{7,6},{8,9},{9,8},{10,11... | collective-permute-start | bytes 786440 | tf_op jit(solution)/shard_map/ppermute | solution.py:29
  5.1 0.0 copy-done
  5.1 0.2 convolution_bitcast_fusion
  5.3 1.2 %fusion.2 = f32[8,16]{1,0:T(8,128)S(1)} fusion(bf16[8,8192]{1,0:T(8,128)(2,1)} %param.7, bf16[8192,16]{0,1:T(8,128)(2,1)} %param.10), kind=kOutput, calls=%fused_computation.13 | convolution fusion | flops 2097152 | bytes 393728 | tf_op jit(solution)/shard_map/dot_general | solution.py:192
  6.5 0.1 pad.13
  6.6 0.7 pad_add_fusion.sent_ref
  7.2 8.1 %all-to-all-start = ((f32[16,8,128]{2,1,0:T(8,128)}), f32[16,8,128]{2,1,0:T(8,128)S(1)}, u32[]{:S(2)}, u32[]{:S(2)}) async-start(f32[16,8,128]{2,1,0:T(8,128)} %pad_add_fusion.sent_ref), calls=%async_computation | async-start | bytes 131072 | tf_op jit(solution)/shard_map/all_to_all | solution.py:194
  15.3 0.7 convert_multiply_fusion
  16.0 0.0 collective-permute-done.refs_1_.got_any
  16.0 6.1 %collective-permute-start.1 = (bf16[128,512]{1,0:T(8,128)(2,1)S(1)}, bf16[128,512]{1,0:T(8,128)(2,1)S(1)}, u32[]{:S(2)}, u32[]{:S(2)}) collective-permute-start(bf16[128,512]{1,0:T(8,128)(2,1)S(1)} %shard_map.102.cot_ref), channel_id=1, source_target_pairs={{0,128},{128,0},{256,384},{384,256},{1,129},{129,1},{257,385},{385... | collective-permute-start | bytes 393224 | tf_op jit(solution)/shard_map/ppermute | solution.py:29
  22.1 0.1 fusion.1.coeff_ref
  22.2 0.0 copy-done.4
  22.2 0.1 pad_add_fusion.1.place_ref
  22.3 1.6 %all-to-all-done.rank_ref = f32[16,8,128]{2,1,0:T(8,128)S(1)} async-done(((f32[16,8,128]{2,1,0:T(8,128)}), f32[16,8,128]{2,1,0:T(8,128)S(1)}, u32[]{:S(2)}, u32[]{:S(2)}) %all-to-all-start) | async-done | bytes 65568 | tf_op jit(solution)/shard_map/all_to_all | solution.py:194
  23.9 4.0 %collective-permute-done.1.after1 = bf16[128,512]{1,0:T(8,128)(2,1)S(1)} collective-permute-done((bf16[128,512]{1,0:T(8,128)(2,1)S(1)}, bf16[128,512]{1,0:T(8,128)(2,1)S(1)}, u32[]{:S(2)}, u32[]{:S(2)}) %collective-permute-start.1) | collective-permute-done | bytes 131104 | tf_op jit(solution)/shard_map/ppermute | solution.py:29
  27.8 0.0 copy-done.3
  27.8 2.3 %shard_map.103 = (bf16[4,320,512]{2,1,0:T(8,128)(2,1)}, bf16[8,128]{1,0:T(8,128)(2,1)S(1)}) custom-call(s32[3]{0:T(128)S(1)} %pad_add_fusion.1.place_ref, f32[16,8,128]{2,1,0:T(8,128)} %pad_add_fusion.sent_ref, f32[16,8,128]{2,1,0:T(8,128)S(1)} %all-to-all-done.rank_ref, f32[1,128]{1,0:T(1,128)S(1)} %fusion.1.coeff_ref, ...), custom_call_target="tpu_custom_call" | custom-call | flops 16777216 | bytes 3145728 | tf_op jit(solution)/shard_map/pallas_call | solution.py:205
  30.1 4.8 %all-to-all-start.1 = ((bf16[4,320,512]{2,1,0:T(8,128)(2,1)}), bf16[4,320,512]{2,1,0:T(8,128)(2,1)S(1)}, u32[]{:S(2)}, u32[]{:S(2)}) async-start(bf16[4,320,512]{2,1,0:T(8,128)(2,1)} %get-tuple-element.11), calls=%async_computation.1 | async-start | bytes 2621440 | tf_op jit(solution)/shard_map/all_to_all | solution.py:214
  34.9 8.5 %collective-permute-start.3 = (bf16[128,512]{1,0:T(8,128)(2,1)S(1)}, bf16[128,512]{1,0:T(8,128)(2,1)S(1)}, u32[]{:S(2)}, u32[]{:S(2)}) collective-permute-start(bf16[128,512]{1,0:T(8,128)(2,1)S(1)} %shard_map.102.cot_ref), channel_id=1, source_target_pairs={{0,256},{128,384},{256,0},{384,128},{1,257},{129,385},{257,1},{385... | collective-permute-start | bytes 393224 | tf_op jit(solution)/shard_map/ppermute | solution.py:29
  43.4 1.9 %collective-permute-start.4 = (bf16[128,512]{1,0:T(8,128)(2,1)S(1)}, bf16[128,512]{1,0:T(8,128)(2,1)S(1)}, u32[]{:S(2)}, u32[]{:S(2)}) collective-permute-start(bf16[128,512]{1,0:T(8,128)(2,1)S(1)} %shard_map.102.cot_ref), channel_id=1, source_target_pairs={{0,384},{128,256},{256,128},{384,0},{1,385},{129,257},{257,129},{3... | collective-permute-start | bytes 393224 | tf_op jit(solution)/shard_map/ppermute | solution.py:29
  45.3 3.6 %collective-permute-start.2 = (bf16[2,128,512]{2,1,0:T(8,128)(2,1)S(1)}, bf16[2,128,512]{2,1,0:T(8,128)(2,1)S(1)}, u32[]{:S(2)}, u32[]{:S(2)}) collective-permute-start(bf16[2,128,512]{2,1,0:T(8,128)(2,1)S(1)} %pad_maximum_fusion.near_ref), channel_id=1, source_target_pairs={{0,1},{1,0},{2,3},{3,2},{4,5},{5,4},{6,7},{7,6},{8,9},{9,8},{10,11... | collective-permute-start | bytes 786440 | tf_op jit(solution)/shard_map/ppermute | solution.py:29
  48.9 0.0 collective-permute-done.3
  48.9 4.7 %collective-permute-done.4 = bf16[128,512]{1,0:T(8,128)(2,1)S(1)} collective-permute-done((bf16[128,512]{1,0:T(8,128)(2,1)S(1)}, bf16[128,512]{1,0:T(8,128)(2,1)S(1)}, u32[]{:S(2)}, u32[]{:S(2)}) %collective-permute-start.4) | collective-permute-done | bytes 131104 | tf_op jit(solution)/shard_map/ppermute | solution.py:29
  53.6 3.7 %collective-permute-start.5 = (bf16[2,128,512]{2,1,0:T(8,128)(2,1)S(1)}, bf16[2,128,512]{2,1,0:T(8,128)(2,1)S(1)}, u32[]{:S(2)}, u32[]{:S(2)}) collective-permute-start(bf16[2,128,512]{2,1,0:T(8,128)(2,1)S(1)} %pad_maximum_fusion.1.last_ref), channel_id=1, source_target_pairs={{0,1},{1,0},{2,3},{3,2},{4,5},{5,4},{6,7},{7,6},{8,9},{9,8},{10,11... | collective-permute-start | bytes 786440 | tf_op jit(solution)/shard_map/ppermute | solution.py:29
  57.3 0.0 collective-permute-done.2.refs_1_.far_ref
  57.3 5.9 %collective-permute-done.5.refs_2_.far_last_ref = bf16[2,128,512]{2,1,0:T(8,128)(2,1)S(1)} collective-permute-done((bf16[2,128,512]{2,1,0:T(8,128)(2,1)S(1)}, bf16[2,128,512]{2,1,0:T(8,128)(2,1)S(1)}, u32[]{:S(2)}, u32[]{:S(2)}) %collective-permute-start.5) | collective-permute-done | bytes 262176 | tf_op jit(solution)/shard_map/ppermute | solution.py:29
  63.2 0.0 all-to-all-done.1.refs_0_
  63.2 1.9 %collective-permute-start.6 = (bf16[4,320,512]{2,1,0:T(8,128)(2,1)S(1)}, bf16[4,320,512]{2,1,0:T(8,128)(2,1)S(1)}, u32[]{:S(2)}, u32[]{:S(2)}) collective-permute-start(bf16[4,320,512]{2,1,0:T(8,128)(2,1)S(1)} %shard_map.104.own_ref), channel_id=1, source_target_pairs={{0,16},{16,0},{1,17},{17,1},{2,18},{18,2},{3,19},{19,3},{4,20},{20... | collective-permute-start | bytes 3932168 | tf_op jit(solution)/shard_map/ppermute | solution.py:29
  65.1 0.7 shard_map.105.done_ref
  65.9 2.3 %collective-permute-done.6.other_ref = bf16[4,320,512]{2,1,0:T(8,128)(2,1)S(1)} collective-permute-done((bf16[4,320,512]{2,1,0:T(8,128)(2,1)S(1)}, bf16[4,320,512]{2,1,0:T(8,128)(2,1)S(1)}, u32[]{:S(2)}, u32[]{:S(2)}) %collective-permute-start.6) | collective-permute-done | bytes 1310752 | tf_op jit(solution)/shard_map/ppermute | solution.py:29
  68.1 1.5 %shard_map.106 = (bf16[4,128,1152]{2,1,0:T(8,128)(2,1)S(1)}, f32[16,512]{1,0:T(8,128)S(1)}) custom-call(s32[3]{0:T(128)S(1)} %pad_add_fusion.1.place_ref, bf16[4,128,512]{2,1,0:T(8,128)(2,1)S(1)} %shard_map.105.done_ref, bf16[4,320,512]{2,1,0:T(8,128)(2,1)S(1)} %shard_map.104.own_ref, bf16[4,320,512]{2,1,0:T(8,128)(2,1)S(1)} %collective-permute-done.6.other_ref, ...), custom_call_target="tpu_custom_call" | custom-call | flops 536870912 | bytes 5242880 | tf_op jit(solution)/shard_map/pallas_call | solution.py:220
  69.6 1.0 copy-done.1
  70.6 12.6 %all-to-all-start.2 = ((bf16[64,8,1152]{2,1,0:T(8,128)(2,1)}), bf16[64,8,1152]{2,1,0:T(8,128)(2,1)S(1)}, u32[]{:S(2)}, u32[]{:S(2)}) async-start(bf16[64,8,1152]{2,1,0:T(8,128)(2,1)} %bitcast.27), calls=%async_computation.2 | async-start | bytes 2359296 | tf_op jit(solution)/shard_map/all_to_all | solution.py:227
  83.2 4.4 %collective-permute-start.7 = (bf16[16,512]{1,0:T(8,128)(2,1)S(1)}, bf16[16,512]{1,0:T(8,128)(2,1)S(1)}, u32[]{:S(2)}, u32[]{:S(2)}) collective-permute-start(bf16[16,512]{1,0:T(8,128)(2,1)S(1)} %convert_element_type.22), channel_id=1, source_target_pairs={{0,128},{128,0},{256,384},{384,256},{1,129},{129,1},{257,385},{385... | collective-permute-start | bytes 49160 | tf_op jit(solution)/shard_map/ppermute | solution.py:29
  87.6 5.7 %collective-permute-start.8 = (bf16[16,512]{1,0:T(8,128)(2,1)S(1)}, bf16[16,512]{1,0:T(8,128)(2,1)S(1)}, u32[]{:S(2)}, u32[]{:S(2)}) collective-permute-start(bf16[16,512]{1,0:T(8,128)(2,1)S(1)} %convert_element_type.22), channel_id=1, source_target_pairs={{0,256},{128,384},{256,0},{384,128},{1,257},{129,385},{257,1},{385... | collective-permute-start | bytes 49160 | tf_op jit(solution)/shard_map/ppermute | solution.py:29
  93.3 2.2 %collective-permute-start.9 = (bf16[16,512]{1,0:T(8,128)(2,1)S(1)}, bf16[16,512]{1,0:T(8,128)(2,1)S(1)}, u32[]{:S(2)}, u32[]{:S(2)}) collective-permute-start(bf16[16,512]{1,0:T(8,128)(2,1)S(1)} %convert_element_type.22), channel_id=1, source_target_pairs={{0,384},{128,256},{256,128},{384,0},{1,385},{129,257},{257,129},{3... | collective-permute-start | bytes 49160 | tf_op jit(solution)/shard_map/ppermute | solution.py:29
  95.5 0.0 copy-done.5
  95.5 9.3 %collective-permute-done.7 = bf16[16,512]{1,0:T(8,128)(2,1)S(1)} collective-permute-done((bf16[16,512]{1,0:T(8,128)(2,1)S(1)}, bf16[16,512]{1,0:T(8,128)(2,1)S(1)}, u32[]{:S(2)}, u32[]{:S(2)}) %collective-permute-start.7) | collective-permute-done | bytes 16416 | tf_op jit(solution)/shard_map/ppermute | solution.py:29
  104.8 0.0 collective-permute-done.8
  104.8 0.0 collective-permute-done.9
  104.8 0.6 add_multiply_fusion
  105.5 10.8 %all-to-all-done.2.back_ref = bf16[64,8,1152]{2,1,0:T(8,128)(2,1)S(1)} async-done(((bf16[64,8,1152]{2,1,0:T(8,128)(2,1)}), bf16[64,8,1152]{2,1,0:T(8,128)(2,1)S(1)}, u32[]{:S(2)}, u32[]{:S(2)}) %all-to-all-start.2) | async-done | bytes 1179680 | tf_op jit(solution)/shard_map/all_to_all | solution.py:227
  116.3 0.0 copy-done.2
  116.3 1.7 %shard_map.107 = (bf16[8,8192]{1,0:T(8,128)(2,1)}, f32[16,16]{1,0:T(8,128)}, f32[1,16]{1,0:T(1,128)}) custom-call(s32[3]{0:T(128)S(1)} %pad_add_fusion.1.place_ref, bf16[64,8,1152]{2,1,0:T(8,128)(2,1)S(1)} %all-to-all-done.2.back_ref, bf16[8,128]{1,0:T(8,128)(2,1)S(1)} %get-tuple-element.13.scaled_ref, bf16[16,8192]{1,0:T(8,128)(2,1)S(1)} %bitcast.28, ...), custom_call_target="tpu_custom_call" | custom-call | flops 2097152 | bytes 2097152 | tf_op jit(solution)/shard_map/pallas_call | solution.py:231
  (10 shorter events, 0.1 us)
Async XLA Ops:
  0.6 4.5 %copy-start = (bf16[16,512]{1,0:T(8,128)(2,1)S(1)}, bf16[16,512]{1,0:T(8,128)(2,1)}, u32[]{:S(2)}) copy-start(bf16[16,512]{1,0:T(8,128)(2,1)} %param.11) | copy-start | bytes 49156
  0.6 21.6 %copy-start.4 = (bf16[8,8192]{1,0:T(8,128)(2,1)S(1)}, bf16[8,8192]{1,0:T(8,128)(2,1)}, u32[]{:S(2)}) copy-start(bf16[8,8192]{1,0:T(8,128)(2,1)} %param.7) | copy-start | bytes 393220
  0.7 27.2 %copy-start.3 = (bf16[256,512]{1,0:T(8,128)(2,1)S(1)}, bf16[256,512]{1,0:T(8,128)(2,1)}, u32[]{:S(2)}) copy-start(bf16[256,512]{1,0:T(8,128)(2,1)} %weight_any.1) | copy-start | bytes 786436
  1.6 14.4 %collective-permute-start = (bf16[256,512]{1,0:T(8,128)(2,1)}, bf16[256,512]{1,0:T(8,128)(2,1)S(1)}, u32[]{:S(2)}, u32[]{:S(2)}) collective-permute-start(bf16[256,512]{1,0:T(8,128)(2,1)} %weight_any.1), channel_id=1, source_target_pairs={{0,1},{1,0},{2,3},{3,2},{4,5},{5,4},{6,7},{7,6},{8,9},{9,8},{10,11... | collective-permute-start | bytes 786440 | tf_op jit(solution)/shard_map/ppermute | solution.py:29
  7.2 16.6 %all-to-all-start = ((f32[16,8,128]{2,1,0:T(8,128)}), f32[16,8,128]{2,1,0:T(8,128)S(1)}, u32[]{:S(2)}, u32[]{:S(2)}) async-start(f32[16,8,128]{2,1,0:T(8,128)} %pad_add_fusion.sent_ref), calls=%async_computation | async-start | bytes 131072 | tf_op jit(solution)/shard_map/all_to_all | solution.py:194
  16.0 11.8 %collective-permute-start.1 = (bf16[128,512]{1,0:T(8,128)(2,1)S(1)}, bf16[128,512]{1,0:T(8,128)(2,1)S(1)}, u32[]{:S(2)}, u32[]{:S(2)}) collective-permute-start(bf16[128,512]{1,0:T(8,128)(2,1)S(1)} %shard_map.102.cot_ref), channel_id=1, source_target_pairs={{0,128},{128,0},{256,384},{384,256},{1,129},{129,1},{257,385},{385... | collective-permute-start | bytes 393224 | tf_op jit(solution)/shard_map/ppermute | solution.py:29
  30.1 33.1 %all-to-all-start.1 = ((bf16[4,320,512]{2,1,0:T(8,128)(2,1)}), bf16[4,320,512]{2,1,0:T(8,128)(2,1)S(1)}, u32[]{:S(2)}, u32[]{:S(2)}) async-start(bf16[4,320,512]{2,1,0:T(8,128)(2,1)} %get-tuple-element.11), calls=%async_computation.1 | async-start | bytes 2621440 | tf_op jit(solution)/shard_map/all_to_all | solution.py:214
  34.9 14.0 %collective-permute-start.3 = (bf16[128,512]{1,0:T(8,128)(2,1)S(1)}, bf16[128,512]{1,0:T(8,128)(2,1)S(1)}, u32[]{:S(2)}, u32[]{:S(2)}) collective-permute-start(bf16[128,512]{1,0:T(8,128)(2,1)S(1)} %shard_map.102.cot_ref), channel_id=1, source_target_pairs={{0,256},{128,384},{256,0},{384,128},{1,257},{129,385},{257,1},{385... | collective-permute-start | bytes 393224 | tf_op jit(solution)/shard_map/ppermute | solution.py:29
  43.4 10.2 %collective-permute-start.4 = (bf16[128,512]{1,0:T(8,128)(2,1)S(1)}, bf16[128,512]{1,0:T(8,128)(2,1)S(1)}, u32[]{:S(2)}, u32[]{:S(2)}) collective-permute-start(bf16[128,512]{1,0:T(8,128)(2,1)S(1)} %shard_map.102.cot_ref), channel_id=1, source_target_pairs={{0,384},{128,256},{256,128},{384,0},{1,385},{129,257},{257,129},{3... | collective-permute-start | bytes 393224 | tf_op jit(solution)/shard_map/ppermute | solution.py:29
  45.3 11.9 %collective-permute-start.2 = (bf16[2,128,512]{2,1,0:T(8,128)(2,1)S(1)}, bf16[2,128,512]{2,1,0:T(8,128)(2,1)S(1)}, u32[]{:S(2)}, u32[]{:S(2)}) collective-permute-start(bf16[2,128,512]{2,1,0:T(8,128)(2,1)S(1)} %pad_maximum_fusion.near_ref), channel_id=1, source_target_pairs={{0,1},{1,0},{2,3},{3,2},{4,5},{5,4},{6,7},{7,6},{8,9},{9,8},{10,11... | collective-permute-start | bytes 786440 | tf_op jit(solution)/shard_map/ppermute | solution.py:29
  53.6 9.6 %collective-permute-start.5 = (bf16[2,128,512]{2,1,0:T(8,128)(2,1)S(1)}, bf16[2,128,512]{2,1,0:T(8,128)(2,1)S(1)}, u32[]{:S(2)}, u32[]{:S(2)}) collective-permute-start(bf16[2,128,512]{2,1,0:T(8,128)(2,1)S(1)} %pad_maximum_fusion.1.last_ref), channel_id=1, source_target_pairs={{0,1},{1,0},{2,3},{3,2},{4,5},{5,4},{6,7},{7,6},{8,9},{9,8},{10,11... | collective-permute-start | bytes 786440 | tf_op jit(solution)/shard_map/ppermute | solution.py:29
  63.2 4.9 %collective-permute-start.6 = (bf16[4,320,512]{2,1,0:T(8,128)(2,1)S(1)}, bf16[4,320,512]{2,1,0:T(8,128)(2,1)S(1)}, u32[]{:S(2)}, u32[]{:S(2)}) collective-permute-start(bf16[4,320,512]{2,1,0:T(8,128)(2,1)S(1)} %shard_map.104.own_ref), channel_id=1, source_target_pairs={{0,16},{16,0},{1,17},{17,1},{2,18},{18,2},{3,19},{19,3},{4,20},{20... | collective-permute-start | bytes 3932168 | tf_op jit(solution)/shard_map/ppermute | solution.py:29
  69.6 1.0 copy-start.1
  70.6 24.8 %copy-start.5 = (s32[16]{0:T(128)S(1)}, s32[16]{0:T(128)}, u32[]{:S(2)}) copy-start(s32[16]{0:T(128)} %param.13) | copy-start | bytes 196
  70.6 45.7 %copy-start.2 = (bf16[8192,16]{0,1:T(8,128)(2,1)S(1)}, bf16[8192,16]{0,1:T(8,128)(2,1)}, u32[]{:S(2)}) copy-start(bf16[8192,16]{0,1:T(8,128)(2,1)} %param.10) | copy-start | bytes 786436
  70.6 45.7 %all-to-all-start.2 = ((bf16[64,8,1152]{2,1,0:T(8,128)(2,1)}), bf16[64,8,1152]{2,1,0:T(8,128)(2,1)S(1)}, u32[]{:S(2)}, u32[]{:S(2)}) async-start(bf16[64,8,1152]{2,1,0:T(8,128)(2,1)} %bitcast.27), calls=%async_computation.2 | async-start | bytes 2359296 | tf_op jit(solution)/shard_map/all_to_all | solution.py:227
  83.2 21.6 %collective-permute-start.7 = (bf16[16,512]{1,0:T(8,128)(2,1)S(1)}, bf16[16,512]{1,0:T(8,128)(2,1)S(1)}, u32[]{:S(2)}, u32[]{:S(2)}) collective-permute-start(bf16[16,512]{1,0:T(8,128)(2,1)S(1)} %convert_element_type.22), channel_id=1, source_target_pairs={{0,128},{128,0},{256,384},{384,256},{1,129},{129,1},{257,385},{385... | collective-permute-start | bytes 49160 | tf_op jit(solution)/shard_map/ppermute | solution.py:29
  87.6 17.2 %collective-permute-start.8 = (bf16[16,512]{1,0:T(8,128)(2,1)S(1)}, bf16[16,512]{1,0:T(8,128)(2,1)S(1)}, u32[]{:S(2)}, u32[]{:S(2)}) collective-permute-start(bf16[16,512]{1,0:T(8,128)(2,1)S(1)} %convert_element_type.22), channel_id=1, source_target_pairs={{0,256},{128,384},{256,0},{384,128},{1,257},{129,385},{257,1},{385... | collective-permute-start | bytes 49160 | tf_op jit(solution)/shard_map/ppermute | solution.py:29
  93.3 11.5 %collective-permute-start.9 = (bf16[16,512]{1,0:T(8,128)(2,1)S(1)}, bf16[16,512]{1,0:T(8,128)(2,1)S(1)}, u32[]{:S(2)}, u32[]{:S(2)}) collective-permute-start(bf16[16,512]{1,0:T(8,128)(2,1)S(1)} %convert_element_type.22), channel_id=1, source_target_pairs={{0,384},{128,256},{256,128},{384,0},{1,385},{129,257},{257,129},{3... | collective-permute-start | bytes 49160 | tf_op jit(solution)/shard_map/ppermute | solution.py:29

commit v10 on v9

--- a/solution.py
+++ b/solution.py
@@ -52,8 +52,13 @@
     )(a, *others)
 
 
+def stack_kernel(c0_ref, c1_ref, c2_ref, c3_ref, out_ref):
+    for k, ref in enumerate((c0_ref, c1_ref, c2_ref, c3_ref)):
+        out_ref[k] = ref[...]
+
+
 def pack_kernel(
-    place_ref, sent_ref, rank_ref, coeff_ref, cot_ref, weight_any, got_any, slices_ref, after1,
+    place_ref, sent_ref, rank_ref, coeff_ref, cot_ref, weight_any, got_any, slices_ref,
     x_any, back_ref, kept_ref, rest_ref, kept_sem, out_sems,
 ):
     rows = pl.ds(pl.multiple_of(place_ref[1] * 128, 128), 128)
@@ -101,19 +106,15 @@
     return total.astype(bf16).reshape(4, 128, 512)
 
 
-def rows_of(first_ref, last_ref):
-    return jnp.concatenate([first_ref[...].reshape(256, 512), last_ref[...].reshape(256, 512)], axis=0)
-
-
-def own_kernel(own_ref, near_ref, last_ref, far_ref, far_last_ref, out_ref):
-    out_ref[...] = products((rows_of(near_ref, last_ref), rows_of(far_ref, far_last_ref)), own_ref)
+def own_kernel(own_ref, near_ref, far_ref, out_ref):
+    out_ref[...] = products((near_ref[...].reshape(512, 512), far_ref[...].reshape(512, 512)), own_ref)
 
 
 def other_kernel(
-    place_ref, done_ref, own_ref, other_ref, near_ref, last_ref, far_ref, far_last_ref, out_ref, right_ref
+    place_ref, done_ref, own_ref, other_ref, near_ref, far_ref, out_ref, right_ref
 ):
     core, z_high = place_ref[0], place_ref[2]
-    total = products((rows_of(near_ref, last_ref), rows_of(far_ref, far_last_ref)), other_ref)
+    total = products((near_ref[...].reshape(512, 512), far_ref[...].reshape(512, 512)), other_ref)
     for k in range(4):
         out_ref[z_high ^ k, :, 0:512] = done_ref[k]
         out_ref[z_high ^ k, :, 512:1024] = total[k]
@@ -195,35 +196,31 @@
 
     cot = after(cotangent, got)
     cots = [cot] + [swap(cot, "zh", 4, k) for k in (1, 2, 3)]
-    near = jnp.stack(cots[:2])
+    near = call(stack_kernel, shape((4, 128, 512), bf16), [in_vmem] * 4, 30 << 30, 1 << 20)(*cots)
     far = swap(near, "yl", 2, 1)
-    last = jnp.stack(cots[2:])
-    far_last = swap(last, "yl", 2, 1)
 
     coeff_lanes = jnp.pad(jnp.concatenate([coeff, coeff]), (0, 96)).reshape(1, 128)
     slices = inputs.reshape(8, 4, 4, 512).transpose(2, 1, 0, 3).reshape(4, 32, 512)
     x_out, scaled_back = call(
         pack_kernel,
         (shape((4, 320, 512), bf16), shape((8, 128), bf16)),
-        [in_smem] + [in_vmem] * 4 + [anywhere] * 2 + [in_vmem] + [anywhere],
-        16 << 20,
+        [in_smem] + [in_vmem] * 4 + [anywhere] * 2 + [in_vmem],
+        30 << 30,
         3 << 20,
         out_specs=(in_hbm, in_vmem),
         scratch=[pltpu.VMEM((128, 512), bf16), pltpu.VMEM((32, 512), bf16), dma, dma((16,))],
-    )(place, rank_out, rank_in, coeff_lanes, cot, weight, got, slices, cots[1])
-    x_in = after(lax.all_to_all(x_out, "x", 0, 0), far, far_last)
+    )(place, rank_out, rank_in, coeff_lanes, cot, weight, got, slices)
+    x_in = after(lax.all_to_all(x_out, "x", 0, 0), far)
     x_other = swap(x_in, "c", 2, 1)
 
-    done = call(own_kernel, shape((4, 128, 512), bf16), [in_vmem] * 5, 1 << 29, 3 << 20)(
-        x_in, near, last, far, far_last
-    )
+    done = call(own_kernel, shape((4, 128, 512), bf16), [in_vmem] * 3, 1 << 29, 3 << 20)(x_in, near, far)
     out, right_part = call(
         other_kernel,
         (shape((4, 128, 1152), bf16), shape((16, 512), f32)),
-        [in_smem] + [in_vmem] * 7,
+        [in_smem] + [in_vmem] * 5,
         1 << 29,
         5 << 20,
-    )(place, done, x_in, x_other, near, last, far, far_last)
+    )(place, done, x_in, x_other, near, far)
     back = lax.all_to_all(out.reshape(64, 8, 1152), ("zh", "zl", "yh", "yl"), 0, 0)
     right_sent = right_part.astype(bf16)
     right_sum = right_part + sum(swap(right_sent, "zh", 4, k).astype(f32) for k in (1, 2, 3))

time: 119 us -> 113 us (0.950)
  starting transfers between devices: 66.7 us -> 61.9 us
  waiting for transfers between devices: 38.6 us -> 37.2 us
    ppermute x10 -> x9, starting transfers between devices: 41.3 us -> 37.2 us  [swap(): return lax.ppermute(a, axis, [(i, i ^ mask) for i in range(count)])]
    all_to_all x1, waiting for transfers between devices: 1.58 us -> 0.01 us  [body(): rank_in = lax.all_to_all(rank_out, ('zl', 'yh', 'yl'), 0, 0)]
    ppermute x10 -> x9, waiting for transfers between devices: 26.2 us -> 26.3 us  [swap(): return lax.ppermute(a, axis, [(i, i ^ mask) for i in range(count)])]
  transfers between devices with their start and end apart: 13 -> 12, of which waited for: 7 -> 5; matrix products, arithmetic and copies ran while one was open for 3% -> 4% of each run, Pallas kernels for 1% -> 3%
where the time goes in v10:
time: 113 us
  starting transfers between devices  61.9 us (55%)
  waiting for transfers between devices  37.2 us (33%)
  Pallas kernels  7.3 us (6%)
  other arithmetic  2.13 us (2%)
  local copies, waits for them, and re-layouts  1.96 us (2%)
  matrix products  1.37 us (1%)
    ppermute x9, starting transfers between devices, swap(): return lax.ppermute(a, axis, [(i, i ^ mask) for i in range(count)])  37.2 us
    ppermute x9, waiting for transfers between devices, swap(): return lax.ppermute(a, axis, [(i, i ^ mask) for i in range(count)])  26.3 us
    all_to_all x1, starting transfers between devices, body(): lax.all_to_all(out.reshape(64, 8, 1152), ('zh', 'zl', 'yh', 'yl'), 0, 0)  11.8 us
    all_to_all x1, waiting for transfers between devices, body(): lax.all_to_all(out.reshape(64, 8, 1152), ('zh', 'zl', 'yh', 'yl'), 0, 0)  10.9 us
    all_to_all x1, starting transfers between devices, body(): rank_in = lax.all_to_all(rank_out, ('zl', 'yh', 'yl'), 0, 0)  8.11 us
    all_to_all x1, starting transfers between devices, body(): x_in = after(lax.all_to_all(x_out, 'x', 0, 0), far)  4.78 us
    pallas_call x1, Pallas kernels, body(): call(other_kernel, (shape((4, 128, 1152), bf16), shape((16, 512), f32)),...  2.54 us
    pallas_call x1, Pallas kernels, body(): call(pack_kernel, (shape((4, 320, 512), bf16), shape((8, 128), bf16)), [i...  2.27 us
  transfers between devices with their start and end apart: 12, of which 5 were waited for; matrix products, arithmetic and copies ran while one was open for 4% of the time, Pallas kernels for 3%

profile of v10, /device:TPU:6, one launch (start us, length us, event | category | flops | bytes accessed | tf_op | source)
XLA Modules:
  0.0 112.7 jit_solution(13618027274993349413)
XLA Ops:
  0.6 0.0 copy-start
  0.6 0.0 copy-start.2
  0.7 0.9 copy.21.refs_0_
  1.6 3.5 %collective-permute-start = (bf16[256,512]{1,0:T(8,128)(2,1)}, bf16[256,512]{1,0:T(8,128)(2,1)S(1)}, u32[]{:S(2)}, u32[]{:S(2)}) collective-permute-start(bf16[256,512]{1,0:T(8,128)(2,1)} %weight_any.1), channel_id=1, source_target_pairs={{0,1},{1,0},{2,3},{3,2},{4,5},{5,4},{6,7},{7,6},{8,9},{9,8},{10,11... | collective-permute-start | bytes 786440 | tf_op jit(solution)/shard_map/ppermute | solution.py:29
  5.1 0.0 copy-done
  5.1 0.2 convolution_bitcast_fusion
  5.3 1.2 %fusion.2 = f32[8,16]{1,0:T(8,128)S(1)} fusion(bf16[8,8192]{1,0:T(8,128)(2,1)} %param.7, bf16[8192,16]{0,1:T(8,128)(2,1)} %param.10), kind=kOutput, calls=%fused_computation.11 | convolution fusion | flops 2097152 | bytes 393728 | tf_op jit(solution)/shard_map/dot_general | solution.py:193
  6.5 0.1 pad.13
  6.5 0.7 pad_add_fusion.sent_ref
  7.2 8.1 %all-to-all-start = ((f32[16,8,128]{2,1,0:T(8,128)}), f32[16,8,128]{2,1,0:T(8,128)S(1)}, u32[]{:S(2)}, u32[]{:S(2)}) async-start(f32[16,8,128]{2,1,0:T(8,128)} %pad_add_fusion.sent_ref), calls=%async_computation | async-start | bytes 131072 | tf_op jit(solution)/shard_map/all_to_all | solution.py:195
  15.3 0.7 convert_multiply_fusion
  16.0 0.1 fusion.1.coeff_ref
  16.1 0.9 copy.17
  17.0 0.1 pad_add_fusion.1.place_ref
  17.1 0.0 collective-permute-done.refs_1_.got_any
  17.1 6.1 %collective-permute-start.1 = (bf16[128,512]{1,0:T(8,128)(2,1)S(1)}, bf16[128,512]{1,0:T(8,128)(2,1)S(1)}, u32[]{:S(2)}, u32[]{:S(2)}) collective-permute-start(bf16[128,512]{1,0:T(8,128)(2,1)S(1)} %shard_map.102.cot_ref.c0_ref), channel_id=1, source_target_pairs={{0,128},{128,0},{256,384},{384,256},{1,129},{129,1},{257,385},{385... | collective-permute-start | bytes 393224 | tf_op jit(solution)/shard_map/ppermute | solution.py:29
  23.2 8.2 %collective-permute-start.2 = (bf16[128,512]{1,0:T(8,128)(2,1)S(1)}, bf16[128,512]{1,0:T(8,128)(2,1)S(1)}, u32[]{:S(2)}, u32[]{:S(2)}) collective-permute-start(bf16[128,512]{1,0:T(8,128)(2,1)S(1)} %shard_map.102.cot_ref.c0_ref), channel_id=1, source_target_pairs={{0,256},{128,384},{256,0},{384,128},{1,257},{129,385},{257,1},{385... | collective-permute-start | bytes 393224 | tf_op jit(solution)/shard_map/ppermute | solution.py:29
  31.4 1.9 %collective-permute-start.3 = (bf16[128,512]{1,0:T(8,128)(2,1)S(1)}, bf16[128,512]{1,0:T(8,128)(2,1)S(1)}, u32[]{:S(2)}, u32[]{:S(2)}) collective-permute-start(bf16[128,512]{1,0:T(8,128)(2,1)S(1)} %shard_map.102.cot_ref.c0_ref), channel_id=1, source_target_pairs={{0,384},{128,256},{256,128},{384,0},{1,385},{129,257},{257,129},{3... | collective-permute-start | bytes 393224 | tf_op jit(solution)/shard_map/ppermute | solution.py:29
  33.3 0.0 all-to-all-done.rank_ref
  33.3 0.0 copy-done.2
  33.4 2.3 %shard_map.103 = (bf16[4,320,512]{2,1,0:T(8,128)(2,1)}, bf16[8,128]{1,0:T(8,128)(2,1)S(1)}) custom-call(s32[3]{0:T(128)S(1)} %pad_add_fusion.1.place_ref, f32[16,8,128]{2,1,0:T(8,128)} %pad_add_fusion.sent_ref, f32[16,8,128]{2,1,0:T(8,128)S(1)} %all-to-all-done.rank_ref, f32[1,128]{1,0:T(1,128)S(1)} %fusion.1.coeff_ref, ...), custom_call_target="tpu_custom_call" | custom-call | flops 32212254720 | bytes 3145728 | tf_op jit(solution)/shard_map/pallas_call | solution.py:204
  35.6 4.8 %all-to-all-start.1 = ((bf16[4,320,512]{2,1,0:T(8,128)(2,1)}), bf16[4,320,512]{2,1,0:T(8,128)(2,1)S(1)}, u32[]{:S(2)}, u32[]{:S(2)}) async-start(bf16[4,320,512]{2,1,0:T(8,128)(2,1)} %get-tuple-element.11), calls=%async_computation.1 | async-start | bytes 2621440 | tf_op jit(solution)/shard_map/all_to_all | solution.py:213
  40.4 0.0 collective-permute-done.1.c1_ref
  40.4 0.0 collective-permute-done.2.c2_ref
  40.4 2.4 %collective-permute-done.3.c3_ref = bf16[128,512]{1,0:T(8,128)(2,1)S(1)} collective-permute-done((bf16[128,512]{1,0:T(8,128)(2,1)S(1)}, bf16[128,512]{1,0:T(8,128)(2,1)S(1)}, u32[]{:S(2)}, u32[]{:S(2)}) %collective-permute-start.3) | collective-permute-done | bytes 131104 | tf_op jit(solution)/shard_map/ppermute | solution.py:29
  42.8 3.4 %collective-permute-start.4 = (bf16[4,128,512]{2,1,0:T(8,128)(2,1)S(1)}, bf16[4,128,512]{2,1,0:T(8,128)(2,1)S(1)}, u32[]{:S(2)}, u32[]{:S(2)}) collective-permute-start(bf16[4,128,512]{2,1,0:T(8,128)(2,1)S(1)} %shard_map.104.near_ref), channel_id=1, source_target_pairs={{0,1},{1,0},{2,3},{3,2},{4,5},{5,4},{6,7},{7,6},{8,9},{9,8},{10,11... | collective-permute-start | bytes 1572872 | tf_op jit(solution)/shard_map/ppermute | solution.py:29
  46.2 12.4 %collective-permute-done.4.refs_1_.far_ref = bf16[4,128,512]{2,1,0:T(8,128)(2,1)S(1)} collective-permute-done((bf16[4,128,512]{2,1,0:T(8,128)(2,1)S(1)}, bf16[4,128,512]{2,1,0:T(8,128)(2,1)S(1)}, u32[]{:S(2)}, u32[]{:S(2)}) %collective-permute-start.4) | collective-permute-done | bytes 524320 | tf_op jit(solution)/shard_map/ppermute | solution.py:29
  58.6 0.0 all-to-all-done.1.refs_0_
  58.6 1.9 %collective-permute-start.5 = (bf16[4,320,512]{2,1,0:T(8,128)(2,1)S(1)}, bf16[4,320,512]{2,1,0:T(8,128)(2,1)S(1)}, u32[]{:S(2)}, u32[]{:S(2)}) collective-permute-start(bf16[4,320,512]{2,1,0:T(8,128)(2,1)S(1)} %shard_map.105.own_ref), channel_id=1, source_target_pairs={{0,16},{16,0},{1,17},{17,1},{2,18},{18,2},{3,19},{19,3},{4,20},{20... | collective-permute-start | bytes 3932168 | tf_op jit(solution)/shard_map/ppermute | solution.py:29
  60.5 0.7 shard_map.106.done_ref
  61.2 2.3 %collective-permute-done.5.other_ref = bf16[4,320,512]{2,1,0:T(8,128)(2,1)S(1)} collective-permute-done((bf16[4,320,512]{2,1,0:T(8,128)(2,1)S(1)}, bf16[4,320,512]{2,1,0:T(8,128)(2,1)S(1)}, u32[]{:S(2)}, u32[]{:S(2)}) %collective-permute-start.5) | collective-permute-done | bytes 1310752 | tf_op jit(solution)/shard_map/ppermute | solution.py:29
  63.5 2.5 %shard_map.107 = (bf16[4,128,1152]{2,1,0:T(8,128)(2,1)}, f32[16,512]{1,0:T(8,128)S(1)}) custom-call(s32[3]{0:T(128)S(1)} %pad_add_fusion.1.place_ref, bf16[4,128,512]{2,1,0:T(8,128)(2,1)S(1)} %shard_map.106.done_ref, bf16[4,320,512]{2,1,0:T(8,128)(2,1)S(1)} %shard_map.105.own_ref, bf16[4,320,512]{2,1,0:T(8,128)(2,1)S(1)} %collective-permute-done.5.other_ref, ...), custom_call_target="tpu_custom_call" | custom-call | flops 536870912 | bytes 5242880 | tf_op jit(solution)/shard_map/pallas_call | solution.py:217
  66.0 0.0 copy-start.3
  66.0 0.0 copy-start.1
  66.0 11.8 %all-to-all-start.2 = ((bf16[64,8,1152]{2,1,0:T(8,128)(2,1)}), bf16[64,8,1152]{2,1,0:T(8,128)(2,1)S(1)}, u32[]{:S(2)}, u32[]{:S(2)}) async-start(bf16[64,8,1152]{2,1,0:T(8,128)(2,1)} %bitcast.8), calls=%async_computation.2 | async-start | bytes 2359296 | tf_op jit(solution)/shard_map/all_to_all | solution.py:224
  77.9 4.4 %collective-permute-start.6 = (bf16[16,512]{1,0:T(8,128)(2,1)S(1)}, bf16[16,512]{1,0:T(8,128)(2,1)S(1)}, u32[]{:S(2)}, u32[]{:S(2)}) collective-permute-start(bf16[16,512]{1,0:T(8,128)(2,1)S(1)} %convert_element_type.22), channel_id=1, source_target_pairs={{0,128},{128,0},{256,384},{384,256},{1,129},{129,1},{257,385},{385... | collective-permute-start | bytes 49160 | tf_op jit(solution)/shard_map/ppermute | solution.py:29
  82.3 5.7 %collective-permute-start.7 = (bf16[16,512]{1,0:T(8,128)(2,1)S(1)}, bf16[16,512]{1,0:T(8,128)(2,1)S(1)}, u32[]{:S(2)}, u32[]{:S(2)}) collective-permute-start(bf16[16,512]{1,0:T(8,128)(2,1)S(1)} %convert_element_type.22), channel_id=1, source_target_pairs={{0,256},{128,384},{256,0},{384,128},{1,257},{129,385},{257,1},{385... | collective-permute-start | bytes 49160 | tf_op jit(solution)/shard_map/ppermute | solution.py:29
  88.0 2.2 %collective-permute-start.8 = (bf16[16,512]{1,0:T(8,128)(2,1)S(1)}, bf16[16,512]{1,0:T(8,128)(2,1)S(1)}, u32[]{:S(2)}, u32[]{:S(2)}) collective-permute-start(bf16[16,512]{1,0:T(8,128)(2,1)S(1)} %convert_element_type.22), channel_id=1, source_target_pairs={{0,384},{128,256},{256,128},{384,0},{1,385},{129,257},{257,129},{3... | collective-permute-start | bytes 49160 | tf_op jit(solution)/shard_map/ppermute | solution.py:29
  90.1 0.0 copy-done.3
  90.1 9.3 %collective-permute-done.6 = bf16[16,512]{1,0:T(8,128)(2,1)S(1)} collective-permute-done((bf16[16,512]{1,0:T(8,128)(2,1)S(1)}, bf16[16,512]{1,0:T(8,128)(2,1)S(1)}, u32[]{:S(2)}, u32[]{:S(2)}) %collective-permute-start.6) | collective-permute-done | bytes 16416 | tf_op jit(solution)/shard_map/ppermute | solution.py:29
  99.5 0.0 collective-permute-done.7
  99.5 0.0 collective-permute-done.8
  99.5 0.6 add_multiply_fusion
  100.1 10.9 %all-to-all-done.2.back_ref = bf16[64,8,1152]{2,1,0:T(8,128)(2,1)S(1)} async-done(((bf16[64,8,1152]{2,1,0:T(8,128)(2,1)}), bf16[64,8,1152]{2,1,0:T(8,128)(2,1)S(1)}, u32[]{:S(2)}, u32[]{:S(2)}) %all-to-all-start.2) | async-done | bytes 1179680 | tf_op jit(solution)/shard_map/all_to_all | solution.py:224
  111.0 0.0 copy-done.1
  111.0 1.7 %shard_map.108 = (bf16[8,8192]{1,0:T(8,128)(2,1)}, f32[16,16]{1,0:T(8,128)}, f32[1,16]{1,0:T(1,128)}) custom-call(s32[3]{0:T(128)S(1)} %pad_add_fusion.1.place_ref, bf16[64,8,1152]{2,1,0:T(8,128)(2,1)S(1)} %all-to-all-done.2.back_ref, bf16[8,128]{1,0:T(8,128)(2,1)S(1)} %get-tuple-element.13.scaled_ref, bf16[16,8192]{1,0:T(8,128)(2,1)S(1)} %bitcast.22, ...), custom_call_target="tpu_custom_call" | custom-call | flops 2097152 | bytes 2097152 | tf_op jit(solution)/shard_map/pallas_call | solution.py:228
  (5 shorter events, 0.0 us)
Async XLA Ops:
  0.6 4.5 %copy-start = (bf16[16,512]{1,0:T(8,128)(2,1)S(1)}, bf16[16,512]{1,0:T(8,128)(2,1)}, u32[]{:S(2)}) copy-start(bf16[16,512]{1,0:T(8,128)(2,1)} %param.11) | copy-start | bytes 49156
  0.6 32.7 %copy-start.2 = (bf16[256,512]{1,0:T(8,128)(2,1)S(1)}, bf16[256,512]{1,0:T(8,128)(2,1)}, u32[]{:S(2)}) copy-start(bf16[256,512]{1,0:T(8,128)(2,1)} %weight_any.1) | copy-start | bytes 786436
  1.6 15.5 %collective-permute-start = (bf16[256,512]{1,0:T(8,128)(2,1)}, bf16[256,512]{1,0:T(8,128)(2,1)S(1)}, u32[]{:S(2)}, u32[]{:S(2)}) collective-permute-start(bf16[256,512]{1,0:T(8,128)(2,1)} %weight_any.1), channel_id=1, source_target_pairs={{0,1},{1,0},{2,3},{3,2},{4,5},{5,4},{6,7},{7,6},{8,9},{9,8},{10,11... | collective-permute-start | bytes 786440 | tf_op jit(solution)/shard_map/ppermute | solution.py:29
  7.2 26.1 %all-to-all-start = ((f32[16,8,128]{2,1,0:T(8,128)}), f32[16,8,128]{2,1,0:T(8,128)S(1)}, u32[]{:S(2)}, u32[]{:S(2)}) async-start(f32[16,8,128]{2,1,0:T(8,128)} %pad_add_fusion.sent_ref), calls=%async_computation | async-start | bytes 131072 | tf_op jit(solution)/shard_map/all_to_all | solution.py:195
  17.1 23.3 %collective-permute-start.1 = (bf16[128,512]{1,0:T(8,128)(2,1)S(1)}, bf16[128,512]{1,0:T(8,128)(2,1)S(1)}, u32[]{:S(2)}, u32[]{:S(2)}) collective-permute-start(bf16[128,512]{1,0:T(8,128)(2,1)S(1)} %shard_map.102.cot_ref.c0_ref), channel_id=1, source_target_pairs={{0,128},{128,0},{256,384},{384,256},{1,129},{129,1},{257,385},{385... | collective-permute-start | bytes 393224 | tf_op jit(solution)/shard_map/ppermute | solution.py:29
  23.2 17.2 %collective-permute-start.2 = (bf16[128,512]{1,0:T(8,128)(2,1)S(1)}, bf16[128,512]{1,0:T(8,128)(2,1)S(1)}, u32[]{:S(2)}, u32[]{:S(2)}) collective-permute-start(bf16[128,512]{1,0:T(8,128)(2,1)S(1)} %shard_map.102.cot_ref.c0_ref), channel_id=1, source_target_pairs={{0,256},{128,384},{256,0},{384,128},{1,257},{129,385},{257,1},{385... | collective-permute-start | bytes 393224 | tf_op jit(solution)/shard_map/ppermute | solution.py:29
  31.4 11.4 %collective-permute-start.3 = (bf16[128,512]{1,0:T(8,128)(2,1)S(1)}, bf16[128,512]{1,0:T(8,128)(2,1)S(1)}, u32[]{:S(2)}, u32[]{:S(2)}) collective-permute-start(bf16[128,512]{1,0:T(8,128)(2,1)S(1)} %shard_map.102.cot_ref.c0_ref), channel_id=1, source_target_pairs={{0,384},{128,256},{256,128},{384,0},{1,385},{129,257},{257,129},{3... | collective-permute-start | bytes 393224 | tf_op jit(solution)/shard_map/ppermute | solution.py:29
  35.6 22.9 %all-to-all-start.1 = ((bf16[4,320,512]{2,1,0:T(8,128)(2,1)}), bf16[4,320,512]{2,1,0:T(8,128)(2,1)S(1)}, u32[]{:S(2)}, u32[]{:S(2)}) async-start(bf16[4,320,512]{2,1,0:T(8,128)(2,1)} %get-tuple-element.11), calls=%async_computation.1 | async-start | bytes 2621440 | tf_op jit(solution)/shard_map/all_to_all | solution.py:213
  42.8 15.7 %collective-permute-start.4 = (bf16[4,128,512]{2,1,0:T(8,128)(2,1)S(1)}, bf16[4,128,512]{2,1,0:T(8,128)(2,1)S(1)}, u32[]{:S(2)}, u32[]{:S(2)}) collective-permute-start(bf16[4,128,512]{2,1,0:T(8,128)(2,1)S(1)} %shard_map.104.near_ref), channel_id=1, source_target_pairs={{0,1},{1,0},{2,3},{3,2},{4,5},{5,4},{6,7},{7,6},{8,9},{9,8},{10,11... | collective-permute-start | bytes 1572872 | tf_op jit(solution)/shard_map/ppermute | solution.py:29
  58.6 4.9 %collective-permute-start.5 = (bf16[4,320,512]{2,1,0:T(8,128)(2,1)S(1)}, bf16[4,320,512]{2,1,0:T(8,128)(2,1)S(1)}, u32[]{:S(2)}, u32[]{:S(2)}) collective-permute-start(bf16[4,320,512]{2,1,0:T(8,128)(2,1)S(1)} %shard_map.105.own_ref), channel_id=1, source_target_pairs={{0,16},{16,0},{1,17},{17,1},{2,18},{18,2},{3,19},{19,3},{4,20},{20... | collective-permute-start | bytes 3932168 | tf_op jit(solution)/shard_map/ppermute | solution.py:29
  66.0 24.1 %copy-start.3 = (s32[16]{0:T(128)S(1)}, s32[16]{0:T(128)}, u32[]{:S(2)}) copy-start(s32[16]{0:T(128)} %param.13) | copy-start | bytes 196
  66.0 44.9 %copy-start.1 = (bf16[8192,16]{0,1:T(8,128)(2,1)S(1)}, bf16[8192,16]{0,1:T(8,128)(2,1)}, u32[]{:S(2)}) copy-start(bf16[8192,16]{0,1:T(8,128)(2,1)} %param.10) | copy-start | bytes 786436
  66.0 44.9 %all-to-all-start.2 = ((bf16[64,8,1152]{2,1,0:T(8,128)(2,1)}), bf16[64,8,1152]{2,1,0:T(8,128)(2,1)S(1)}, u32[]{:S(2)}, u32[]{:S(2)}) async-start(bf16[64,8,1152]{2,1,0:T(8,128)(2,1)} %bitcast.8), calls=%async_computation.2 | async-start | bytes 2359296 | tf_op jit(solution)/shard_map/all_to_all | solution.py:224
  77.9 21.6 %collective-permute-start.6 = (bf16[16,512]{1,0:T(8,128)(2,1)S(1)}, bf16[16,512]{1,0:T(8,128)(2,1)S(1)}, u32[]{:S(2)}, u32[]{:S(2)}) collective-permute-start(bf16[16,512]{1,0:T(8,128)(2,1)S(1)} %convert_element_type.22), channel_id=1, source_target_pairs={{0,128},{128,0},{256,384},{384,256},{1,129},{129,1},{257,385},{385... | collective-permute-start | bytes 49160 | tf_op jit(solution)/shard_map/ppermute | solution.py:29
  82.3 17.2 %collective-permute-start.7 = (bf16[16,512]{1,0:T(8,128)(2,1)S(1)}, bf16[16,512]{1,0:T(8,128)(2,1)S(1)}, u32[]{:S(2)}, u32[]{:S(2)}) collective-permute-start(bf16[16,512]{1,0:T(8,128)(2,1)S(1)} %convert_element_type.22), channel_id=1, source_target_pairs={{0,256},{128,384},{256,0},{384,128},{1,257},{129,385},{257,1},{385... | collective-permute-start | bytes 49160 | tf_op jit(solution)/shard_map/ppermute | solution.py:29
  88.0 11.5 %collective-permute-start.8 = (bf16[16,512]{1,0:T(8,128)(2,1)S(1)}, bf16[16,512]{1,0:T(8,128)(2,1)S(1)}, u32[]{:S(2)}, u32[]{:S(2)}) collective-permute-start(bf16[16,512]{1,0:T(8,128)(2,1)S(1)} %convert_element_type.22), channel_id=1, source_target_pairs={{0,384},{128,256},{256,128},{384,0},{1,385},{129,257},{257,129},{3... | collective-permute-start | bytes 49160 | tf_op jit(solution)/shard_map/ppermute | solution.py:29

commit v11 on v8

--- a/solution.py
+++ b/solution.py
@@ -52,14 +52,21 @@
     )(a, *others)
 
 
+def copy_kernel(in_ref, out_ref):
+    out_ref[...] = in_ref[...]
+
+
+def rows_of(first_ref, last_ref):
+    return jnp.concatenate([first_ref[...].reshape(256, 512), last_ref[...].reshape(256, 512)], axis=0)
+
+
 def pack_kernel(
-    place_ref, sent_ref, rank_ref, coeff_ref, cot_ref, weight_any, got_any, slices_ref, after1, after3,
-    x_any, back_ref, kept_ref, rest_ref, kept_sem, out_sems,
+    place_ref, sent_ref, rank_ref, coeff_ref, cot_ref, weight_any, got_any, slices_ref,
+    x_any, back_ref, rest_ref, out_sems,
 ):
     rows = pl.ds(pl.multiple_of(place_ref[1] * 128, 128), 128)
-    kept_in = pltpu.make_async_copy(weight_any.at[rows], kept_ref, kept_sem)
-    kept_in.start()
     outs = [pltpu.make_async_copy(got_any.at[rows], x_any.at[x, 128:256], out_sems.at[x]) for x in range(4)]
+    outs += [pltpu.make_async_copy(weight_any.at[rows], x_any.at[x, 0:128], out_sems.at[8 + x]) for x in range(4)]
     outs += [pltpu.make_async_copy(slices_ref.at[x], x_any.at[x, 256:288], out_sems.at[4 + x]) for x in range(4)]
     for copy in outs:
         copy.start()
@@ -85,11 +92,8 @@
     ).astype(bf16)
     rest_ref[0:16, :] = small
     rest_ref[16:32, :] = right.astype(bf16)
-    kept_in.wait()
     for x in range(4):
-        outs.append(pltpu.make_async_copy(kept_ref, x_any.at[x, 0:128], out_sems.at[8 + x]))
         outs.append(pltpu.make_async_copy(rest_ref, x_any.at[x, 288:320], out_sems.at[12 + x]))
-        outs[-2].start()
         outs[-1].start()
     for copy in outs:
         copy.wait()
@@ -99,10 +103,6 @@
     total = dot_t(parts[0], ref[:, 0:128, :].reshape(512, 512))
     total += dot_t(parts[1], ref[:, 128:256, :].reshape(512, 512))
     return total.astype(bf16).reshape(4, 128, 512)
-
-
-def rows_of(three_ref, last_ref):
-    return jnp.concatenate([three_ref[...].reshape(384, 512), last_ref[...]], axis=0)
 
 
 def own_kernel(own_ref, near_ref, last_ref, far_ref, far_last_ref, out_ref):
@@ -194,10 +194,9 @@
     rank_in = lax.all_to_all(rank_out, ("zl", "yh", "yl"), 0, 0)
 
     cot = after(cotangent, got)
-    cots = [cot] + [swap(cot, "zh", 4, k) for k in (1, 2, 3)]
-    near = jnp.stack([cots[0], cots[1], cots[3]])
+    near = jnp.stack([cot, swap(cot, "zh", 4, 1)])
     far = swap(near, "yl", 2, 1)
-    last = cots[2]
+    last = call(copy_kernel, shape((2, 128, 512), bf16), [in_vmem], 30 << 30, 1 << 20)(swap(near, "zh", 4, 3))
     far_last = swap(last, "yl", 2, 1)
 
     coeff_lanes = jnp.pad(jnp.concatenate([coeff, coeff]), (0, 96)).reshape(1, 128)
@@ -205,12 +204,12 @@
     x_out, scaled_back = call(
         pack_kernel,
         (shape((4, 320, 512), bf16), shape((8, 128), bf16)),
-        [in_smem] + [in_vmem] * 4 + [anywhere] * 2 + [in_vmem] + [anywhere] * 2,
-        16 << 20,
+        [in_smem] + [in_vmem] * 4 + [anywhere] * 2 + [in_vmem],
+        30 << 30,
         3 << 20,
         out_specs=(in_hbm, in_vmem),
-        scratch=[pltpu.VMEM((128, 512), bf16), pltpu.VMEM((32, 512), bf16), dma, dma((16,))],
-    )(place, rank_out, rank_in, coeff_lanes, cot, weight, got, slices, cots[1], cots[3])
+        scratch=[pltpu.VMEM((32, 512), bf16), dma((16,))],
+    )(place, rank_out, rank_in, coeff_lanes, cot, weight, got, slices)
     x_in = after(lax.all_to_all(x_out, "x", 0, 0), far, far_last)
     x_other = swap(x_in, "c", 2, 1)
 

time: 118 us -> 112 us (0.949)
  starting transfers between devices: 65.1 us -> 61.7 us
  waiting for transfers between devices: 39 us -> 35.7 us
    ppermute x10 -> x9, starting transfers between devices: 41.4 us -> 36.2 us  [swap(): return lax.ppermute(a, axis, [(i, i ^ mask) for i in range(count)])]
    ppermute x10 -> x9, waiting for transfers between devices: 28.1 us -> 24.5 us  [swap(): return lax.ppermute(a, axis, [(i, i ^ mask) for i in range(count)])]
    all_to_all x1, starting transfers between devices: 10.8 us -> 12.6 us  [body(): lax.all_to_all(out.reshape(64, 8, 1152), ('zh', 'zl', 'yh', 'yl'), 0, 0)]
  transfers between devices with their start and end apart: 13 -> 12, of which waited for: 6 -> 7; matrix products, arithmetic and copies ran while one was open for 3% -> 3% of each run, Pallas kernels for 1% -> 3%
where the time goes in v11:
time: 112 us; the launch traced here: 110 us
  starting transfers between devices  61.7 us (55%)
  waiting for transfers between devices  35.7 us (32%)
  Pallas kernels  7.08 us (6%)
  other arithmetic  2.15 us (2%)
  matrix products  1.37 us (1%)
    ppermute x9, starting transfers between devices, swap(): return lax.ppermute(a, axis, [(i, i ^ mask) for i in range(count)])  36.2 us
    ppermute x9, waiting for transfers between devices, swap(): return lax.ppermute(a, axis, [(i, i ^ mask) for i in range(count)])  24.5 us
    all_to_all x1, starting transfers between devices, body(): lax.all_to_all(out.reshape(64, 8, 1152), ('zh', 'zl', 'yh', 'yl'), 0, 0)  12.6 us
    all_to_all x1, waiting for transfers between devices, body(): lax.all_to_all(out.reshape(64, 8, 1152), ('zh', 'zl', 'yh', 'yl'), 0, 0)  10.8 us
    all_to_all x1, starting transfers between devices, body(): rank_in = lax.all_to_all(rank_out, ('zl', 'yh', 'yl'), 0, 0)  8.11 us
    all_to_all x1, starting transfers between devices, body(): x_in = after(lax.all_to_all(x_out, 'x', 0, 0), far, far_last)  4.78 us
    pallas_call x1, Pallas kernels, body(): call(other_kernel, (shape((4, 128, 1152), bf16), shape((16, 512), f32)),...  2.53 us
  transfers between devices with their start and end apart: 12, of which 7 were waited for; matrix products, arithmetic and copies ran while one was open for 3% of the time, Pallas kernels for 3%

profile of v11, /device:TPU:6, one launch (start us, length us, event | category | flops | bytes accessed | tf_op | source)
XLA Modules:
  0.0 110.0 jit_solution(7322150896369217251)
XLA Ops:
  0.6 0.0 copy-start
  0.6 0.0 copy-start.3
  0.7 0.0 copy-start.2
  0.7 1.0 copy.21.refs_0_
  1.6 3.5 %collective-permute-start = (bf16[256,512]{1,0:T(8,128)(2,1)}, bf16[256,512]{1,0:T(8,128)(2,1)S(1)}, u32[]{:S(2)}, u32[]{:S(2)}) collective-permute-start(bf16[256,512]{1,0:T(8,128)(2,1)} %weight_any.1), channel_id=1, source_target_pairs={{0,1},{1,0},{2,3},{3,2},{4,5},{5,4},{6,7},{7,6},{8,9},{9,8},{10,11... | collective-permute-start | bytes 786440 | tf_op jit(solution)/shard_map/ppermute | solution.py:29
  5.1 0.0 copy-done
  5.1 0.2 convolution_bitcast_fusion
  5.3 1.2 %fusion.2 = f32[8,16]{1,0:T(8,128)S(1)} fusion(bf16[8,8192]{1,0:T(8,128)(2,1)} %param.7, bf16[8192,16]{0,1:T(8,128)(2,1)} %param.10), kind=kOutput, calls=%fused_computation.12 | convolution fusion | flops 2097152 | bytes 393728 | tf_op jit(solution)/shard_map/dot_general | solution.py:192
  6.5 0.1 pad.13
  6.6 0.7 pad_add_fusion.sent_ref
  7.2 8.1 %all-to-all-start = ((f32[16,8,128]{2,1,0:T(8,128)}), f32[16,8,128]{2,1,0:T(8,128)S(1)}, u32[]{:S(2)}, u32[]{:S(2)}) async-start(f32[16,8,128]{2,1,0:T(8,128)} %pad_add_fusion.sent_ref), calls=%async_computation | async-start | bytes 131072 | tf_op jit(solution)/shard_map/all_to_all | solution.py:194
  15.3 0.7 convert_multiply_fusion
  16.0 0.0 collective-permute-done.refs_1_.got_any
  16.0 6.1 %collective-permute-start.1 = (bf16[128,512]{1,0:T(8,128)(2,1)S(1)}, bf16[128,512]{1,0:T(8,128)(2,1)S(1)}, u32[]{:S(2)}, u32[]{:S(2)}) collective-permute-start(bf16[128,512]{1,0:T(8,128)(2,1)S(1)} %shard_map.102.cot_ref), channel_id=1, source_target_pairs={{0,128},{128,0},{256,384},{384,256},{1,129},{129,1},{257,385},{385... | collective-permute-start | bytes 393224 | tf_op jit(solution)/shard_map/ppermute | solution.py:29
  22.1 0.1 fusion.1.coeff_ref
  22.2 0.1 pad_add_fusion.1.place_ref
  22.3 0.0 copy-done.3
  22.3 5.6 %collective-permute-done.1 = bf16[128,512]{1,0:T(8,128)(2,1)S(1)} collective-permute-done((bf16[128,512]{1,0:T(8,128)(2,1)S(1)}, bf16[128,512]{1,0:T(8,128)(2,1)S(1)}, u32[]{:S(2)}, u32[]{:S(2)}) %collective-permute-start.1) | collective-permute-done | bytes 131104 | tf_op jit(solution)/shard_map/ppermute | solution.py:29
  27.9 6.0 %collective-permute-start.3 = (bf16[2,128,512]{2,1,0:T(8,128)(2,1)S(1)}, bf16[2,128,512]{2,1,0:T(8,128)(2,1)S(1)}, u32[]{:S(2)}, u32[]{:S(2)}) collective-permute-start(bf16[2,128,512]{2,1,0:T(8,128)(2,1)S(1)} %pad_maximum_fusion.near_ref), channel_id=1, source_target_pairs={{0,384},{128,256},{256,128},{384,0},{1,385},{129,257},{257,129},{3... | collective-permute-start | bytes 786440 | tf_op jit(solution)/shard_map/ppermute | solution.py:29
  33.9 0.0 all-to-all-done.rank_ref
  33.9 0.0 copy-done.2
  33.9 2.1 %shard_map.103 = (bf16[4,320,512]{2,1,0:T(8,128)(2,1)}, bf16[8,128]{1,0:T(8,128)(2,1)S(1)}) custom-call(s32[3]{0:T(128)S(1)} %pad_add_fusion.1.place_ref, f32[16,8,128]{2,1,0:T(8,128)} %pad_add_fusion.sent_ref, f32[16,8,128]{2,1,0:T(8,128)S(1)} %all-to-all-done.rank_ref, f32[1,128]{1,0:T(1,128)S(1)} %fusion.1.coeff_ref, ...), custom_call_target="tpu_custom_call" | custom-call | flops 32212254720 | bytes 3145728 | tf_op jit(solution)/shard_map/pallas_call | solution.py:204
  36.0 4.8 %all-to-all-start.1 = ((bf16[4,320,512]{2,1,0:T(8,128)(2,1)}), bf16[4,320,512]{2,1,0:T(8,128)(2,1)S(1)}, u32[]{:S(2)}, u32[]{:S(2)}) async-start(bf16[4,320,512]{2,1,0:T(8,128)(2,1)} %get-tuple-element.11), calls=%async_computation.1 | async-start | bytes 2621440 | tf_op jit(solution)/shard_map/all_to_all | solution.py:213
  40.8 3.8 %collective-permute-start.2 = (bf16[2,128,512]{2,1,0:T(8,128)(2,1)S(1)}, bf16[2,128,512]{2,1,0:T(8,128)(2,1)S(1)}, u32[]{:S(2)}, u32[]{:S(2)}) collective-permute-start(bf16[2,128,512]{2,1,0:T(8,128)(2,1)S(1)} %pad_maximum_fusion.near_ref), channel_id=1, source_target_pairs={{0,1},{1,0},{2,3},{3,2},{4,5},{5,4},{6,7},{7,6},{8,9},{9,8},{10,11... | collective-permute-start | bytes 786440 | tf_op jit(solution)/shard_map/ppermute | solution.py:29
  44.6 0.0 collective-permute-done.3.in_ref
  44.6 2.7 %collective-permute-start.4 = (bf16[2,128,512]{2,1,0:T(8,128)(2,1)S(1)}, bf16[2,128,512]{2,1,0:T(8,128)(2,1)S(1)}, u32[]{:S(2)}, u32[]{:S(2)}) collective-permute-start(bf16[2,128,512]{2,1,0:T(8,128)(2,1)S(1)} %shard_map.104.last_ref), channel_id=1, source_target_pairs={{0,1},{1,0},{2,3},{3,2},{4,5},{5,4},{6,7},{7,6},{8,9},{9,8},{10,11... | collective-permute-start | bytes 786440 | tf_op jit(solution)/shard_map/ppermute | solution.py:29
  47.3 4.5 %collective-permute-done.2.refs_1_.far_ref = bf16[2,128,512]{2,1,0:T(8,128)(2,1)S(1)} collective-permute-done((bf16[2,128,512]{2,1,0:T(8,128)(2,1)S(1)}, bf16[2,128,512]{2,1,0:T(8,128)(2,1)S(1)}, u32[]{:S(2)}, u32[]{:S(2)}) %collective-permute-start.2) | collective-permute-done | bytes 262176 | tf_op jit(solution)/shard_map/ppermute | solution.py:29
  51.8 2.8 %collective-permute-done.4.refs_2_.far_last_ref = bf16[2,128,512]{2,1,0:T(8,128)(2,1)S(1)} collective-permute-done((bf16[2,128,512]{2,1,0:T(8,128)(2,1)S(1)}, bf16[2,128,512]{2,1,0:T(8,128)(2,1)S(1)}, u32[]{:S(2)}, u32[]{:S(2)}) %collective-permute-start.4) | collective-permute-done | bytes 262176 | tf_op jit(solution)/shard_map/ppermute | solution.py:29
  54.7 0.4 all-to-all-done.1.refs_0_
  55.1 1.9 %collective-permute-start.5 = (bf16[4,320,512]{2,1,0:T(8,128)(2,1)S(1)}, bf16[4,320,512]{2,1,0:T(8,128)(2,1)S(1)}, u32[]{:S(2)}, u32[]{:S(2)}) collective-permute-start(bf16[4,320,512]{2,1,0:T(8,128)(2,1)S(1)} %shard_map.105.own_ref), channel_id=1, source_target_pairs={{0,16},{16,0},{1,17},{17,1},{2,18},{18,2},{3,19},{19,3},{4,20},{20... | collective-permute-start | bytes 3932168 | tf_op jit(solution)/shard_map/ppermute | solution.py:29
  57.0 0.7 shard_map.106.done_ref
  57.7 2.3 %collective-permute-done.5.other_ref = bf16[4,320,512]{2,1,0:T(8,128)(2,1)S(1)} collective-permute-done((bf16[4,320,512]{2,1,0:T(8,128)(2,1)S(1)}, bf16[4,320,512]{2,1,0:T(8,128)(2,1)S(1)}, u32[]{:S(2)}, u32[]{:S(2)}) %collective-permute-start.5) | collective-permute-done | bytes 1310752 | tf_op jit(solution)/shard_map/ppermute | solution.py:29
  60.0 2.5 %shard_map.107 = (bf16[4,128,1152]{2,1,0:T(8,128)(2,1)}, f32[16,512]{1,0:T(8,128)S(1)}) custom-call(s32[3]{0:T(128)S(1)} %pad_add_fusion.1.place_ref, bf16[4,128,512]{2,1,0:T(8,128)(2,1)S(1)} %shard_map.106.done_ref, bf16[4,320,512]{2,1,0:T(8,128)(2,1)S(1)} %shard_map.105.own_ref, bf16[4,320,512]{2,1,0:T(8,128)(2,1)S(1)} %collective-permute-done.5.other_ref, ...), custom_call_target="tpu_custom_call" | custom-call | flops 536870912 | bytes 5242880 | tf_op jit(solution)/shard_map/pallas_call | solution.py:219
  62.5 0.0 copy-start.4
  62.5 0.0 copy-start.1
  62.5 12.6 %all-to-all-start.2 = ((bf16[64,8,1152]{2,1,0:T(8,128)(2,1)}), bf16[64,8,1152]{2,1,0:T(8,128)(2,1)S(1)}, u32[]{:S(2)}, u32[]{:S(2)}) async-start(bf16[64,8,1152]{2,1,0:T(8,128)(2,1)} %bitcast.10), calls=%async_computation.2 | async-start | bytes 2359296 | tf_op jit(solution)/shard_map/all_to_all | solution.py:226
  75.1 4.4 %collective-permute-start.6 = (bf16[16,512]{1,0:T(8,128)(2,1)S(1)}, bf16[16,512]{1,0:T(8,128)(2,1)S(1)}, u32[]{:S(2)}, u32[]{:S(2)}) collective-permute-start(bf16[16,512]{1,0:T(8,128)(2,1)S(1)} %convert_element_type.22), channel_id=1, source_target_pairs={{0,128},{128,0},{256,384},{384,256},{1,129},{129,1},{257,385},{385... | collective-permute-start | bytes 49160 | tf_op jit(solution)/shard_map/ppermute | solution.py:29
  79.5 5.7 %collective-permute-start.7 = (bf16[16,512]{1,0:T(8,128)(2,1)S(1)}, bf16[16,512]{1,0:T(8,128)(2,1)S(1)}, u32[]{:S(2)}, u32[]{:S(2)}) collective-permute-start(bf16[16,512]{1,0:T(8,128)(2,1)S(1)} %convert_element_type.22), channel_id=1, source_target_pairs={{0,256},{128,384},{256,0},{384,128},{1,257},{129,385},{257,1},{385... | collective-permute-start | bytes 49160 | tf_op jit(solution)/shard_map/ppermute | solution.py:29
  85.2 2.2 %collective-permute-start.8 = (bf16[16,512]{1,0:T(8,128)(2,1)S(1)}, bf16[16,512]{1,0:T(8,128)(2,1)S(1)}, u32[]{:S(2)}, u32[]{:S(2)}) collective-permute-start(bf16[16,512]{1,0:T(8,128)(2,1)S(1)} %convert_element_type.22), channel_id=1, source_target_pairs={{0,384},{128,256},{256,128},{384,0},{1,385},{129,257},{257,129},{3... | collective-permute-start | bytes 49160 | tf_op jit(solution)/shard_map/ppermute | solution.py:29
  87.4 0.0 copy-done.4
  87.4 9.3 %collective-permute-done.6 = bf16[16,512]{1,0:T(8,128)(2,1)S(1)} collective-permute-done((bf16[16,512]{1,0:T(8,128)(2,1)S(1)}, bf16[16,512]{1,0:T(8,128)(2,1)S(1)}, u32[]{:S(2)}, u32[]{:S(2)}) %collective-permute-start.6) | collective-permute-done | bytes 16416 | tf_op jit(solution)/shard_map/ppermute | solution.py:29
  96.7 0.0 collective-permute-done.7
  96.8 0.0 collective-permute-done.8
  96.8 0.6 add_multiply_fusion
  97.4 10.8 %all-to-all-done.2.back_ref = bf16[64,8,1152]{2,1,0:T(8,128)(2,1)S(1)} async-done(((bf16[64,8,1152]{2,1,0:T(8,128)(2,1)}), bf16[64,8,1152]{2,1,0:T(8,128)(2,1)S(1)}, u32[]{:S(2)}, u32[]{:S(2)}) %all-to-all-start.2) | async-done | bytes 1179680 | tf_op jit(solution)/shard_map/all_to_all | solution.py:226
  108.2 0.0 copy-done.1
  108.2 1.7 %shard_map.108 = (bf16[8,8192]{1,0:T(8,128)(2,1)}, f32[16,16]{1,0:T(8,128)}, f32[1,16]{1,0:T(1,128)}) custom-call(s32[3]{0:T(128)S(1)} %pad_add_fusion.1.place_ref, bf16[64,8,1152]{2,1,0:T(8,128)(2,1)S(1)} %all-to-all-done.2.back_ref, bf16[8,128]{1,0:T(8,128)(2,1)S(1)} %get-tuple-element.13.scaled_ref, bf16[16,8192]{1,0:T(8,128)(2,1)S(1)} %bitcast.25, ...), custom_call_target="tpu_custom_call" | custom-call | flops 2097152 | bytes 2097152 | tf_op jit(solution)/shard_map/pallas_call | solution.py:230
  (7 shorter events, 0.1 us)
Async XLA Ops:
  0.6 4.5 %copy-start = (bf16[16,512]{1,0:T(8,128)(2,1)S(1)}, bf16[16,512]{1,0:T(8,128)(2,1)}, u32[]{:S(2)}) copy-start(bf16[16,512]{1,0:T(8,128)(2,1)} %param.11) | copy-start | bytes 49156
  0.6 21.6 %copy-start.3 = (bf16[8,8192]{1,0:T(8,128)(2,1)S(1)}, bf16[8,8192]{1,0:T(8,128)(2,1)}, u32[]{:S(2)}) copy-start(bf16[8,8192]{1,0:T(8,128)(2,1)} %param.7) | copy-start | bytes 393220
  0.7 33.3 %copy-start.2 = (bf16[256,512]{1,0:T(8,128)(2,1)S(1)}, bf16[256,512]{1,0:T(8,128)(2,1)}, u32[]{:S(2)}) copy-start(bf16[256,512]{1,0:T(8,128)(2,1)} %weight_any.1) | copy-start | bytes 786436
  1.6 14.4 %collective-permute-start = (bf16[256,512]{1,0:T(8,128)(2,1)}, bf16[256,512]{1,0:T(8,128)(2,1)S(1)}, u32[]{:S(2)}, u32[]{:S(2)}) collective-permute-start(bf16[256,512]{1,0:T(8,128)(2,1)} %weight_any.1), channel_id=1, source_target_pairs={{0,1},{1,0},{2,3},{3,2},{4,5},{5,4},{6,7},{7,6},{8,9},{9,8},{10,11... | collective-permute-start | bytes 786440 | tf_op jit(solution)/shard_map/ppermute | solution.py:29
  7.2 26.7 %all-to-all-start = ((f32[16,8,128]{2,1,0:T(8,128)}), f32[16,8,128]{2,1,0:T(8,128)S(1)}, u32[]{:S(2)}, u32[]{:S(2)}) async-start(f32[16,8,128]{2,1,0:T(8,128)} %pad_add_fusion.sent_ref), calls=%async_computation | async-start | bytes 131072 | tf_op jit(solution)/shard_map/all_to_all | solution.py:194
  16.0 11.8 %collective-permute-start.1 = (bf16[128,512]{1,0:T(8,128)(2,1)S(1)}, bf16[128,512]{1,0:T(8,128)(2,1)S(1)}, u32[]{:S(2)}, u32[]{:S(2)}) collective-permute-start(bf16[128,512]{1,0:T(8,128)(2,1)S(1)} %shard_map.102.cot_ref), channel_id=1, source_target_pairs={{0,128},{128,0},{256,384},{384,256},{1,129},{129,1},{257,385},{385... | collective-permute-start | bytes 393224 | tf_op jit(solution)/shard_map/ppermute | solution.py:29
  27.9 16.7 %collective-permute-start.3 = (bf16[2,128,512]{2,1,0:T(8,128)(2,1)S(1)}, bf16[2,128,512]{2,1,0:T(8,128)(2,1)S(1)}, u32[]{:S(2)}, u32[]{:S(2)}) collective-permute-start(bf16[2,128,512]{2,1,0:T(8,128)(2,1)S(1)} %pad_maximum_fusion.near_ref), channel_id=1, source_target_pairs={{0,384},{128,256},{256,128},{384,0},{1,385},{129,257},{257,129},{3... | collective-permute-start | bytes 786440 | tf_op jit(solution)/shard_map/ppermute | solution.py:29
  36.0 19.1 %all-to-all-start.1 = ((bf16[4,320,512]{2,1,0:T(8,128)(2,1)}), bf16[4,320,512]{2,1,0:T(8,128)(2,1)S(1)}, u32[]{:S(2)}, u32[]{:S(2)}) async-start(bf16[4,320,512]{2,1,0:T(8,128)(2,1)} %get-tuple-element.11), calls=%async_computation.1 | async-start | bytes 2621440 | tf_op jit(solution)/shard_map/all_to_all | solution.py:213
  40.8 11.0 %collective-permute-start.2 = (bf16[2,128,512]{2,1,0:T(8,128)(2,1)S(1)}, bf16[2,128,512]{2,1,0:T(8,128)(2,1)S(1)}, u32[]{:S(2)}, u32[]{:S(2)}) collective-permute-start(bf16[2,128,512]{2,1,0:T(8,128)(2,1)S(1)} %pad_maximum_fusion.near_ref), channel_id=1, source_target_pairs={{0,1},{1,0},{2,3},{3,2},{4,5},{5,4},{6,7},{7,6},{8,9},{9,8},{10,11... | collective-permute-start | bytes 786440 | tf_op jit(solution)/shard_map/ppermute | solution.py:29
  44.6 10.1 %collective-permute-start.4 = (bf16[2,128,512]{2,1,0:T(8,128)(2,1)S(1)}, bf16[2,128,512]{2,1,0:T(8,128)(2,1)S(1)}, u32[]{:S(2)}, u32[]{:S(2)}) collective-permute-start(bf16[2,128,512]{2,1,0:T(8,128)(2,1)S(1)} %shard_map.104.last_ref), channel_id=1, source_target_pairs={{0,1},{1,0},{2,3},{3,2},{4,5},{5,4},{6,7},{7,6},{8,9},{9,8},{10,11... | collective-permute-start | bytes 786440 | tf_op jit(solution)/shard_map/ppermute | solution.py:29
  55.1 4.9 %collective-permute-start.5 = (bf16[4,320,512]{2,1,0:T(8,128)(2,1)S(1)}, bf16[4,320,512]{2,1,0:T(8,128)(2,1)S(1)}, u32[]{:S(2)}, u32[]{:S(2)}) collective-permute-start(bf16[4,320,512]{2,1,0:T(8,128)(2,1)S(1)} %shard_map.105.own_ref), channel_id=1, source_target_pairs={{0,16},{16,0},{1,17},{17,1},{2,18},{18,2},{3,19},{19,3},{4,20},{20... | collective-permute-start | bytes 3932168 | tf_op jit(solution)/shard_map/ppermute | solution.py:29
  62.5 24.9 %copy-start.4 = (s32[16]{0:T(128)S(1)}, s32[16]{0:T(128)}, u32[]{:S(2)}) copy-start(s32[16]{0:T(128)} %param.13) | copy-start | bytes 196
  62.5 45.7 %copy-start.1 = (bf16[8192,16]{0,1:T(8,128)(2,1)S(1)}, bf16[8192,16]{0,1:T(8,128)(2,1)}, u32[]{:S(2)}) copy-start(bf16[8192,16]{0,1:T(8,128)(2,1)} %param.10) | copy-start | bytes 786436
  62.5 45.7 %all-to-all-start.2 = ((bf16[64,8,1152]{2,1,0:T(8,128)(2,1)}), bf16[64,8,1152]{2,1,0:T(8,128)(2,1)S(1)}, u32[]{:S(2)}, u32[]{:S(2)}) async-start(bf16[64,8,1152]{2,1,0:T(8,128)(2,1)} %bitcast.10), calls=%async_computation.2 | async-start | bytes 2359296 | tf_op jit(solution)/shard_map/all_to_all | solution.py:226
  75.1 21.6 %collective-permute-start.6 = (bf16[16,512]{1,0:T(8,128)(2,1)S(1)}, bf16[16,512]{1,0:T(8,128)(2,1)S(1)}, u32[]{:S(2)}, u32[]{:S(2)}) collective-permute-start(bf16[16,512]{1,0:T(8,128)(2,1)S(1)} %convert_element_type.22), channel_id=1, source_target_pairs={{0,128},{128,0},{256,384},{384,256},{1,129},{129,1},{257,385},{385... | collective-permute-start | bytes 49160 | tf_op jit(solution)/shard_map/ppermute | solution.py:29
  79.5 17.2 %collective-permute-start.7 = (bf16[16,512]{1,0:T(8,128)(2,1)S(1)}, bf16[16,512]{1,0:T(8,128)(2,1)S(1)}, u32[]{:S(2)}, u32[]{:S(2)}) collective-permute-start(bf16[16,512]{1,0:T(8,128)(2,1)S(1)} %convert_element_type.22), channel_id=1, source_target_pairs={{0,256},{128,384},{256,0},{384,128},{1,257},{129,385},{257,1},{385... | collective-permute-start | bytes 49160 | tf_op jit(solution)/shard_map/ppermute | solution.py:29
  85.2 11.5 %collective-permute-start.8 = (bf16[16,512]{1,0:T(8,128)(2,1)S(1)}, bf16[16,512]{1,0:T(8,128)(2,1)S(1)}, u32[]{:S(2)}, u32[]{:S(2)}) collective-permute-start(bf16[16,512]{1,0:T(8,128)(2,1)S(1)} %convert_element_type.22), channel_id=1, source_target_pairs={{0,384},{128,256},{256,128},{384,0},{1,385},{129,257},{257,129},{3... | collective-permute-start | bytes 49160 | tf_op jit(solution)/shard_map/ppermute | solution.py:29

commit v12 on v11

--- a/solution.py
+++ b/solution.py
@@ -52,8 +52,9 @@
     )(a, *others)
 
 
-def copy_kernel(in_ref, out_ref):
-    out_ref[...] = in_ref[...]
+def stack_kernel(first_ref, second_ref, out_ref):
+    out_ref[0] = first_ref[...]
+    out_ref[1] = second_ref[...]
 
 
 def rows_of(first_ref, last_ref):
@@ -194,10 +195,7 @@
     rank_in = lax.all_to_all(rank_out, ("zl", "yh", "yl"), 0, 0)
 
     cot = after(cotangent, got)
-    near = jnp.stack([cot, swap(cot, "zh", 4, 1)])
-    far = swap(near, "yl", 2, 1)
-    last = call(copy_kernel, shape((2, 128, 512), bf16), [in_vmem], 30 << 30, 1 << 20)(swap(near, "zh", 4, 3))
-    far_last = swap(last, "yl", 2, 1)
+    first, third = swap(cot, "zh", 4, 1), swap(cot, "zh", 4, 3)
 
     coeff_lanes = jnp.pad(jnp.concatenate([coeff, coeff]), (0, 96)).reshape(1, 128)
     slices = inputs.reshape(8, 4, 4, 512).transpose(2, 1, 0, 3).reshape(4, 32, 512)
@@ -210,6 +208,13 @@
         out_specs=(in_hbm, in_vmem),
         scratch=[pltpu.VMEM((32, 512), bf16), dma((16,))],
     )(place, rank_out, rank_in, coeff_lanes, cot, weight, got, slices)
+    first = after(first, scaled_back)
+    near = call(stack_kernel, shape((2, 128, 512), bf16), [in_vmem] * 2, 30 << 30, 1 << 20)(cot, first)
+    far = swap(near, "yl", 2, 1)
+    last = call(stack_kernel, shape((2, 128, 512), bf16), [in_vmem] * 2, 30 << 30, 1 << 20)(
+        third, swap(first, "zh", 4, 3)
+    )
+    far_last = swap(last, "yl", 2, 1)
     x_in = after(lax.all_to_all(x_out, "x", 0, 0), far, far_last)
     x_other = swap(x_in, "c", 2, 1)
 

time: 112 us -> 109 us (0.973); the launches traced: 110 us -> 108 us
  waiting for transfers between devices: 35.7 us -> 29.5 us
  starting transfers between devices: 61.7 us -> 65.3 us
    ppermute x9 -> x10, waiting for transfers between devices: 24.5 us -> 18.7 us  [swap(): return lax.ppermute(a, axis, [(i, i ^ mask) for i in range(count)])]
    ppermute x9 -> x10, starting transfers between devices: 36.2 us -> 41.2 us  [swap(): return lax.ppermute(a, axis, [(i, i ^ mask) for i in range(count)])]
    all_to_all x1, starting transfers between devices: 12.6 us -> 11.2 us  [body(): lax.all_to_all(out.reshape(64, 8, 1152), ('zh', 'zl', 'yh', 'yl'), 0, 0)]
  transfers between devices with their start and end apart: 12 -> 13, of which waited for: 7 -> 6; matrix products, arithmetic and copies ran while one was open for 3% -> 4% of each run, Pallas kernels for 3% -> 3%
where the time goes in v12:
time: 109 us; the launch traced here: 108 us
  starting transfers between devices  65.3 us (60%)
  waiting for transfers between devices  29.5 us (27%)
  Pallas kernels  7.1 us (7%)
  other arithmetic  2.13 us (2%)
  local copies, waits for them, and re-layouts  1.96 us (2%)
  matrix products  1.37 us (1%)
    ppermute x10, starting transfers between devices, swap(): return lax.ppermute(a, axis, [(i, i ^ mask) for i in range(count)])  41.2 us
    ppermute x10, waiting for transfers between devices, swap(): return lax.ppermute(a, axis, [(i, i ^ mask) for i in range(count)])  18.7 us
    all_to_all x1, starting transfers between devices, body(): lax.all_to_all(out.reshape(64, 8, 1152), ('zh', 'zl', 'yh', 'yl'), 0, 0)  11.2 us
    all_to_all x1, waiting for transfers between devices, body(): lax.all_to_all(out.reshape(64, 8, 1152), ('zh', 'zl', 'yh', 'yl'), 0, 0)  10.9 us
    all_to_all x1, starting transfers between devices, body(): rank_in = lax.all_to_all(rank_out, ('zl', 'yh', 'yl'), 0, 0)  8.11 us
    all_to_all x1, starting transfers between devices, body(): x_in = after(lax.all_to_all(x_out, 'x', 0, 0), far, far_last)  4.78 us
    pallas_call x1, Pallas kernels, body(): call(other_kernel, (shape((4, 128, 1152), bf16), shape((16, 512), f32)),...  2.53 us
  transfers between devices with their start and end apart: 13, of which 6 were waited for; matrix products, arithmetic and copies ran while one was open for 4% of the time, Pallas kernels for 3%

profile of v12, /device:TPU:6, one launch (start us, length us, event | category | flops | bytes accessed | tf_op | source)
XLA Modules:
  0.0 108.2 jit_solution(14588989478790904179)
XLA Ops:
  0.6 0.0 copy-start
  0.6 0.0 copy-start.2
  0.7 0.9 copy.23.refs_0_
  1.6 3.5 %collective-permute-start = (bf16[256,512]{1,0:T(8,128)(2,1)}, bf16[256,512]{1,0:T(8,128)(2,1)S(1)}, u32[]{:S(2)}, u32[]{:S(2)}) collective-permute-start(bf16[256,512]{1,0:T(8,128)(2,1)} %weight_any.1), channel_id=1, source_target_pairs={{0,1},{1,0},{2,3},{3,2},{4,5},{5,4},{6,7},{7,6},{8,9},{9,8},{10,11... | collective-permute-start | bytes 786440 | tf_op jit(solution)/shard_map/ppermute | solution.py:29
  5.1 0.0 copy-done
  5.1 0.2 convolution_bitcast_fusion
  5.3 1.2 %fusion.2 = f32[8,16]{1,0:T(8,128)S(1)} fusion(bf16[8,8192]{1,0:T(8,128)(2,1)} %param.7, bf16[8192,16]{0,1:T(8,128)(2,1)} %param.10), kind=kOutput, calls=%fused_computation.11 | convolution fusion | flops 2097152 | bytes 393728 | tf_op jit(solution)/shard_map/dot_general | solution.py:193
  6.5 0.1 pad.13
  6.5 0.7 pad_add_fusion.sent_ref
  7.2 8.1 %all-to-all-start = ((f32[16,8,128]{2,1,0:T(8,128)}), f32[16,8,128]{2,1,0:T(8,128)S(1)}, u32[]{:S(2)}, u32[]{:S(2)}) async-start(f32[16,8,128]{2,1,0:T(8,128)} %pad_add_fusion.sent_ref), calls=%async_computation | async-start | bytes 131072 | tf_op jit(solution)/shard_map/all_to_all | solution.py:195
  15.3 0.7 convert_multiply_fusion
  16.0 0.1 fusion.1.coeff_ref
  16.1 0.9 copy.18
  17.0 0.1 pad_add_fusion.1.place_ref
  17.1 0.0 collective-permute-done.refs_1_.got_any
  17.1 6.1 %collective-permute-start.1 = (bf16[128,512]{1,0:T(8,128)(2,1)S(1)}, bf16[128,512]{1,0:T(8,128)(2,1)S(1)}, u32[]{:S(2)}, u32[]{:S(2)}) collective-permute-start(bf16[128,512]{1,0:T(8,128)(2,1)S(1)} %shard_map.102.cot_ref.first_ref), channel_id=1, source_target_pairs={{0,128},{128,0},{256,384},{384,256},{1,129},{129,1},{257,385},{385... | collective-permute-start | bytes 393224 | tf_op jit(solution)/shard_map/ppermute | solution.py:29
  23.2 6.4 %collective-permute-start.3 = (bf16[128,512]{1,0:T(8,128)(2,1)S(1)}, bf16[128,512]{1,0:T(8,128)(2,1)S(1)}, u32[]{:S(2)}, u32[]{:S(2)}) collective-permute-start(bf16[128,512]{1,0:T(8,128)(2,1)S(1)} %shard_map.102.cot_ref.first_ref), channel_id=1, source_target_pairs={{0,384},{128,256},{256,128},{384,0},{1,385},{129,257},{257,129},{3... | collective-permute-start | bytes 393224 | tf_op jit(solution)/shard_map/ppermute | solution.py:29
  29.6 0.0 all-to-all-done.rank_ref
  29.6 0.0 copy-done.2
  29.6 2.1 %shard_map.103 = (bf16[4,320,512]{2,1,0:T(8,128)(2,1)}, bf16[8,128]{1,0:T(8,128)(2,1)S(1)}) custom-call(s32[3]{0:T(128)S(1)} %pad_add_fusion.1.place_ref, f32[16,8,128]{2,1,0:T(8,128)} %pad_add_fusion.sent_ref, f32[16,8,128]{2,1,0:T(8,128)S(1)} %all-to-all-done.rank_ref, f32[1,128]{1,0:T(1,128)S(1)} %fusion.1.coeff_ref, ...), custom_call_target="tpu_custom_call" | custom-call | flops 32212254720 | bytes 3145728 | tf_op jit(solution)/shard_map/pallas_call | solution.py:202
  31.7 4.8 %all-to-all-start.1 = ((bf16[4,320,512]{2,1,0:T(8,128)(2,1)}), bf16[4,320,512]{2,1,0:T(8,128)(2,1)S(1)}, u32[]{:S(2)}, u32[]{:S(2)}) async-start(bf16[4,320,512]{2,1,0:T(8,128)(2,1)} %get-tuple-element.11), calls=%async_computation.1 | async-start | bytes 2621440 | tf_op jit(solution)/shard_map/all_to_all | solution.py:218
  36.5 0.0 collective-permute-done.1.refs_0_
  36.5 4.4 %collective-permute-start.4 = (bf16[128,512]{1,0:T(8,128)(2,1)S(1)}, bf16[128,512]{1,0:T(8,128)(2,1)S(1)}, u32[]{:S(2)}, u32[]{:S(2)}) collective-permute-start(bf16[128,512]{1,0:T(8,128)(2,1)S(1)} %shard_map.104.second_ref), channel_id=1, source_target_pairs={{0,384},{128,256},{256,128},{384,0},{1,385},{129,257},{257,129},{3... | collective-permute-start | bytes 393224 | tf_op jit(solution)/shard_map/ppermute | solution.py:29
  40.9 2.9 %collective-permute-start.2 = (bf16[2,128,512]{2,1,0:T(8,128)(2,1)S(1)}, bf16[2,128,512]{2,1,0:T(8,128)(2,1)S(1)}, u32[]{:S(2)}, u32[]{:S(2)}) collective-permute-start(bf16[2,128,512]{2,1,0:T(8,128)(2,1)S(1)} %shard_map.105.near_ref), channel_id=1, source_target_pairs={{0,1},{1,0},{2,3},{3,2},{4,5},{5,4},{6,7},{7,6},{8,9},{9,8},{10,11... | collective-permute-start | bytes 786440 | tf_op jit(solution)/shard_map/ppermute | solution.py:29
  43.8 0.0 collective-permute-done.3.first_ref
  43.8 1.7 %collective-permute-done.4.second_ref = bf16[128,512]{1,0:T(8,128)(2,1)S(1)} collective-permute-done((bf16[128,512]{1,0:T(8,128)(2,1)S(1)}, bf16[128,512]{1,0:T(8,128)(2,1)S(1)}, u32[]{:S(2)}, u32[]{:S(2)}) %collective-permute-start.4) | collective-permute-done | bytes 131104 | tf_op jit(solution)/shard_map/ppermute | solution.py:29
  45.5 3.8 %collective-permute-start.5 = (bf16[2,128,512]{2,1,0:T(8,128)(2,1)S(1)}, bf16[2,128,512]{2,1,0:T(8,128)(2,1)S(1)}, u32[]{:S(2)}, u32[]{:S(2)}) collective-permute-start(bf16[2,128,512]{2,1,0:T(8,128)(2,1)S(1)} %shard_map.106.last_ref), channel_id=1, source_target_pairs={{0,1},{1,0},{2,3},{3,2},{4,5},{5,4},{6,7},{7,6},{8,9},{9,8},{10,11... | collective-permute-start | bytes 786440 | tf_op jit(solution)/shard_map/ppermute | solution.py:29
  49.4 1.9 %collective-permute-done.2.refs_1_.far_ref = bf16[2,128,512]{2,1,0:T(8,128)(2,1)S(1)} collective-permute-done((bf16[2,128,512]{2,1,0:T(8,128)(2,1)S(1)}, bf16[2,128,512]{2,1,0:T(8,128)(2,1)S(1)}, u32[]{:S(2)}, u32[]{:S(2)}) %collective-permute-start.2) | collective-permute-done | bytes 262176 | tf_op jit(solution)/shard_map/ppermute | solution.py:29
  51.3 3.5 %collective-permute-done.5.refs_2_.far_last_ref = bf16[2,128,512]{2,1,0:T(8,128)(2,1)S(1)} collective-permute-done((bf16[2,128,512]{2,1,0:T(8,128)(2,1)S(1)}, bf16[2,128,512]{2,1,0:T(8,128)(2,1)S(1)}, u32[]{:S(2)}, u32[]{:S(2)}) %collective-permute-start.5) | collective-permute-done | bytes 262176 | tf_op jit(solution)/shard_map/ppermute | solution.py:29
  54.8 0.0 all-to-all-done.1.refs_0_
  54.8 1.9 %collective-permute-start.6 = (bf16[4,320,512]{2,1,0:T(8,128)(2,1)S(1)}, bf16[4,320,512]{2,1,0:T(8,128)(2,1)S(1)}, u32[]{:S(2)}, u32[]{:S(2)}) collective-permute-start(bf16[4,320,512]{2,1,0:T(8,128)(2,1)S(1)} %shard_map.107.own_ref), channel_id=1, source_target_pairs={{0,16},{16,0},{1,17},{17,1},{2,18},{18,2},{3,19},{19,3},{4,20},{20... | collective-permute-start | bytes 3932168 | tf_op jit(solution)/shard_map/ppermute | solution.py:29
  56.7 0.7 shard_map.108.done_ref
  57.4 2.3 %collective-permute-done.6.other_ref = bf16[4,320,512]{2,1,0:T(8,128)(2,1)S(1)} collective-permute-done((bf16[4,320,512]{2,1,0:T(8,128)(2,1)S(1)}, bf16[4,320,512]{2,1,0:T(8,128)(2,1)S(1)}, u32[]{:S(2)}, u32[]{:S(2)}) %collective-permute-start.6) | collective-permute-done | bytes 1310752 | tf_op jit(solution)/shard_map/ppermute | solution.py:29
  59.7 2.5 %shard_map.109 = (bf16[4,128,1152]{2,1,0:T(8,128)(2,1)}, f32[16,512]{1,0:T(8,128)S(1)}) custom-call(s32[3]{0:T(128)S(1)} %pad_add_fusion.1.place_ref, bf16[4,128,512]{2,1,0:T(8,128)(2,1)S(1)} %shard_map.108.done_ref, bf16[4,320,512]{2,1,0:T(8,128)(2,1)S(1)} %shard_map.107.own_ref, bf16[4,320,512]{2,1,0:T(8,128)(2,1)S(1)} %collective-permute-done.6.other_ref, ...), custom_call_target="tpu_custom_call" | custom-call | flops 536870912 | bytes 5242880 | tf_op jit(solution)/shard_map/pallas_call | solution.py:224
  62.2 0.0 copy-start.3
  62.2 0.0 copy-start.1
  62.2 11.2 %all-to-all-start.2 = ((bf16[64,8,1152]{2,1,0:T(8,128)(2,1)}), bf16[64,8,1152]{2,1,0:T(8,128)(2,1)S(1)}, u32[]{:S(2)}, u32[]{:S(2)}) async-start(bf16[64,8,1152]{2,1,0:T(8,128)(2,1)} %bitcast.8), calls=%async_computation.2 | async-start | bytes 2359296 | tf_op jit(solution)/shard_map/all_to_all | solution.py:231
  73.4 4.4 %collective-permute-start.7 = (bf16[16,512]{1,0:T(8,128)(2,1)S(1)}, bf16[16,512]{1,0:T(8,128)(2,1)S(1)}, u32[]{:S(2)}, u32[]{:S(2)}) collective-permute-start(bf16[16,512]{1,0:T(8,128)(2,1)S(1)} %convert_element_type.22), channel_id=1, source_target_pairs={{0,128},{128,0},{256,384},{384,256},{1,129},{129,1},{257,385},{385... | collective-permute-start | bytes 49160 | tf_op jit(solution)/shard_map/ppermute | solution.py:29
  77.8 5.7 %collective-permute-start.8 = (bf16[16,512]{1,0:T(8,128)(2,1)S(1)}, bf16[16,512]{1,0:T(8,128)(2,1)S(1)}, u32[]{:S(2)}, u32[]{:S(2)}) collective-permute-start(bf16[16,512]{1,0:T(8,128)(2,1)S(1)} %convert_element_type.22), channel_id=1, source_target_pairs={{0,256},{128,384},{256,0},{384,128},{1,257},{129,385},{257,1},{385... | collective-permute-start | bytes 49160 | tf_op jit(solution)/shard_map/ppermute | solution.py:29
  83.5 2.2 %collective-permute-start.9 = (bf16[16,512]{1,0:T(8,128)(2,1)S(1)}, bf16[16,512]{1,0:T(8,128)(2,1)S(1)}, u32[]{:S(2)}, u32[]{:S(2)}) collective-permute-start(bf16[16,512]{1,0:T(8,128)(2,1)S(1)} %convert_element_type.22), channel_id=1, source_target_pairs={{0,384},{128,256},{256,128},{384,0},{1,385},{129,257},{257,129},{3... | collective-permute-start | bytes 49160 | tf_op jit(solution)/shard_map/ppermute | solution.py:29
  85.6 0.0 copy-done.3
  85.7 9.3 %collective-permute-done.7 = bf16[16,512]{1,0:T(8,128)(2,1)S(1)} collective-permute-done((bf16[16,512]{1,0:T(8,128)(2,1)S(1)}, bf16[16,512]{1,0:T(8,128)(2,1)S(1)}, u32[]{:S(2)}, u32[]{:S(2)}) %collective-permute-start.7) | collective-permute-done | bytes 16416 | tf_op jit(solution)/shard_map/ppermute | solution.py:29
  95.0 0.0 collective-permute-done.8
  95.0 0.0 collective-permute-done.9
  95.0 0.6 add_multiply_fusion
  95.6 10.9 %all-to-all-done.2.back_ref = bf16[64,8,1152]{2,1,0:T(8,128)(2,1)S(1)} async-done(((bf16[64,8,1152]{2,1,0:T(8,128)(2,1)}), bf16[64,8,1152]{2,1,0:T(8,128)(2,1)S(1)}, u32[]{:S(2)}, u32[]{:S(2)}) %all-to-all-start.2) | async-done | bytes 1179680 | tf_op jit(solution)/shard_map/all_to_all | solution.py:231
  106.5 0.0 copy-done.1
  106.5 1.7 %shard_map.110 = (bf16[8,8192]{1,0:T(8,128)(2,1)}, f32[16,16]{1,0:T(8,128)}, f32[1,16]{1,0:T(1,128)}) custom-call(s32[3]{0:T(128)S(1)} %pad_add_fusion.1.place_ref, bf16[64,8,1152]{2,1,0:T(8,128)(2,1)S(1)} %all-to-all-done.2.back_ref, bf16[8,128]{1,0:T(8,128)(2,1)S(1)} %get-tuple-element.12.refs_1_.scaled_ref, bf16[16,8192]{1,0:T(8,128)(2,1)S(1)} %bitcast.22, ...), custom_call_target="tpu_custom_call" | custom-call | flops 2097152 | bytes 2097152 | tf_op jit(solution)/shard_map/pallas_call | solution.py:235
  (7 shorter events, 0.0 us)
Async XLA Ops:
  0.6 4.5 %copy-start = (bf16[16,512]{1,0:T(8,128)(2,1)S(1)}, bf16[16,512]{1,0:T(8,128)(2,1)}, u32[]{:S(2)}) copy-start(bf16[16,512]{1,0:T(8,128)(2,1)} %param.11) | copy-start | bytes 49156
  0.6 28.9 %copy-start.2 = (bf16[256,512]{1,0:T(8,128)(2,1)S(1)}, bf16[256,512]{1,0:T(8,128)(2,1)}, u32[]{:S(2)}) copy-start(bf16[256,512]{1,0:T(8,128)(2,1)} %weight_any.1) | copy-start | bytes 786436
  1.6 15.5 %collective-permute-start = (bf16[256,512]{1,0:T(8,128)(2,1)}, bf16[256,512]{1,0:T(8,128)(2,1)S(1)}, u32[]{:S(2)}, u32[]{:S(2)}) collective-permute-start(bf16[256,512]{1,0:T(8,128)(2,1)} %weight_any.1), channel_id=1, source_target_pairs={{0,1},{1,0},{2,3},{3,2},{4,5},{5,4},{6,7},{7,6},{8,9},{9,8},{10,11... | collective-permute-start | bytes 786440 | tf_op jit(solution)/shard_map/ppermute | solution.py:29
  7.2 22.4 %all-to-all-start = ((f32[16,8,128]{2,1,0:T(8,128)}), f32[16,8,128]{2,1,0:T(8,128)S(1)}, u32[]{:S(2)}, u32[]{:S(2)}) async-start(f32[16,8,128]{2,1,0:T(8,128)} %pad_add_fusion.sent_ref), calls=%async_computation | async-start | bytes 131072 | tf_op jit(solution)/shard_map/all_to_all | solution.py:195
  17.1 19.4 %collective-permute-start.1 = (bf16[128,512]{1,0:T(8,128)(2,1)S(1)}, bf16[128,512]{1,0:T(8,128)(2,1)S(1)}, u32[]{:S(2)}, u32[]{:S(2)}) collective-permute-start(bf16[128,512]{1,0:T(8,128)(2,1)S(1)} %shard_map.102.cot_ref.first_ref), channel_id=1, source_target_pairs={{0,128},{128,0},{256,384},{384,256},{1,129},{129,1},{257,385},{385... | collective-permute-start | bytes 393224 | tf_op jit(solution)/shard_map/ppermute | solution.py:29
  23.2 20.6 %collective-permute-start.3 = (bf16[128,512]{1,0:T(8,128)(2,1)S(1)}, bf16[128,512]{1,0:T(8,128)(2,1)S(1)}, u32[]{:S(2)}, u32[]{:S(2)}) collective-permute-start(bf16[128,512]{1,0:T(8,128)(2,1)S(1)} %shard_map.102.cot_ref.first_ref), channel_id=1, source_target_pairs={{0,384},{128,256},{256,128},{384,0},{1,385},{129,257},{257,129},{3... | collective-permute-start | bytes 393224 | tf_op jit(solution)/shard_map/ppermute | solution.py:29
  31.7 23.1 %all-to-all-start.1 = ((bf16[4,320,512]{2,1,0:T(8,128)(2,1)}), bf16[4,320,512]{2,1,0:T(8,128)(2,1)S(1)}, u32[]{:S(2)}, u32[]{:S(2)}) async-start(bf16[4,320,512]{2,1,0:T(8,128)(2,1)} %get-tuple-element.11), calls=%async_computation.1 | async-start | bytes 2621440 | tf_op jit(solution)/shard_map/all_to_all | solution.py:218
  36.5 9.1 %collective-permute-start.4 = (bf16[128,512]{1,0:T(8,128)(2,1)S(1)}, bf16[128,512]{1,0:T(8,128)(2,1)S(1)}, u32[]{:S(2)}, u32[]{:S(2)}) collective-permute-start(bf16[128,512]{1,0:T(8,128)(2,1)S(1)} %shard_map.104.second_ref), channel_id=1, source_target_pairs={{0,384},{128,256},{256,128},{384,0},{1,385},{129,257},{257,129},{3... | collective-permute-start | bytes 393224 | tf_op jit(solution)/shard_map/ppermute | solution.py:29
  40.9 10.4 %collective-permute-start.2 = (bf16[2,128,512]{2,1,0:T(8,128)(2,1)S(1)}, bf16[2,128,512]{2,1,0:T(8,128)(2,1)S(1)}, u32[]{:S(2)}, u32[]{:S(2)}) collective-permute-start(bf16[2,128,512]{2,1,0:T(8,128)(2,1)S(1)} %shard_map.105.near_ref), channel_id=1, source_target_pairs={{0,1},{1,0},{2,3},{3,2},{4,5},{5,4},{6,7},{7,6},{8,9},{9,8},{10,11... | collective-permute-start | bytes 786440 | tf_op jit(solution)/shard_map/ppermute | solution.py:29
  45.5 9.2 %collective-permute-start.5 = (bf16[2,128,512]{2,1,0:T(8,128)(2,1)S(1)}, bf16[2,128,512]{2,1,0:T(8,128)(2,1)S(1)}, u32[]{:S(2)}, u32[]{:S(2)}) collective-permute-start(bf16[2,128,512]{2,1,0:T(8,128)(2,1)S(1)} %shard_map.106.last_ref), channel_id=1, source_target_pairs={{0,1},{1,0},{2,3},{3,2},{4,5},{5,4},{6,7},{7,6},{8,9},{9,8},{10,11... | collective-permute-start | bytes 786440 | tf_op jit(solution)/shard_map/ppermute | solution.py:29
  54.8 4.9 %collective-permute-start.6 = (bf16[4,320,512]{2,1,0:T(8,128)(2,1)S(1)}, bf16[4,320,512]{2,1,0:T(8,128)(2,1)S(1)}, u32[]{:S(2)}, u32[]{:S(2)}) collective-permute-start(bf16[4,320,512]{2,1,0:T(8,128)(2,1)S(1)} %shard_map.107.own_ref), channel_id=1, source_target_pairs={{0,16},{16,0},{1,17},{17,1},{2,18},{18,2},{3,19},{19,3},{4,20},{20... | collective-permute-start | bytes 3932168 | tf_op jit(solution)/shard_map/ppermute | solution.py:29
  62.2 23.4 %copy-start.3 = (s32[16]{0:T(128)S(1)}, s32[16]{0:T(128)}, u32[]{:S(2)}) copy-start(s32[16]{0:T(128)} %param.13) | copy-start | bytes 196
  62.2 44.3 %copy-start.1 = (bf16[8192,16]{0,1:T(8,128)(2,1)S(1)}, bf16[8192,16]{0,1:T(8,128)(2,1)}, u32[]{:S(2)}) copy-start(bf16[8192,16]{0,1:T(8,128)(2,1)} %param.10) | copy-start | bytes 786436
  62.2 44.3 %all-to-all-start.2 = ((bf16[64,8,1152]{2,1,0:T(8,128)(2,1)}), bf16[64,8,1152]{2,1,0:T(8,128)(2,1)S(1)}, u32[]{:S(2)}, u32[]{:S(2)}) async-start(bf16[64,8,1152]{2,1,0:T(8,128)(2,1)} %bitcast.8), calls=%async_computation.2 | async-start | bytes 2359296 | tf_op jit(solution)/shard_map/all_to_all | solution.py:231
  73.4 21.6 %collective-permute-start.7 = (bf16[16,512]{1,0:T(8,128)(2,1)S(1)}, bf16[16,512]{1,0:T(8,128)(2,1)S(1)}, u32[]{:S(2)}, u32[]{:S(2)}) collective-permute-start(bf16[16,512]{1,0:T(8,128)(2,1)S(1)} %convert_element_type.22), channel_id=1, source_target_pairs={{0,128},{128,0},{256,384},{384,256},{1,129},{129,1},{257,385},{385... | collective-permute-start | bytes 49160 | tf_op jit(solution)/shard_map/ppermute | solution.py:29
  77.8 17.2 %collective-permute-start.8 = (bf16[16,512]{1,0:T(8,128)(2,1)S(1)}, bf16[16,512]{1,0:T(8,128)(2,1)S(1)}, u32[]{:S(2)}, u32[]{:S(2)}) collective-permute-start(bf16[16,512]{1,0:T(8,128)(2,1)S(1)} %convert_element_type.22), channel_id=1, source_target_pairs={{0,256},{128,384},{256,0},{384,128},{1,257},{129,385},{257,1},{385... | collective-permute-start | bytes 49160 | tf_op jit(solution)/shard_map/ppermute | solution.py:29
  83.5 11.5 %collective-permute-start.9 = (bf16[16,512]{1,0:T(8,128)(2,1)S(1)}, bf16[16,512]{1,0:T(8,128)(2,1)S(1)}, u32[]{:S(2)}, u32[]{:S(2)}) collective-permute-start(bf16[16,512]{1,0:T(8,128)(2,1)S(1)} %convert_element_type.22), channel_id=1, source_target_pairs={{0,384},{128,256},{256,128},{384,0},{1,385},{129,257},{257,129},{3... | collective-permute-start | bytes 49160 | tf_op jit(solution)/shard_map/ppermute | solution.py:29

commit v13 on v12

--- a/solution.py
+++ b/solution.py
@@ -52,6 +52,10 @@
     )(a, *others)
 
 
+def hold_kernel(in_ref, after_ref, out_ref):
+    out_ref[...] = in_ref[...]
+
+
 def stack_kernel(first_ref, second_ref, out_ref):
     out_ref[0] = first_ref[...]
     out_ref[1] = second_ref[...]
@@ -62,7 +66,7 @@
 
 
 def pack_kernel(
-    place_ref, sent_ref, rank_ref, coeff_ref, cot_ref, weight_any, got_any, slices_ref,
+    place_ref, singular_ref, keep_ref, sent_ref, rank_ref, cot_ref, weight_any, got_any, slices_ref,
     x_any, back_ref, rest_ref, out_sems,
 ):
     rows = pl.ds(pl.multiple_of(place_ref[1] * 128, 128), 128)
@@ -73,7 +77,10 @@
         copy.start()
     lane = lax.broadcasted_iota(jnp.int32, (1, 128), 1)
     rank = rank_ref[...]
-    coeff = coeff_ref[...]
+    coeff = jnp.zeros((1, 128), f32)
+    for r in range(16):
+        value = adapter_scale * singular_ref[r] * keep_ref[r].astype(f32)
+        coeff = jnp.where((lane == r) | (lane == 16 + r), value, coeff)
     own = jnp.where(lane < 16, jnp.sum(rank, axis=0), 0.0)
     back = (own * coeff).astype(bf16)
     back_ref[...] = back
@@ -106,41 +113,51 @@
     return total.astype(bf16).reshape(4, 128, 512)
 
 
-def own_kernel(own_ref, near_ref, last_ref, far_ref, far_last_ref, out_ref):
+def adapter_terms(ref, core):
+    tok, back, singular = [], [], jnp.zeros((1, 128), f32)
+    for x in range(4):
+        rows = ref[x, 256:288, :]
+        tok.append(jnp.where(core == 0, rows[:, :256], rows[:, 256:]))
+        small = ref[x, 288:304, :].astype(f32)
+        back.extend([small[0:8, :256]] * 4)
+        singular += small[8:9, 256:384] + small[8:9, 384:512]
+    tok = jnp.concatenate(tok, axis=0)
+    back = jnp.concatenate(back, axis=0)
+    group = lax.rem(lax.broadcasted_iota(jnp.int32, (128, 1), 0), 32) // 8
+    out = []
+    for h in range(4):
+        both = t_dot(tok, jnp.where(group == h, back, 0.0).astype(bf16))
+        a = both[:, :128].reshape(16, 2, 8, 128)[:, 0]
+        b = both[:, 128:].reshape(16, 2, 8, 128)[:, 1]
+        out.append((a + b + singular).reshape(128, 128))
+    right = sum(ref[x, 304:320, :].astype(f32) for x in range(4))
+    return out, right
+
+
+def own_kernel(
+    place_ref, own_ref, near_ref, last_ref, far_ref, far_last_ref, out_ref, terms_ref, right_ref
+):
     out_ref[...] = products((rows_of(near_ref, last_ref), rows_of(far_ref, far_last_ref)), own_ref)
+    terms, right_ref[...] = adapter_terms(own_ref, place_ref[0])
+    for h in range(4):
+        terms_ref[h] = terms[h]
 
 
 def other_kernel(
-    place_ref, done_ref, own_ref, other_ref, near_ref, last_ref, far_ref, far_last_ref, out_ref, right_ref
-):
-    core, z_high = place_ref[0], place_ref[2]
+    place_ref, done_ref, terms_ref, own_right_ref, other_ref, near_ref, last_ref, far_ref, far_last_ref,
+    out_ref, right_ref,
+):
+    z_high = place_ref[2]
     total = products((rows_of(near_ref, last_ref), rows_of(far_ref, far_last_ref)), other_ref)
     for i, k in enumerate((0, 1, 3, 2)):
         out_ref[z_high ^ k, :, 0:512] = done_ref[i]
         out_ref[z_high ^ k, :, 512:1024] = total[i]
-    tok, back, singular = [], [], jnp.zeros((1, 128), f32)
-    for ref in (own_ref, other_ref):
-        for x in range(4):
-            rows = ref[x, 256:288, :]
-            tok.append(jnp.where(core == 0, rows[:, :256], rows[:, 256:]))
-            small = ref[x, 288:304, :].astype(f32)
-            back.extend([small[0:8, :256]] * 4)
-            singular += small[8:9, 256:384] + small[8:9, 384:512]
-    tok = jnp.concatenate(tok, axis=0)
-    back = jnp.concatenate(back, axis=0)
-    group = lax.rem(lax.broadcasted_iota(jnp.int32, (256, 1), 0), 32) // 8
-    for h in range(4):
-        both = t_dot(tok, jnp.where(group == h, back, 0.0).astype(bf16))
-        a = both[:, :128].reshape(16, 2, 8, 128)[:, 0]
-        b = both[:, 128:].reshape(16, 2, 8, 128)[:, 1]
-        z = (a + b + singular).reshape(128, 128)
+    terms, right = adapter_terms(other_ref, place_ref[0])
+    right_ref[...] = own_right_ref[...] + right
+    for h in range(4):
+        z = terms_ref[h] + terms[h]
         high = z.astype(bf16).astype(f32)
         out_ref[h, :, 1024:1152] = (high + pltpu.roll(z - high, 64, 1)).astype(bf16)
-    right = jnp.zeros((16, 512), f32)
-    for ref in (own_ref, other_ref):
-        for x in range(4):
-            right += ref[x, 304:320, :].astype(f32)
-    right_ref[...] = right
 
 
 def final_kernel(
@@ -184,8 +201,6 @@
     z_high = lax.axis_index("zh")
     place = jnp.stack([core, y_low, z_high]).astype(jnp.int32)
     shape = jax.ShapeDtypeStruct
-    keep_float = keep_mask.astype(f32)
-    coeff = adapter_scale * singular * keep_float
 
     got = swap(weight, "yl", 2, 1)
 
@@ -194,20 +209,19 @@
     rank_out = jnp.pad(back_part, ((0, 0), (0, 0), (0, 112))) + jnp.pad(own_projected, ((0, 0), (16, 96)))
     rank_in = lax.all_to_all(rank_out, ("zl", "yh", "yl"), 0, 0)
 
-    cot = after(cotangent, got)
+    cot = call(hold_kernel, shape((128, 512), bf16), [in_vmem, anywhere], 1, 1 << 18)(cotangent, got)
     first, third = swap(cot, "zh", 4, 1), swap(cot, "zh", 4, 3)
 
-    coeff_lanes = jnp.pad(jnp.concatenate([coeff, coeff]), (0, 96)).reshape(1, 128)
     slices = inputs.reshape(8, 4, 4, 512).transpose(2, 1, 0, 3).reshape(4, 32, 512)
     x_out, scaled_back = call(
         pack_kernel,
         (shape((4, 320, 512), bf16), shape((8, 128), bf16)),
-        [in_smem] + [in_vmem] * 4 + [anywhere] * 2 + [in_vmem],
+        [in_smem] * 3 + [in_vmem] * 3 + [anywhere] * 2 + [in_vmem],
         30 << 30,
         3 << 20,
         out_specs=(in_hbm, in_vmem),
         scratch=[pltpu.VMEM((32, 512), bf16), dma((16,))],
-    )(place, rank_out, rank_in, coeff_lanes, cot, weight, got, slices)
+    )(place, singular, keep_mask, rank_out, rank_in, cot, weight, got, slices)
     first = after(first, scaled_back)
     near = call(stack_kernel, shape((2, 128, 512), bf16), [in_vmem] * 2, 30 << 30, 1 << 20)(cot, first)
     far = swap(near, "yl", 2, 1)
@@ -218,16 +232,20 @@
     x_in = after(lax.all_to_all(x_out, "x", 0, 0), far, far_last)
     x_other = swap(x_in, "c", 2, 1)
 
-    done = call(own_kernel, shape((4, 128, 512), bf16), [in_vmem] * 5, 1 << 29, 3 << 20)(
-        x_in, near, last, far, far_last
-    )
+    done, terms, own_right = call(
+        own_kernel,
+        (shape((4, 128, 512), bf16), shape((4, 128, 128), f32), shape((16, 512), f32)),
+        [in_smem] + [in_vmem] * 5,
+        1 << 29,
+        3 << 20,
+    )(place, x_in, near, last, far, far_last)
     out, right_part = call(
         other_kernel,
         (shape((4, 128, 1152), bf16), shape((16, 512), f32)),
-        [in_smem] + [in_vmem] * 7,
+        [in_smem] + [in_vmem] * 8,
         1 << 29,
         5 << 20,
-    )(place, done, x_in, x_other, near, last, far, far_last)
+    )(place, done, terms, own_right, x_other, near, last, far, far_last)
     back = lax.all_to_all(out.reshape(64, 8, 1152), ("zh", "zl", "yh", "yl"), 0, 0)
     right_sent = right_part.astype(bf16)
     right_sum = right_part + sum(swap(right_sent, "zh", 4, k).astype(f32) for k in (1, 2, 3))
@@ -246,7 +264,7 @@
             pltpu.VMEM((1, 16), f32),
             dma((4,)),
         ],
-    )(place, back, scaled_back, left_factor.T, keep_float.reshape(1, 16))
+    )(place, back, scaled_back, left_factor.T, keep_mask.astype(f32).reshape(1, 16))
     grad_right = right_sum / n_dp
     return (grad_inputs, grad_left, grad_right, grad_singular.reshape(16))
 

time: 109 us -> 109 us (level)
  no operation moved by 1% of the time
where the time goes in v13:
time: 109 us
  starting transfers between devices  65.4 us (60%)
  waiting for transfers between devices  28.9 us (27%)
  Pallas kernels  7.82 us (7%)
  matrix products  2.27 us (2%)
  local copies, waits for them, and re-layouts  1.92 us (2%)
  other arithmetic  1.38 us (1%)
    ppermute x10, starting transfers between devices, swap(): return lax.ppermute(a, axis, [(i, i ^ mask) for i in range(count)])  41.2 us
    ppermute x10, waiting for transfers between devices, swap(): return lax.ppermute(a, axis, [(i, i ^ mask) for i in range(count)])  18 us
    all_to_all x1, starting transfers between devices, body(): lax.all_to_all(out.reshape(64, 8, 1152), ('zh', 'zl', 'yh', 'yl'), 0, 0)  11.3 us
    all_to_all x1, waiting for transfers between devices, body(): lax.all_to_all(out.reshape(64, 8, 1152), ('zh', 'zl', 'yh', 'yl'), 0, 0)  10.9 us
    all_to_all x1, starting transfers between devices, body(): rank_in = lax.all_to_all(rank_out, ('zl', 'yh', 'yl'), 0, 0)  8.11 us
    all_to_all x1, starting transfers between devices, body(): x_in = after(lax.all_to_all(x_out, 'x', 0, 0), far, far_last)  4.78 us
    pallas_call x1, Pallas kernels, body(): call(other_kernel, (shape((4, 128, 1152), bf16), shape((16, 512), f32)),...  2.53 us
  transfers between devices with their start and end apart: 13, of which 6 were waited for; matrix products, arithmetic and copies ran while one was open for 4% of the time, Pallas kernels for 3%

profile of v13, /device:TPU:6, one launch (start us, length us, event | category | flops | bytes accessed | tf_op | source)
XLA Modules:
  0.0 108.6 jit_solution(9157143101469878399)
XLA Ops:
  0.6 0.0 copy-start
  0.6 0.0 copy-start.3
  0.7 0.0 copy-start.4
  0.7 0.0 copy-start.5
  0.7 3.6 %collective-permute-start = (bf16[256,512]{1,0:T(8,128)(2,1)}, bf16[256,512]{1,0:T(8,128)(2,1)S(1)}, u32[]{:S(2)}, u32[]{:S(2)}) collective-permute-start(bf16[256,512]{1,0:T(8,128)(2,1)} %weight_any.1), channel_id=1, source_target_pairs={{0,1},{1,0},{2,3},{3,2},{4,5},{5,4},{6,7},{7,6},{8,9},{9,8},{10,11... | collective-permute-start | bytes 786440 | tf_op jit(solution)/shard_map/ppermute | solution.py:29
  4.3 0.0 copy-done
  4.3 1.1 convolution_bitcast_fusion
  5.4 1.2 %fusion = f32[8,16]{1,0:T(8,128)S(1)} fusion(bf16[8,8192]{1,0:T(8,128)(2,1)} %param.7, bf16[8192,16]{0,1:T(8,128)(2,1)} %param.10), kind=kOutput, calls=%fused_computation.6 | convolution fusion | flops 2097152 | bytes 393728 | tf_op jit(solution)/shard_map/dot_general | solution.py:208
  6.6 0.1 pad.9
  6.7 0.7 pad_add_fusion.sent_ref
  7.3 8.1 %all-to-all-start = ((f32[16,8,128]{2,1,0:T(8,128)}), f32[16,8,128]{2,1,0:T(8,128)S(1)}, u32[]{:S(2)}, u32[]{:S(2)}) async-start(f32[16,8,128]{2,1,0:T(8,128)} %pad_add_fusion.sent_ref), calls=%async_computation | async-start | bytes 131072 | tf_op jit(solution)/shard_map/all_to_all | solution.py:210
  15.5 0.9 copy.17
  16.4 0.1 pad_add_fusion.1.place_ref
  16.5 0.0 collective-permute-done.after_ref.got_any
  16.5 0.0 copy-start.2
  16.5 0.9 copy-done.2
  17.4 6.1 %collective-permute-start.1 = (bf16[128,512]{1,0:T(8,128)(2,1)S(1)}, bf16[128,512]{1,0:T(8,128)(2,1)S(1)}, u32[]{:S(2)}, u32[]{:S(2)}) collective-permute-start(bf16[128,512]{1,0:T(8,128)(2,1)S(1)} %shard_map.102.cot_ref.first_ref), channel_id=1, source_target_pairs={{0,128},{128,0},{256,384},{384,256},{1,129},{129,1},{257,385},{385... | collective-permute-start | bytes 393224 | tf_op jit(solution)/shard_map/ppermute | solution.py:29
  23.5 6.4 %collective-permute-start.3 = (bf16[128,512]{1,0:T(8,128)(2,1)S(1)}, bf16[128,512]{1,0:T(8,128)(2,1)S(1)}, u32[]{:S(2)}, u32[]{:S(2)}) collective-permute-start(bf16[128,512]{1,0:T(8,128)(2,1)S(1)} %shard_map.102.cot_ref.first_ref), channel_id=1, source_target_pairs={{0,384},{128,256},{256,128},{384,0},{1,385},{129,257},{257,129},{3... | collective-permute-start | bytes 393224 | tf_op jit(solution)/shard_map/ppermute | solution.py:29
  29.9 0.0 all-to-all-done.rank_ref
  29.9 0.0 copy-done.3
  29.9 0.0 copy-done.4
  29.9 0.0 copy-done.5
  29.9 2.1 %shard_map.103 = (bf16[4,320,512]{2,1,0:T(8,128)(2,1)}, bf16[8,128]{1,0:T(8,128)(2,1)S(1)}) custom-call(s32[3]{0:T(128)S(1)} %pad_add_fusion.1.place_ref, f32[16]{0:T(128)S(1)} %copy-done.4, s32[16]{0:T(128)S(1)} %copy-done.5, f32[16,8,128]{2,1,0:T(8,128)} %pad_add_fusion.sent_ref, f32[16,8,128]{2,1,0:T(8,128)S(1)} %all-to-all-done.rank_ref, ...), custom_call_target="tpu_custom_call" | custom-call | flops 32212254720 | bytes 3145728 | tf_op jit(solution)/shard_map/pallas_call | solution.py:216
  32.0 4.8 %all-to-all-start.1 = ((bf16[4,320,512]{2,1,0:T(8,128)(2,1)}), bf16[4,320,512]{2,1,0:T(8,128)(2,1)S(1)}, u32[]{:S(2)}, u32[]{:S(2)}) async-start(bf16[4,320,512]{2,1,0:T(8,128)(2,1)} %get-tuple-element.14), calls=%async_computation.1 | async-start | bytes 2621440 | tf_op jit(solution)/shard_map/all_to_all | solution.py:232
  36.8 0.0 collective-permute-done.1.refs_0_
  36.8 4.2 %collective-permute-start.4 = (bf16[128,512]{1,0:T(8,128)(2,1)S(1)}, bf16[128,512]{1,0:T(8,128)(2,1)S(1)}, u32[]{:S(2)}, u32[]{:S(2)}) collective-permute-start(bf16[128,512]{1,0:T(8,128)(2,1)S(1)} %shard_map.104.second_ref), channel_id=1, source_target_pairs={{0,384},{128,256},{256,128},{384,0},{1,385},{129,257},{257,129},{3... | collective-permute-start | bytes 393224 | tf_op jit(solution)/shard_map/ppermute | solution.py:29
  41.0 2.9 %collective-permute-start.2 = (bf16[2,128,512]{2,1,0:T(8,128)(2,1)S(1)}, bf16[2,128,512]{2,1,0:T(8,128)(2,1)S(1)}, u32[]{:S(2)}, u32[]{:S(2)}) collective-permute-start(bf16[2,128,512]{2,1,0:T(8,128)(2,1)S(1)} %shard_map.105.near_ref), channel_id=1, source_target_pairs={{0,1},{1,0},{2,3},{3,2},{4,5},{5,4},{6,7},{7,6},{8,9},{9,8},{10,11... | collective-permute-start | bytes 786440 | tf_op jit(solution)/shard_map/ppermute | solution.py:29
  44.0 0.0 collective-permute-done.3.first_ref
  44.0 1.9 %collective-permute-done.4.second_ref = bf16[128,512]{1,0:T(8,128)(2,1)S(1)} collective-permute-done((bf16[128,512]{1,0:T(8,128)(2,1)S(1)}, bf16[128,512]{1,0:T(8,128)(2,1)S(1)}, u32[]{:S(2)}, u32[]{:S(2)}) %collective-permute-start.4) | collective-permute-done | bytes 131104 | tf_op jit(solution)/shard_map/ppermute | solution.py:29
  45.9 3.8 %collective-permute-start.5 = (bf16[2,128,512]{2,1,0:T(8,128)(2,1)S(1)}, bf16[2,128,512]{2,1,0:T(8,128)(2,1)S(1)}, u32[]{:S(2)}, u32[]{:S(2)}) collective-permute-start(bf16[2,128,512]{2,1,0:T(8,128)(2,1)S(1)} %shard_map.106.last_ref), channel_id=1, source_target_pairs={{0,1},{1,0},{2,3},{3,2},{4,5},{5,4},{6,7},{7,6},{8,9},{9,8},{10,11... | collective-permute-start | bytes 786440 | tf_op jit(solution)/shard_map/ppermute | solution.py:29
  49.7 1.5 %collective-permute-done.2.refs_1_.far_ref = bf16[2,128,512]{2,1,0:T(8,128)(2,1)S(1)} collective-permute-done((bf16[2,128,512]{2,1,0:T(8,128)(2,1)S(1)}, bf16[2,128,512]{2,1,0:T(8,128)(2,1)S(1)}, u32[]{:S(2)}, u32[]{:S(2)}) %collective-permute-start.2) | collective-permute-done | bytes 262176 | tf_op jit(solution)/shard_map/ppermute | solution.py:29
  51.2 3.7 %collective-permute-done.5.refs_2_.far_last_ref = bf16[2,128,512]{2,1,0:T(8,128)(2,1)S(1)} collective-permute-done((bf16[2,128,512]{2,1,0:T(8,128)(2,1)S(1)}, bf16[2,128,512]{2,1,0:T(8,128)(2,1)S(1)}, u32[]{:S(2)}, u32[]{:S(2)}) %collective-permute-start.5) | collective-permute-done | bytes 262176 | tf_op jit(solution)/shard_map/ppermute | solution.py:29
  54.9 0.0 all-to-all-done.1.refs_0_
  54.9 1.9 %collective-permute-start.6 = (bf16[4,320,512]{2,1,0:T(8,128)(2,1)S(1)}, bf16[4,320,512]{2,1,0:T(8,128)(2,1)S(1)}, u32[]{:S(2)}, u32[]{:S(2)}) collective-permute-start(bf16[4,320,512]{2,1,0:T(8,128)(2,1)S(1)} %shard_map.107.own_ref), channel_id=1, source_target_pairs={{0,16},{16,0},{1,17},{17,1},{2,18},{18,2},{3,19},{19,3},{4,20},{20... | collective-permute-start | bytes 3932168 | tf_op jit(solution)/shard_map/ppermute | solution.py:29
  56.8 1.4 %shard_map.108 = (bf16[4,128,512]{2,1,0:T(8,128)(2,1)S(1)}, f32[4,128,128]{2,1,0:T(8,128)S(1)}, f32[16,512]{1,0:T(8,128)S(1)}) custom-call(s32[3]{0:T(128)S(1)} %pad_add_fusion.1.place_ref, bf16[4,320,512]{2,1,0:T(8,128)(2,1)S(1)} %shard_map.107.own_ref, bf16[2,128,512]{2,1,0:T(8,128)(2,1)S(1)} %shard_map.105.near_ref, ...), custom_call_target="tpu_custom_call" | custom-call | flops 536870912 | bytes 3145728 | tf_op jit(solution)/shard_map/pallas_call | solution.py:235
  58.3 1.6 %collective-permute-done.6.other_ref = bf16[4,320,512]{2,1,0:T(8,128)(2,1)S(1)} collective-permute-done((bf16[4,320,512]{2,1,0:T(8,128)(2,1)S(1)}, bf16[4,320,512]{2,1,0:T(8,128)(2,1)S(1)}, u32[]{:S(2)}, u32[]{:S(2)}) %collective-permute-start.6) | collective-permute-done | bytes 1310752 | tf_op jit(solution)/shard_map/ppermute | solution.py:29
  59.8 2.5 %shard_map.109 = (bf16[4,128,1152]{2,1,0:T(8,128)(2,1)}, f32[16,512]{1,0:T(8,128)S(1)}) custom-call(s32[3]{0:T(128)S(1)} %pad_add_fusion.1.place_ref, bf16[4,128,512]{2,1,0:T(8,128)(2,1)S(1)} %get-tuple-element.16.done_ref, f32[4,128,128]{2,1,0:T(8,128)S(1)} %get-tuple-element.17.terms_ref, f32[16,512]{1,0:T(8,128)S(1)} %get-tuple-element.18.own_right_ref, ...), custom_call_target="tpu_custom_call" | custom-call | flops 536870912 | bytes 5242880 | tf_op jit(solution)/shard_map/pallas_call | solution.py:242
  62.4 11.3 %all-to-all-start.2 = ((bf16[64,8,1152]{2,1,0:T(8,128)(2,1)}), bf16[64,8,1152]{2,1,0:T(8,128)(2,1)S(1)}, u32[]{:S(2)}, u32[]{:S(2)}) async-start(bf16[64,8,1152]{2,1,0:T(8,128)(2,1)} %bitcast.7), calls=%async_computation.2 | async-start | bytes 2359296 | tf_op jit(solution)/shard_map/all_to_all | solution.py:249
  73.8 4.4 %collective-permute-start.7 = (bf16[16,512]{1,0:T(8,128)(2,1)S(1)}, bf16[16,512]{1,0:T(8,128)(2,1)S(1)}, u32[]{:S(2)}, u32[]{:S(2)}) collective-permute-start(bf16[16,512]{1,0:T(8,128)(2,1)S(1)} %convert_element_type.20), channel_id=1, source_target_pairs={{0,128},{128,0},{256,384},{384,256},{1,129},{129,1},{257,385},{385... | collective-permute-start | bytes 49160 | tf_op jit(solution)/shard_map/ppermute | solution.py:29
  78.1 5.7 %collective-permute-start.8 = (bf16[16,512]{1,0:T(8,128)(2,1)S(1)}, bf16[16,512]{1,0:T(8,128)(2,1)S(1)}, u32[]{:S(2)}, u32[]{:S(2)}) collective-permute-start(bf16[16,512]{1,0:T(8,128)(2,1)S(1)} %convert_element_type.20), channel_id=1, source_target_pairs={{0,256},{128,384},{256,0},{384,128},{1,257},{129,385},{257,1},{385... | collective-permute-start | bytes 49160 | tf_op jit(solution)/shard_map/ppermute | solution.py:29
  83.8 2.2 %collective-permute-start.9 = (bf16[16,512]{1,0:T(8,128)(2,1)S(1)}, bf16[16,512]{1,0:T(8,128)(2,1)S(1)}, u32[]{:S(2)}, u32[]{:S(2)}) collective-permute-start(bf16[16,512]{1,0:T(8,128)(2,1)S(1)} %convert_element_type.20), channel_id=1, source_target_pairs={{0,384},{128,256},{256,128},{384,0},{1,385},{129,257},{257,129},{3... | collective-permute-start | bytes 49160 | tf_op jit(solution)/shard_map/ppermute | solution.py:29
  86.0 9.3 %collective-permute-done.7 = bf16[16,512]{1,0:T(8,128)(2,1)S(1)} collective-permute-done((bf16[16,512]{1,0:T(8,128)(2,1)S(1)}, bf16[16,512]{1,0:T(8,128)(2,1)S(1)}, u32[]{:S(2)}, u32[]{:S(2)}) %collective-permute-start.7) | collective-permute-done | bytes 16416 | tf_op jit(solution)/shard_map/ppermute | solution.py:29
  95.3 0.0 collective-permute-done.8
  95.3 0.0 collective-permute-done.9
  95.3 0.6 add_multiply_fusion
  96.0 10.9 %all-to-all-done.2.back_ref = bf16[64,8,1152]{2,1,0:T(8,128)(2,1)S(1)} async-done(((bf16[64,8,1152]{2,1,0:T(8,128)(2,1)}), bf16[64,8,1152]{2,1,0:T(8,128)(2,1)S(1)}, u32[]{:S(2)}, u32[]{:S(2)}) %all-to-all-start.2) | async-done | bytes 1179680 | tf_op jit(solution)/shard_map/all_to_all | solution.py:249
  106.8 0.0 copy-done.1
  106.8 1.7 %shard_map.110 = (bf16[8,8192]{1,0:T(8,128)(2,1)}, f32[16,16]{1,0:T(8,128)}, f32[1,16]{1,0:T(1,128)}) custom-call(s32[3]{0:T(128)S(1)} %pad_add_fusion.1.place_ref, bf16[64,8,1152]{2,1,0:T(8,128)(2,1)S(1)} %all-to-all-done.2.back_ref, bf16[8,128]{1,0:T(8,128)(2,1)S(1)} %get-tuple-element.15.refs_1_.scaled_ref, bf16[16,8192]{1,0:T(8,128)(2,1)S(1)} %bitcast.20, ...), custom_call_target="tpu_custom_call" | custom-call | flops 2097152 | bytes 2097152 | tf_op jit(solution)/shard_map/pallas_call | solution.py:253
  (8 shorter events, 0.1 us)
Async XLA Ops:
  0.6 3.7 %copy-start = (bf16[16,512]{1,0:T(8,128)(2,1)S(1)}, bf16[16,512]{1,0:T(8,128)(2,1)}, u32[]{:S(2)}) copy-start(bf16[16,512]{1,0:T(8,128)(2,1)} %param.11) | copy-start | bytes 49156
  0.6 29.2 %copy-start.3 = (bf16[256,512]{1,0:T(8,128)(2,1)S(1)}, bf16[256,512]{1,0:T(8,128)(2,1)}, u32[]{:S(2)}) copy-start(bf16[256,512]{1,0:T(8,128)(2,1)} %weight_any.1) | copy-start | bytes 786436
  0.7 29.2 %copy-start.4 = (f32[16]{0:T(128)S(1)}, f32[16]{0:T(128)}, u32[]{:S(2)}) copy-start(f32[16]{0:T(128)} %singular_ref.1) | copy-start | bytes 196
  0.7 29.2 %copy-start.5 = (s32[16]{0:T(128)S(1)}, s32[16]{0:T(128)}, u32[]{:S(2)}) copy-start(s32[16]{0:T(128)} %keep_ref.1) | copy-start | bytes 196
  0.7 15.8 %collective-permute-start = (bf16[256,512]{1,0:T(8,128)(2,1)}, bf16[256,512]{1,0:T(8,128)(2,1)S(1)}, u32[]{:S(2)}, u32[]{:S(2)}) collective-permute-start(bf16[256,512]{1,0:T(8,128)(2,1)} %weight_any.1), channel_id=1, source_target_pairs={{0,1},{1,0},{2,3},{3,2},{4,5},{5,4},{6,7},{7,6},{8,9},{9,8},{10,11... | collective-permute-start | bytes 786440 | tf_op jit(solution)/shard_map/ppermute | solution.py:29
  7.3 22.6 %all-to-all-start = ((f32[16,8,128]{2,1,0:T(8,128)}), f32[16,8,128]{2,1,0:T(8,128)S(1)}, u32[]{:S(2)}, u32[]{:S(2)}) async-start(f32[16,8,128]{2,1,0:T(8,128)} %pad_add_fusion.sent_ref), calls=%async_computation | async-start | bytes 131072 | tf_op jit(solution)/shard_map/all_to_all | solution.py:210
  16.5 0.9 copy-start.2
  17.4 19.4 %collective-permute-start.1 = (bf16[128,512]{1,0:T(8,128)(2,1)S(1)}, bf16[128,512]{1,0:T(8,128)(2,1)S(1)}, u32[]{:S(2)}, u32[]{:S(2)}) collective-permute-start(bf16[128,512]{1,0:T(8,128)(2,1)S(1)} %shard_map.102.cot_ref.first_ref), channel_id=1, source_target_pairs={{0,128},{128,0},{256,384},{384,256},{1,129},{129,1},{257,385},{385... | collective-permute-start | bytes 393224 | tf_op jit(solution)/shard_map/ppermute | solution.py:29
  23.5 20.5 %collective-permute-start.3 = (bf16[128,512]{1,0:T(8,128)(2,1)S(1)}, bf16[128,512]{1,0:T(8,128)(2,1)S(1)}, u32[]{:S(2)}, u32[]{:S(2)}) collective-permute-start(bf16[128,512]{1,0:T(8,128)(2,1)S(1)} %shard_map.102.cot_ref.first_ref), channel_id=1, source_target_pairs={{0,384},{128,256},{256,128},{384,0},{1,385},{129,257},{257,129},{3... | collective-permute-start | bytes 393224 | tf_op jit(solution)/shard_map/ppermute | solution.py:29
  32.0 22.9 %all-to-all-start.1 = ((bf16[4,320,512]{2,1,0:T(8,128)(2,1)}), bf16[4,320,512]{2,1,0:T(8,128)(2,1)S(1)}, u32[]{:S(2)}, u32[]{:S(2)}) async-start(bf16[4,320,512]{2,1,0:T(8,128)(2,1)} %get-tuple-element.14), calls=%async_computation.1 | async-start | bytes 2621440 | tf_op jit(solution)/shard_map/all_to_all | solution.py:232
  36.8 9.1 %collective-permute-start.4 = (bf16[128,512]{1,0:T(8,128)(2,1)S(1)}, bf16[128,512]{1,0:T(8,128)(2,1)S(1)}, u32[]{:S(2)}, u32[]{:S(2)}) collective-permute-start(bf16[128,512]{1,0:T(8,128)(2,1)S(1)} %shard_map.104.second_ref), channel_id=1, source_target_pairs={{0,384},{128,256},{256,128},{384,0},{1,385},{129,257},{257,129},{3... | collective-permute-start | bytes 393224 | tf_op jit(solution)/shard_map/ppermute | solution.py:29
  41.0 10.2 %collective-permute-start.2 = (bf16[2,128,512]{2,1,0:T(8,128)(2,1)S(1)}, bf16[2,128,512]{2,1,0:T(8,128)(2,1)S(1)}, u32[]{:S(2)}, u32[]{:S(2)}) collective-permute-start(bf16[2,128,512]{2,1,0:T(8,128)(2,1)S(1)} %shard_map.105.near_ref), channel_id=1, source_target_pairs={{0,1},{1,0},{2,3},{3,2},{4,5},{5,4},{6,7},{7,6},{8,9},{9,8},{10,11... | collective-permute-start | bytes 786440 | tf_op jit(solution)/shard_map/ppermute | solution.py:29
  45.9 9.0 %collective-permute-start.5 = (bf16[2,128,512]{2,1,0:T(8,128)(2,1)S(1)}, bf16[2,128,512]{2,1,0:T(8,128)(2,1)S(1)}, u32[]{:S(2)}, u32[]{:S(2)}) collective-permute-start(bf16[2,128,512]{2,1,0:T(8,128)(2,1)S(1)} %shard_map.106.last_ref), channel_id=1, source_target_pairs={{0,1},{1,0},{2,3},{3,2},{4,5},{5,4},{6,7},{7,6},{8,9},{9,8},{10,11... | collective-permute-start | bytes 786440 | tf_op jit(solution)/shard_map/ppermute | solution.py:29
  54.9 4.9 %collective-permute-start.6 = (bf16[4,320,512]{2,1,0:T(8,128)(2,1)S(1)}, bf16[4,320,512]{2,1,0:T(8,128)(2,1)S(1)}, u32[]{:S(2)}, u32[]{:S(2)}) collective-permute-start(bf16[4,320,512]{2,1,0:T(8,128)(2,1)S(1)} %shard_map.107.own_ref), channel_id=1, source_target_pairs={{0,16},{16,0},{1,17},{17,1},{2,18},{18,2},{3,19},{19,3},{4,20},{20... | collective-permute-start | bytes 3932168 | tf_op jit(solution)/shard_map/ppermute | solution.py:29
  62.4 44.5 %copy-start.1 = (bf16[8192,16]{0,1:T(8,128)(2,1)S(1)}, bf16[8192,16]{0,1:T(8,128)(2,1)}, u32[]{:S(2)}) copy-start(bf16[8192,16]{0,1:T(8,128)(2,1)} %param.10) | copy-start | bytes 786436
  62.4 44.5 %all-to-all-start.2 = ((bf16[64,8,1152]{2,1,0:T(8,128)(2,1)}), bf16[64,8,1152]{2,1,0:T(8,128)(2,1)S(1)}, u32[]{:S(2)}, u32[]{:S(2)}) async-start(bf16[64,8,1152]{2,1,0:T(8,128)(2,1)} %bitcast.7), calls=%async_computation.2 | async-start | bytes 2359296 | tf_op jit(solution)/shard_map/all_to_all | solution.py:249
  73.8 21.6 %collective-permute-start.7 = (bf16[16,512]{1,0:T(8,128)(2,1)S(1)}, bf16[16,512]{1,0:T(8,128)(2,1)S(1)}, u32[]{:S(2)}, u32[]{:S(2)}) collective-permute-start(bf16[16,512]{1,0:T(8,128)(2,1)S(1)} %convert_element_type.20), channel_id=1, source_target_pairs={{0,128},{128,0},{256,384},{384,256},{1,129},{129,1},{257,385},{385... | collective-permute-start | bytes 49160 | tf_op jit(solution)/shard_map/ppermute | solution.py:29
  78.1 17.2 %collective-permute-start.8 = (bf16[16,512]{1,0:T(8,128)(2,1)S(1)}, bf16[16,512]{1,0:T(8,128)(2,1)S(1)}, u32[]{:S(2)}, u32[]{:S(2)}) collective-permute-start(bf16[16,512]{1,0:T(8,128)(2,1)S(1)} %convert_element_type.20), channel_id=1, source_target_pairs={{0,256},{128,384},{256,0},{384,128},{1,257},{129,385},{257,1},{385... | collective-permute-start | bytes 49160 | tf_op jit(solution)/shard_map/ppermute | solution.py:29
  83.8 11.5 %collective-permute-start.9 = (bf16[16,512]{1,0:T(8,128)(2,1)S(1)}, bf16[16,512]{1,0:T(8,128)(2,1)S(1)}, u32[]{:S(2)}, u32[]{:S(2)}) collective-permute-start(bf16[16,512]{1,0:T(8,128)(2,1)S(1)} %convert_element_type.20), channel_id=1, source_target_pairs={{0,384},{128,256},{256,128},{384,0},{1,385},{129,257},{257,129},{3... | collective-permute-start | bytes 49160 | tf_op jit(solution)/shard_map/ppermute | solution.py:29

commit v14 on v13

--- a/solution.py
+++ b/solution.py
@@ -52,10 +52,6 @@
     )(a, *others)
 
 
-def hold_kernel(in_ref, after_ref, out_ref):
-    out_ref[...] = in_ref[...]
-
-
 def stack_kernel(first_ref, second_ref, out_ref):
     out_ref[0] = first_ref[...]
     out_ref[1] = second_ref[...]
@@ -66,13 +62,12 @@
 
 
 def pack_kernel(
-    place_ref, singular_ref, keep_ref, sent_ref, rank_ref, cot_ref, weight_any, got_any, slices_ref,
+    place_ref, singular_ref, keep_ref, sent_ref, rank_ref, cot_ref, weight_any, got_any, inputs_ref,
     x_any, back_ref, rest_ref, out_sems,
 ):
     rows = pl.ds(pl.multiple_of(place_ref[1] * 128, 128), 128)
     outs = [pltpu.make_async_copy(got_any.at[rows], x_any.at[x, 128:256], out_sems.at[x]) for x in range(4)]
     outs += [pltpu.make_async_copy(weight_any.at[rows], x_any.at[x, 0:128], out_sems.at[8 + x]) for x in range(4)]
-    outs += [pltpu.make_async_copy(slices_ref.at[x], x_any.at[x, 256:288], out_sems.at[4 + x]) for x in range(4)]
     for copy in outs:
         copy.start()
     lane = lax.broadcasted_iota(jnp.int32, (1, 128), 1)
@@ -98,10 +93,13 @@
         ],
         axis=0,
     ).astype(bf16)
-    rest_ref[0:16, :] = small
-    rest_ref[16:32, :] = right.astype(bf16)
+    inputs = inputs_ref[...].astype(f32)
     for x in range(4):
-        outs.append(pltpu.make_async_copy(rest_ref, x_any.at[x, 288:320], out_sems.at[12 + x]))
+        parts = [inputs[:, (h * 4 + x) * 512 : (h * 4 + x + 1) * 512] for h in range(4)]
+        rest_ref[x, 0:32, :] = jnp.concatenate(parts, axis=0).astype(bf16)
+        rest_ref[x, 32:48, :] = small
+        rest_ref[x, 48:64, :] = right.astype(bf16)
+        outs.append(pltpu.make_async_copy(rest_ref.at[x], x_any.at[x, 256:320], out_sems.at[4 + x]))
         outs[-1].start()
     for copy in outs:
         copy.wait()
@@ -110,7 +108,7 @@
 def products(parts, ref):
     total = dot_t(parts[0], ref[:, 0:128, :].reshape(512, 512))
     total += dot_t(parts[1], ref[:, 128:256, :].reshape(512, 512))
-    return total.astype(bf16).reshape(4, 128, 512)
+    return total.astype(bf16)
 
 
 def adapter_terms(ref, core):
@@ -137,7 +135,8 @@
 def own_kernel(
     place_ref, own_ref, near_ref, last_ref, far_ref, far_last_ref, out_ref, terms_ref, right_ref
 ):
-    out_ref[...] = products((rows_of(near_ref, last_ref), rows_of(far_ref, far_last_ref)), own_ref)
+    parts = (rows_of(near_ref, last_ref), rows_of(far_ref, far_last_ref))
+    out_ref[...] = products(parts, own_ref).reshape(4, 128, 512)
     terms, right_ref[...] = adapter_terms(own_ref, place_ref[0])
     for h in range(4):
         terms_ref[h] = terms[h]
@@ -145,19 +144,27 @@
 
 def other_kernel(
     place_ref, done_ref, terms_ref, own_right_ref, other_ref, near_ref, last_ref, far_ref, far_last_ref,
-    out_ref, right_ref,
+    out_any, right_ref, out_ref, sems,
 ):
     z_high = place_ref[2]
-    total = products((rows_of(near_ref, last_ref), rows_of(far_ref, far_last_ref)), other_ref)
-    for i, k in enumerate((0, 1, 3, 2)):
-        out_ref[z_high ^ k, :, 0:512] = done_ref[i]
-        out_ref[z_high ^ k, :, 512:1024] = total[i]
     terms, right = adapter_terms(other_ref, place_ref[0])
     right_ref[...] = own_right_ref[...] + right
     for h in range(4):
         z = terms_ref[h] + terms[h]
         high = z.astype(bf16).astype(f32)
         out_ref[h, :, 1024:1152] = (high + pltpu.roll(z - high, 64, 1)).astype(bf16)
+    copies = []
+    for half, (first, second) in enumerate(((near_ref, far_ref), (last_ref, far_last_ref))):
+        parts = (first[...].reshape(256, 512), second[...].reshape(256, 512))
+        total = products(parts, other_ref).reshape(2, 128, 512)
+        for i in range(2):
+            at = z_high ^ ((0, 1), (3, 2))[half][i]
+            out_ref[at, :, 0:512] = done_ref[half * 2 + i]
+            out_ref[at, :, 512:1024] = total[i]
+            copies.append(pltpu.make_async_copy(out_ref.at[at], out_any.at[at], sems.at[half * 2 + i]))
+            copies[-1].start()
+    for copy in copies:
+        copy.wait()
 
 
 def final_kernel(
@@ -209,10 +216,9 @@
     rank_out = jnp.pad(back_part, ((0, 0), (0, 0), (0, 112))) + jnp.pad(own_projected, ((0, 0), (16, 96)))
     rank_in = lax.all_to_all(rank_out, ("zl", "yh", "yl"), 0, 0)
 
-    cot = call(hold_kernel, shape((128, 512), bf16), [in_vmem, anywhere], 1, 1 << 18)(cotangent, got)
+    cot = after(cotangent, got)
     first, third = swap(cot, "zh", 4, 1), swap(cot, "zh", 4, 3)
 
-    slices = inputs.reshape(8, 4, 4, 512).transpose(2, 1, 0, 3).reshape(4, 32, 512)
     x_out, scaled_back = call(
         pack_kernel,
         (shape((4, 320, 512), bf16), shape((8, 128), bf16)),
@@ -220,8 +226,8 @@
         30 << 30,
         3 << 20,
         out_specs=(in_hbm, in_vmem),
-        scratch=[pltpu.VMEM((32, 512), bf16), dma((16,))],
-    )(place, singular, keep_mask, rank_out, rank_in, cot, weight, got, slices)
+        scratch=[pltpu.VMEM((4, 64, 512), bf16), dma((12,))],
+    )(place, singular, keep_mask, rank_out, rank_in, cot, weight, got, inputs)
     first = after(first, scaled_back)
     near = call(stack_kernel, shape((2, 128, 512), bf16), [in_vmem] * 2, 30 << 30, 1 << 20)(cot, first)
     far = swap(near, "yl", 2, 1)
@@ -245,6 +251,8 @@
         [in_smem] + [in_vmem] * 8,
         1 << 29,
         5 << 20,
+        out_specs=(in_hbm, in_vmem),
+        scratch=[pltpu.VMEM((4, 128, 1152), bf16), dma((4,))],
     )(place, done, terms, own_right, x_other, near, last, far, far_last)
     back = lax.all_to_all(out.reshape(64, 8, 1152), ("zh", "zl", "yh", "yl"), 0, 0)
     right_sent = right_part.astype(bf16)

time: 109 us -> 107 us (0.982)
    all_to_all x1, starting transfers between devices: 11.3 us -> 9.91 us  [body(): lax.all_to_all(out.reshape(64, 8, 1152), ('zh', 'zl', 'yh', 'yl'), 0, 0)]
  transfers between devices with their start and end apart: 13 -> 13, of which waited for: 6 -> 6; matrix products, arithmetic and copies ran while one was open for 4% -> 3% of each run, Pallas kernels for 3% -> 3%
where the time goes in v14:
time: 107 us; the launch traced here: 106 us
  starting transfers between devices  64.8 us (61%)
  waiting for transfers between devices  29.4 us (27%)
  Pallas kernels  7.5 us (7%)
  other arithmetic  1.37 us (1%)
  matrix products  1.36 us (1%)
  local copies, waits for them, and re-layouts  1.07 us (1%)
    ppermute x10, starting transfers between devices, swap(): return lax.ppermute(a, axis, [(i, i ^ mask) for i in range(count)])  41.9 us
    ppermute x10, waiting for transfers between devices, swap(): return lax.ppermute(a, axis, [(i, i ^ mask) for i in range(count)])  18.6 us
    all_to_all x1, waiting for transfers between devices, body(): lax.all_to_all(out.reshape(64, 8, 1152), ('zh', 'zl', 'yh', 'yl'), 0, 0)  10.9 us
    all_to_all x1, starting transfers between devices, body(): lax.all_to_all(out.reshape(64, 8, 1152), ('zh', 'zl', 'yh', 'yl'), 0, 0)  9.91 us
    all_to_all x1, starting transfers between devices, body(): rank_in = lax.all_to_all(rank_out, ('zl', 'yh', 'yl'), 0, 0)  8.11 us
    all_to_all x1, starting transfers between devices, body(): x_in = after(lax.all_to_all(x_out, 'x', 0, 0), far, far_last)  4.78 us
    pallas_call x1, Pallas kernels, body(): call(other_kernel, (shape((4, 128, 1152), bf16), shape((16, 512), f32)),...  2.26 us
  transfers between devices with their start and end apart: 13, of which 6 were waited for; matrix products, arithmetic and copies ran while one was open for 3% of the time, Pallas kernels for 3%

profile of v14, /device:TPU:6, one launch (start us, length us, event | category | flops | bytes accessed | tf_op | source)
XLA Modules:
  0.0 106.4 jit_solution(3720112669328251862)
XLA Ops:
  0.6 0.0 copy-start
  0.6 0.0 copy-start.2
  0.7 0.0 copy-start.3
  0.7 0.0 copy-start.4
  0.7 0.0 copy-start.5
  0.7 1.0 copy.20.refs_0_
  1.6 3.5 %collective-permute-start = (bf16[256,512]{1,0:T(8,128)(2,1)}, bf16[256,512]{1,0:T(8,128)(2,1)S(1)}, u32[]{:S(2)}, u32[]{:S(2)}) collective-permute-start(bf16[256,512]{1,0:T(8,128)(2,1)} %weight_any.1), channel_id=1, source_target_pairs={{0,1},{1,0},{2,3},{3,2},{4,5},{5,4},{6,7},{7,6},{8,9},{9,8},{10,11... | collective-permute-start | bytes 786440 | tf_op jit(solution)/shard_map/ppermute | solution.py:29
  5.1 0.0 copy-done
  5.1 0.1 convolution_bitcast_fusion
  5.3 1.2 %fusion = f32[8,16]{1,0:T(8,128)S(1)} fusion(bf16[8,8192]{1,0:T(8,128)(2,1)} %inputs_ref.1, bf16[8192,16]{0,1:T(8,128)(2,1)} %param.10), kind=kOutput, calls=%fused_computation.5 | convolution fusion | flops 2097152 | bytes 393728 | tf_op jit(solution)/shard_map/dot_general | solution.py:215
  6.5 0.1 pad.9
  6.6 0.7 pad_add_fusion.sent_ref
  7.2 8.1 %all-to-all-start = ((f32[16,8,128]{2,1,0:T(8,128)}), f32[16,8,128]{2,1,0:T(8,128)S(1)}, u32[]{:S(2)}, u32[]{:S(2)}) async-start(f32[16,8,128]{2,1,0:T(8,128)} %pad_add_fusion.sent_ref), calls=%async_computation | async-start | bytes 131072 | tf_op jit(solution)/shard_map/all_to_all | solution.py:217
  15.4 0.1 pad_add_fusion.1.place_ref
  15.4 0.0 collective-permute-done.refs_1_.got_any
  15.5 6.1 %collective-permute-start.1 = (bf16[128,512]{1,0:T(8,128)(2,1)S(1)}, bf16[128,512]{1,0:T(8,128)(2,1)S(1)}, u32[]{:S(2)}, u32[]{:S(2)}) collective-permute-start(bf16[128,512]{1,0:T(8,128)(2,1)S(1)} %shard_map.102.cot_ref.first_ref), channel_id=1, source_target_pairs={{0,128},{128,0},{256,384},{384,256},{1,129},{129,1},{257,385},{385... | collective-permute-start | bytes 393224 | tf_op jit(solution)/shard_map/ppermute | solution.py:29
  21.5 6.4 %collective-permute-start.3 = (bf16[128,512]{1,0:T(8,128)(2,1)S(1)}, bf16[128,512]{1,0:T(8,128)(2,1)S(1)}, u32[]{:S(2)}, u32[]{:S(2)}) collective-permute-start(bf16[128,512]{1,0:T(8,128)(2,1)S(1)} %shard_map.102.cot_ref.first_ref), channel_id=1, source_target_pairs={{0,384},{128,256},{256,128},{384,0},{1,385},{129,257},{257,129},{3... | collective-permute-start | bytes 393224 | tf_op jit(solution)/shard_map/ppermute | solution.py:29
  28.0 0.0 all-to-all-done.rank_ref
  28.0 0.0 copy-done.2
  28.0 0.0 copy-done.3
  28.0 0.0 copy-done.4
  28.0 0.0 copy-done.5
  28.0 2.1 %shard_map.103 = (bf16[4,320,512]{2,1,0:T(8,128)(2,1)}, bf16[8,128]{1,0:T(8,128)(2,1)S(1)}) custom-call(s32[3]{0:T(128)S(1)} %pad_add_fusion.1.place_ref, f32[16]{0:T(128)S(1)} %copy-done.4, s32[16]{0:T(128)S(1)} %copy-done.5, f32[16,8,128]{2,1,0:T(8,128)} %pad_add_fusion.sent_ref, f32[16,8,128]{2,1,0:T(8,128)S(1)} %all-to-all-done.rank_ref, ...), custom_call_target="tpu_custom_call" | custom-call | flops 32212254720 | bytes 3145728 | tf_op jit(solution)/shard_map/pallas_call | solution.py:222
  30.1 4.8 %all-to-all-start.1 = ((bf16[4,320,512]{2,1,0:T(8,128)(2,1)}), bf16[4,320,512]{2,1,0:T(8,128)(2,1)S(1)}, u32[]{:S(2)}, u32[]{:S(2)}) async-start(bf16[4,320,512]{2,1,0:T(8,128)(2,1)} %get-tuple-element.14), calls=%async_computation.1 | async-start | bytes 2621440 | tf_op jit(solution)/shard_map/all_to_all | solution.py:238
  34.9 0.0 collective-permute-done.1.refs_0_
  34.9 6.0 %collective-permute-start.4 = (bf16[128,512]{1,0:T(8,128)(2,1)S(1)}, bf16[128,512]{1,0:T(8,128)(2,1)S(1)}, u32[]{:S(2)}, u32[]{:S(2)}) collective-permute-start(bf16[128,512]{1,0:T(8,128)(2,1)S(1)} %shard_map.104.second_ref), channel_id=1, source_target_pairs={{0,384},{128,256},{256,128},{384,0},{1,385},{129,257},{257,129},{3... | collective-permute-start | bytes 393224 | tf_op jit(solution)/shard_map/ppermute | solution.py:29
  40.9 2.9 %collective-permute-start.2 = (bf16[2,128,512]{2,1,0:T(8,128)(2,1)S(1)}, bf16[2,128,512]{2,1,0:T(8,128)(2,1)S(1)}, u32[]{:S(2)}, u32[]{:S(2)}) collective-permute-start(bf16[2,128,512]{2,1,0:T(8,128)(2,1)S(1)} %shard_map.105.near_ref), channel_id=1, source_target_pairs={{0,1},{1,0},{2,3},{3,2},{4,5},{5,4},{6,7},{7,6},{8,9},{9,8},{10,11... | collective-permute-start | bytes 786440 | tf_op jit(solution)/shard_map/ppermute | solution.py:29
  43.8 0.0 collective-permute-done.3.first_ref
  43.8 1.0 collective-permute-done.4.second_ref
  44.8 3.0 %collective-permute-start.5 = (bf16[2,128,512]{2,1,0:T(8,128)(2,1)S(1)}, bf16[2,128,512]{2,1,0:T(8,128)(2,1)S(1)}, u32[]{:S(2)}, u32[]{:S(2)}) collective-permute-start(bf16[2,128,512]{2,1,0:T(8,128)(2,1)S(1)} %shard_map.106.last_ref), channel_id=1, source_target_pairs={{0,1},{1,0},{2,3},{3,2},{4,5},{5,4},{6,7},{7,6},{8,9},{9,8},{10,11... | collective-permute-start | bytes 786440 | tf_op jit(solution)/shard_map/ppermute | solution.py:29
  47.8 3.8 %collective-permute-done.2.refs_1_.far_ref = bf16[2,128,512]{2,1,0:T(8,128)(2,1)S(1)} collective-permute-done((bf16[2,128,512]{2,1,0:T(8,128)(2,1)S(1)}, bf16[2,128,512]{2,1,0:T(8,128)(2,1)S(1)}, u32[]{:S(2)}, u32[]{:S(2)}) %collective-permute-start.2) | collective-permute-done | bytes 262176 | tf_op jit(solution)/shard_map/ppermute | solution.py:29
  51.6 2.8 %collective-permute-done.5.refs_2_.far_last_ref = bf16[2,128,512]{2,1,0:T(8,128)(2,1)S(1)} collective-permute-done((bf16[2,128,512]{2,1,0:T(8,128)(2,1)S(1)}, bf16[2,128,512]{2,1,0:T(8,128)(2,1)S(1)}, u32[]{:S(2)}, u32[]{:S(2)}) %collective-permute-start.5) | collective-permute-done | bytes 262176 | tf_op jit(solution)/shard_map/ppermute | solution.py:29
  54.4 0.0 all-to-all-done.1.refs_0_
  54.4 1.9 %collective-permute-start.6 = (bf16[4,320,512]{2,1,0:T(8,128)(2,1)S(1)}, bf16[4,320,512]{2,1,0:T(8,128)(2,1)S(1)}, u32[]{:S(2)}, u32[]{:S(2)}) collective-permute-start(bf16[4,320,512]{2,1,0:T(8,128)(2,1)S(1)} %shard_map.107.own_ref), channel_id=1, source_target_pairs={{0,16},{16,0},{1,17},{17,1},{2,18},{18,2},{3,19},{19,3},{4,20},{20... | collective-permute-start | bytes 3932168 | tf_op jit(solution)/shard_map/ppermute | solution.py:29
  56.3 1.4 %shard_map.108 = (bf16[4,128,512]{2,1,0:T(8,128)(2,1)S(1)}, f32[4,128,128]{2,1,0:T(8,128)S(1)}, f32[16,512]{1,0:T(8,128)S(1)}) custom-call(s32[3]{0:T(128)S(1)} %pad_add_fusion.1.place_ref, bf16[4,320,512]{2,1,0:T(8,128)(2,1)S(1)} %shard_map.107.own_ref, bf16[2,128,512]{2,1,0:T(8,128)(2,1)S(1)} %shard_map.105.near_ref, ...), custom_call_target="tpu_custom_call" | custom-call | flops 536870912 | bytes 3145728 | tf_op jit(solution)/shard_map/pallas_call | solution.py:241
  57.8 1.6 %collective-permute-done.6.other_ref = bf16[4,320,512]{2,1,0:T(8,128)(2,1)S(1)} collective-permute-done((bf16[4,320,512]{2,1,0:T(8,128)(2,1)S(1)}, bf16[4,320,512]{2,1,0:T(8,128)(2,1)S(1)}, u32[]{:S(2)}, u32[]{:S(2)}) %collective-permute-start.6) | collective-permute-done | bytes 1310752 | tf_op jit(solution)/shard_map/ppermute | solution.py:29
  59.3 2.3 %shard_map.109 = (bf16[4,128,1152]{2,1,0:T(8,128)(2,1)}, f32[16,512]{1,0:T(8,128)S(1)}) custom-call(s32[3]{0:T(128)S(1)} %pad_add_fusion.1.place_ref, bf16[4,128,512]{2,1,0:T(8,128)(2,1)S(1)} %get-tuple-element.16.done_ref, f32[4,128,128]{2,1,0:T(8,128)S(1)} %get-tuple-element.17.terms_ref, f32[16,512]{1,0:T(8,128)S(1)} %get-tuple-element.18.own_right_ref, ...), custom_call_target="tpu_custom_call" | custom-call | flops 536870912 | bytes 5242880 | tf_op jit(solution)/shard_map/pallas_call | solution.py:248
  61.6 0.0 copy-start.1
  61.6 9.9 %all-to-all-start.2 = ((bf16[64,8,1152]{2,1,0:T(8,128)(2,1)}), bf16[64,8,1152]{2,1,0:T(8,128)(2,1)S(1)}, u32[]{:S(2)}, u32[]{:S(2)}) async-start(bf16[64,8,1152]{2,1,0:T(8,128)(2,1)} %bitcast.4), calls=%async_computation.2 | async-start | bytes 2359296 | tf_op jit(solution)/shard_map/all_to_all | solution.py:257
  71.6 4.4 %collective-permute-start.7 = (bf16[16,512]{1,0:T(8,128)(2,1)S(1)}, bf16[16,512]{1,0:T(8,128)(2,1)S(1)}, u32[]{:S(2)}, u32[]{:S(2)}) collective-permute-start(bf16[16,512]{1,0:T(8,128)(2,1)S(1)} %convert_element_type.20), channel_id=1, source_target_pairs={{0,128},{128,0},{256,384},{384,256},{1,129},{129,1},{257,385},{385... | collective-permute-start | bytes 49160 | tf_op jit(solution)/shard_map/ppermute | solution.py:29
  75.9 5.7 %collective-permute-start.8 = (bf16[16,512]{1,0:T(8,128)(2,1)S(1)}, bf16[16,512]{1,0:T(8,128)(2,1)S(1)}, u32[]{:S(2)}, u32[]{:S(2)}) collective-permute-start(bf16[16,512]{1,0:T(8,128)(2,1)S(1)} %convert_element_type.20), channel_id=1, source_target_pairs={{0,256},{128,384},{256,0},{384,128},{1,257},{129,385},{257,1},{385... | collective-permute-start | bytes 49160 | tf_op jit(solution)/shard_map/ppermute | solution.py:29
  81.6 2.2 %collective-permute-start.9 = (bf16[16,512]{1,0:T(8,128)(2,1)S(1)}, bf16[16,512]{1,0:T(8,128)(2,1)S(1)}, u32[]{:S(2)}, u32[]{:S(2)}) collective-permute-start(bf16[16,512]{1,0:T(8,128)(2,1)S(1)} %convert_element_type.20), channel_id=1, source_target_pairs={{0,384},{128,256},{256,128},{384,0},{1,385},{129,257},{257,129},{3... | collective-permute-start | bytes 49160 | tf_op jit(solution)/shard_map/ppermute | solution.py:29
  83.8 9.3 %collective-permute-done.7 = bf16[16,512]{1,0:T(8,128)(2,1)S(1)} collective-permute-done((bf16[16,512]{1,0:T(8,128)(2,1)S(1)}, bf16[16,512]{1,0:T(8,128)(2,1)S(1)}, u32[]{:S(2)}, u32[]{:S(2)}) %collective-permute-start.7) | collective-permute-done | bytes 16416 | tf_op jit(solution)/shard_map/ppermute | solution.py:29
  93.2 0.0 collective-permute-done.8
  93.2 0.0 collective-permute-done.9
  93.2 0.6 add_multiply_fusion
  93.8 10.9 %all-to-all-done.2.back_ref = bf16[64,8,1152]{2,1,0:T(8,128)(2,1)S(1)} async-done(((bf16[64,8,1152]{2,1,0:T(8,128)(2,1)}), bf16[64,8,1152]{2,1,0:T(8,128)(2,1)S(1)}, u32[]{:S(2)}, u32[]{:S(2)}) %all-to-all-start.2) | async-done | bytes 1179680 | tf_op jit(solution)/shard_map/all_to_all | solution.py:257
  104.7 1.7 %shard_map.110 = (bf16[8,8192]{1,0:T(8,128)(2,1)}, f32[16,16]{1,0:T(8,128)}, f32[1,16]{1,0:T(1,128)}) custom-call(s32[3]{0:T(128)S(1)} %pad_add_fusion.1.place_ref, bf16[64,8,1152]{2,1,0:T(8,128)(2,1)S(1)} %all-to-all-done.2.back_ref, bf16[8,128]{1,0:T(8,128)(2,1)S(1)} %get-tuple-element.15.refs_1_.scaled_ref, bf16[16,8192]{1,0:T(8,128)(2,1)S(1)} %bitcast.14, ...), custom_call_target="tpu_custom_call" | custom-call | flops 2097152 | bytes 2097152 | tf_op jit(solution)/shard_map/pallas_call | solution.py:261
  (8 shorter events, 0.1 us)
Async XLA Ops:
  0.6 4.5 %copy-start = (bf16[16,512]{1,0:T(8,128)(2,1)S(1)}, bf16[16,512]{1,0:T(8,128)(2,1)}, u32[]{:S(2)}) copy-start(bf16[16,512]{1,0:T(8,128)(2,1)} %param.11) | copy-start | bytes 49156
  0.6 27.3 %copy-start.2 = (bf16[8,8192]{1,0:T(8,128)(2,1)S(1)}, bf16[8,8192]{1,0:T(8,128)(2,1)}, u32[]{:S(2)}) copy-start(bf16[8,8192]{1,0:T(8,128)(2,1)} %inputs_ref.1) | copy-start | bytes 393220
  0.7 27.3 %copy-start.3 = (bf16[256,512]{1,0:T(8,128)(2,1)S(1)}, bf16[256,512]{1,0:T(8,128)(2,1)}, u32[]{:S(2)}) copy-start(bf16[256,512]{1,0:T(8,128)(2,1)} %weight_any.1) | copy-start | bytes 786436
  0.7 27.3 %copy-start.4 = (f32[16]{0:T(128)S(1)}, f32[16]{0:T(128)}, u32[]{:S(2)}) copy-start(f32[16]{0:T(128)} %singular_ref.1) | copy-start | bytes 196
  0.7 27.3 %copy-start.5 = (s32[16]{0:T(128)S(1)}, s32[16]{0:T(128)}, u32[]{:S(2)}) copy-start(s32[16]{0:T(128)} %keep_ref.1) | copy-start | bytes 196
  1.6 13.8 %collective-permute-start = (bf16[256,512]{1,0:T(8,128)(2,1)}, bf16[256,512]{1,0:T(8,128)(2,1)S(1)}, u32[]{:S(2)}, u32[]{:S(2)}) collective-permute-start(bf16[256,512]{1,0:T(8,128)(2,1)} %weight_any.1), channel_id=1, source_target_pairs={{0,1},{1,0},{2,3},{3,2},{4,5},{5,4},{6,7},{7,6},{8,9},{9,8},{10,11... | collective-permute-start | bytes 786440 | tf_op jit(solution)/shard_map/ppermute | solution.py:29
  7.2 20.7 %all-to-all-start = ((f32[16,8,128]{2,1,0:T(8,128)}), f32[16,8,128]{2,1,0:T(8,128)S(1)}, u32[]{:S(2)}, u32[]{:S(2)}) async-start(f32[16,8,128]{2,1,0:T(8,128)} %pad_add_fusion.sent_ref), calls=%async_computation | async-start | bytes 131072 | tf_op jit(solution)/shard_map/all_to_all | solution.py:217
  15.5 19.4 %collective-permute-start.1 = (bf16[128,512]{1,0:T(8,128)(2,1)S(1)}, bf16[128,512]{1,0:T(8,128)(2,1)S(1)}, u32[]{:S(2)}, u32[]{:S(2)}) collective-permute-start(bf16[128,512]{1,0:T(8,128)(2,1)S(1)} %shard_map.102.cot_ref.first_ref), channel_id=1, source_target_pairs={{0,128},{128,0},{256,384},{384,256},{1,129},{129,1},{257,385},{385... | collective-permute-start | bytes 393224 | tf_op jit(solution)/shard_map/ppermute | solution.py:29
  21.5 22.2 %collective-permute-start.3 = (bf16[128,512]{1,0:T(8,128)(2,1)S(1)}, bf16[128,512]{1,0:T(8,128)(2,1)S(1)}, u32[]{:S(2)}, u32[]{:S(2)}) collective-permute-start(bf16[128,512]{1,0:T(8,128)(2,1)S(1)} %shard_map.102.cot_ref.first_ref), channel_id=1, source_target_pairs={{0,384},{128,256},{256,128},{384,0},{1,385},{129,257},{257,129},{3... | collective-permute-start | bytes 393224 | tf_op jit(solution)/shard_map/ppermute | solution.py:29
  30.1 24.3 %all-to-all-start.1 = ((bf16[4,320,512]{2,1,0:T(8,128)(2,1)}), bf16[4,320,512]{2,1,0:T(8,128)(2,1)S(1)}, u32[]{:S(2)}, u32[]{:S(2)}) async-start(bf16[4,320,512]{2,1,0:T(8,128)(2,1)} %get-tuple-element.14), calls=%async_computation.1 | async-start | bytes 2621440 | tf_op jit(solution)/shard_map/all_to_all | solution.py:238
  34.9 9.9 %collective-permute-start.4 = (bf16[128,512]{1,0:T(8,128)(2,1)S(1)}, bf16[128,512]{1,0:T(8,128)(2,1)S(1)}, u32[]{:S(2)}, u32[]{:S(2)}) collective-permute-start(bf16[128,512]{1,0:T(8,128)(2,1)S(1)} %shard_map.104.second_ref), channel_id=1, source_target_pairs={{0,384},{128,256},{256,128},{384,0},{1,385},{129,257},{257,129},{3... | collective-permute-start | bytes 393224 | tf_op jit(solution)/shard_map/ppermute | solution.py:29
  40.9 10.7 %collective-permute-start.2 = (bf16[2,128,512]{2,1,0:T(8,128)(2,1)S(1)}, bf16[2,128,512]{2,1,0:T(8,128)(2,1)S(1)}, u32[]{:S(2)}, u32[]{:S(2)}) collective-permute-start(bf16[2,128,512]{2,1,0:T(8,128)(2,1)S(1)} %shard_map.105.near_ref), channel_id=1, source_target_pairs={{0,1},{1,0},{2,3},{3,2},{4,5},{5,4},{6,7},{7,6},{8,9},{9,8},{10,11... | collective-permute-start | bytes 786440 | tf_op jit(solution)/shard_map/ppermute | solution.py:29
  44.8 9.7 %collective-permute-start.5 = (bf16[2,128,512]{2,1,0:T(8,128)(2,1)S(1)}, bf16[2,128,512]{2,1,0:T(8,128)(2,1)S(1)}, u32[]{:S(2)}, u32[]{:S(2)}) collective-permute-start(bf16[2,128,512]{2,1,0:T(8,128)(2,1)S(1)} %shard_map.106.last_ref), channel_id=1, source_target_pairs={{0,1},{1,0},{2,3},{3,2},{4,5},{5,4},{6,7},{7,6},{8,9},{9,8},{10,11... | collective-permute-start | bytes 786440 | tf_op jit(solution)/shard_map/ppermute | solution.py:29
  54.4 4.9 %collective-permute-start.6 = (bf16[4,320,512]{2,1,0:T(8,128)(2,1)S(1)}, bf16[4,320,512]{2,1,0:T(8,128)(2,1)S(1)}, u32[]{:S(2)}, u32[]{:S(2)}) collective-permute-start(bf16[4,320,512]{2,1,0:T(8,128)(2,1)S(1)} %shard_map.107.own_ref), channel_id=1, source_target_pairs={{0,16},{16,0},{1,17},{17,1},{2,18},{18,2},{3,19},{19,3},{4,20},{20... | collective-permute-start | bytes 3932168 | tf_op jit(solution)/shard_map/ppermute | solution.py:29
  61.6 43.0 %copy-start.1 = (bf16[8192,16]{0,1:T(8,128)(2,1)S(1)}, bf16[8192,16]{0,1:T(8,128)(2,1)}, u32[]{:S(2)}) copy-start(bf16[8192,16]{0,1:T(8,128)(2,1)} %param.10) | copy-start | bytes 786436
  61.6 43.0 %all-to-all-start.2 = ((bf16[64,8,1152]{2,1,0:T(8,128)(2,1)}), bf16[64,8,1152]{2,1,0:T(8,128)(2,1)S(1)}, u32[]{:S(2)}, u32[]{:S(2)}) async-start(bf16[64,8,1152]{2,1,0:T(8,128)(2,1)} %bitcast.4), calls=%async_computation.2 | async-start | bytes 2359296 | tf_op jit(solution)/shard_map/all_to_all | solution.py:257
  71.6 21.6 %collective-permute-start.7 = (bf16[16,512]{1,0:T(8,128)(2,1)S(1)}, bf16[16,512]{1,0:T(8,128)(2,1)S(1)}, u32[]{:S(2)}, u32[]{:S(2)}) collective-permute-start(bf16[16,512]{1,0:T(8,128)(2,1)S(1)} %convert_element_type.20), channel_id=1, source_target_pairs={{0,128},{128,0},{256,384},{384,256},{1,129},{129,1},{257,385},{385... | collective-permute-start | bytes 49160 | tf_op jit(solution)/shard_map/ppermute | solution.py:29
  75.9 17.2 %collective-permute-start.8 = (bf16[16,512]{1,0:T(8,128)(2,1)S(1)}, bf16[16,512]{1,0:T(8,128)(2,1)S(1)}, u32[]{:S(2)}, u32[]{:S(2)}) collective-permute-start(bf16[16,512]{1,0:T(8,128)(2,1)S(1)} %convert_element_type.20), channel_id=1, source_target_pairs={{0,256},{128,384},{256,0},{384,128},{1,257},{129,385},{257,1},{385... | collective-permute-start | bytes 49160 | tf_op jit(solution)/shard_map/ppermute | solution.py:29
  81.6 11.5 %collective-permute-start.9 = (bf16[16,512]{1,0:T(8,128)(2,1)S(1)}, bf16[16,512]{1,0:T(8,128)(2,1)S(1)}, u32[]{:S(2)}, u32[]{:S(2)}) collective-permute-start(bf16[16,512]{1,0:T(8,128)(2,1)S(1)} %convert_element_type.20), channel_id=1, source_target_pairs={{0,384},{128,256},{256,128},{384,0},{1,385},{129,257},{257,129},{3... | collective-permute-start | bytes 49160 | tf_op jit(solution)/shard_map/ppermute | solution.py:29

commit v15 on v14

--- a/solution.py
+++ b/solution.py
@@ -52,13 +52,27 @@
     )(a, *others)
 
 
-def stack_kernel(first_ref, second_ref, out_ref):
+def rank_kernel(mixed_ref, right_ref, projected_ref, out_ref):
+    out_ref[...] = jnp.zeros((16, 8, 128), f32)
+    out_ref[:, :, 16:32] = jnp.broadcast_to(projected_ref[...][None], (16, 8, 16))
+    out_ref[:, :, 0:16] = dot_t(mixed_ref[0:128, :], right_ref[...]).reshape(16, 8, 16)
+
+
+def pick_kernel(mixed_ref, after_ref, out_ref):
+    out_ref[...] = mixed_ref[0:128, :]
+
+
+def copy_kernel(in_ref, out_ref):
+    out_ref[...] = in_ref[...]
+
+
+def stack_kernel(first_ref, second_ref, after_ref, out_ref):
     out_ref[0] = first_ref[...]
     out_ref[1] = second_ref[...]
 
 
-def rows_of(first_ref, last_ref):
-    return jnp.concatenate([first_ref[...].reshape(256, 512), last_ref[...].reshape(256, 512)], axis=0)
+def rows_of(own, first_ref, last_ref):
+    return jnp.concatenate([own, first_ref[...], last_ref[...].reshape(256, 512)], axis=0)
 
 
 def pack_kernel(
@@ -66,7 +80,7 @@
     x_any, back_ref, rest_ref, out_sems,
 ):
     rows = pl.ds(pl.multiple_of(place_ref[1] * 128, 128), 128)
-    outs = [pltpu.make_async_copy(got_any.at[rows], x_any.at[x, 128:256], out_sems.at[x]) for x in range(4)]
+    outs = [pltpu.make_async_copy(got_any.at[128:256], x_any.at[x, 128:256], out_sems.at[x]) for x in range(4)]
     outs += [pltpu.make_async_copy(weight_any.at[rows], x_any.at[x, 0:128], out_sems.at[8 + x]) for x in range(4)]
     for copy in outs:
         copy.start()
@@ -133,9 +147,9 @@
 
 
 def own_kernel(
-    place_ref, own_ref, near_ref, last_ref, far_ref, far_last_ref, out_ref, terms_ref, right_ref
+    place_ref, own_ref, cot_ref, first_ref, last_ref, got_ref, far_ref, far_last_ref, out_ref, terms_ref, right_ref
 ):
-    parts = (rows_of(near_ref, last_ref), rows_of(far_ref, far_last_ref))
+    parts = (rows_of(cot_ref[...], first_ref, last_ref), rows_of(got_ref[0:128, :], far_ref, far_last_ref))
     out_ref[...] = products(parts, own_ref).reshape(4, 128, 512)
     terms, right_ref[...] = adapter_terms(own_ref, place_ref[0])
     for h in range(4):
@@ -143,7 +157,7 @@
 
 
 def other_kernel(
-    place_ref, done_ref, terms_ref, own_right_ref, other_ref, near_ref, last_ref, far_ref, far_last_ref,
+    place_ref, done_ref, terms_ref, own_right_ref, other_ref, cot_ref, first_ref, last_ref, got_ref, far_ref, far_last_ref,
     out_any, right_ref, out_ref, sems,
 ):
     z_high = place_ref[2]
@@ -154,8 +168,13 @@
         high = z.astype(bf16).astype(f32)
         out_ref[h, :, 1024:1152] = (high + pltpu.roll(z - high, 64, 1)).astype(bf16)
     copies = []
-    for half, (first, second) in enumerate(((near_ref, far_ref), (last_ref, far_last_ref))):
-        parts = (first[...].reshape(256, 512), second[...].reshape(256, 512))
+    for half in range(2):
+        if half == 0:
+            near = jnp.concatenate([cot_ref[...], first_ref[...]], axis=0)
+            far = jnp.concatenate([got_ref[0:128, :], far_ref[...]], axis=0)
+        else:
+            near, far = last_ref[...].reshape(256, 512), far_last_ref[...].reshape(256, 512)
+        parts = (near, far)
         total = products(parts, other_ref).reshape(2, 128, 512)
         for i in range(2):
             at = z_high ^ ((0, 1), (3, 2))[half][i]
@@ -168,11 +187,9 @@
 
 
 def final_kernel(
-    place_ref, back_ref, scaled_ref, left_any, keep_ref, inputs_any, grad_left_any, singular_any,
-    left_ref, inputs_ref, grad_left_ref, singular_ref, sems,
+    place_ref, back_ref, scaled_ref, left_ref, keep_ref, inputs_any, grad_left_any, singular_any,
+    inputs_ref, grad_left_ref, singular_ref, sems,
 ):
-    left_in = pltpu.make_async_copy(left_any, left_ref, sems.at[0])
-    left_in.start()
     core = place_ref[0]
     tail = jnp.sum(back_ref[:, :, 1024:].astype(f32), axis=0)
     tail = (tail + pltpu.roll(tail, 64, 1)) / n_dp
@@ -185,7 +202,6 @@
     ]
     outs[0].start()
     outs[1].start()
-    left_in.wait()
     scaled = scaled_ref[:, 0:16]
     for h in range(4):
         for low in range(2):
@@ -209,14 +225,17 @@
     place = jnp.stack([core, y_low, z_high]).astype(jnp.int32)
     shape = jax.ShapeDtypeStruct
 
-    got = swap(weight, "yl", 2, 1)
-
-    back_part = dot_t(cotangent, right_factor).reshape(16, 8, 16)
+    given = jnp.where(y_low == 0, weight[128:], weight[:128])
+    mixed = jnp.concatenate([cotangent, given], axis=0)
+    got = swap(mixed, "yl", 2, 1)
+
     own_projected = jnp.dot(inputs, left_factor, preferred_element_type=f32)
-    rank_out = jnp.pad(back_part, ((0, 0), (0, 0), (0, 112))) + jnp.pad(own_projected, ((0, 0), (16, 96)))
+    rank_out = call(rank_kernel, shape((16, 8, 128), f32), [in_vmem] * 3, 2 << 20, 1 << 20)(
+        mixed, right_factor, own_projected
+    )
     rank_in = lax.all_to_all(rank_out, ("zl", "yh", "yl"), 0, 0)
 
-    cot = after(cotangent, got)
+    cot = call(pick_kernel, shape((128, 512), bf16), [in_vmem, anywhere], 1, 1 << 18)(mixed, got)
     first, third = swap(cot, "zh", 4, 1), swap(cot, "zh", 4, 3)
 
     x_out, scaled_back = call(
@@ -229,10 +248,10 @@
         scratch=[pltpu.VMEM((4, 64, 512), bf16), dma((12,))],
     )(place, singular, keep_mask, rank_out, rank_in, cot, weight, got, inputs)
     first = after(first, scaled_back)
-    near = call(stack_kernel, shape((2, 128, 512), bf16), [in_vmem] * 2, 30 << 30, 1 << 20)(cot, first)
-    far = swap(near, "yl", 2, 1)
-    last = call(stack_kernel, shape((2, 128, 512), bf16), [in_vmem] * 2, 30 << 30, 1 << 20)(
-        third, swap(first, "zh", 4, 3)
+    held = call(copy_kernel, shape((128, 512), bf16), [in_vmem], 30 << 30, 1 << 18)(first)
+    far = call(copy_kernel, shape((128, 512), bf16), [in_vmem], 30 << 30, 1 << 18)(swap(held, "yl", 2, 1))
+    last = call(stack_kernel, shape((2, 128, 512), bf16), [in_vmem] * 2 + [anywhere], 30 << 30, 1 << 20)(
+        third, swap(first, "zh", 4, 3), held
     )
     far_last = swap(last, "yl", 2, 1)
     x_in = after(lax.all_to_all(x_out, "x", 0, 0), far, far_last)
@@ -241,19 +260,19 @@
     done, terms, own_right = call(
         own_kernel,
         (shape((4, 128, 512), bf16), shape((4, 128, 128), f32), shape((16, 512), f32)),
-        [in_smem] + [in_vmem] * 5,
+        [in_smem] + [in_vmem] * 7,
         1 << 29,
         3 << 20,
-    )(place, x_in, near, last, far, far_last)
+    )(place, x_in, cot, held, last, got, far, far_last)
     out, right_part = call(
         other_kernel,
         (shape((4, 128, 1152), bf16), shape((16, 512), f32)),
-        [in_smem] + [in_vmem] * 8,
+        [in_smem] + [in_vmem] * 10,
         1 << 29,
         5 << 20,
         out_specs=(in_hbm, in_vmem),
         scratch=[pltpu.VMEM((4, 128, 1152), bf16), dma((4,))],
-    )(place, done, terms, own_right, x_other, near, last, far, far_last)
+    )(place, done, terms, own_right, x_other, cot, held, last, got, far, far_last)
     back = lax.all_to_all(out.reshape(64, 8, 1152), ("zh", "zl", "yh", "yl"), 0, 0)
     right_sent = right_part.astype(bf16)
     right_sum = right_part + sum(swap(right_sent, "zh", 4, k).astype(f32) for k in (1, 2, 3))
@@ -261,12 +280,11 @@
     grad_inputs, grad_left, grad_singular = call(
         final_kernel,
         (shape((8, 8192), bf16), shape((16, 16), f32), shape((1, 16), f32)),
-        [in_smem, in_vmem, in_vmem, in_hbm, in_vmem],
+        [in_smem] + [in_vmem] * 4,
         2 << 20,
         2 << 20,
         out_specs=(in_hbm, in_hbm, in_hbm),
         scratch=[
-            pltpu.VMEM((16, 8192), bf16),
             pltpu.VMEM((8, 8192), bf16),
             pltpu.VMEM((16, 16), f32),
             pltpu.VMEM((1, 16), f32),

time: 107 us -> 107 us (level)
  waiting for transfers between devices: 29.4 us -> 28 us
  other arithmetic: 1.37 us -> 2.66 us
    ppermute x10, waiting for transfers between devices: 18.6 us -> 17.1 us  [swap(): return lax.ppermute(a, axis, [(i, i ^ mask) for i in range(count)])]
  transfers between devices with their start and end apart: 13 -> 13, of which waited for: 6 -> 6; matrix products, arithmetic and copies ran while one was open for 3% -> 2% of each run, Pallas kernels for 3% -> 4%
where the time goes in v15:
time: 107 us; the launch traced here: 106 us
  starting transfers between devices  65.5 us (61%)
  waiting for transfers between devices  28 us (26%)
  Pallas kernels  8.11 us (8%)
  other arithmetic  2.66 us (2%)
  matrix products  1.21 us (1%)
    ppermute x10, starting transfers between devices, swap(): return lax.ppermute(a, axis, [(i, i ^ mask) for i in range(count)])  42 us
    ppermute x10, waiting for transfers between devices, swap(): return lax.ppermute(a, axis, [(i, i ^ mask) for i in range(count)])  17.1 us
    all_to_all x1, waiting for transfers between devices, body(): lax.all_to_all(out.reshape(64, 8, 1152), ('zh', 'zl', 'yh', 'yl'), 0, 0)  10.8 us
    all_to_all x1, starting transfers between devices, body(): lax.all_to_all(out.reshape(64, 8, 1152), ('zh', 'zl', 'yh', 'yl'), 0, 0)  10.6 us
    all_to_all x1, starting transfers between devices, body(): rank_in = lax.all_to_all(rank_out, ('zl', 'yh', 'yl'), 0, 0)  8.11 us
    all_to_all x1, starting transfers between devices, body(): x_in = after(lax.all_to_all(x_out, 'x', 0, 0), far, far_last)  4.78 us
    pallas_call x1, Pallas kernels, body(): call(other_kernel, (shape((4, 128, 1152), bf16), shape((16, 512), f32)),...  2.26 us
  transfers between devices with their start and end apart: 13, of which 6 were waited for; matrix products, arithmetic and copies ran while one was open for 2% of the time, Pallas kernels for 4%

profile of v15, /device:TPU:6, one launch (start us, length us, event | category | flops | bytes accessed | tf_op | source)
XLA Modules:
  0.0 106.4 jit_solution(12094318013525211323)
XLA Ops:
  0.6 0.0 copy-start.1
  0.6 0.0 copy-start.2
  0.7 0.0 copy-start.3
  0.7 0.0 copy-start.4
  0.7 0.0 copy-start.5
  0.7 1.0 slice_select_fusion
  1.7 0.9 pad_maximum_fusion.mixed_ref
  2.6 3.5 %collective-permute-start = (bf16[256,512]{1,0:T(8,128)(2,1)S(1)}, bf16[256,512]{1,0:T(8,128)(2,1)S(1)}, u32[]{:S(2)}, u32[]{:S(2)}) collective-permute-start(bf16[256,512]{1,0:T(8,128)(2,1)S(1)} %pad_maximum_fusion.mixed_ref), channel_id=1, source_target_pairs={{0,1},{1,0},{2,3},{3,2},{4,5},{5,4},{6,7},{7,6},{8,9},{9,8},{10,11... | collective-permute-start | bytes 786440 | tf_op jit(solution)/shard_map/ppermute | solution.py:29
  6.1 1.2 %fusion.projected_ref = f32[8,16]{1,0:T(8,128)S(1)} fusion(bf16[8,8192]{1,0:T(8,128)(2,1)} %inputs_ref.1, bf16[8192,16]{0,1:T(8,128)(2,1)} %param.10), kind=kOutput, calls=%fused_computation.5 | convolution fusion | flops 2097152 | bytes 393728 | tf_op jit(solution)/shard_map/dot_general | solution.py:232
  7.4 0.0 copy-done.3
  7.4 0.8 shard_map.102.sent_ref
  8.2 8.1 %all-to-all-start = ((f32[16,8,128]{2,1,0:T(8,128)}), f32[16,8,128]{2,1,0:T(8,128)S(1)}, u32[]{:S(2)}, u32[]{:S(2)}) async-start(f32[16,8,128]{2,1,0:T(8,128)} %shard_map.102.sent_ref), calls=%async_computation | async-start | bytes 131072 | tf_op jit(solution)/shard_map/all_to_all | solution.py:236
  16.3 0.1 pad_add_fusion.place_ref
  16.4 0.0 collective-permute-done.after_ref.got_any.got_ref
  16.4 6.1 %collective-permute-start.1 = (bf16[128,512]{1,0:T(8,128)(2,1)S(1)}, bf16[128,512]{1,0:T(8,128)(2,1)S(1)}, u32[]{:S(2)}, u32[]{:S(2)}) collective-permute-start(bf16[128,512]{1,0:T(8,128)(2,1)S(1)} %shard_map.103.cot_ref), channel_id=1, source_target_pairs={{0,128},{128,0},{256,384},{384,256},{1,129},{129,1},{257,385},{385... | collective-permute-start | bytes 393224 | tf_op jit(solution)/shard_map/ppermute | solution.py:29
  22.5 6.4 %collective-permute-start.3 = (bf16[128,512]{1,0:T(8,128)(2,1)S(1)}, bf16[128,512]{1,0:T(8,128)(2,1)S(1)}, u32[]{:S(2)}, u32[]{:S(2)}) collective-permute-start(bf16[128,512]{1,0:T(8,128)(2,1)S(1)} %shard_map.103.cot_ref), channel_id=1, source_target_pairs={{0,384},{128,256},{256,128},{384,0},{1,385},{129,257},{257,129},{3... | collective-permute-start | bytes 393224 | tf_op jit(solution)/shard_map/ppermute | solution.py:29
  28.9 0.0 all-to-all-done.rank_ref
  28.9 0.0 copy-done.1
  28.9 0.0 copy-done.2
  28.9 0.0 copy-done.4
  28.9 0.0 copy-done.5
  28.9 2.1 %shard_map.104 = (bf16[4,320,512]{2,1,0:T(8,128)(2,1)}, bf16[8,128]{1,0:T(8,128)(2,1)S(1)}) custom-call(s32[3]{0:T(128)S(1)} %pad_add_fusion.place_ref, f32[16]{0:T(128)S(1)} %copy-done.4, s32[16]{0:T(128)S(1)} %copy-done.5, f32[16,8,128]{2,1,0:T(8,128)} %shard_map.102.sent_ref, f32[16,8,128]{2,1,0:T(8,128)S(1)} %all-to-all-done.rank_ref, ...), custom_call_target="tpu_custom_call" | custom-call | flops 32212254720 | bytes 3145728 | tf_op jit(solution)/shard_map/pallas_call | solution.py:241
  31.0 4.8 %all-to-all-start.1 = ((bf16[4,320,512]{2,1,0:T(8,128)(2,1)}), bf16[4,320,512]{2,1,0:T(8,128)(2,1)S(1)}, u32[]{:S(2)}, u32[]{:S(2)}) async-start(bf16[4,320,512]{2,1,0:T(8,128)(2,1)} %get-tuple-element.14), calls=%async_computation.1 | async-start | bytes 2621440 | tf_op jit(solution)/shard_map/all_to_all | solution.py:257
  35.8 0.0 collective-permute-done.1.refs_0_
  35.8 6.0 %collective-permute-start.4 = (bf16[128,512]{1,0:T(8,128)(2,1)S(1)}, bf16[128,512]{1,0:T(8,128)(2,1)S(1)}, u32[]{:S(2)}, u32[]{:S(2)}) collective-permute-start(bf16[128,512]{1,0:T(8,128)(2,1)S(1)} %shard_map.105.in_ref), channel_id=1, source_target_pairs={{0,384},{128,256},{256,128},{384,0},{1,385},{129,257},{257,129},{3... | collective-permute-start | bytes 393224 | tf_op jit(solution)/shard_map/ppermute | solution.py:29
  41.8 2.9 %collective-permute-start.2 = (bf16[128,512]{1,0:T(8,128)(2,1)S(1)}, bf16[128,512]{1,0:T(8,128)(2,1)S(1)}, u32[]{:S(2)}, u32[]{:S(2)}) collective-permute-start(bf16[128,512]{1,0:T(8,128)(2,1)S(1)} %shard_map.106.after_ref.first_ref), channel_id=1, source_target_pairs={{0,1},{1,0},{2,3},{3,2},{4,5},{5,4},{6,7},{7,6},{8,9},{9,8},{10,11... | collective-permute-start | bytes 393224 | tf_op jit(solution)/shard_map/ppermute | solution.py:29
  44.7 0.0 collective-permute-done.3.first_ref
  44.7 1.0 collective-permute-done.4.second_ref
  45.7 3.0 %collective-permute-start.5 = (bf16[2,128,512]{2,1,0:T(8,128)(2,1)S(1)}, bf16[2,128,512]{2,1,0:T(8,128)(2,1)S(1)}, u32[]{:S(2)}, u32[]{:S(2)}) collective-permute-start(bf16[2,128,512]{2,1,0:T(8,128)(2,1)S(1)} %shard_map.108.last_ref), channel_id=1, source_target_pairs={{0,1},{1,0},{2,3},{3,2},{4,5},{5,4},{6,7},{7,6},{8,9},{9,8},{10,11... | collective-permute-start | bytes 786440 | tf_op jit(solution)/shard_map/ppermute | solution.py:29
  48.7 1.3 %collective-permute-done.2.in_ref = bf16[128,512]{1,0:T(8,128)(2,1)S(1)} collective-permute-done((bf16[128,512]{1,0:T(8,128)(2,1)S(1)}, bf16[128,512]{1,0:T(8,128)(2,1)S(1)}, u32[]{:S(2)}, u32[]{:S(2)}) %collective-permute-start.2) | collective-permute-done | bytes 131104 | tf_op jit(solution)/shard_map/ppermute | solution.py:29
  50.1 3.9 %collective-permute-done.5.refs_2_.far_last_ref = bf16[2,128,512]{2,1,0:T(8,128)(2,1)S(1)} collective-permute-done((bf16[2,128,512]{2,1,0:T(8,128)(2,1)S(1)}, bf16[2,128,512]{2,1,0:T(8,128)(2,1)S(1)}, u32[]{:S(2)}, u32[]{:S(2)}) %collective-permute-start.5) | collective-permute-done | bytes 262176 | tf_op jit(solution)/shard_map/ppermute | solution.py:29
  53.9 0.0 all-to-all-done.1.refs_0_
  54.0 1.9 %collective-permute-start.6 = (bf16[4,320,512]{2,1,0:T(8,128)(2,1)S(1)}, bf16[4,320,512]{2,1,0:T(8,128)(2,1)S(1)}, u32[]{:S(2)}, u32[]{:S(2)}) collective-permute-start(bf16[4,320,512]{2,1,0:T(8,128)(2,1)S(1)} %shard_map.109.own_ref), channel_id=1, source_target_pairs={{0,16},{16,0},{1,17},{17,1},{2,18},{18,2},{3,19},{19,3},{4,20},{20... | collective-permute-start | bytes 3932168 | tf_op jit(solution)/shard_map/ppermute | solution.py:29
  55.9 1.4 %shard_map.110 = (bf16[4,128,512]{2,1,0:T(8,128)(2,1)S(1)}, f32[4,128,128]{2,1,0:T(8,128)S(1)}, f32[16,512]{1,0:T(8,128)S(1)}) custom-call(s32[3]{0:T(128)S(1)} %pad_add_fusion.place_ref, bf16[4,320,512]{2,1,0:T(8,128)(2,1)S(1)} %shard_map.109.own_ref, bf16[128,512]{1,0:T(8,128)(2,1)S(1)} %shard_map.103.cot_ref, ...), custom_call_target="tpu_custom_call" | custom-call | flops 536870912 | bytes 3145728 | tf_op jit(solution)/shard_map/pallas_call | solution.py:260
  57.3 1.6 %collective-permute-done.6.other_ref = bf16[4,320,512]{2,1,0:T(8,128)(2,1)S(1)} collective-permute-done((bf16[4,320,512]{2,1,0:T(8,128)(2,1)S(1)}, bf16[4,320,512]{2,1,0:T(8,128)(2,1)S(1)}, u32[]{:S(2)}, u32[]{:S(2)}) %collective-permute-start.6) | collective-permute-done | bytes 1310752 | tf_op jit(solution)/shard_map/ppermute | solution.py:29
  58.9 2.3 %shard_map.111 = (bf16[4,128,1152]{2,1,0:T(8,128)(2,1)}, f32[16,512]{1,0:T(8,128)S(1)}) custom-call(s32[3]{0:T(128)S(1)} %pad_add_fusion.place_ref, bf16[4,128,512]{2,1,0:T(8,128)(2,1)S(1)} %get-tuple-element.16.done_ref, f32[4,128,128]{2,1,0:T(8,128)S(1)} %get-tuple-element.17.terms_ref, f32[16,512]{1,0:T(8,128)S(1)} %get-tuple-element.18.own_right_ref, ...), custom_call_target="tpu_custom_call" | custom-call | flops 536870912 | bytes 5242880 | tf_op jit(solution)/shard_map/pallas_call | solution.py:267
  61.1 0.0 copy-start
  61.2 10.6 %all-to-all-start.2 = ((bf16[64,8,1152]{2,1,0:T(8,128)(2,1)}), bf16[64,8,1152]{2,1,0:T(8,128)(2,1)S(1)}, u32[]{:S(2)}, u32[]{:S(2)}) async-start(bf16[64,8,1152]{2,1,0:T(8,128)(2,1)} %bitcast.3), calls=%async_computation.2 | async-start | bytes 2359296 | tf_op jit(solution)/shard_map/all_to_all | solution.py:276
  71.8 4.4 %collective-permute-start.7 = (bf16[16,512]{1,0:T(8,128)(2,1)S(1)}, bf16[16,512]{1,0:T(8,128)(2,1)S(1)}, u32[]{:S(2)}, u32[]{:S(2)}) collective-permute-start(bf16[16,512]{1,0:T(8,128)(2,1)S(1)} %convert_element_type.16), channel_id=1, source_target_pairs={{0,128},{128,0},{256,384},{384,256},{1,129},{129,1},{257,385},{385... | collective-permute-start | bytes 49160 | tf_op jit(solution)/shard_map/ppermute | solution.py:29
  76.2 5.7 %collective-permute-start.8 = (bf16[16,512]{1,0:T(8,128)(2,1)S(1)}, bf16[16,512]{1,0:T(8,128)(2,1)S(1)}, u32[]{:S(2)}, u32[]{:S(2)}) collective-permute-start(bf16[16,512]{1,0:T(8,128)(2,1)S(1)} %convert_element_type.16), channel_id=1, source_target_pairs={{0,256},{128,384},{256,0},{384,128},{1,257},{129,385},{257,1},{385... | collective-permute-start | bytes 49160 | tf_op jit(solution)/shard_map/ppermute | solution.py:29
  81.8 2.2 %collective-permute-start.9 = (bf16[16,512]{1,0:T(8,128)(2,1)S(1)}, bf16[16,512]{1,0:T(8,128)(2,1)S(1)}, u32[]{:S(2)}, u32[]{:S(2)}) collective-permute-start(bf16[16,512]{1,0:T(8,128)(2,1)S(1)} %convert_element_type.16), channel_id=1, source_target_pairs={{0,384},{128,256},{256,128},{384,0},{1,385},{129,257},{257,129},{3... | collective-permute-start | bytes 49160 | tf_op jit(solution)/shard_map/ppermute | solution.py:29
  84.0 9.3 %collective-permute-done.7 = bf16[16,512]{1,0:T(8,128)(2,1)S(1)} collective-permute-done((bf16[16,512]{1,0:T(8,128)(2,1)S(1)}, bf16[16,512]{1,0:T(8,128)(2,1)S(1)}, u32[]{:S(2)}, u32[]{:S(2)}) %collective-permute-start.7) | collective-permute-done | bytes 16416 | tf_op jit(solution)/shard_map/ppermute | solution.py:29
  93.4 0.0 collective-permute-done.8
  93.4 0.0 collective-permute-done.9
  93.4 0.6 add_multiply_fusion
  94.0 10.8 %all-to-all-done.2.back_ref = bf16[64,8,1152]{2,1,0:T(8,128)(2,1)S(1)} async-done(((bf16[64,8,1152]{2,1,0:T(8,128)(2,1)}), bf16[64,8,1152]{2,1,0:T(8,128)(2,1)S(1)}, u32[]{:S(2)}, u32[]{:S(2)}) %all-to-all-start.2) | async-done | bytes 1179680 | tf_op jit(solution)/shard_map/all_to_all | solution.py:276
  104.8 0.0 copy-done
  104.8 1.5 %shard_map.112 = (bf16[8,8192]{1,0:T(8,128)(2,1)}, f32[16,16]{1,0:T(8,128)}, f32[1,16]{1,0:T(1,128)}) custom-call(s32[3]{0:T(128)S(1)} %pad_add_fusion.place_ref, bf16[64,8,1152]{2,1,0:T(8,128)(2,1)S(1)} %all-to-all-done.2.back_ref, bf16[8,128]{1,0:T(8,128)(2,1)S(1)} %get-tuple-element.15.refs_1_.scaled_ref, bf16[16,8192]{1,0:T(8,128)(2,1)S(1)} %bitcast.10, ...), custom_call_target="tpu_custom_call" | custom-call | flops 2097152 | bytes 2097152 | tf_op jit(solution)/shard_map/pallas_call | solution.py:280
  (8 shorter events, 0.1 us)
Async XLA Ops:
  0.6 28.3 %copy-start.1 = (bf16[256,512]{1,0:T(8,128)(2,1)S(1)}, bf16[256,512]{1,0:T(8,128)(2,1)}, u32[]{:S(2)}) copy-start(bf16[256,512]{1,0:T(8,128)(2,1)} %weight_any.1) | copy-start | bytes 786436
  0.6 28.3 %copy-start.2 = (bf16[8,8192]{1,0:T(8,128)(2,1)S(1)}, bf16[8,8192]{1,0:T(8,128)(2,1)}, u32[]{:S(2)}) copy-start(bf16[8,8192]{1,0:T(8,128)(2,1)} %inputs_ref.1) | copy-start | bytes 393220
  0.7 6.7 %copy-start.3 = (bf16[16,512]{1,0:T(8,128)(2,1)S(1)}, bf16[16,512]{1,0:T(8,128)(2,1)}, u32[]{:S(2)}) copy-start(bf16[16,512]{1,0:T(8,128)(2,1)} %right_ref.1) | copy-start | bytes 49156
  0.7 28.3 %copy-start.4 = (f32[16]{0:T(128)S(1)}, f32[16]{0:T(128)}, u32[]{:S(2)}) copy-start(f32[16]{0:T(128)} %singular_ref.1) | copy-start | bytes 196
  0.7 28.3 %copy-start.5 = (s32[16]{0:T(128)S(1)}, s32[16]{0:T(128)}, u32[]{:S(2)}) copy-start(s32[16]{0:T(128)} %keep_ref.1) | copy-start | bytes 196
  2.6 13.7 %collective-permute-start = (bf16[256,512]{1,0:T(8,128)(2,1)S(1)}, bf16[256,512]{1,0:T(8,128)(2,1)S(1)}, u32[]{:S(2)}, u32[]{:S(2)}) collective-permute-start(bf16[256,512]{1,0:T(8,128)(2,1)S(1)} %pad_maximum_fusion.mixed_ref), channel_id=1, source_target_pairs={{0,1},{1,0},{2,3},{3,2},{4,5},{5,4},{6,7},{7,6},{8,9},{9,8},{10,11... | collective-permute-start | bytes 786440 | tf_op jit(solution)/shard_map/ppermute | solution.py:29
  8.2 20.7 %all-to-all-start = ((f32[16,8,128]{2,1,0:T(8,128)}), f32[16,8,128]{2,1,0:T(8,128)S(1)}, u32[]{:S(2)}, u32[]{:S(2)}) async-start(f32[16,8,128]{2,1,0:T(8,128)} %shard_map.102.sent_ref), calls=%async_computation | async-start | bytes 131072 | tf_op jit(solution)/shard_map/all_to_all | solution.py:236
  16.4 19.4 %collective-permute-start.1 = (bf16[128,512]{1,0:T(8,128)(2,1)S(1)}, bf16[128,512]{1,0:T(8,128)(2,1)S(1)}, u32[]{:S(2)}, u32[]{:S(2)}) collective-permute-start(bf16[128,512]{1,0:T(8,128)(2,1)S(1)} %shard_map.103.cot_ref), channel_id=1, source_target_pairs={{0,128},{128,0},{256,384},{384,256},{1,129},{129,1},{257,385},{385... | collective-permute-start | bytes 393224 | tf_op jit(solution)/shard_map/ppermute | solution.py:29
  22.5 22.2 %collective-permute-start.3 = (bf16[128,512]{1,0:T(8,128)(2,1)S(1)}, bf16[128,512]{1,0:T(8,128)(2,1)S(1)}, u32[]{:S(2)}, u32[]{:S(2)}) collective-permute-start(bf16[128,512]{1,0:T(8,128)(2,1)S(1)} %shard_map.103.cot_ref), channel_id=1, source_target_pairs={{0,384},{128,256},{256,128},{384,0},{1,385},{129,257},{257,129},{3... | collective-permute-start | bytes 393224 | tf_op jit(solution)/shard_map/ppermute | solution.py:29
  31.0 22.9 %all-to-all-start.1 = ((bf16[4,320,512]{2,1,0:T(8,128)(2,1)}), bf16[4,320,512]{2,1,0:T(8,128)(2,1)S(1)}, u32[]{:S(2)}, u32[]{:S(2)}) async-start(bf16[4,320,512]{2,1,0:T(8,128)(2,1)} %get-tuple-element.14), calls=%async_computation.1 | async-start | bytes 2621440 | tf_op jit(solution)/shard_map/all_to_all | solution.py:257
  35.8 9.9 %collective-permute-start.4 = (bf16[128,512]{1,0:T(8,128)(2,1)S(1)}, bf16[128,512]{1,0:T(8,128)(2,1)S(1)}, u32[]{:S(2)}, u32[]{:S(2)}) collective-permute-start(bf16[128,512]{1,0:T(8,128)(2,1)S(1)} %shard_map.105.in_ref), channel_id=1, source_target_pairs={{0,384},{128,256},{256,128},{384,0},{1,385},{129,257},{257,129},{3... | collective-permute-start | bytes 393224 | tf_op jit(solution)/shard_map/ppermute | solution.py:29
  41.8 8.3 %collective-permute-start.2 = (bf16[128,512]{1,0:T(8,128)(2,1)S(1)}, bf16[128,512]{1,0:T(8,128)(2,1)S(1)}, u32[]{:S(2)}, u32[]{:S(2)}) collective-permute-start(bf16[128,512]{1,0:T(8,128)(2,1)S(1)} %shard_map.106.after_ref.first_ref), channel_id=1, source_target_pairs={{0,1},{1,0},{2,3},{3,2},{4,5},{5,4},{6,7},{7,6},{8,9},{9,8},{10,11... | collective-permute-start | bytes 393224 | tf_op jit(solution)/shard_map/ppermute | solution.py:29
  45.7 8.3 %collective-permute-start.5 = (bf16[2,128,512]{2,1,0:T(8,128)(2,1)S(1)}, bf16[2,128,512]{2,1,0:T(8,128)(2,1)S(1)}, u32[]{:S(2)}, u32[]{:S(2)}) collective-permute-start(bf16[2,128,512]{2,1,0:T(8,128)(2,1)S(1)} %shard_map.108.last_ref), channel_id=1, source_target_pairs={{0,1},{1,0},{2,3},{3,2},{4,5},{5,4},{6,7},{7,6},{8,9},{9,8},{10,11... | collective-permute-start | bytes 786440 | tf_op jit(solution)/shard_map/ppermute | solution.py:29
  54.0 4.9 %collective-permute-start.6 = (bf16[4,320,512]{2,1,0:T(8,128)(2,1)S(1)}, bf16[4,320,512]{2,1,0:T(8,128)(2,1)S(1)}, u32[]{:S(2)}, u32[]{:S(2)}) collective-permute-start(bf16[4,320,512]{2,1,0:T(8,128)(2,1)S(1)} %shard_map.109.own_ref), channel_id=1, source_target_pairs={{0,16},{16,0},{1,17},{17,1},{2,18},{18,2},{3,19},{19,3},{4,20},{20... | collective-permute-start | bytes 3932168 | tf_op jit(solution)/shard_map/ppermute | solution.py:29
  61.1 43.7 %copy-start = (bf16[8192,16]{0,1:T(8,128)(2,1)S(1)}, bf16[8192,16]{0,1:T(8,128)(2,1)}, u32[]{:S(2)}) copy-start(bf16[8192,16]{0,1:T(8,128)(2,1)} %param.10) | copy-start | bytes 786436
  61.2 43.7 %all-to-all-start.2 = ((bf16[64,8,1152]{2,1,0:T(8,128)(2,1)}), bf16[64,8,1152]{2,1,0:T(8,128)(2,1)S(1)}, u32[]{:S(2)}, u32[]{:S(2)}) async-start(bf16[64,8,1152]{2,1,0:T(8,128)(2,1)} %bitcast.3), calls=%async_computation.2 | async-start | bytes 2359296 | tf_op jit(solution)/shard_map/all_to_all | solution.py:276
  71.8 21.6 %collective-permute-start.7 = (bf16[16,512]{1,0:T(8,128)(2,1)S(1)}, bf16[16,512]{1,0:T(8,128)(2,1)S(1)}, u32[]{:S(2)}, u32[]{:S(2)}) collective-permute-start(bf16[16,512]{1,0:T(8,128)(2,1)S(1)} %convert_element_type.16), channel_id=1, source_target_pairs={{0,128},{128,0},{256,384},{384,256},{1,129},{129,1},{257,385},{385... | collective-permute-start | bytes 49160 | tf_op jit(solution)/shard_map/ppermute | solution.py:29
  76.2 17.2 %collective-permute-start.8 = (bf16[16,512]{1,0:T(8,128)(2,1)S(1)}, bf16[16,512]{1,0:T(8,128)(2,1)S(1)}, u32[]{:S(2)}, u32[]{:S(2)}) collective-permute-start(bf16[16,512]{1,0:T(8,128)(2,1)S(1)} %convert_element_type.16), channel_id=1, source_target_pairs={{0,256},{128,384},{256,0},{384,128},{1,257},{129,385},{257,1},{385... | collective-permute-start | bytes 49160 | tf_op jit(solution)/shard_map/ppermute | solution.py:29
  81.8 11.5 %collective-permute-start.9 = (bf16[16,512]{1,0:T(8,128)(2,1)S(1)}, bf16[16,512]{1,0:T(8,128)(2,1)S(1)}, u32[]{:S(2)}, u32[]{:S(2)}) collective-permute-start(bf16[16,512]{1,0:T(8,128)(2,1)S(1)} %convert_element_type.16), channel_id=1, source_target_pairs={{0,384},{128,256},{256,128},{384,0},{1,385},{129,257},{257,129},{3... | collective-permute-start | bytes 49160 | tf_op jit(solution)/shard_map/ppermute | solution.py:29

commit v16 on v15

--- a/solution.py
+++ b/solution.py
@@ -77,13 +77,19 @@
 
 def pack_kernel(
     place_ref, singular_ref, keep_ref, sent_ref, rank_ref, cot_ref, weight_any, got_any, inputs_ref,
-    x_any, back_ref, rest_ref, out_sems,
+    x_any, back_ref, slices_ref, rest_ref, out_sems,
 ):
     rows = pl.ds(pl.multiple_of(place_ref[1] * 128, 128), 128)
     outs = [pltpu.make_async_copy(got_any.at[128:256], x_any.at[x, 128:256], out_sems.at[x]) for x in range(4)]
     outs += [pltpu.make_async_copy(weight_any.at[rows], x_any.at[x, 0:128], out_sems.at[8 + x]) for x in range(4)]
     for copy in outs:
         copy.start()
+    inputs = inputs_ref[...].astype(f32)
+    for x in range(4):
+        parts = [inputs[:, (h * 4 + x) * 512 : (h * 4 + x + 1) * 512] for h in range(4)]
+        slices_ref[x] = jnp.concatenate(parts, axis=0).astype(bf16)
+        outs.append(pltpu.make_async_copy(slices_ref.at[x], x_any.at[x, 256:288], out_sems.at[4 + x]))
+        outs[-1].start()
     lane = lax.broadcasted_iota(jnp.int32, (1, 128), 1)
     rank = rank_ref[...]
     coeff = jnp.zeros((1, 128), f32)
@@ -107,13 +113,10 @@
         ],
         axis=0,
     ).astype(bf16)
-    inputs = inputs_ref[...].astype(f32)
+    rest_ref[0:16, :] = small
+    rest_ref[16:32, :] = right.astype(bf16)
     for x in range(4):
-        parts = [inputs[:, (h * 4 + x) * 512 : (h * 4 + x + 1) * 512] for h in range(4)]
-        rest_ref[x, 0:32, :] = jnp.concatenate(parts, axis=0).astype(bf16)
-        rest_ref[x, 32:48, :] = small
-        rest_ref[x, 48:64, :] = right.astype(bf16)
-        outs.append(pltpu.make_async_copy(rest_ref.at[x], x_any.at[x, 256:320], out_sems.at[4 + x]))
+        outs.append(pltpu.make_async_copy(rest_ref, x_any.at[x, 288:320], out_sems.at[12 + x]))
         outs[-1].start()
     for copy in outs:
         copy.wait()
@@ -225,8 +228,8 @@
     place = jnp.stack([core, y_low, z_high]).astype(jnp.int32)
     shape = jax.ShapeDtypeStruct
 
-    given = jnp.where(y_low == 0, weight[128:], weight[:128])
-    mixed = jnp.concatenate([cotangent, given], axis=0)
+    both = jnp.concatenate([cotangent, weight], axis=0)
+    mixed = jnp.where(y_low == 0, jnp.concatenate([both[:128], both[256:]]), both[:256])
     got = swap(mixed, "yl", 2, 1)
 
     own_projected = jnp.dot(inputs, left_factor, preferred_element_type=f32)
@@ -245,7 +248,7 @@
         30 << 30,
         3 << 20,
         out_specs=(in_hbm, in_vmem),
-        scratch=[pltpu.VMEM((4, 64, 512), bf16), dma((12,))],
+        scratch=[pltpu.VMEM((4, 32, 512), bf16), pltpu.VMEM((32, 512), bf16), dma((16,))],
     )(place, singular, keep_mask, rank_out, rank_in, cot, weight, got, inputs)
     first = after(first, scaled_back)
     held = call(copy_kernel, shape((128, 512), bf16), [in_vmem], 30 << 30, 1 << 18)(first)

time: 107 us -> 107 us (level)
  no operation moved by 1% of the time
where the time goes in v16:
time: 107 us; the launch traced here: 106 us
  starting transfers between devices  65.4 us (61%)
  waiting for transfers between devices  28 us (26%)
  Pallas kernels  8.15 us (8%)
  other arithmetic  1.72 us (2%)
  matrix products  1.21 us (1%)
    ppermute x10, starting transfers between devices, swap(): return lax.ppermute(a, axis, [(i, i ^ mask) for i in range(count)])  42 us
    ppermute x10, waiting for transfers between devices, swap(): return lax.ppermute(a, axis, [(i, i ^ mask) for i in range(count)])  17.1 us
    all_to_all x1, waiting for transfers between devices, body(): lax.all_to_all(out.reshape(64, 8, 1152), ('zh', 'zl', 'yh', 'yl'), 0, 0)  10.9 us
    all_to_all x1, starting transfers between devices, body(): lax.all_to_all(out.reshape(64, 8, 1152), ('zh', 'zl', 'yh', 'yl'), 0, 0)  10.6 us
    all_to_all x1, starting transfers between devices, body(): rank_in = lax.all_to_all(rank_out, ('zl', 'yh', 'yl'), 0, 0)  8.11 us
    all_to_all x1, starting transfers between devices, body(): x_in = after(lax.all_to_all(x_out, 'x', 0, 0), far, far_last)  4.78 us
    pallas_call x1, Pallas kernels, body(): call(other_kernel, (shape((4, 128, 1152), bf16), shape((16, 512), f32)),...  2.26 us
  transfers between devices with their start and end apart: 13, of which 6 were waited for; matrix products, arithmetic and copies ran while one was open for 2% of the time, Pallas kernels for 4%

profile of v16, /device:TPU:6, one launch (start us, length us, event | category | flops | bytes accessed | tf_op | source)
XLA Modules:
  0.0 106.4 jit_solution(17277937659411458446)
XLA Ops:
  0.6 0.0 copy-start.1
  0.6 0.0 copy-start.2
  0.7 0.0 copy-start.3
  0.7 0.0 copy-start.4
  0.7 0.0 copy-start.5
  0.7 1.0 slice.6
  1.7 1.0 fusion.mixed_ref
  2.7 3.5 %collective-permute-start = (bf16[256,512]{1,0:T(8,128)(2,1)S(1)}, bf16[256,512]{1,0:T(8,128)(2,1)S(1)}, u32[]{:S(2)}, u32[]{:S(2)}) collective-permute-start(bf16[256,512]{1,0:T(8,128)(2,1)S(1)} %fusion.mixed_ref), channel_id=1, source_target_pairs={{0,1},{1,0},{2,3},{3,2},{4,5},{5,4},{6,7},{7,6},{8,9},{9,8},{10,11... | collective-permute-start | bytes 786440 | tf_op jit(solution)/shard_map/ppermute | solution.py:29
  6.2 1.2 %fusion.1.projected_ref = f32[8,16]{1,0:T(8,128)S(1)} fusion(bf16[8,8192]{1,0:T(8,128)(2,1)} %inputs_ref.1, bf16[8192,16]{0,1:T(8,128)(2,1)} %param.10), kind=kOutput, calls=%fused_computation.6 | convolution fusion | flops 2097152 | bytes 393728 | tf_op jit(solution)/shard_map/dot_general | solution.py:235
  7.4 0.0 copy-done.3
  7.4 0.8 shard_map.102.sent_ref
  8.2 8.1 %all-to-all-start = ((f32[16,8,128]{2,1,0:T(8,128)}), f32[16,8,128]{2,1,0:T(8,128)S(1)}, u32[]{:S(2)}, u32[]{:S(2)}) async-start(f32[16,8,128]{2,1,0:T(8,128)} %shard_map.102.sent_ref), calls=%async_computation | async-start | bytes 131072 | tf_op jit(solution)/shard_map/all_to_all | solution.py:239
  16.3 0.1 pad_add_fusion.place_ref
  16.4 0.0 collective-permute-done.after_ref.got_any.got_ref
  16.4 6.1 %collective-permute-start.1 = (bf16[128,512]{1,0:T(8,128)(2,1)S(1)}, bf16[128,512]{1,0:T(8,128)(2,1)S(1)}, u32[]{:S(2)}, u32[]{:S(2)}) collective-permute-start(bf16[128,512]{1,0:T(8,128)(2,1)S(1)} %shard_map.103.cot_ref), channel_id=1, source_target_pairs={{0,128},{128,0},{256,384},{384,256},{1,129},{129,1},{257,385},{385... | collective-permute-start | bytes 393224 | tf_op jit(solution)/shard_map/ppermute | solution.py:29
  22.5 6.4 %collective-permute-start.3 = (bf16[128,512]{1,0:T(8,128)(2,1)S(1)}, bf16[128,512]{1,0:T(8,128)(2,1)S(1)}, u32[]{:S(2)}, u32[]{:S(2)}) collective-permute-start(bf16[128,512]{1,0:T(8,128)(2,1)S(1)} %shard_map.103.cot_ref), channel_id=1, source_target_pairs={{0,384},{128,256},{256,128},{384,0},{1,385},{129,257},{257,129},{3... | collective-permute-start | bytes 393224 | tf_op jit(solution)/shard_map/ppermute | solution.py:29
  28.9 0.0 all-to-all-done.rank_ref
  28.9 0.0 copy-done.1
  28.9 0.0 copy-done.2
  28.9 0.0 copy-done.4
  28.9 0.0 copy-done.5
  29.0 2.1 %shard_map.104 = (bf16[4,320,512]{2,1,0:T(8,128)(2,1)}, bf16[8,128]{1,0:T(8,128)(2,1)S(1)}) custom-call(s32[3]{0:T(128)S(1)} %pad_add_fusion.place_ref, f32[16]{0:T(128)S(1)} %copy-done.4, s32[16]{0:T(128)S(1)} %copy-done.5, f32[16,8,128]{2,1,0:T(8,128)} %shard_map.102.sent_ref, f32[16,8,128]{2,1,0:T(8,128)S(1)} %all-to-all-done.rank_ref, ...), custom_call_target="tpu_custom_call" | custom-call | flops 32212254720 | bytes 3145728 | tf_op jit(solution)/shard_map/pallas_call | solution.py:244
  31.1 4.8 %all-to-all-start.1 = ((bf16[4,320,512]{2,1,0:T(8,128)(2,1)}), bf16[4,320,512]{2,1,0:T(8,128)(2,1)S(1)}, u32[]{:S(2)}, u32[]{:S(2)}) async-start(bf16[4,320,512]{2,1,0:T(8,128)(2,1)} %get-tuple-element.14), calls=%async_computation.1 | async-start | bytes 2621440 | tf_op jit(solution)/shard_map/all_to_all | solution.py:260
  35.8 0.0 collective-permute-done.1.refs_0_
  35.8 6.0 %collective-permute-start.4 = (bf16[128,512]{1,0:T(8,128)(2,1)S(1)}, bf16[128,512]{1,0:T(8,128)(2,1)S(1)}, u32[]{:S(2)}, u32[]{:S(2)}) collective-permute-start(bf16[128,512]{1,0:T(8,128)(2,1)S(1)} %shard_map.105.in_ref), channel_id=1, source_target_pairs={{0,384},{128,256},{256,128},{384,0},{1,385},{129,257},{257,129},{3... | collective-permute-start | bytes 393224 | tf_op jit(solution)/shard_map/ppermute | solution.py:29
  41.8 2.9 %collective-permute-start.2 = (bf16[128,512]{1,0:T(8,128)(2,1)S(1)}, bf16[128,512]{1,0:T(8,128)(2,1)S(1)}, u32[]{:S(2)}, u32[]{:S(2)}) collective-permute-start(bf16[128,512]{1,0:T(8,128)(2,1)S(1)} %shard_map.106.after_ref.first_ref), channel_id=1, source_target_pairs={{0,1},{1,0},{2,3},{3,2},{4,5},{5,4},{6,7},{7,6},{8,9},{9,8},{10,11... | collective-permute-start | bytes 393224 | tf_op jit(solution)/shard_map/ppermute | solution.py:29
  44.7 0.0 collective-permute-done.3.first_ref
  44.7 1.0 collective-permute-done.4.second_ref
  45.7 3.0 %collective-permute-start.5 = (bf16[2,128,512]{2,1,0:T(8,128)(2,1)S(1)}, bf16[2,128,512]{2,1,0:T(8,128)(2,1)S(1)}, u32[]{:S(2)}, u32[]{:S(2)}) collective-permute-start(bf16[2,128,512]{2,1,0:T(8,128)(2,1)S(1)} %shard_map.108.last_ref), channel_id=1, source_target_pairs={{0,1},{1,0},{2,3},{3,2},{4,5},{5,4},{6,7},{7,6},{8,9},{9,8},{10,11... | collective-permute-start | bytes 786440 | tf_op jit(solution)/shard_map/ppermute | solution.py:29
  48.8 1.3 %collective-permute-done.2.in_ref = bf16[128,512]{1,0:T(8,128)(2,1)S(1)} collective-permute-done((bf16[128,512]{1,0:T(8,128)(2,1)S(1)}, bf16[128,512]{1,0:T(8,128)(2,1)S(1)}, u32[]{:S(2)}, u32[]{:S(2)}) %collective-permute-start.2) | collective-permute-done | bytes 131104 | tf_op jit(solution)/shard_map/ppermute | solution.py:29
  50.1 3.9 %collective-permute-done.5.refs_2_.far_last_ref = bf16[2,128,512]{2,1,0:T(8,128)(2,1)S(1)} collective-permute-done((bf16[2,128,512]{2,1,0:T(8,128)(2,1)S(1)}, bf16[2,128,512]{2,1,0:T(8,128)(2,1)S(1)}, u32[]{:S(2)}, u32[]{:S(2)}) %collective-permute-start.5) | collective-permute-done | bytes 262176 | tf_op jit(solution)/shard_map/ppermute | solution.py:29
  54.0 0.0 all-to-all-done.1.refs_0_
  54.0 1.9 %collective-permute-start.6 = (bf16[4,320,512]{2,1,0:T(8,128)(2,1)S(1)}, bf16[4,320,512]{2,1,0:T(8,128)(2,1)S(1)}, u32[]{:S(2)}, u32[]{:S(2)}) collective-permute-start(bf16[4,320,512]{2,1,0:T(8,128)(2,1)S(1)} %shard_map.109.own_ref), channel_id=1, source_target_pairs={{0,16},{16,0},{1,17},{17,1},{2,18},{18,2},{3,19},{19,3},{4,20},{20... | collective-permute-start | bytes 3932168 | tf_op jit(solution)/shard_map/ppermute | solution.py:29
  55.9 1.4 %shard_map.110 = (bf16[4,128,512]{2,1,0:T(8,128)(2,1)S(1)}, f32[4,128,128]{2,1,0:T(8,128)S(1)}, f32[16,512]{1,0:T(8,128)S(1)}) custom-call(s32[3]{0:T(128)S(1)} %pad_add_fusion.place_ref, bf16[4,320,512]{2,1,0:T(8,128)(2,1)S(1)} %shard_map.109.own_ref, bf16[128,512]{1,0:T(8,128)(2,1)S(1)} %shard_map.103.cot_ref, ...), custom_call_target="tpu_custom_call" | custom-call | flops 536870912 | bytes 3145728 | tf_op jit(solution)/shard_map/pallas_call | solution.py:263
  57.3 1.6 %collective-permute-done.6.other_ref = bf16[4,320,512]{2,1,0:T(8,128)(2,1)S(1)} collective-permute-done((bf16[4,320,512]{2,1,0:T(8,128)(2,1)S(1)}, bf16[4,320,512]{2,1,0:T(8,128)(2,1)S(1)}, u32[]{:S(2)}, u32[]{:S(2)}) %collective-permute-start.6) | collective-permute-done | bytes 1310752 | tf_op jit(solution)/shard_map/ppermute | solution.py:29
  58.9 2.3 %shard_map.111 = (bf16[4,128,1152]{2,1,0:T(8,128)(2,1)}, f32[16,512]{1,0:T(8,128)S(1)}) custom-call(s32[3]{0:T(128)S(1)} %pad_add_fusion.place_ref, bf16[4,128,512]{2,1,0:T(8,128)(2,1)S(1)} %get-tuple-element.16.done_ref, f32[4,128,128]{2,1,0:T(8,128)S(1)} %get-tuple-element.17.terms_ref, f32[16,512]{1,0:T(8,128)S(1)} %get-tuple-element.18.own_right_ref, ...), custom_call_target="tpu_custom_call" | custom-call | flops 536870912 | bytes 5242880 | tf_op jit(solution)/shard_map/pallas_call | solution.py:270
  61.2 0.0 copy-start
  61.2 10.6 %all-to-all-start.2 = ((bf16[64,8,1152]{2,1,0:T(8,128)(2,1)}), bf16[64,8,1152]{2,1,0:T(8,128)(2,1)S(1)}, u32[]{:S(2)}, u32[]{:S(2)}) async-start(bf16[64,8,1152]{2,1,0:T(8,128)(2,1)} %bitcast.3), calls=%async_computation.2 | async-start | bytes 2359296 | tf_op jit(solution)/shard_map/all_to_all | solution.py:279
  71.8 4.4 %collective-permute-start.7 = (bf16[16,512]{1,0:T(8,128)(2,1)S(1)}, bf16[16,512]{1,0:T(8,128)(2,1)S(1)}, u32[]{:S(2)}, u32[]{:S(2)}) collective-permute-start(bf16[16,512]{1,0:T(8,128)(2,1)S(1)} %convert_element_type.16), channel_id=1, source_target_pairs={{0,128},{128,0},{256,384},{384,256},{1,129},{129,1},{257,385},{385... | collective-permute-start | bytes 49160 | tf_op jit(solution)/shard_map/ppermute | solution.py:29
  76.2 5.7 %collective-permute-start.8 = (bf16[16,512]{1,0:T(8,128)(2,1)S(1)}, bf16[16,512]{1,0:T(8,128)(2,1)S(1)}, u32[]{:S(2)}, u32[]{:S(2)}) collective-permute-start(bf16[16,512]{1,0:T(8,128)(2,1)S(1)} %convert_element_type.16), channel_id=1, source_target_pairs={{0,256},{128,384},{256,0},{384,128},{1,257},{129,385},{257,1},{385... | collective-permute-start | bytes 49160 | tf_op jit(solution)/shard_map/ppermute | solution.py:29
  81.9 2.2 %collective-permute-start.9 = (bf16[16,512]{1,0:T(8,128)(2,1)S(1)}, bf16[16,512]{1,0:T(8,128)(2,1)S(1)}, u32[]{:S(2)}, u32[]{:S(2)}) collective-permute-start(bf16[16,512]{1,0:T(8,128)(2,1)S(1)} %convert_element_type.16), channel_id=1, source_target_pairs={{0,384},{128,256},{256,128},{384,0},{1,385},{129,257},{257,129},{3... | collective-permute-start | bytes 49160 | tf_op jit(solution)/shard_map/ppermute | solution.py:29
  84.1 9.3 %collective-permute-done.7 = bf16[16,512]{1,0:T(8,128)(2,1)S(1)} collective-permute-done((bf16[16,512]{1,0:T(8,128)(2,1)S(1)}, bf16[16,512]{1,0:T(8,128)(2,1)S(1)}, u32[]{:S(2)}, u32[]{:S(2)}) %collective-permute-start.7) | collective-permute-done | bytes 16416 | tf_op jit(solution)/shard_map/ppermute | solution.py:29
  93.4 0.0 collective-permute-done.8
  93.4 0.0 collective-permute-done.9
  93.4 0.6 add_multiply_fusion
  94.0 10.9 %all-to-all-done.2.back_ref = bf16[64,8,1152]{2,1,0:T(8,128)(2,1)S(1)} async-done(((bf16[64,8,1152]{2,1,0:T(8,128)(2,1)}), bf16[64,8,1152]{2,1,0:T(8,128)(2,1)S(1)}, u32[]{:S(2)}, u32[]{:S(2)}) %all-to-all-start.2) | async-done | bytes 1179680 | tf_op jit(solution)/shard_map/all_to_all | solution.py:279
  104.9 0.0 copy-done
  104.9 1.5 %shard_map.112 = (bf16[8,8192]{1,0:T(8,128)(2,1)}, f32[16,16]{1,0:T(8,128)}, f32[1,16]{1,0:T(1,128)}) custom-call(s32[3]{0:T(128)S(1)} %pad_add_fusion.place_ref, bf16[64,8,1152]{2,1,0:T(8,128)(2,1)S(1)} %all-to-all-done.2.back_ref, bf16[8,128]{1,0:T(8,128)(2,1)S(1)} %get-tuple-element.15.refs_1_.scaled_ref, bf16[16,8192]{1,0:T(8,128)(2,1)S(1)} %bitcast.10, ...), custom_call_target="tpu_custom_call" | custom-call | flops 2097152 | bytes 2097152 | tf_op jit(solution)/shard_map/pallas_call | solution.py:283
  (8 shorter events, 0.1 us)
Async XLA Ops:
  0.6 28.3 %copy-start.1 = (bf16[256,512]{1,0:T(8,128)(2,1)S(1)}, bf16[256,512]{1,0:T(8,128)(2,1)}, u32[]{:S(2)}) copy-start(bf16[256,512]{1,0:T(8,128)(2,1)} %weight_any.1) | copy-start | bytes 786436
  0.6 28.3 %copy-start.2 = (bf16[8,8192]{1,0:T(8,128)(2,1)S(1)}, bf16[8,8192]{1,0:T(8,128)(2,1)}, u32[]{:S(2)}) copy-start(bf16[8,8192]{1,0:T(8,128)(2,1)} %inputs_ref.1) | copy-start | bytes 393220
  0.7 6.7 %copy-start.3 = (bf16[16,512]{1,0:T(8,128)(2,1)S(1)}, bf16[16,512]{1,0:T(8,128)(2,1)}, u32[]{:S(2)}) copy-start(bf16[16,512]{1,0:T(8,128)(2,1)} %right_ref.1) | copy-start | bytes 49156
  0.7 28.3 %copy-start.4 = (f32[16]{0:T(128)S(1)}, f32[16]{0:T(128)}, u32[]{:S(2)}) copy-start(f32[16]{0:T(128)} %singular_ref.1) | copy-start | bytes 196
  0.7 28.3 %copy-start.5 = (s32[16]{0:T(128)S(1)}, s32[16]{0:T(128)}, u32[]{:S(2)}) copy-start(s32[16]{0:T(128)} %keep_ref.1) | copy-start | bytes 196
  2.7 13.7 %collective-permute-start = (bf16[256,512]{1,0:T(8,128)(2,1)S(1)}, bf16[256,512]{1,0:T(8,128)(2,1)S(1)}, u32[]{:S(2)}, u32[]{:S(2)}) collective-permute-start(bf16[256,512]{1,0:T(8,128)(2,1)S(1)} %fusion.mixed_ref), channel_id=1, source_target_pairs={{0,1},{1,0},{2,3},{3,2},{4,5},{5,4},{6,7},{7,6},{8,9},{9,8},{10,11... | collective-permute-start | bytes 786440 | tf_op jit(solution)/shard_map/ppermute | solution.py:29
  8.2 20.7 %all-to-all-start = ((f32[16,8,128]{2,1,0:T(8,128)}), f32[16,8,128]{2,1,0:T(8,128)S(1)}, u32[]{:S(2)}, u32[]{:S(2)}) async-start(f32[16,8,128]{2,1,0:T(8,128)} %shard_map.102.sent_ref), calls=%async_computation | async-start | bytes 131072 | tf_op jit(solution)/shard_map/all_to_all | solution.py:239
  16.4 19.4 %collective-permute-start.1 = (bf16[128,512]{1,0:T(8,128)(2,1)S(1)}, bf16[128,512]{1,0:T(8,128)(2,1)S(1)}, u32[]{:S(2)}, u32[]{:S(2)}) collective-permute-start(bf16[128,512]{1,0:T(8,128)(2,1)S(1)} %shard_map.103.cot_ref), channel_id=1, source_target_pairs={{0,128},{128,0},{256,384},{384,256},{1,129},{129,1},{257,385},{385... | collective-permute-start | bytes 393224 | tf_op jit(solution)/shard_map/ppermute | solution.py:29
  22.5 22.2 %collective-permute-start.3 = (bf16[128,512]{1,0:T(8,128)(2,1)S(1)}, bf16[128,512]{1,0:T(8,128)(2,1)S(1)}, u32[]{:S(2)}, u32[]{:S(2)}) collective-permute-start(bf16[128,512]{1,0:T(8,128)(2,1)S(1)} %shard_map.103.cot_ref), channel_id=1, source_target_pairs={{0,384},{128,256},{256,128},{384,0},{1,385},{129,257},{257,129},{3... | collective-permute-start | bytes 393224 | tf_op jit(solution)/shard_map/ppermute | solution.py:29
  31.1 22.9 %all-to-all-start.1 = ((bf16[4,320,512]{2,1,0:T(8,128)(2,1)}), bf16[4,320,512]{2,1,0:T(8,128)(2,1)S(1)}, u32[]{:S(2)}, u32[]{:S(2)}) async-start(bf16[4,320,512]{2,1,0:T(8,128)(2,1)} %get-tuple-element.14), calls=%async_computation.1 | async-start | bytes 2621440 | tf_op jit(solution)/shard_map/all_to_all | solution.py:260
  35.8 9.9 %collective-permute-start.4 = (bf16[128,512]{1,0:T(8,128)(2,1)S(1)}, bf16[128,512]{1,0:T(8,128)(2,1)S(1)}, u32[]{:S(2)}, u32[]{:S(2)}) collective-permute-start(bf16[128,512]{1,0:T(8,128)(2,1)S(1)} %shard_map.105.in_ref), channel_id=1, source_target_pairs={{0,384},{128,256},{256,128},{384,0},{1,385},{129,257},{257,129},{3... | collective-permute-start | bytes 393224 | tf_op jit(solution)/shard_map/ppermute | solution.py:29
  41.8 8.3 %collective-permute-start.2 = (bf16[128,512]{1,0:T(8,128)(2,1)S(1)}, bf16[128,512]{1,0:T(8,128)(2,1)S(1)}, u32[]{:S(2)}, u32[]{:S(2)}) collective-permute-start(bf16[128,512]{1,0:T(8,128)(2,1)S(1)} %shard_map.106.after_ref.first_ref), channel_id=1, source_target_pairs={{0,1},{1,0},{2,3},{3,2},{4,5},{5,4},{6,7},{7,6},{8,9},{9,8},{10,11... | collective-permute-start | bytes 393224 | tf_op jit(solution)/shard_map/ppermute | solution.py:29
  45.7 8.3 %collective-permute-start.5 = (bf16[2,128,512]{2,1,0:T(8,128)(2,1)S(1)}, bf16[2,128,512]{2,1,0:T(8,128)(2,1)S(1)}, u32[]{:S(2)}, u32[]{:S(2)}) collective-permute-start(bf16[2,128,512]{2,1,0:T(8,128)(2,1)S(1)} %shard_map.108.last_ref), channel_id=1, source_target_pairs={{0,1},{1,0},{2,3},{3,2},{4,5},{5,4},{6,7},{7,6},{8,9},{9,8},{10,11... | collective-permute-start | bytes 786440 | tf_op jit(solution)/shard_map/ppermute | solution.py:29
  54.0 4.9 %collective-permute-start.6 = (bf16[4,320,512]{2,1,0:T(8,128)(2,1)S(1)}, bf16[4,320,512]{2,1,0:T(8,128)(2,1)S(1)}, u32[]{:S(2)}, u32[]{:S(2)}) collective-permute-start(bf16[4,320,512]{2,1,0:T(8,128)(2,1)S(1)} %shard_map.109.own_ref), channel_id=1, source_target_pairs={{0,16},{16,0},{1,17},{17,1},{2,18},{18,2},{3,19},{19,3},{4,20},{20... | collective-permute-start | bytes 3932168 | tf_op jit(solution)/shard_map/ppermute | solution.py:29
  61.2 43.7 %copy-start = (bf16[8192,16]{0,1:T(8,128)(2,1)S(1)}, bf16[8192,16]{0,1:T(8,128)(2,1)}, u32[]{:S(2)}) copy-start(bf16[8192,16]{0,1:T(8,128)(2,1)} %param.10) | copy-start | bytes 786436
  61.2 43.7 %all-to-all-start.2 = ((bf16[64,8,1152]{2,1,0:T(8,128)(2,1)}), bf16[64,8,1152]{2,1,0:T(8,128)(2,1)S(1)}, u32[]{:S(2)}, u32[]{:S(2)}) async-start(bf16[64,8,1152]{2,1,0:T(8,128)(2,1)} %bitcast.3), calls=%async_computation.2 | async-start | bytes 2359296 | tf_op jit(solution)/shard_map/all_to_all | solution.py:279
  71.8 21.6 %collective-permute-start.7 = (bf16[16,512]{1,0:T(8,128)(2,1)S(1)}, bf16[16,512]{1,0:T(8,128)(2,1)S(1)}, u32[]{:S(2)}, u32[]{:S(2)}) collective-permute-start(bf16[16,512]{1,0:T(8,128)(2,1)S(1)} %convert_element_type.16), channel_id=1, source_target_pairs={{0,128},{128,0},{256,384},{384,256},{1,129},{129,1},{257,385},{385... | collective-permute-start | bytes 49160 | tf_op jit(solution)/shard_map/ppermute | solution.py:29
  76.2 17.2 %collective-permute-start.8 = (bf16[16,512]{1,0:T(8,128)(2,1)S(1)}, bf16[16,512]{1,0:T(8,128)(2,1)S(1)}, u32[]{:S(2)}, u32[]{:S(2)}) collective-permute-start(bf16[16,512]{1,0:T(8,128)(2,1)S(1)} %convert_element_type.16), channel_id=1, source_target_pairs={{0,256},{128,384},{256,0},{384,128},{1,257},{129,385},{257,1},{385... | collective-permute-start | bytes 49160 | tf_op jit(solution)/shard_map/ppermute | solution.py:29
  81.9 11.5 %collective-permute-start.9 = (bf16[16,512]{1,0:T(8,128)(2,1)S(1)}, bf16[16,512]{1,0:T(8,128)(2,1)S(1)}, u32[]{:S(2)}, u32[]{:S(2)}) collective-permute-start(bf16[16,512]{1,0:T(8,128)(2,1)S(1)} %convert_element_type.16), channel_id=1, source_target_pairs={{0,384},{128,256},{256,128},{384,0},{1,385},{129,257},{257,129},{3... | collective-permute-start | bytes 49160 | tf_op jit(solution)/shard_map/ppermute | solution.py:29

commit v17 on v15

--- a/solution.py
+++ b/solution.py
@@ -58,8 +58,9 @@
     out_ref[:, :, 0:16] = dot_t(mixed_ref[0:128, :], right_ref[...]).reshape(16, 8, 16)
 
 
-def pick_kernel(mixed_ref, after_ref, out_ref):
-    out_ref[...] = mixed_ref[0:128, :]
+def pick_kernel(mixed_ref, got_ref, out_ref):
+    out_ref[0] = mixed_ref[0:128, :]
+    out_ref[1] = got_ref[0:128, :]
 
 
 def copy_kernel(in_ref, out_ref):
@@ -71,8 +72,8 @@
     out_ref[1] = second_ref[...]
 
 
-def rows_of(own, first_ref, last_ref):
-    return jnp.concatenate([own, first_ref[...], last_ref[...].reshape(256, 512)], axis=0)
+def rows_of(refs):
+    return [jnp.concatenate([ref[half] for ref in refs], axis=0) for half in (0, 1)]
 
 
 def pack_kernel(
@@ -94,7 +95,7 @@
     back = (own * coeff).astype(bf16)
     back_ref[...] = back
     fwd = (jnp.where((lane >= 16) & (lane < 32), rank, 0.0) * coeff).astype(bf16)
-    right = t_dot(fwd.reshape(128, 128), cot_ref[...])[16:32]
+    right = t_dot(fwd.reshape(128, 128), cot_ref[0])[16:32]
     projected = pltpu.roll(sent_ref[0], 112, 1)
     singular = jnp.broadcast_to(jnp.sum(projected * own, axis=0, keepdims=True), (8, 128))
     high = singular.astype(bf16).astype(f32)
@@ -147,9 +148,9 @@
 
 
 def own_kernel(
-    place_ref, own_ref, cot_ref, first_ref, last_ref, got_ref, far_ref, far_last_ref, out_ref, terms_ref, right_ref
+    place_ref, own_ref, cot_ref, first_ref, third_ref, last_ref, out_ref, terms_ref, right_ref
 ):
-    parts = (rows_of(cot_ref[...], first_ref, last_ref), rows_of(got_ref[0:128, :], far_ref, far_last_ref))
+    parts = rows_of((cot_ref, first_ref, third_ref, last_ref))
     out_ref[...] = products(parts, own_ref).reshape(4, 128, 512)
     terms, right_ref[...] = adapter_terms(own_ref, place_ref[0])
     for h in range(4):
@@ -157,7 +158,7 @@
 
 
 def other_kernel(
-    place_ref, done_ref, terms_ref, own_right_ref, other_ref, cot_ref, first_ref, last_ref, got_ref, far_ref, far_last_ref,
+    place_ref, done_ref, terms_ref, own_right_ref, other_ref, cot_ref, first_ref, third_ref, last_ref,
     out_any, right_ref, out_ref, sems,
 ):
     z_high = place_ref[2]
@@ -168,13 +169,8 @@
         high = z.astype(bf16).astype(f32)
         out_ref[h, :, 1024:1152] = (high + pltpu.roll(z - high, 64, 1)).astype(bf16)
     copies = []
-    for half in range(2):
-        if half == 0:
-            near = jnp.concatenate([cot_ref[...], first_ref[...]], axis=0)
-            far = jnp.concatenate([got_ref[0:128, :], far_ref[...]], axis=0)
-        else:
-            near, far = last_ref[...].reshape(256, 512), far_last_ref[...].reshape(256, 512)
-        parts = (near, far)
+    for half, refs in enumerate(((cot_ref, first_ref), (third_ref, last_ref))):
+        parts = rows_of(refs)
         total = products(parts, other_ref).reshape(2, 128, 512)
         for i in range(2):
             at = z_high ^ ((0, 1), (3, 2))[half][i]
@@ -235,7 +231,7 @@
     )
     rank_in = lax.all_to_all(rank_out, ("zl", "yh", "yl"), 0, 0)
 
-    cot = call(pick_kernel, shape((128, 512), bf16), [in_vmem, anywhere], 1, 1 << 18)(mixed, got)
+    cot = call(pick_kernel, shape((2, 128, 512), bf16), [in_vmem] * 2, 1, 1 << 18)(mixed, got)
     first, third = swap(cot, "zh", 4, 1), swap(cot, "zh", 4, 3)
 
     x_out, scaled_back = call(
@@ -248,31 +244,29 @@
         scratch=[pltpu.VMEM((4, 64, 512), bf16), dma((12,))],
     )(place, singular, keep_mask, rank_out, rank_in, cot, weight, got, inputs)
     first = after(first, scaled_back)
-    held = call(copy_kernel, shape((128, 512), bf16), [in_vmem], 30 << 30, 1 << 18)(first)
-    far = call(copy_kernel, shape((128, 512), bf16), [in_vmem], 30 << 30, 1 << 18)(swap(held, "yl", 2, 1))
+    held = call(copy_kernel, shape((2, 128, 512), bf16), [in_vmem], 30 << 30, 1 << 18)(first)
     last = call(stack_kernel, shape((2, 128, 512), bf16), [in_vmem] * 2 + [anywhere], 30 << 30, 1 << 20)(
-        third, swap(first, "zh", 4, 3), held
+        swap(first[0], "zh", 4, 3), swap(third[1], "zh", 4, 1), held
     )
-    far_last = swap(last, "yl", 2, 1)
-    x_in = after(lax.all_to_all(x_out, "x", 0, 0), far, far_last)
+    x_in = after(lax.all_to_all(x_out, "x", 0, 0), last)
     x_other = swap(x_in, "c", 2, 1)
 
     done, terms, own_right = call(
         own_kernel,
         (shape((4, 128, 512), bf16), shape((4, 128, 128), f32), shape((16, 512), f32)),
-        [in_smem] + [in_vmem] * 7,
+        [in_smem] + [in_vmem] * 5,
         1 << 29,
         3 << 20,
-    )(place, x_in, cot, held, last, got, far, far_last)
+    )(place, x_in, cot, held, third, last)
     out, right_part = call(
         other_kernel,
         (shape((4, 128, 1152), bf16), shape((16, 512), f32)),
-        [in_smem] + [in_vmem] * 10,
+        [in_smem] + [in_vmem] * 8,
         1 << 29,
         5 << 20,
         out_specs=(in_hbm, in_vmem),
         scratch=[pltpu.VMEM((4, 128, 1152), bf16), dma((4,))],
-    )(place, done, terms, own_right, x_other, cot, held, last, got, far, far_last)
+    )(place, done, terms, own_right, x_other, cot, held, third, last)
     back = lax.all_to_all(out.reshape(64, 8, 1152), ("zh", "zl", "yh", "yl"), 0, 0)
     right_sent = right_part.astype(bf16)
     right_sum = right_part + sum(swap(right_sent, "zh", 4, k).astype(f32) for k in (1, 2, 3))

time: 107 us -> 107 us (level)
  starting transfers between devices: 65.5 us -> 63.4 us
  waiting for transfers between devices: 28 us -> 29.5 us
    ppermute x10 -> x9, starting transfers between devices: 42 us -> 38.5 us  [swap(): return lax.ppermute(a, axis, [(i, i ^ mask) for i in range(count)])]
    ppermute x10 -> x9, waiting for transfers between devices: 17.1 us -> 18.7 us  [swap(): return lax.ppermute(a, axis, [(i, i ^ mask) for i in range(count)])]
    all_to_all x1, starting transfers between devices: 10.6 us -> 12 us  [body(): lax.all_to_all(out.reshape(64, 8, 1152), ('zh', 'zl', 'yh', 'yl'), 0, 0)]
  transfers between devices with their start and end apart: 13 -> 12, of which waited for: 6 -> 5; matrix products, arithmetic and copies ran while one was open for 2% -> 2% of each run, Pallas kernels for 4% -> 4%
where the time goes in v17:
time: 107 us; the launch traced here: 106 us
  starting transfers between devices  63.4 us (59%)
  waiting for transfers between devices  29.5 us (28%)
  Pallas kernels  8.13 us (8%)
  other arithmetic  2.66 us (2%)
  matrix products  1.21 us (1%)
    ppermute x9, starting transfers between devices, swap(): return lax.ppermute(a, axis, [(i, i ^ mask) for i in range(count)])  38.5 us
    ppermute x9, waiting for transfers between devices, swap(): return lax.ppermute(a, axis, [(i, i ^ mask) for i in range(count)])  18.7 us
    all_to_all x1, starting transfers between devices, body(): lax.all_to_all(out.reshape(64, 8, 1152), ('zh', 'zl', 'yh', 'yl'), 0, 0)  12 us
    all_to_all x1, waiting for transfers between devices, body(): lax.all_to_all(out.reshape(64, 8, 1152), ('zh', 'zl', 'yh', 'yl'), 0, 0)  10.9 us
    all_to_all x1, starting transfers between devices, body(): rank_in = lax.all_to_all(rank_out, ('zl', 'yh', 'yl'), 0, 0)  8.11 us
    all_to_all x1, starting transfers between devices, body(): x_in = after(lax.all_to_all(x_out, 'x', 0, 0), last)  4.78 us
    pallas_call x1, Pallas kernels, body(): call(other_kernel, (shape((4, 128, 1152), bf16), shape((16, 512), f32)),...  2.27 us
  transfers between devices with their start and end apart: 12, of which 5 were waited for; matrix products, arithmetic and copies ran while one was open for 2% of the time, Pallas kernels for 4%

profile of v17, /device:TPU:6, one launch (start us, length us, event | category | flops | bytes accessed | tf_op | source)
XLA Modules:
  0.0 105.9 jit_solution(3371987918018679813)
XLA Ops:
  0.6 0.0 copy-start.1
  0.6 0.0 copy-start.2
  0.7 0.0 copy-start.3
  0.7 0.0 copy-start.4
  0.7 0.0 copy-start.5
  0.7 1.0 slice_select_fusion
  1.7 0.9 pad_maximum_fusion.mixed_ref
  2.6 3.5 %collective-permute-start = (bf16[256,512]{1,0:T(8,128)(2,1)S(1)}, bf16[256,512]{1,0:T(8,128)(2,1)S(1)}, u32[]{:S(2)}, u32[]{:S(2)}) collective-permute-start(bf16[256,512]{1,0:T(8,128)(2,1)S(1)} %pad_maximum_fusion.mixed_ref), channel_id=1, source_target_pairs={{0,1},{1,0},{2,3},{3,2},{4,5},{5,4},{6,7},{7,6},{8,9},{9,8},{10,11... | collective-permute-start | bytes 786440 | tf_op jit(solution)/shard_map/ppermute | solution.py:29
  6.1 1.2 %fusion.projected_ref = f32[8,16]{1,0:T(8,128)S(1)} fusion(bf16[8,8192]{1,0:T(8,128)(2,1)} %inputs_ref.1, bf16[8192,16]{0,1:T(8,128)(2,1)} %param.10), kind=kOutput, calls=%fused_computation.7 | convolution fusion | flops 2097152 | bytes 393728 | tf_op jit(solution)/shard_map/dot_general | solution.py:228
  7.4 0.0 copy-done.3
  7.4 0.8 shard_map.102.sent_ref
  8.2 8.1 %all-to-all-start = ((f32[16,8,128]{2,1,0:T(8,128)}), f32[16,8,128]{2,1,0:T(8,128)S(1)}, u32[]{:S(2)}, u32[]{:S(2)}) async-start(f32[16,8,128]{2,1,0:T(8,128)} %shard_map.102.sent_ref), calls=%async_computation | async-start | bytes 131072 | tf_op jit(solution)/shard_map/all_to_all | solution.py:232
  16.3 0.1 pad_add_fusion.place_ref
  16.4 0.0 collective-permute-done.got_ref.got_any
  16.4 6.1 %collective-permute-start.1 = (bf16[2,128,512]{2,1,0:T(8,128)(2,1)S(1)}, bf16[2,128,512]{2,1,0:T(8,128)(2,1)S(1)}, u32[]{:S(2)}, u32[]{:S(2)}) collective-permute-start(bf16[2,128,512]{2,1,0:T(8,128)(2,1)S(1)} %shard_map.103.cot_ref), channel_id=1, source_target_pairs={{0,128},{128,0},{256,384},{384,256},{1,129},{129,1},{257,385},{385... | collective-permute-start | bytes 786440 | tf_op jit(solution)/shard_map/ppermute | solution.py:29
  22.5 6.4 %collective-permute-start.3 = (bf16[2,128,512]{2,1,0:T(8,128)(2,1)S(1)}, bf16[2,128,512]{2,1,0:T(8,128)(2,1)S(1)}, u32[]{:S(2)}, u32[]{:S(2)}) collective-permute-start(bf16[2,128,512]{2,1,0:T(8,128)(2,1)S(1)} %shard_map.103.cot_ref), channel_id=1, source_target_pairs={{0,384},{128,256},{256,128},{384,0},{1,385},{129,257},{257,129},{3... | collective-permute-start | bytes 786440 | tf_op jit(solution)/shard_map/ppermute | solution.py:29
  28.9 0.0 all-to-all-done.rank_ref
  28.9 0.0 copy-done.1
  28.9 0.0 copy-done.2
  28.9 0.0 copy-done.4
  28.9 0.0 copy-done.5
  29.0 2.0 %shard_map.104 = (bf16[4,320,512]{2,1,0:T(8,128)(2,1)}, bf16[8,128]{1,0:T(8,128)(2,1)S(1)}) custom-call(s32[3]{0:T(128)S(1)} %pad_add_fusion.place_ref, f32[16]{0:T(128)S(1)} %copy-done.4, s32[16]{0:T(128)S(1)} %copy-done.5, f32[16,8,128]{2,1,0:T(8,128)} %shard_map.102.sent_ref, f32[16,8,128]{2,1,0:T(8,128)S(1)} %all-to-all-done.rank_ref, ...), custom_call_target="tpu_custom_call" | custom-call | flops 32212254720 | bytes 3145728 | tf_op jit(solution)/shard_map/pallas_call | solution.py:237
  31.0 4.8 %all-to-all-start.1 = ((bf16[4,320,512]{2,1,0:T(8,128)(2,1)}), bf16[4,320,512]{2,1,0:T(8,128)(2,1)S(1)}, u32[]{:S(2)}, u32[]{:S(2)}) async-start(bf16[4,320,512]{2,1,0:T(8,128)(2,1)} %get-tuple-element.14), calls=%async_computation.1 | async-start | bytes 2621440 | tf_op jit(solution)/shard_map/all_to_all | solution.py:251
  35.8 0.0 collective-permute-done.1.refs_0_
  35.8 6.4 %collective-permute-start.2 = (bf16[128,512]{1,0:T(8,128)(2,1)S(1)}, bf16[128,512]{1,0:T(8,128)(2,1)S(1)}, u32[]{:S(2)}, u32[]{:S(2)}) collective-permute-start(bf16[128,512]{1,0:T(8,128)(2,1)S(1)} %slice_bitcast_fusion.1), channel_id=1, source_target_pairs={{0,384},{128,256},{256,128},{384,0},{1,385},{129,257},{257,129},{3... | collective-permute-start | bytes 393224 | tf_op jit(solution)/shard_map/ppermute | solution.py:29
  42.2 0.0 collective-permute-done.3.third_ref
  42.2 2.1 %collective-permute-start.4 = (bf16[128,512]{1,0:T(8,128)(2,1)S(1)}, bf16[128,512]{1,0:T(8,128)(2,1)S(1)}, u32[]{:S(2)}, u32[]{:S(2)}) collective-permute-start(bf16[128,512]{1,0:T(8,128)(2,1)S(1)} %slice_bitcast_fusion), channel_id=1, source_target_pairs={{0,128},{128,0},{256,384},{384,256},{1,129},{129,1},{257,385},{385... | collective-permute-start | bytes 393224 | tf_op jit(solution)/shard_map/ppermute | solution.py:29
  44.3 0.9 collective-permute-done.2.first_ref
  45.2 6.9 %collective-permute-done.4.second_ref = bf16[128,512]{1,0:T(8,128)(2,1)S(1)} collective-permute-done((bf16[128,512]{1,0:T(8,128)(2,1)S(1)}, bf16[128,512]{1,0:T(8,128)(2,1)S(1)}, u32[]{:S(2)}, u32[]{:S(2)}) %collective-permute-start.4) | collective-permute-done | bytes 131104 | tf_op jit(solution)/shard_map/ppermute | solution.py:29
  52.1 0.0 all-to-all-done.1.refs_0_
  52.1 1.9 %collective-permute-start.5 = (bf16[4,320,512]{2,1,0:T(8,128)(2,1)S(1)}, bf16[4,320,512]{2,1,0:T(8,128)(2,1)S(1)}, u32[]{:S(2)}, u32[]{:S(2)}) collective-permute-start(bf16[4,320,512]{2,1,0:T(8,128)(2,1)S(1)} %shard_map.108.own_ref), channel_id=1, source_target_pairs={{0,16},{16,0},{1,17},{17,1},{2,18},{18,2},{3,19},{19,3},{4,20},{20... | collective-permute-start | bytes 3932168 | tf_op jit(solution)/shard_map/ppermute | solution.py:29
  54.0 1.4 %shard_map.109 = (bf16[4,128,512]{2,1,0:T(8,128)(2,1)S(1)}, f32[4,128,128]{2,1,0:T(8,128)S(1)}, f32[16,512]{1,0:T(8,128)S(1)}) custom-call(s32[3]{0:T(128)S(1)} %pad_add_fusion.place_ref, bf16[4,320,512]{2,1,0:T(8,128)(2,1)S(1)} %shard_map.108.own_ref, bf16[2,128,512]{2,1,0:T(8,128)(2,1)S(1)} %shard_map.103.cot_ref, ...), custom_call_target="tpu_custom_call" | custom-call | flops 536870912 | bytes 3145728 | tf_op jit(solution)/shard_map/pallas_call | solution.py:254
  55.4 1.6 %collective-permute-done.5.other_ref = bf16[4,320,512]{2,1,0:T(8,128)(2,1)S(1)} collective-permute-done((bf16[4,320,512]{2,1,0:T(8,128)(2,1)S(1)}, bf16[4,320,512]{2,1,0:T(8,128)(2,1)S(1)}, u32[]{:S(2)}, u32[]{:S(2)}) %collective-permute-start.5) | collective-permute-done | bytes 1310752 | tf_op jit(solution)/shard_map/ppermute | solution.py:29
  57.0 2.3 %shard_map.110 = (bf16[4,128,1152]{2,1,0:T(8,128)(2,1)}, f32[16,512]{1,0:T(8,128)S(1)}) custom-call(s32[3]{0:T(128)S(1)} %pad_add_fusion.place_ref, bf16[4,128,512]{2,1,0:T(8,128)(2,1)S(1)} %get-tuple-element.16.done_ref, f32[4,128,128]{2,1,0:T(8,128)S(1)} %get-tuple-element.17.terms_ref, f32[16,512]{1,0:T(8,128)S(1)} %get-tuple-element.18.own_right_ref, ...), custom_call_target="tpu_custom_call" | custom-call | flops 536870912 | bytes 5242880 | tf_op jit(solution)/shard_map/pallas_call | solution.py:261
  59.3 0.0 copy-start
  59.3 12.0 %all-to-all-start.2 = ((bf16[64,8,1152]{2,1,0:T(8,128)(2,1)}), bf16[64,8,1152]{2,1,0:T(8,128)(2,1)S(1)}, u32[]{:S(2)}, u32[]{:S(2)}) async-start(bf16[64,8,1152]{2,1,0:T(8,128)(2,1)} %bitcast.5), calls=%async_computation.2 | async-start | bytes 2359296 | tf_op jit(solution)/shard_map/all_to_all | solution.py:270
  71.3 4.4 %collective-permute-start.6 = (bf16[16,512]{1,0:T(8,128)(2,1)S(1)}, bf16[16,512]{1,0:T(8,128)(2,1)S(1)}, u32[]{:S(2)}, u32[]{:S(2)}) collective-permute-start(bf16[16,512]{1,0:T(8,128)(2,1)S(1)} %convert_element_type.16), channel_id=1, source_target_pairs={{0,128},{128,0},{256,384},{384,256},{1,129},{129,1},{257,385},{385... | collective-permute-start | bytes 49160 | tf_op jit(solution)/shard_map/ppermute | solution.py:29
  75.7 5.7 %collective-permute-start.7 = (bf16[16,512]{1,0:T(8,128)(2,1)S(1)}, bf16[16,512]{1,0:T(8,128)(2,1)S(1)}, u32[]{:S(2)}, u32[]{:S(2)}) collective-permute-start(bf16[16,512]{1,0:T(8,128)(2,1)S(1)} %convert_element_type.16), channel_id=1, source_target_pairs={{0,256},{128,384},{256,0},{384,128},{1,257},{129,385},{257,1},{385... | collective-permute-start | bytes 49160 | tf_op jit(solution)/shard_map/ppermute | solution.py:29
  81.4 2.2 %collective-permute-start.8 = (bf16[16,512]{1,0:T(8,128)(2,1)S(1)}, bf16[16,512]{1,0:T(8,128)(2,1)S(1)}, u32[]{:S(2)}, u32[]{:S(2)}) collective-permute-start(bf16[16,512]{1,0:T(8,128)(2,1)S(1)} %convert_element_type.16), channel_id=1, source_target_pairs={{0,384},{128,256},{256,128},{384,0},{1,385},{129,257},{257,129},{3... | collective-permute-start | bytes 49160 | tf_op jit(solution)/shard_map/ppermute | solution.py:29
  83.6 9.3 %collective-permute-done.6 = bf16[16,512]{1,0:T(8,128)(2,1)S(1)} collective-permute-done((bf16[16,512]{1,0:T(8,128)(2,1)S(1)}, bf16[16,512]{1,0:T(8,128)(2,1)S(1)}, u32[]{:S(2)}, u32[]{:S(2)}) %collective-permute-start.6) | collective-permute-done | bytes 16416 | tf_op jit(solution)/shard_map/ppermute | solution.py:29
  92.9 0.0 collective-permute-done.7
  92.9 0.0 collective-permute-done.8
  92.9 0.6 add_multiply_fusion
  93.5 10.9 %all-to-all-done.2.back_ref = bf16[64,8,1152]{2,1,0:T(8,128)(2,1)S(1)} async-done(((bf16[64,8,1152]{2,1,0:T(8,128)(2,1)}), bf16[64,8,1152]{2,1,0:T(8,128)(2,1)S(1)}, u32[]{:S(2)}, u32[]{:S(2)}) %all-to-all-start.2) | async-done | bytes 1179680 | tf_op jit(solution)/shard_map/all_to_all | solution.py:270
  104.4 0.0 copy-done
  104.4 1.5 %shard_map.111 = (bf16[8,8192]{1,0:T(8,128)(2,1)}, f32[16,16]{1,0:T(8,128)}, f32[1,16]{1,0:T(1,128)}) custom-call(s32[3]{0:T(128)S(1)} %pad_add_fusion.place_ref, bf16[64,8,1152]{2,1,0:T(8,128)(2,1)S(1)} %all-to-all-done.2.back_ref, bf16[8,128]{1,0:T(8,128)(2,1)S(1)} %get-tuple-element.15.refs_1_.scaled_ref, bf16[16,8192]{1,0:T(8,128)(2,1)S(1)} %bitcast.14, ...), custom_call_target="tpu_custom_call" | custom-call | flops 2097152 | bytes 2097152 | tf_op jit(solution)/shard_map/pallas_call | solution.py:274
  (9 shorter events, 0.1 us)
Async XLA Ops:
  0.6 28.3 %copy-start.1 = (bf16[256,512]{1,0:T(8,128)(2,1)S(1)}, bf16[256,512]{1,0:T(8,128)(2,1)}, u32[]{:S(2)}) copy-start(bf16[256,512]{1,0:T(8,128)(2,1)} %weight_any.1) | copy-start | bytes 786436
  0.6 28.3 %copy-start.2 = (bf16[8,8192]{1,0:T(8,128)(2,1)S(1)}, bf16[8,8192]{1,0:T(8,128)(2,1)}, u32[]{:S(2)}) copy-start(bf16[8,8192]{1,0:T(8,128)(2,1)} %inputs_ref.1) | copy-start | bytes 393220
  0.7 6.7 %copy-start.3 = (bf16[16,512]{1,0:T(8,128)(2,1)S(1)}, bf16[16,512]{1,0:T(8,128)(2,1)}, u32[]{:S(2)}) copy-start(bf16[16,512]{1,0:T(8,128)(2,1)} %right_ref.1) | copy-start | bytes 49156
  0.7 28.3 %copy-start.4 = (f32[16]{0:T(128)S(1)}, f32[16]{0:T(128)}, u32[]{:S(2)}) copy-start(f32[16]{0:T(128)} %singular_ref.1) | copy-start | bytes 196
  0.7 28.3 %copy-start.5 = (s32[16]{0:T(128)S(1)}, s32[16]{0:T(128)}, u32[]{:S(2)}) copy-start(s32[16]{0:T(128)} %keep_ref.1) | copy-start | bytes 196
  2.6 13.7 %collective-permute-start = (bf16[256,512]{1,0:T(8,128)(2,1)S(1)}, bf16[256,512]{1,0:T(8,128)(2,1)S(1)}, u32[]{:S(2)}, u32[]{:S(2)}) collective-permute-start(bf16[256,512]{1,0:T(8,128)(2,1)S(1)} %pad_maximum_fusion.mixed_ref), channel_id=1, source_target_pairs={{0,1},{1,0},{2,3},{3,2},{4,5},{5,4},{6,7},{7,6},{8,9},{9,8},{10,11... | collective-permute-start | bytes 786440 | tf_op jit(solution)/shard_map/ppermute | solution.py:29
  8.2 20.7 %all-to-all-start = ((f32[16,8,128]{2,1,0:T(8,128)}), f32[16,8,128]{2,1,0:T(8,128)S(1)}, u32[]{:S(2)}, u32[]{:S(2)}) async-start(f32[16,8,128]{2,1,0:T(8,128)} %shard_map.102.sent_ref), calls=%async_computation | async-start | bytes 131072 | tf_op jit(solution)/shard_map/all_to_all | solution.py:232
  16.4 19.4 %collective-permute-start.1 = (bf16[2,128,512]{2,1,0:T(8,128)(2,1)S(1)}, bf16[2,128,512]{2,1,0:T(8,128)(2,1)S(1)}, u32[]{:S(2)}, u32[]{:S(2)}) collective-permute-start(bf16[2,128,512]{2,1,0:T(8,128)(2,1)S(1)} %shard_map.103.cot_ref), channel_id=1, source_target_pairs={{0,128},{128,0},{256,384},{384,256},{1,129},{129,1},{257,385},{385... | collective-permute-start | bytes 786440 | tf_op jit(solution)/shard_map/ppermute | solution.py:29
  22.5 19.7 %collective-permute-start.3 = (bf16[2,128,512]{2,1,0:T(8,128)(2,1)S(1)}, bf16[2,128,512]{2,1,0:T(8,128)(2,1)S(1)}, u32[]{:S(2)}, u32[]{:S(2)}) collective-permute-start(bf16[2,128,512]{2,1,0:T(8,128)(2,1)S(1)} %shard_map.103.cot_ref), channel_id=1, source_target_pairs={{0,384},{128,256},{256,128},{384,0},{1,385},{129,257},{257,129},{3... | collective-permute-start | bytes 786440 | tf_op jit(solution)/shard_map/ppermute | solution.py:29
  31.0 21.1 %all-to-all-start.1 = ((bf16[4,320,512]{2,1,0:T(8,128)(2,1)}), bf16[4,320,512]{2,1,0:T(8,128)(2,1)S(1)}, u32[]{:S(2)}, u32[]{:S(2)}) async-start(bf16[4,320,512]{2,1,0:T(8,128)(2,1)} %get-tuple-element.14), calls=%async_computation.1 | async-start | bytes 2621440 | tf_op jit(solution)/shard_map/all_to_all | solution.py:251
  35.8 9.4 %collective-permute-start.2 = (bf16[128,512]{1,0:T(8,128)(2,1)S(1)}, bf16[128,512]{1,0:T(8,128)(2,1)S(1)}, u32[]{:S(2)}, u32[]{:S(2)}) collective-permute-start(bf16[128,512]{1,0:T(8,128)(2,1)S(1)} %slice_bitcast_fusion.1), channel_id=1, source_target_pairs={{0,384},{128,256},{256,128},{384,0},{1,385},{129,257},{257,129},{3... | collective-permute-start | bytes 393224 | tf_op jit(solution)/shard_map/ppermute | solution.py:29
  42.2 9.9 %collective-permute-start.4 = (bf16[128,512]{1,0:T(8,128)(2,1)S(1)}, bf16[128,512]{1,0:T(8,128)(2,1)S(1)}, u32[]{:S(2)}, u32[]{:S(2)}) collective-permute-start(bf16[128,512]{1,0:T(8,128)(2,1)S(1)} %slice_bitcast_fusion), channel_id=1, source_target_pairs={{0,128},{128,0},{256,384},{384,256},{1,129},{129,1},{257,385},{385... | collective-permute-start | bytes 393224 | tf_op jit(solution)/shard_map/ppermute | solution.py:29
  52.1 4.9 %collective-permute-start.5 = (bf16[4,320,512]{2,1,0:T(8,128)(2,1)S(1)}, bf16[4,320,512]{2,1,0:T(8,128)(2,1)S(1)}, u32[]{:S(2)}, u32[]{:S(2)}) collective-permute-start(bf16[4,320,512]{2,1,0:T(8,128)(2,1)S(1)} %shard_map.108.own_ref), channel_id=1, source_target_pairs={{0,16},{16,0},{1,17},{17,1},{2,18},{18,2},{3,19},{19,3},{4,20},{20... | collective-permute-start | bytes 3932168 | tf_op jit(solution)/shard_map/ppermute | solution.py:29
  59.3 45.1 %copy-start = (bf16[8192,16]{0,1:T(8,128)(2,1)S(1)}, bf16[8192,16]{0,1:T(8,128)(2,1)}, u32[]{:S(2)}) copy-start(bf16[8192,16]{0,1:T(8,128)(2,1)} %param.10) | copy-start | bytes 786436
  59.3 45.1 %all-to-all-start.2 = ((bf16[64,8,1152]{2,1,0:T(8,128)(2,1)}), bf16[64,8,1152]{2,1,0:T(8,128)(2,1)S(1)}, u32[]{:S(2)}, u32[]{:S(2)}) async-start(bf16[64,8,1152]{2,1,0:T(8,128)(2,1)} %bitcast.5), calls=%async_computation.2 | async-start | bytes 2359296 | tf_op jit(solution)/shard_map/all_to_all | solution.py:270
  71.3 21.6 %collective-permute-start.6 = (bf16[16,512]{1,0:T(8,128)(2,1)S(1)}, bf16[16,512]{1,0:T(8,128)(2,1)S(1)}, u32[]{:S(2)}, u32[]{:S(2)}) collective-permute-start(bf16[16,512]{1,0:T(8,128)(2,1)S(1)} %convert_element_type.16), channel_id=1, source_target_pairs={{0,128},{128,0},{256,384},{384,256},{1,129},{129,1},{257,385},{385... | collective-permute-start | bytes 49160 | tf_op jit(solution)/shard_map/ppermute | solution.py:29
  75.7 17.2 %collective-permute-start.7 = (bf16[16,512]{1,0:T(8,128)(2,1)S(1)}, bf16[16,512]{1,0:T(8,128)(2,1)S(1)}, u32[]{:S(2)}, u32[]{:S(2)}) collective-permute-start(bf16[16,512]{1,0:T(8,128)(2,1)S(1)} %convert_element_type.16), channel_id=1, source_target_pairs={{0,256},{128,384},{256,0},{384,128},{1,257},{129,385},{257,1},{385... | collective-permute-start | bytes 49160 | tf_op jit(solution)/shard_map/ppermute | solution.py:29
  81.4 11.5 %collective-permute-start.8 = (bf16[16,512]{1,0:T(8,128)(2,1)S(1)}, bf16[16,512]{1,0:T(8,128)(2,1)S(1)}, u32[]{:S(2)}, u32[]{:S(2)}) collective-permute-start(bf16[16,512]{1,0:T(8,128)(2,1)S(1)} %convert_element_type.16), channel_id=1, source_target_pairs={{0,384},{128,256},{256,128},{384,0},{1,385},{129,257},{257,129},{3... | collective-permute-start | bytes 49160 | tf_op jit(solution)/shard_map/ppermute | solution.py:29

commit v18 on v17

--- a/solution.py
+++ b/solution.py
@@ -58,7 +58,8 @@
     out_ref[:, :, 0:16] = dot_t(mixed_ref[0:128, :], right_ref[...]).reshape(16, 8, 16)
 
 
-def pick_kernel(mixed_ref, got_ref, out_ref):
+def pick_kernel(mixed_ref, got_ref, out_ref, own_ref):
+    own_ref[...] = mixed_ref[0:128, :]
     out_ref[0] = mixed_ref[0:128, :]
     out_ref[1] = got_ref[0:128, :]
 
@@ -72,8 +73,8 @@
     out_ref[1] = second_ref[...]
 
 
-def rows_of(refs):
-    return [jnp.concatenate([ref[half] for ref in refs], axis=0) for half in (0, 1)]
+def rows_of(*pairs):
+    return [jnp.concatenate([pair[half] for pair in pairs], axis=0) for half in (0, 1)]
 
 
 def pack_kernel(
@@ -148,9 +149,9 @@
 
 
 def own_kernel(
-    place_ref, own_ref, cot_ref, first_ref, third_ref, last_ref, out_ref, terms_ref, right_ref
+    place_ref, own_ref, cot_ref, first_ref, far_ref, third_ref, last_ref, out_ref, terms_ref, right_ref
 ):
-    parts = rows_of((cot_ref, first_ref, third_ref, last_ref))
+    parts = rows_of(cot_ref, (first_ref[...], far_ref[...]), third_ref, last_ref)
     out_ref[...] = products(parts, own_ref).reshape(4, 128, 512)
     terms, right_ref[...] = adapter_terms(own_ref, place_ref[0])
     for h in range(4):
@@ -158,7 +159,7 @@
 
 
 def other_kernel(
-    place_ref, done_ref, terms_ref, own_right_ref, other_ref, cot_ref, first_ref, third_ref, last_ref,
+    place_ref, done_ref, terms_ref, own_right_ref, other_ref, cot_ref, first_ref, far_ref, third_ref, last_ref,
     out_any, right_ref, out_ref, sems,
 ):
     z_high = place_ref[2]
@@ -169,8 +170,8 @@
         high = z.astype(bf16).astype(f32)
         out_ref[h, :, 1024:1152] = (high + pltpu.roll(z - high, 64, 1)).astype(bf16)
     copies = []
-    for half, refs in enumerate(((cot_ref, first_ref), (third_ref, last_ref))):
-        parts = rows_of(refs)
+    first_half = rows_of(cot_ref, (first_ref[...], far_ref[...]))
+    for half, parts in enumerate((first_half, rows_of(third_ref, last_ref))):
         total = products(parts, other_ref).reshape(2, 128, 512)
         for i in range(2):
             at = z_high ^ ((0, 1), (3, 2))[half][i]
@@ -231,8 +232,10 @@
     )
     rank_in = lax.all_to_all(rank_out, ("zl", "yh", "yl"), 0, 0)
 
-    cot = call(pick_kernel, shape((2, 128, 512), bf16), [in_vmem] * 2, 1, 1 << 18)(mixed, got)
-    first, third = swap(cot, "zh", 4, 1), swap(cot, "zh", 4, 3)
+    cot, own = call(
+        pick_kernel, (shape((2, 128, 512), bf16), shape((128, 512), bf16)), [in_vmem] * 2, 1, 1 << 18
+    )(mixed, got)
+    first, third = swap(own, "zh", 4, 1), swap(cot, "zh", 4, 3)
 
     x_out, scaled_back = call(
         pack_kernel,
@@ -244,29 +247,30 @@
         scratch=[pltpu.VMEM((4, 64, 512), bf16), dma((12,))],
     )(place, singular, keep_mask, rank_out, rank_in, cot, weight, got, inputs)
     first = after(first, scaled_back)
-    held = call(copy_kernel, shape((2, 128, 512), bf16), [in_vmem], 30 << 30, 1 << 18)(first)
+    held = call(copy_kernel, shape((128, 512), bf16), [in_vmem], 30 << 30, 1 << 18)(first)
+    far = call(copy_kernel, shape((128, 512), bf16), [in_vmem], 30 << 30, 1 << 18)(swap(held, "yl", 2, 1))
     last = call(stack_kernel, shape((2, 128, 512), bf16), [in_vmem] * 2 + [anywhere], 30 << 30, 1 << 20)(
-        swap(first[0], "zh", 4, 3), swap(third[1], "zh", 4, 1), held
+        swap(first, "zh", 4, 3), swap(third[1], "zh", 4, 1), held
     )
-    x_in = after(lax.all_to_all(x_out, "x", 0, 0), last)
+    x_in = after(lax.all_to_all(x_out, "x", 0, 0), last, far)
     x_other = swap(x_in, "c", 2, 1)
 
     done, terms, own_right = call(
         own_kernel,
         (shape((4, 128, 512), bf16), shape((4, 128, 128), f32), shape((16, 512), f32)),
-        [in_smem] + [in_vmem] * 5,
+        [in_smem] + [in_vmem] * 6,
         1 << 29,
         3 << 20,
-    )(place, x_in, cot, held, third, last)
+    )(place, x_in, cot, held, far, third, last)
     out, right_part = call(
         other_kernel,
         (shape((4, 128, 1152), bf16), shape((16, 512), f32)),
-        [in_smem] + [in_vmem] * 8,
+        [in_smem] + [in_vmem] * 9,
         1 << 29,
         5 << 20,
         out_specs=(in_hbm, in_vmem),
         scratch=[pltpu.VMEM((4, 128, 1152), bf16), dma((4,))],
-    )(place, done, terms, own_right, x_other, cot, held, third, last)
+    )(place, done, terms, own_right, x_other, cot, held, far, third, last)
     back = lax.all_to_all(out.reshape(64, 8, 1152), ("zh", "zl", "yh", "yl"), 0, 0)
     right_sent = right_part.astype(bf16)
     right_sum = right_part + sum(swap(right_sent, "zh", 4, k).astype(f32) for k in (1, 2, 3))

time: 107 us -> 108 us (level)
  starting transfers between devices: 63.4 us -> 65.6 us
  waiting for transfers between devices: 29.5 us -> 28.4 us
    ppermute x9 -> x10, starting transfers between devices: 38.5 us -> 41.4 us  [swap(): return lax.ppermute(a, axis, [(i, i ^ mask) for i in range(count)])]
    ppermute x9 -> x10, waiting for transfers between devices: 18.7 us -> 17.6 us  [swap(): return lax.ppermute(a, axis, [(i, i ^ mask) for i in range(count)])]
  transfers between devices with their start and end apart: 12 -> 13, of which waited for: 5 -> 5; matrix products, arithmetic and copies ran while one was open for 2% -> 2% of each run, Pallas kernels for 4% -> 4%
where the time goes in v18:
time: 108 us; the launch traced here: 107 us
  starting transfers between devices  65.6 us (61%)
  waiting for transfers between devices  28.4 us (26%)
  Pallas kernels  8.12 us (8%)
  other arithmetic  2.66 us (2%)
  matrix products  1.21 us (1%)
    ppermute x10, starting transfers between devices, swap(): return lax.ppermute(a, axis, [(i, i ^ mask) for i in range(count)])  41.4 us
    ppermute x10, waiting for transfers between devices, swap(): return lax.ppermute(a, axis, [(i, i ^ mask) for i in range(count)])  17.6 us
    all_to_all x1, starting transfers between devices, body(): lax.all_to_all(out.reshape(64, 8, 1152), ('zh', 'zl', 'yh', 'yl'), 0, 0)  11.3 us
    all_to_all x1, waiting for transfers between devices, body(): lax.all_to_all(out.reshape(64, 8, 1152), ('zh', 'zl', 'yh', 'yl'), 0, 0)  10.8 us
    all_to_all x1, starting transfers between devices, body(): rank_in = lax.all_to_all(rank_out, ('zl', 'yh', 'yl'), 0, 0)  8.11 us
    all_to_all x1, starting transfers between devices, body(): x_in = after(lax.all_to_all(x_out, 'x', 0, 0), last, far)  4.78 us
    pallas_call x1, Pallas kernels, body(): call(other_kernel, (shape((4, 128, 1152), bf16), shape((16, 512), f32)),...  2.26 us
  transfers between devices with their start and end apart: 13, of which 5 were waited for; matrix products, arithmetic and copies ran while one was open for 2% of the time, Pallas kernels for 4%

profile of v18, /device:TPU:6, one launch (start us, length us, event | category | flops | bytes accessed | tf_op | source)
XLA Modules:
  0.0 107.0 jit_solution(13679239180363653293)
XLA Ops:
  0.6 0.0 copy-start.1
  0.6 0.0 copy-start.2
  0.7 0.0 copy-start.3
  0.7 0.0 copy-start.4
  0.7 0.0 copy-start.5
  0.7 1.0 slice_select_fusion
  1.7 0.9 pad_maximum_fusion.mixed_ref
  2.6 3.5 %collective-permute-start = (bf16[256,512]{1,0:T(8,128)(2,1)S(1)}, bf16[256,512]{1,0:T(8,128)(2,1)S(1)}, u32[]{:S(2)}, u32[]{:S(2)}) collective-permute-start(bf16[256,512]{1,0:T(8,128)(2,1)S(1)} %pad_maximum_fusion.mixed_ref), channel_id=1, source_target_pairs={{0,1},{1,0},{2,3},{3,2},{4,5},{5,4},{6,7},{7,6},{8,9},{9,8},{10,11... | collective-permute-start | bytes 786440 | tf_op jit(solution)/shard_map/ppermute | solution.py:29
  6.1 1.2 %fusion.projected_ref = f32[8,16]{1,0:T(8,128)S(1)} fusion(bf16[8,8192]{1,0:T(8,128)(2,1)} %inputs_ref.1, bf16[8192,16]{0,1:T(8,128)(2,1)} %param.10), kind=kOutput, calls=%fused_computation.6 | convolution fusion | flops 2097152 | bytes 393728 | tf_op jit(solution)/shard_map/dot_general | solution.py:229
  7.4 0.0 copy-done.3
  7.4 0.8 shard_map.102.sent_ref
  8.2 8.1 %all-to-all-start = ((f32[16,8,128]{2,1,0:T(8,128)}), f32[16,8,128]{2,1,0:T(8,128)S(1)}, u32[]{:S(2)}, u32[]{:S(2)}) async-start(f32[16,8,128]{2,1,0:T(8,128)} %shard_map.102.sent_ref), calls=%async_computation | async-start | bytes 131072 | tf_op jit(solution)/shard_map/all_to_all | solution.py:233
  16.3 0.1 pad_add_fusion.place_ref
  16.4 0.0 collective-permute-done.got_ref.got_any
  16.4 6.1 %collective-permute-start.1 = (bf16[128,512]{1,0:T(8,128)(2,1)S(1)}, bf16[128,512]{1,0:T(8,128)(2,1)S(1)}, u32[]{:S(2)}, u32[]{:S(2)}) collective-permute-start(bf16[128,512]{1,0:T(8,128)(2,1)S(1)} %get-tuple-element.18), channel_id=1, source_target_pairs={{0,128},{128,0},{256,384},{384,256},{1,129},{129,1},{257,385},{385... | collective-permute-start | bytes 393224 | tf_op jit(solution)/shard_map/ppermute | solution.py:29
  22.5 6.4 %collective-permute-start.3 = (bf16[2,128,512]{2,1,0:T(8,128)(2,1)S(1)}, bf16[2,128,512]{2,1,0:T(8,128)(2,1)S(1)}, u32[]{:S(2)}, u32[]{:S(2)}) collective-permute-start(bf16[2,128,512]{2,1,0:T(8,128)(2,1)S(1)} %get-tuple-element.16.cot_ref), channel_id=1, source_target_pairs={{0,384},{128,256},{256,128},{384,0},{1,385},{129,257},{257,129},{3... | collective-permute-start | bytes 786440 | tf_op jit(solution)/shard_map/ppermute | solution.py:29
  28.9 0.0 all-to-all-done.rank_ref
  28.9 0.0 copy-done.1
  28.9 0.0 copy-done.2
  28.9 0.0 copy-done.4
  28.9 0.0 copy-done.5
  29.0 2.1 %shard_map.104 = (bf16[4,320,512]{2,1,0:T(8,128)(2,1)}, bf16[8,128]{1,0:T(8,128)(2,1)S(1)}) custom-call(s32[3]{0:T(128)S(1)} %pad_add_fusion.place_ref, f32[16]{0:T(128)S(1)} %copy-done.4, s32[16]{0:T(128)S(1)} %copy-done.5, f32[16,8,128]{2,1,0:T(8,128)} %shard_map.102.sent_ref, f32[16,8,128]{2,1,0:T(8,128)S(1)} %all-to-all-done.rank_ref, ...), custom_call_target="tpu_custom_call" | custom-call | flops 32212254720 | bytes 3145728 | tf_op jit(solution)/shard_map/pallas_call | solution.py:240
  31.0 4.8 %all-to-all-start.1 = ((bf16[4,320,512]{2,1,0:T(8,128)(2,1)}), bf16[4,320,512]{2,1,0:T(8,128)(2,1)S(1)}, u32[]{:S(2)}, u32[]{:S(2)}) async-start(bf16[4,320,512]{2,1,0:T(8,128)(2,1)} %get-tuple-element.17), calls=%async_computation.1 | async-start | bytes 2621440 | tf_op jit(solution)/shard_map/all_to_all | solution.py:255
  35.8 0.0 collective-permute-done.1.refs_0_
  35.8 6.0 %collective-permute-start.2 = (bf16[128,512]{1,0:T(8,128)(2,1)S(1)}, bf16[128,512]{1,0:T(8,128)(2,1)S(1)}, u32[]{:S(2)}, u32[]{:S(2)}) collective-permute-start(bf16[128,512]{1,0:T(8,128)(2,1)S(1)} %shard_map.105.in_ref), channel_id=1, source_target_pairs={{0,384},{128,256},{256,128},{384,0},{1,385},{129,257},{257,129},{3... | collective-permute-start | bytes 393224 | tf_op jit(solution)/shard_map/ppermute | solution.py:29
  41.8 2.9 %collective-permute-start.5 = (bf16[128,512]{1,0:T(8,128)(2,1)S(1)}, bf16[128,512]{1,0:T(8,128)(2,1)S(1)}, u32[]{:S(2)}, u32[]{:S(2)}) collective-permute-start(bf16[128,512]{1,0:T(8,128)(2,1)S(1)} %shard_map.106.after_ref.first_ref), channel_id=1, source_target_pairs={{0,1},{1,0},{2,3},{3,2},{4,5},{5,4},{6,7},{7,6},{8,9},{9,8},{10,11... | collective-permute-start | bytes 393224 | tf_op jit(solution)/shard_map/ppermute | solution.py:29
  44.7 0.0 collective-permute-done.3.third_ref
  44.7 2.5 %collective-permute-start.4 = (bf16[128,512]{1,0:T(8,128)(2,1)S(1)}, bf16[128,512]{1,0:T(8,128)(2,1)S(1)}, u32[]{:S(2)}, u32[]{:S(2)}) collective-permute-start(bf16[128,512]{1,0:T(8,128)(2,1)S(1)} %slice_bitcast_fusion), channel_id=1, source_target_pairs={{0,128},{128,0},{256,384},{384,256},{1,129},{129,1},{257,385},{385... | collective-permute-start | bytes 393224 | tf_op jit(solution)/shard_map/ppermute | solution.py:29
  47.2 1.4 %collective-permute-done.5.in_ref = bf16[128,512]{1,0:T(8,128)(2,1)S(1)} collective-permute-done((bf16[128,512]{1,0:T(8,128)(2,1)S(1)}, bf16[128,512]{1,0:T(8,128)(2,1)S(1)}, u32[]{:S(2)}, u32[]{:S(2)}) %collective-permute-start.5) | collective-permute-done | bytes 131104 | tf_op jit(solution)/shard_map/ppermute | solution.py:29
  48.7 0.0 collective-permute-done.2.first_ref
  48.7 5.2 %collective-permute-done.4.second_ref = bf16[128,512]{1,0:T(8,128)(2,1)S(1)} collective-permute-done((bf16[128,512]{1,0:T(8,128)(2,1)S(1)}, bf16[128,512]{1,0:T(8,128)(2,1)S(1)}, u32[]{:S(2)}, u32[]{:S(2)}) %collective-permute-start.4) | collective-permute-done | bytes 131104 | tf_op jit(solution)/shard_map/ppermute | solution.py:29
  53.9 0.0 all-to-all-done.1.refs_0_
  53.9 1.9 %collective-permute-start.6 = (bf16[4,320,512]{2,1,0:T(8,128)(2,1)S(1)}, bf16[4,320,512]{2,1,0:T(8,128)(2,1)S(1)}, u32[]{:S(2)}, u32[]{:S(2)}) collective-permute-start(bf16[4,320,512]{2,1,0:T(8,128)(2,1)S(1)} %shard_map.109.own_ref), channel_id=1, source_target_pairs={{0,16},{16,0},{1,17},{17,1},{2,18},{18,2},{3,19},{19,3},{4,20},{20... | collective-permute-start | bytes 3932168 | tf_op jit(solution)/shard_map/ppermute | solution.py:29
  55.8 1.4 %shard_map.110 = (bf16[4,128,512]{2,1,0:T(8,128)(2,1)S(1)}, f32[4,128,128]{2,1,0:T(8,128)S(1)}, f32[16,512]{1,0:T(8,128)S(1)}) custom-call(s32[3]{0:T(128)S(1)} %pad_add_fusion.place_ref, bf16[4,320,512]{2,1,0:T(8,128)(2,1)S(1)} %shard_map.109.own_ref, bf16[2,128,512]{2,1,0:T(8,128)(2,1)S(1)} %get-tuple-element.16.cot_ref, ...), custom_call_target="tpu_custom_call" | custom-call | flops 536870912 | bytes 3145728 | tf_op jit(solution)/shard_map/pallas_call | solution.py:258
  57.3 1.6 %collective-permute-done.6.other_ref = bf16[4,320,512]{2,1,0:T(8,128)(2,1)S(1)} collective-permute-done((bf16[4,320,512]{2,1,0:T(8,128)(2,1)S(1)}, bf16[4,320,512]{2,1,0:T(8,128)(2,1)S(1)}, u32[]{:S(2)}, u32[]{:S(2)}) %collective-permute-start.6) | collective-permute-done | bytes 1310752 | tf_op jit(solution)/shard_map/ppermute | solution.py:29
  58.8 2.3 %shard_map.111 = (bf16[4,128,1152]{2,1,0:T(8,128)(2,1)}, f32[16,512]{1,0:T(8,128)S(1)}) custom-call(s32[3]{0:T(128)S(1)} %pad_add_fusion.place_ref, bf16[4,128,512]{2,1,0:T(8,128)(2,1)S(1)} %get-tuple-element.20.done_ref, f32[4,128,128]{2,1,0:T(8,128)S(1)} %get-tuple-element.21.terms_ref, f32[16,512]{1,0:T(8,128)S(1)} %get-tuple-element.22.own_right_ref, ...), custom_call_target="tpu_custom_call" | custom-call | flops 536870912 | bytes 5242880 | tf_op jit(solution)/shard_map/pallas_call | solution.py:265
  61.1 0.0 copy-start
  61.1 11.3 %all-to-all-start.2 = ((bf16[64,8,1152]{2,1,0:T(8,128)(2,1)}), bf16[64,8,1152]{2,1,0:T(8,128)(2,1)S(1)}, u32[]{:S(2)}, u32[]{:S(2)}) async-start(bf16[64,8,1152]{2,1,0:T(8,128)(2,1)} %bitcast.4), calls=%async_computation.2 | async-start | bytes 2359296 | tf_op jit(solution)/shard_map/all_to_all | solution.py:274
  72.4 4.4 %collective-permute-start.7 = (bf16[16,512]{1,0:T(8,128)(2,1)S(1)}, bf16[16,512]{1,0:T(8,128)(2,1)S(1)}, u32[]{:S(2)}, u32[]{:S(2)}) collective-permute-start(bf16[16,512]{1,0:T(8,128)(2,1)S(1)} %convert_element_type.16), channel_id=1, source_target_pairs={{0,128},{128,0},{256,384},{384,256},{1,129},{129,1},{257,385},{385... | collective-permute-start | bytes 49160 | tf_op jit(solution)/shard_map/ppermute | solution.py:29
  76.8 5.7 %collective-permute-start.8 = (bf16[16,512]{1,0:T(8,128)(2,1)S(1)}, bf16[16,512]{1,0:T(8,128)(2,1)S(1)}, u32[]{:S(2)}, u32[]{:S(2)}) collective-permute-start(bf16[16,512]{1,0:T(8,128)(2,1)S(1)} %convert_element_type.16), channel_id=1, source_target_pairs={{0,256},{128,384},{256,0},{384,128},{1,257},{129,385},{257,1},{385... | collective-permute-start | bytes 49160 | tf_op jit(solution)/shard_map/ppermute | solution.py:29
  82.5 2.2 %collective-permute-start.9 = (bf16[16,512]{1,0:T(8,128)(2,1)S(1)}, bf16[16,512]{1,0:T(8,128)(2,1)S(1)}, u32[]{:S(2)}, u32[]{:S(2)}) collective-permute-start(bf16[16,512]{1,0:T(8,128)(2,1)S(1)} %convert_element_type.16), channel_id=1, source_target_pairs={{0,384},{128,256},{256,128},{384,0},{1,385},{129,257},{257,129},{3... | collective-permute-start | bytes 49160 | tf_op jit(solution)/shard_map/ppermute | solution.py:29
  84.7 9.3 %collective-permute-done.7 = bf16[16,512]{1,0:T(8,128)(2,1)S(1)} collective-permute-done((bf16[16,512]{1,0:T(8,128)(2,1)S(1)}, bf16[16,512]{1,0:T(8,128)(2,1)S(1)}, u32[]{:S(2)}, u32[]{:S(2)}) %collective-permute-start.7) | collective-permute-done | bytes 16416 | tf_op jit(solution)/shard_map/ppermute | solution.py:29
  94.0 0.0 collective-permute-done.8
  94.0 0.0 collective-permute-done.9
  94.0 0.6 add_multiply_fusion
  94.7 10.8 %all-to-all-done.2.back_ref = bf16[64,8,1152]{2,1,0:T(8,128)(2,1)S(1)} async-done(((bf16[64,8,1152]{2,1,0:T(8,128)(2,1)}), bf16[64,8,1152]{2,1,0:T(8,128)(2,1)S(1)}, u32[]{:S(2)}, u32[]{:S(2)}) %all-to-all-start.2) | async-done | bytes 1179680 | tf_op jit(solution)/shard_map/all_to_all | solution.py:274
  105.5 0.0 copy-done
  105.5 1.5 %shard_map.112 = (bf16[8,8192]{1,0:T(8,128)(2,1)}, f32[16,16]{1,0:T(8,128)}, f32[1,16]{1,0:T(1,128)}) custom-call(s32[3]{0:T(128)S(1)} %pad_add_fusion.place_ref, bf16[64,8,1152]{2,1,0:T(8,128)(2,1)S(1)} %all-to-all-done.2.back_ref, bf16[8,128]{1,0:T(8,128)(2,1)S(1)} %get-tuple-element.19.refs_1_.scaled_ref, bf16[16,8192]{1,0:T(8,128)(2,1)S(1)} %bitcast.12, ...), custom_call_target="tpu_custom_call" | custom-call | flops 2097152 | bytes 2097152 | tf_op jit(solution)/shard_map/pallas_call | solution.py:278
  (9 shorter events, 0.1 us)
Async XLA Ops:
  0.6 28.3 %copy-start.1 = (bf16[256,512]{1,0:T(8,128)(2,1)S(1)}, bf16[256,512]{1,0:T(8,128)(2,1)}, u32[]{:S(2)}) copy-start(bf16[256,512]{1,0:T(8,128)(2,1)} %weight_any.1) | copy-start | bytes 786436
  0.6 28.3 %copy-start.2 = (bf16[8,8192]{1,0:T(8,128)(2,1)S(1)}, bf16[8,8192]{1,0:T(8,128)(2,1)}, u32[]{:S(2)}) copy-start(bf16[8,8192]{1,0:T(8,128)(2,1)} %inputs_ref.1) | copy-start | bytes 393220
  0.7 6.7 %copy-start.3 = (bf16[16,512]{1,0:T(8,128)(2,1)S(1)}, bf16[16,512]{1,0:T(8,128)(2,1)}, u32[]{:S(2)}) copy-start(bf16[16,512]{1,0:T(8,128)(2,1)} %right_ref.1) | copy-start | bytes 49156
  0.7 28.3 %copy-start.4 = (f32[16]{0:T(128)S(1)}, f32[16]{0:T(128)}, u32[]{:S(2)}) copy-start(f32[16]{0:T(128)} %singular_ref.1) | copy-start | bytes 196
  0.7 28.3 %copy-start.5 = (s32[16]{0:T(128)S(1)}, s32[16]{0:T(128)}, u32[]{:S(2)}) copy-start(s32[16]{0:T(128)} %keep_ref.1) | copy-start | bytes 196
  2.6 13.7 %collective-permute-start = (bf16[256,512]{1,0:T(8,128)(2,1)S(1)}, bf16[256,512]{1,0:T(8,128)(2,1)S(1)}, u32[]{:S(2)}, u32[]{:S(2)}) collective-permute-start(bf16[256,512]{1,0:T(8,128)(2,1)S(1)} %pad_maximum_fusion.mixed_ref), channel_id=1, source_target_pairs={{0,1},{1,0},{2,3},{3,2},{4,5},{5,4},{6,7},{7,6},{8,9},{9,8},{10,11... | collective-permute-start | bytes 786440 | tf_op jit(solution)/shard_map/ppermute | solution.py:29
  8.2 20.7 %all-to-all-start = ((f32[16,8,128]{2,1,0:T(8,128)}), f32[16,8,128]{2,1,0:T(8,128)S(1)}, u32[]{:S(2)}, u32[]{:S(2)}) async-start(f32[16,8,128]{2,1,0:T(8,128)} %shard_map.102.sent_ref), calls=%async_computation | async-start | bytes 131072 | tf_op jit(solution)/shard_map/all_to_all | solution.py:233
  16.4 19.4 %collective-permute-start.1 = (bf16[128,512]{1,0:T(8,128)(2,1)S(1)}, bf16[128,512]{1,0:T(8,128)(2,1)S(1)}, u32[]{:S(2)}, u32[]{:S(2)}) collective-permute-start(bf16[128,512]{1,0:T(8,128)(2,1)S(1)} %get-tuple-element.18), channel_id=1, source_target_pairs={{0,128},{128,0},{256,384},{384,256},{1,129},{129,1},{257,385},{385... | collective-permute-start | bytes 393224 | tf_op jit(solution)/shard_map/ppermute | solution.py:29
  22.5 22.2 %collective-permute-start.3 = (bf16[2,128,512]{2,1,0:T(8,128)(2,1)S(1)}, bf16[2,128,512]{2,1,0:T(8,128)(2,1)S(1)}, u32[]{:S(2)}, u32[]{:S(2)}) collective-permute-start(bf16[2,128,512]{2,1,0:T(8,128)(2,1)S(1)} %get-tuple-element.16.cot_ref), channel_id=1, source_target_pairs={{0,384},{128,256},{256,128},{384,0},{1,385},{129,257},{257,129},{3... | collective-permute-start | bytes 786440 | tf_op jit(solution)/shard_map/ppermute | solution.py:29
  31.0 22.9 %all-to-all-start.1 = ((bf16[4,320,512]{2,1,0:T(8,128)(2,1)}), bf16[4,320,512]{2,1,0:T(8,128)(2,1)S(1)}, u32[]{:S(2)}, u32[]{:S(2)}) async-start(bf16[4,320,512]{2,1,0:T(8,128)(2,1)} %get-tuple-element.17), calls=%async_computation.1 | async-start | bytes 2621440 | tf_op jit(solution)/shard_map/all_to_all | solution.py:255
  35.8 12.8 %collective-permute-start.2 = (bf16[128,512]{1,0:T(8,128)(2,1)S(1)}, bf16[128,512]{1,0:T(8,128)(2,1)S(1)}, u32[]{:S(2)}, u32[]{:S(2)}) collective-permute-start(bf16[128,512]{1,0:T(8,128)(2,1)S(1)} %shard_map.105.in_ref), channel_id=1, source_target_pairs={{0,384},{128,256},{256,128},{384,0},{1,385},{129,257},{257,129},{3... | collective-permute-start | bytes 393224 | tf_op jit(solution)/shard_map/ppermute | solution.py:29
  41.8 6.9 %collective-permute-start.5 = (bf16[128,512]{1,0:T(8,128)(2,1)S(1)}, bf16[128,512]{1,0:T(8,128)(2,1)S(1)}, u32[]{:S(2)}, u32[]{:S(2)}) collective-permute-start(bf16[128,512]{1,0:T(8,128)(2,1)S(1)} %shard_map.106.after_ref.first_ref), channel_id=1, source_target_pairs={{0,1},{1,0},{2,3},{3,2},{4,5},{5,4},{6,7},{7,6},{8,9},{9,8},{10,11... | collective-permute-start | bytes 393224 | tf_op jit(solution)/shard_map/ppermute | solution.py:29
  44.7 9.2 %collective-permute-start.4 = (bf16[128,512]{1,0:T(8,128)(2,1)S(1)}, bf16[128,512]{1,0:T(8,128)(2,1)S(1)}, u32[]{:S(2)}, u32[]{:S(2)}) collective-permute-start(bf16[128,512]{1,0:T(8,128)(2,1)S(1)} %slice_bitcast_fusion), channel_id=1, source_target_pairs={{0,128},{128,0},{256,384},{384,256},{1,129},{129,1},{257,385},{385... | collective-permute-start | bytes 393224 | tf_op jit(solution)/shard_map/ppermute | solution.py:29
  53.9 4.9 %collective-permute-start.6 = (bf16[4,320,512]{2,1,0:T(8,128)(2,1)S(1)}, bf16[4,320,512]{2,1,0:T(8,128)(2,1)S(1)}, u32[]{:S(2)}, u32[]{:S(2)}) collective-permute-start(bf16[4,320,512]{2,1,0:T(8,128)(2,1)S(1)} %shard_map.109.own_ref), channel_id=1, source_target_pairs={{0,16},{16,0},{1,17},{17,1},{2,18},{18,2},{3,19},{19,3},{4,20},{20... | collective-permute-start | bytes 3932168 | tf_op jit(solution)/shard_map/ppermute | solution.py:29
  61.1 44.4 %copy-start = (bf16[8192,16]{0,1:T(8,128)(2,1)S(1)}, bf16[8192,16]{0,1:T(8,128)(2,1)}, u32[]{:S(2)}) copy-start(bf16[8192,16]{0,1:T(8,128)(2,1)} %param.10) | copy-start | bytes 786436
  61.1 44.4 %all-to-all-start.2 = ((bf16[64,8,1152]{2,1,0:T(8,128)(2,1)}), bf16[64,8,1152]{2,1,0:T(8,128)(2,1)S(1)}, u32[]{:S(2)}, u32[]{:S(2)}) async-start(bf16[64,8,1152]{2,1,0:T(8,128)(2,1)} %bitcast.4), calls=%async_computation.2 | async-start | bytes 2359296 | tf_op jit(solution)/shard_map/all_to_all | solution.py:274
  72.4 21.6 %collective-permute-start.7 = (bf16[16,512]{1,0:T(8,128)(2,1)S(1)}, bf16[16,512]{1,0:T(8,128)(2,1)S(1)}, u32[]{:S(2)}, u32[]{:S(2)}) collective-permute-start(bf16[16,512]{1,0:T(8,128)(2,1)S(1)} %convert_element_type.16), channel_id=1, source_target_pairs={{0,128},{128,0},{256,384},{384,256},{1,129},{129,1},{257,385},{385... | collective-permute-start | bytes 49160 | tf_op jit(solution)/shard_map/ppermute | solution.py:29
  76.8 17.2 %collective-permute-start.8 = (bf16[16,512]{1,0:T(8,128)(2,1)S(1)}, bf16[16,512]{1,0:T(8,128)(2,1)S(1)}, u32[]{:S(2)}, u32[]{:S(2)}) collective-permute-start(bf16[16,512]{1,0:T(8,128)(2,1)S(1)} %convert_element_type.16), channel_id=1, source_target_pairs={{0,256},{128,384},{256,0},{384,128},{1,257},{129,385},{257,1},{385... | collective-permute-start | bytes 49160 | tf_op jit(solution)/shard_map/ppermute | solution.py:29
  82.5 11.5 %collective-permute-start.9 = (bf16[16,512]{1,0:T(8,128)(2,1)S(1)}, bf16[16,512]{1,0:T(8,128)(2,1)S(1)}, u32[]{:S(2)}, u32[]{:S(2)}) collective-permute-start(bf16[16,512]{1,0:T(8,128)(2,1)S(1)} %convert_element_type.16), channel_id=1, source_target_pairs={{0,384},{128,256},{256,128},{384,0},{1,385},{129,257},{257,129},{3... | collective-permute-start | bytes 49160 | tf_op jit(solution)/shard_map/ppermute | solution.py:29

commit v19 on v17

--- a/solution.py
+++ b/solution.py
@@ -248,7 +248,7 @@
     last = call(stack_kernel, shape((2, 128, 512), bf16), [in_vmem] * 2 + [anywhere], 30 << 30, 1 << 20)(
         swap(first[0], "zh", 4, 3), swap(third[1], "zh", 4, 1), held
     )
-    x_in = after(lax.all_to_all(x_out, "x", 0, 0), last)
+    x_in = lax.all_to_all(x_out, "x", 0, 0)
     x_other = swap(x_in, "c", 2, 1)
 
     done, terms, own_right = call(

time: 107 us -> 105 us (0.981)
  waiting for transfers between devices: 29.5 us -> 27.9 us
  starting transfers between devices: 63.4 us -> 62.1 us
    ppermute x9, waiting for transfers between devices: 18.7 us -> 10.9 us  [swap(): return lax.ppermute(a, axis, [(i, i ^ mask) for i in range(count)])]
    all_to_all x1, waiting for transfers between devices: 0.01 us -> 6.2 us  [body(): x_in = lax.all_to_all(x_out, 'x', 0, 0)]
    all_to_all x1, starting transfers between devices: 12 us -> 10.7 us  [body(): lax.all_to_all(out.reshape(64, 8, 1152), ('zh', 'zl', 'yh', 'yl'), 0, 0)]
  transfers between devices with their start and end apart: 12 -> 12, of which waited for: 5 -> 4; matrix products, arithmetic and copies ran while one was open for 2% -> 2% of each run, Pallas kernels for 4% -> 4%
where the time goes in v19:
time: 105 us; the launch traced here: 103 us
  starting transfers between devices  62.1 us (59%)
  waiting for transfers between devices  27.9 us (27%)
  Pallas kernels  8.11 us (8%)
  other arithmetic  2.66 us (3%)
  matrix products  1.21 us (1%)
    ppermute x9, starting transfers between devices, swap(): return lax.ppermute(a, axis, [(i, i ^ mask) for i in range(count)])  38.5 us
    ppermute x9, waiting for transfers between devices, swap(): return lax.ppermute(a, axis, [(i, i ^ mask) for i in range(count)])  10.9 us
    all_to_all x1, waiting for transfers between devices, body(): lax.all_to_all(out.reshape(64, 8, 1152), ('zh', 'zl', 'yh', 'yl'), 0, 0)  10.8 us
    all_to_all x1, starting transfers between devices, body(): lax.all_to_all(out.reshape(64, 8, 1152), ('zh', 'zl', 'yh', 'yl'), 0, 0)  10.7 us
    all_to_all x1, starting transfers between devices, body(): rank_in = lax.all_to_all(rank_out, ('zl', 'yh', 'yl'), 0, 0)  8.11 us
    all_to_all x1, waiting for transfers between devices, body(): x_in = lax.all_to_all(x_out, 'x', 0, 0)  6.2 us
    all_to_all x1, starting transfers between devices, body(): x_in = lax.all_to_all(x_out, 'x', 0, 0)  4.78 us
    pallas_call x1, Pallas kernels, body(): call(other_kernel, (shape((4, 128, 1152), bf16), shape((16, 512), f32)),...  2.26 us
  transfers between devices with their start and end apart: 12, of which 4 were waited for; matrix products, arithmetic and copies ran while one was open for 2% of the time, Pallas kernels for 4%

profile of v19, /device:TPU:6, one launch (start us, length us, event | category | flops | bytes accessed | tf_op | source)
XLA Modules:
  0.0 103.0 jit_solution(16339112375141018931)
XLA Ops:
  0.6 0.0 copy-start.1
  0.6 0.0 copy-start.2
  0.7 0.0 copy-start.3
  0.7 0.0 copy-start.4
  0.7 0.0 copy-start.5
  0.7 1.0 slice_select_fusion
  1.7 0.9 pad_maximum_fusion.mixed_ref
  2.6 3.5 %collective-permute-start = (bf16[256,512]{1,0:T(8,128)(2,1)S(1)}, bf16[256,512]{1,0:T(8,128)(2,1)S(1)}, u32[]{:S(2)}, u32[]{:S(2)}) collective-permute-start(bf16[256,512]{1,0:T(8,128)(2,1)S(1)} %pad_maximum_fusion.mixed_ref), channel_id=1, source_target_pairs={{0,1},{1,0},{2,3},{3,2},{4,5},{5,4},{6,7},{7,6},{8,9},{9,8},{10,11... | collective-permute-start | bytes 786440 | tf_op jit(solution)/shard_map/ppermute | solution.py:29
  6.1 1.2 %fusion.projected_ref = f32[8,16]{1,0:T(8,128)S(1)} fusion(bf16[8,8192]{1,0:T(8,128)(2,1)} %inputs_ref.1, bf16[8192,16]{0,1:T(8,128)(2,1)} %param.10), kind=kOutput, calls=%fused_computation.7 | convolution fusion | flops 2097152 | bytes 393728 | tf_op jit(solution)/shard_map/dot_general | solution.py:228
  7.4 0.0 copy-done.3
  7.4 0.8 shard_map.102.sent_ref
  8.2 8.1 %all-to-all-start = ((f32[16,8,128]{2,1,0:T(8,128)}), f32[16,8,128]{2,1,0:T(8,128)S(1)}, u32[]{:S(2)}, u32[]{:S(2)}) async-start(f32[16,8,128]{2,1,0:T(8,128)} %shard_map.102.sent_ref), calls=%async_computation | async-start | bytes 131072 | tf_op jit(solution)/shard_map/all_to_all | solution.py:232
  16.3 0.1 pad_add_fusion.place_ref
  16.4 0.0 collective-permute-done.got_ref.got_any
  16.4 6.1 %collective-permute-start.1 = (bf16[2,128,512]{2,1,0:T(8,128)(2,1)S(1)}, bf16[2,128,512]{2,1,0:T(8,128)(2,1)S(1)}, u32[]{:S(2)}, u32[]{:S(2)}) collective-permute-start(bf16[2,128,512]{2,1,0:T(8,128)(2,1)S(1)} %shard_map.103.cot_ref), channel_id=1, source_target_pairs={{0,128},{128,0},{256,384},{384,256},{1,129},{129,1},{257,385},{385... | collective-permute-start | bytes 786440 | tf_op jit(solution)/shard_map/ppermute | solution.py:29
  22.5 6.4 %collective-permute-start.2 = (bf16[2,128,512]{2,1,0:T(8,128)(2,1)S(1)}, bf16[2,128,512]{2,1,0:T(8,128)(2,1)S(1)}, u32[]{:S(2)}, u32[]{:S(2)}) collective-permute-start(bf16[2,128,512]{2,1,0:T(8,128)(2,1)S(1)} %shard_map.103.cot_ref), channel_id=1, source_target_pairs={{0,384},{128,256},{256,128},{384,0},{1,385},{129,257},{257,129},{3... | collective-permute-start | bytes 786440 | tf_op jit(solution)/shard_map/ppermute | solution.py:29
  28.9 0.0 all-to-all-done.rank_ref
  28.9 0.0 copy-done.1
  28.9 0.0 copy-done.2
  28.9 0.0 copy-done.4
  28.9 0.0 copy-done.5
  29.0 2.0 %shard_map.104 = (bf16[4,320,512]{2,1,0:T(8,128)(2,1)}, bf16[8,128]{1,0:T(8,128)(2,1)S(1)}) custom-call(s32[3]{0:T(128)S(1)} %pad_add_fusion.place_ref, f32[16]{0:T(128)S(1)} %copy-done.4, s32[16]{0:T(128)S(1)} %copy-done.5, f32[16,8,128]{2,1,0:T(8,128)} %shard_map.102.sent_ref, f32[16,8,128]{2,1,0:T(8,128)S(1)} %all-to-all-done.rank_ref, ...), custom_call_target="tpu_custom_call" | custom-call | flops 32212254720 | bytes 3145728 | tf_op jit(solution)/shard_map/pallas_call | solution.py:237
  31.0 4.8 %all-to-all-start.1 = ((bf16[4,320,512]{2,1,0:T(8,128)(2,1)}), bf16[4,320,512]{2,1,0:T(8,128)(2,1)S(1)}, u32[]{:S(2)}, u32[]{:S(2)}) async-start(bf16[4,320,512]{2,1,0:T(8,128)(2,1)} %get-tuple-element.14), calls=%async_computation.1 | async-start | bytes 2621440 | tf_op jit(solution)/shard_map/all_to_all | solution.py:251
  35.8 0.0 collective-permute-done.1.refs_0_
  35.8 6.4 %collective-permute-start.3 = (bf16[128,512]{1,0:T(8,128)(2,1)S(1)}, bf16[128,512]{1,0:T(8,128)(2,1)S(1)}, u32[]{:S(2)}, u32[]{:S(2)}) collective-permute-start(bf16[128,512]{1,0:T(8,128)(2,1)S(1)} %slice_bitcast_fusion.1), channel_id=1, source_target_pairs={{0,384},{128,256},{256,128},{384,0},{1,385},{129,257},{257,129},{3... | collective-permute-start | bytes 393224 | tf_op jit(solution)/shard_map/ppermute | solution.py:29
  42.2 0.0 collective-permute-done.2.third_ref
  42.2 2.1 %collective-permute-start.4 = (bf16[128,512]{1,0:T(8,128)(2,1)S(1)}, bf16[128,512]{1,0:T(8,128)(2,1)S(1)}, u32[]{:S(2)}, u32[]{:S(2)}) collective-permute-start(bf16[128,512]{1,0:T(8,128)(2,1)S(1)} %slice_bitcast_fusion), channel_id=1, source_target_pairs={{0,128},{128,0},{256,384},{384,256},{1,129},{129,1},{257,385},{385... | collective-permute-start | bytes 393224 | tf_op jit(solution)/shard_map/ppermute | solution.py:29
  44.3 6.2 %all-to-all-done.1.own_ref = bf16[4,320,512]{2,1,0:T(8,128)(2,1)S(1)} async-done(((bf16[4,320,512]{2,1,0:T(8,128)(2,1)}), bf16[4,320,512]{2,1,0:T(8,128)(2,1)S(1)}, u32[]{:S(2)}, u32[]{:S(2)}) %all-to-all-start.1) | async-done | bytes 1310752 | tf_op jit(solution)/shard_map/all_to_all | solution.py:251
  50.5 1.9 %collective-permute-start.5 = (bf16[4,320,512]{2,1,0:T(8,128)(2,1)S(1)}, bf16[4,320,512]{2,1,0:T(8,128)(2,1)S(1)}, u32[]{:S(2)}, u32[]{:S(2)}) collective-permute-start(bf16[4,320,512]{2,1,0:T(8,128)(2,1)S(1)} %all-to-all-done.1.own_ref), channel_id=1, source_target_pairs={{0,16},{16,0},{1,17},{17,1},{2,18},{18,2},{3,19},{19,3},{4,20},{20... | collective-permute-start | bytes 3932168 | tf_op jit(solution)/shard_map/ppermute | solution.py:29
  52.4 0.0 collective-permute-done.3.first_ref
  52.4 0.0 collective-permute-done.4.second_ref
  52.5 1.4 %shard_map.108 = (bf16[4,128,512]{2,1,0:T(8,128)(2,1)S(1)}, f32[4,128,128]{2,1,0:T(8,128)S(1)}, f32[16,512]{1,0:T(8,128)S(1)}) custom-call(s32[3]{0:T(128)S(1)} %pad_add_fusion.place_ref, bf16[4,320,512]{2,1,0:T(8,128)(2,1)S(1)} %all-to-all-done.1.own_ref, bf16[2,128,512]{2,1,0:T(8,128)(2,1)S(1)} %shard_map.103.cot_ref, ...), custom_call_target="tpu_custom_call" | custom-call | flops 536870912 | bytes 3145728 | tf_op jit(solution)/shard_map/pallas_call | solution.py:254
  53.9 1.5 %collective-permute-done.5.other_ref = bf16[4,320,512]{2,1,0:T(8,128)(2,1)S(1)} collective-permute-done((bf16[4,320,512]{2,1,0:T(8,128)(2,1)S(1)}, bf16[4,320,512]{2,1,0:T(8,128)(2,1)S(1)}, u32[]{:S(2)}, u32[]{:S(2)}) %collective-permute-start.5) | collective-permute-done | bytes 1310752 | tf_op jit(solution)/shard_map/ppermute | solution.py:29
  55.4 2.3 %shard_map.109 = (bf16[4,128,1152]{2,1,0:T(8,128)(2,1)}, f32[16,512]{1,0:T(8,128)S(1)}) custom-call(s32[3]{0:T(128)S(1)} %pad_add_fusion.place_ref, bf16[4,128,512]{2,1,0:T(8,128)(2,1)S(1)} %get-tuple-element.16.done_ref, f32[4,128,128]{2,1,0:T(8,128)S(1)} %get-tuple-element.17.terms_ref, f32[16,512]{1,0:T(8,128)S(1)} %get-tuple-element.18.own_right_ref, ...), custom_call_target="tpu_custom_call" | custom-call | flops 536870912 | bytes 5242880 | tf_op jit(solution)/shard_map/pallas_call | solution.py:261
  57.7 0.0 copy-start
  57.7 10.7 %all-to-all-start.2 = ((bf16[64,8,1152]{2,1,0:T(8,128)(2,1)}), bf16[64,8,1152]{2,1,0:T(8,128)(2,1)S(1)}, u32[]{:S(2)}, u32[]{:S(2)}) async-start(bf16[64,8,1152]{2,1,0:T(8,128)(2,1)} %bitcast.5), calls=%async_computation.2 | async-start | bytes 2359296 | tf_op jit(solution)/shard_map/all_to_all | solution.py:270
  68.4 4.4 %collective-permute-start.6 = (bf16[16,512]{1,0:T(8,128)(2,1)S(1)}, bf16[16,512]{1,0:T(8,128)(2,1)S(1)}, u32[]{:S(2)}, u32[]{:S(2)}) collective-permute-start(bf16[16,512]{1,0:T(8,128)(2,1)S(1)} %convert_element_type.16), channel_id=1, source_target_pairs={{0,128},{128,0},{256,384},{384,256},{1,129},{129,1},{257,385},{385... | collective-permute-start | bytes 49160 | tf_op jit(solution)/shard_map/ppermute | solution.py:29
  72.8 5.7 %collective-permute-start.7 = (bf16[16,512]{1,0:T(8,128)(2,1)S(1)}, bf16[16,512]{1,0:T(8,128)(2,1)S(1)}, u32[]{:S(2)}, u32[]{:S(2)}) collective-permute-start(bf16[16,512]{1,0:T(8,128)(2,1)S(1)} %convert_element_type.16), channel_id=1, source_target_pairs={{0,256},{128,384},{256,0},{384,128},{1,257},{129,385},{257,1},{385... | collective-permute-start | bytes 49160 | tf_op jit(solution)/shard_map/ppermute | solution.py:29
  78.5 2.2 %collective-permute-start.8 = (bf16[16,512]{1,0:T(8,128)(2,1)S(1)}, bf16[16,512]{1,0:T(8,128)(2,1)S(1)}, u32[]{:S(2)}, u32[]{:S(2)}) collective-permute-start(bf16[16,512]{1,0:T(8,128)(2,1)S(1)} %convert_element_type.16), channel_id=1, source_target_pairs={{0,384},{128,256},{256,128},{384,0},{1,385},{129,257},{257,129},{3... | collective-permute-start | bytes 49160 | tf_op jit(solution)/shard_map/ppermute | solution.py:29
  80.7 9.3 %collective-permute-done.6 = bf16[16,512]{1,0:T(8,128)(2,1)S(1)} collective-permute-done((bf16[16,512]{1,0:T(8,128)(2,1)S(1)}, bf16[16,512]{1,0:T(8,128)(2,1)S(1)}, u32[]{:S(2)}, u32[]{:S(2)}) %collective-permute-start.6) | collective-permute-done | bytes 16416 | tf_op jit(solution)/shard_map/ppermute | solution.py:29
  90.0 0.0 collective-permute-done.7
  90.0 0.0 collective-permute-done.8
  90.0 0.6 add_multiply_fusion
  90.7 10.8 %all-to-all-done.2.back_ref = bf16[64,8,1152]{2,1,0:T(8,128)(2,1)S(1)} async-done(((bf16[64,8,1152]{2,1,0:T(8,128)(2,1)}), bf16[64,8,1152]{2,1,0:T(8,128)(2,1)S(1)}, u32[]{:S(2)}, u32[]{:S(2)}) %all-to-all-start.2) | async-done | bytes 1179680 | tf_op jit(solution)/shard_map/all_to_all | solution.py:270
  101.5 0.0 copy-done
  101.5 1.5 %shard_map.110 = (bf16[8,8192]{1,0:T(8,128)(2,1)}, f32[16,16]{1,0:T(8,128)}, f32[1,16]{1,0:T(1,128)}) custom-call(s32[3]{0:T(128)S(1)} %pad_add_fusion.place_ref, bf16[64,8,1152]{2,1,0:T(8,128)(2,1)S(1)} %all-to-all-done.2.back_ref, bf16[8,128]{1,0:T(8,128)(2,1)S(1)} %get-tuple-element.15.refs_1_.scaled_ref, bf16[16,8192]{1,0:T(8,128)(2,1)S(1)} %bitcast.14, ...), custom_call_target="tpu_custom_call" | custom-call | flops 2097152 | bytes 2097152 | tf_op jit(solution)/shard_map/pallas_call | solution.py:274
  (8 shorter events, 0.1 us)
Async XLA Ops:
  0.6 28.3 %copy-start.1 = (bf16[256,512]{1,0:T(8,128)(2,1)S(1)}, bf16[256,512]{1,0:T(8,128)(2,1)}, u32[]{:S(2)}) copy-start(bf16[256,512]{1,0:T(8,128)(2,1)} %weight_any.1) | copy-start | bytes 786436
  0.6 28.3 %copy-start.2 = (bf16[8,8192]{1,0:T(8,128)(2,1)S(1)}, bf16[8,8192]{1,0:T(8,128)(2,1)}, u32[]{:S(2)}) copy-start(bf16[8,8192]{1,0:T(8,128)(2,1)} %inputs_ref.1) | copy-start | bytes 393220
  0.7 6.7 %copy-start.3 = (bf16[16,512]{1,0:T(8,128)(2,1)S(1)}, bf16[16,512]{1,0:T(8,128)(2,1)}, u32[]{:S(2)}) copy-start(bf16[16,512]{1,0:T(8,128)(2,1)} %right_ref.1) | copy-start | bytes 49156
  0.7 28.3 %copy-start.4 = (f32[16]{0:T(128)S(1)}, f32[16]{0:T(128)}, u32[]{:S(2)}) copy-start(f32[16]{0:T(128)} %singular_ref.1) | copy-start | bytes 196
  0.7 28.3 %copy-start.5 = (s32[16]{0:T(128)S(1)}, s32[16]{0:T(128)}, u32[]{:S(2)}) copy-start(s32[16]{0:T(128)} %keep_ref.1) | copy-start | bytes 196
  2.6 13.7 %collective-permute-start = (bf16[256,512]{1,0:T(8,128)(2,1)S(1)}, bf16[256,512]{1,0:T(8,128)(2,1)S(1)}, u32[]{:S(2)}, u32[]{:S(2)}) collective-permute-start(bf16[256,512]{1,0:T(8,128)(2,1)S(1)} %pad_maximum_fusion.mixed_ref), channel_id=1, source_target_pairs={{0,1},{1,0},{2,3},{3,2},{4,5},{5,4},{6,7},{7,6},{8,9},{9,8},{10,11... | collective-permute-start | bytes 786440 | tf_op jit(solution)/shard_map/ppermute | solution.py:29
  8.2 20.7 %all-to-all-start = ((f32[16,8,128]{2,1,0:T(8,128)}), f32[16,8,128]{2,1,0:T(8,128)S(1)}, u32[]{:S(2)}, u32[]{:S(2)}) async-start(f32[16,8,128]{2,1,0:T(8,128)} %shard_map.102.sent_ref), calls=%async_computation | async-start | bytes 131072 | tf_op jit(solution)/shard_map/all_to_all | solution.py:232
  16.4 19.4 %collective-permute-start.1 = (bf16[2,128,512]{2,1,0:T(8,128)(2,1)S(1)}, bf16[2,128,512]{2,1,0:T(8,128)(2,1)S(1)}, u32[]{:S(2)}, u32[]{:S(2)}) collective-permute-start(bf16[2,128,512]{2,1,0:T(8,128)(2,1)S(1)} %shard_map.103.cot_ref), channel_id=1, source_target_pairs={{0,128},{128,0},{256,384},{384,256},{1,129},{129,1},{257,385},{385... | collective-permute-start | bytes 786440 | tf_op jit(solution)/shard_map/ppermute | solution.py:29
  22.5 19.7 %collective-permute-start.2 = (bf16[2,128,512]{2,1,0:T(8,128)(2,1)S(1)}, bf16[2,128,512]{2,1,0:T(8,128)(2,1)S(1)}, u32[]{:S(2)}, u32[]{:S(2)}) collective-permute-start(bf16[2,128,512]{2,1,0:T(8,128)(2,1)S(1)} %shard_map.103.cot_ref), channel_id=1, source_target_pairs={{0,384},{128,256},{256,128},{384,0},{1,385},{129,257},{257,129},{3... | collective-permute-start | bytes 786440 | tf_op jit(solution)/shard_map/ppermute | solution.py:29
  31.0 19.5 %all-to-all-start.1 = ((bf16[4,320,512]{2,1,0:T(8,128)(2,1)}), bf16[4,320,512]{2,1,0:T(8,128)(2,1)S(1)}, u32[]{:S(2)}, u32[]{:S(2)}) async-start(bf16[4,320,512]{2,1,0:T(8,128)(2,1)} %get-tuple-element.14), calls=%async_computation.1 | async-start | bytes 2621440 | tf_op jit(solution)/shard_map/all_to_all | solution.py:251
  35.8 16.6 %collective-permute-start.3 = (bf16[128,512]{1,0:T(8,128)(2,1)S(1)}, bf16[128,512]{1,0:T(8,128)(2,1)S(1)}, u32[]{:S(2)}, u32[]{:S(2)}) collective-permute-start(bf16[128,512]{1,0:T(8,128)(2,1)S(1)} %slice_bitcast_fusion.1), channel_id=1, source_target_pairs={{0,384},{128,256},{256,128},{384,0},{1,385},{129,257},{257,129},{3... | collective-permute-start | bytes 393224 | tf_op jit(solution)/shard_map/ppermute | solution.py:29
  42.2 10.2 %collective-permute-start.4 = (bf16[128,512]{1,0:T(8,128)(2,1)S(1)}, bf16[128,512]{1,0:T(8,128)(2,1)S(1)}, u32[]{:S(2)}, u32[]{:S(2)}) collective-permute-start(bf16[128,512]{1,0:T(8,128)(2,1)S(1)} %slice_bitcast_fusion), channel_id=1, source_target_pairs={{0,128},{128,0},{256,384},{384,256},{1,129},{129,1},{257,385},{385... | collective-permute-start | bytes 393224 | tf_op jit(solution)/shard_map/ppermute | solution.py:29
  50.5 4.9 %collective-permute-start.5 = (bf16[4,320,512]{2,1,0:T(8,128)(2,1)S(1)}, bf16[4,320,512]{2,1,0:T(8,128)(2,1)S(1)}, u32[]{:S(2)}, u32[]{:S(2)}) collective-permute-start(bf16[4,320,512]{2,1,0:T(8,128)(2,1)S(1)} %all-to-all-done.1.own_ref), channel_id=1, source_target_pairs={{0,16},{16,0},{1,17},{17,1},{2,18},{18,2},{3,19},{19,3},{4,20},{20... | collective-permute-start | bytes 3932168 | tf_op jit(solution)/shard_map/ppermute | solution.py:29
  57.7 43.8 %copy-start = (bf16[8192,16]{0,1:T(8,128)(2,1)S(1)}, bf16[8192,16]{0,1:T(8,128)(2,1)}, u32[]{:S(2)}) copy-start(bf16[8192,16]{0,1:T(8,128)(2,1)} %param.10) | copy-start | bytes 786436
  57.7 43.8 %all-to-all-start.2 = ((bf16[64,8,1152]{2,1,0:T(8,128)(2,1)}), bf16[64,8,1152]{2,1,0:T(8,128)(2,1)S(1)}, u32[]{:S(2)}, u32[]{:S(2)}) async-start(bf16[64,8,1152]{2,1,0:T(8,128)(2,1)} %bitcast.5), calls=%async_computation.2 | async-start | bytes 2359296 | tf_op jit(solution)/shard_map/all_to_all | solution.py:270
  68.4 21.6 %collective-permute-start.6 = (bf16[16,512]{1,0:T(8,128)(2,1)S(1)}, bf16[16,512]{1,0:T(8,128)(2,1)S(1)}, u32[]{:S(2)}, u32[]{:S(2)}) collective-permute-start(bf16[16,512]{1,0:T(8,128)(2,1)S(1)} %convert_element_type.16), channel_id=1, source_target_pairs={{0,128},{128,0},{256,384},{384,256},{1,129},{129,1},{257,385},{385... | collective-permute-start | bytes 49160 | tf_op jit(solution)/shard_map/ppermute | solution.py:29
  72.8 17.2 %collective-permute-start.7 = (bf16[16,512]{1,0:T(8,128)(2,1)S(1)}, bf16[16,512]{1,0:T(8,128)(2,1)S(1)}, u32[]{:S(2)}, u32[]{:S(2)}) collective-permute-start(bf16[16,512]{1,0:T(8,128)(2,1)S(1)} %convert_element_type.16), channel_id=1, source_target_pairs={{0,256},{128,384},{256,0},{384,128},{1,257},{129,385},{257,1},{385... | collective-permute-start | bytes 49160 | tf_op jit(solution)/shard_map/ppermute | solution.py:29
  78.5 11.5 %collective-permute-start.8 = (bf16[16,512]{1,0:T(8,128)(2,1)S(1)}, bf16[16,512]{1,0:T(8,128)(2,1)S(1)}, u32[]{:S(2)}, u32[]{:S(2)}) collective-permute-start(bf16[16,512]{1,0:T(8,128)(2,1)S(1)} %convert_element_type.16), channel_id=1, source_target_pairs={{0,384},{128,256},{256,128},{384,0},{1,385},{129,257},{257,129},{3... | collective-permute-start | bytes 49160 | tf_op jit(solution)/shard_map/ppermute | solution.py:29

commit v20 on v18

--- a/solution.py
+++ b/solution.py
@@ -252,7 +252,7 @@
     last = call(stack_kernel, shape((2, 128, 512), bf16), [in_vmem] * 2 + [anywhere], 30 << 30, 1 << 20)(
         swap(first, "zh", 4, 3), swap(third[1], "zh", 4, 1), held
     )
-    x_in = after(lax.all_to_all(x_out, "x", 0, 0), last, far)
+    x_in = lax.all_to_all(x_out, "x", 0, 0)
     x_other = swap(x_in, "c", 2, 1)
 
     done, terms, own_right = call(

time: 108 us -> 105 us (0.972)
  the two profiles are of different devices: /device:TPU:6 before, /device:TPU:33 now
where the time goes in v20:
time: 105 us; the launch traced here: 104 us
  starting transfers between devices  60.9 us (58%)
  waiting for transfers between devices  30.4 us (29%)
  Pallas kernels  8.11 us (8%)
  other arithmetic  2.66 us (3%)
  matrix products  1.21 us (1%)
    ppermute x10, starting transfers between devices, swap(): return lax.ppermute(a, axis, [(i, i ^ mask) for i in range(count)])  38.4 us
    ppermute x10, waiting for transfers between devices, swap(): return lax.ppermute(a, axis, [(i, i ^ mask) for i in range(count)])  24.1 us
    all_to_all x1, starting transfers between devices, body(): lax.all_to_all(out.reshape(64, 8, 1152), ('zh', 'zl', 'yh', 'yl'), 0, 0)  10.1 us
    all_to_all x1, starting transfers between devices, body(): rank_in = lax.all_to_all(rank_out, ('zl', 'yh', 'yl'), 0, 0)  8.47 us
    all_to_all x1, waiting for transfers between devices, body(): x_in = lax.all_to_all(x_out, 'x', 0, 0)  6.28 us
    all_to_all x1, starting transfers between devices, body(): x_in = lax.all_to_all(x_out, 'x', 0, 0)  4.03 us
    pallas_call x1, Pallas kernels, body(): call(other_kernel, (shape((4, 128, 1152), bf16), shape((16, 512), f32)),...  2.26 us
  transfers between devices with their start and end apart: 13, of which 5 were waited for; matrix products, arithmetic and copies ran while one was open for 2% of the time, Pallas kernels for 4%

profile of v20, /device:TPU:33, one launch (start us, length us, event | category | flops | bytes accessed | tf_op | source)
XLA Modules:
  0.0 104.3 jit_solution(8324410707556315291)
XLA Ops:
  0.6 0.0 copy-start.1
  0.6 0.0 copy-start.2
  0.7 0.0 copy-start.3
  0.7 0.0 copy-start.4
  0.7 0.0 copy-start.5
  0.7 1.0 slice_select_fusion
  1.7 0.9 pad_maximum_fusion.mixed_ref
  2.6 2.3 %collective-permute-start = (bf16[256,512]{1,0:T(8,128)(2,1)S(1)}, bf16[256,512]{1,0:T(8,128)(2,1)S(1)}, u32[]{:S(2)}, u32[]{:S(2)}) collective-permute-start(bf16[256,512]{1,0:T(8,128)(2,1)S(1)} %pad_maximum_fusion.mixed_ref), channel_id=1, source_target_pairs={{0,1},{1,0},{2,3},{3,2},{4,5},{5,4},{6,7},{7,6},{8,9},{9,8},{10,11... | collective-permute-start | bytes 786440 | tf_op jit(solution)/shard_map/ppermute | solution.py:29
  5.0 1.2 %fusion.projected_ref = f32[8,16]{1,0:T(8,128)S(1)} fusion(bf16[8,8192]{1,0:T(8,128)(2,1)} %inputs_ref.1, bf16[8192,16]{0,1:T(8,128)(2,1)} %param.10), kind=kOutput, calls=%fused_computation.6 | convolution fusion | flops 2097152 | bytes 393728 | tf_op jit(solution)/shard_map/dot_general | solution.py:229
  6.2 0.0 copy-done.3
  6.2 0.8 shard_map.102.sent_ref
  7.0 8.5 %all-to-all-start = ((f32[16,8,128]{2,1,0:T(8,128)}), f32[16,8,128]{2,1,0:T(8,128)S(1)}, u32[]{:S(2)}, u32[]{:S(2)}) async-start(f32[16,8,128]{2,1,0:T(8,128)} %shard_map.102.sent_ref), calls=%async_computation | async-start | bytes 131072 | tf_op jit(solution)/shard_map/all_to_all | solution.py:233
  15.5 0.1 pad_add_fusion.place_ref
  15.5 0.0 collective-permute-done.got_ref.got_any
  15.6 5.8 %collective-permute-start.1 = (bf16[128,512]{1,0:T(8,128)(2,1)S(1)}, bf16[128,512]{1,0:T(8,128)(2,1)S(1)}, u32[]{:S(2)}, u32[]{:S(2)}) collective-permute-start(bf16[128,512]{1,0:T(8,128)(2,1)S(1)} %get-tuple-element.18), channel_id=1, source_target_pairs={{0,128},{128,0},{256,384},{384,256},{1,129},{129,1},{257,385},{385... | collective-permute-start | bytes 393224 | tf_op jit(solution)/shard_map/ppermute | solution.py:29
  21.4 6.1 %collective-permute-start.3 = (bf16[2,128,512]{2,1,0:T(8,128)(2,1)S(1)}, bf16[2,128,512]{2,1,0:T(8,128)(2,1)S(1)}, u32[]{:S(2)}, u32[]{:S(2)}) collective-permute-start(bf16[2,128,512]{2,1,0:T(8,128)(2,1)S(1)} %get-tuple-element.16.cot_ref), channel_id=1, source_target_pairs={{0,384},{128,256},{256,128},{384,0},{1,385},{129,257},{257,129},{3... | collective-permute-start | bytes 786440 | tf_op jit(solution)/shard_map/ppermute | solution.py:29
  27.5 0.0 all-to-all-done.rank_ref
  27.5 0.0 copy-done.1
  27.5 0.0 copy-done.2
  27.5 0.0 copy-done.4
  27.6 0.0 copy-done.5
  27.6 2.1 %shard_map.104 = (bf16[4,320,512]{2,1,0:T(8,128)(2,1)}, bf16[8,128]{1,0:T(8,128)(2,1)S(1)}) custom-call(s32[3]{0:T(128)S(1)} %pad_add_fusion.place_ref, f32[16]{0:T(128)S(1)} %copy-done.4, s32[16]{0:T(128)S(1)} %copy-done.5, f32[16,8,128]{2,1,0:T(8,128)} %shard_map.102.sent_ref, f32[16,8,128]{2,1,0:T(8,128)S(1)} %all-to-all-done.rank_ref, ...), custom_call_target="tpu_custom_call" | custom-call | flops 32212254720 | bytes 3145728 | tf_op jit(solution)/shard_map/pallas_call | solution.py:240
  29.6 4.0 %all-to-all-start.1 = ((bf16[4,320,512]{2,1,0:T(8,128)(2,1)}), bf16[4,320,512]{2,1,0:T(8,128)(2,1)S(1)}, u32[]{:S(2)}, u32[]{:S(2)}) async-start(bf16[4,320,512]{2,1,0:T(8,128)(2,1)} %get-tuple-element.17), calls=%async_computation.1 | async-start | bytes 2621440 | tf_op jit(solution)/shard_map/all_to_all | solution.py:255
  33.6 0.0 collective-permute-done.1.refs_0_
  33.7 1.9 %collective-permute-start.4 = (bf16[128,512]{1,0:T(8,128)(2,1)S(1)}, bf16[128,512]{1,0:T(8,128)(2,1)S(1)}, u32[]{:S(2)}, u32[]{:S(2)}) collective-permute-start(bf16[128,512]{1,0:T(8,128)(2,1)S(1)} %shard_map.105.in_ref), channel_id=1, source_target_pairs={{0,384},{128,256},{256,128},{384,0},{1,385},{129,257},{257,129},{3... | collective-permute-start | bytes 393224 | tf_op jit(solution)/shard_map/ppermute | solution.py:29
  35.6 2.2 %collective-permute-start.2 = (bf16[128,512]{1,0:T(8,128)(2,1)S(1)}, bf16[128,512]{1,0:T(8,128)(2,1)S(1)}, u32[]{:S(2)}, u32[]{:S(2)}) collective-permute-start(bf16[128,512]{1,0:T(8,128)(2,1)S(1)} %shard_map.106.after_ref.first_ref), channel_id=1, source_target_pairs={{0,1},{1,0},{2,3},{3,2},{4,5},{5,4},{6,7},{7,6},{8,9},{9,8},{10,11... | collective-permute-start | bytes 393224 | tf_op jit(solution)/shard_map/ppermute | solution.py:29
  37.8 1.6 %collective-permute-done.3.third_ref = bf16[2,128,512]{2,1,0:T(8,128)(2,1)S(1)} collective-permute-done((bf16[2,128,512]{2,1,0:T(8,128)(2,1)S(1)}, bf16[2,128,512]{2,1,0:T(8,128)(2,1)S(1)}, u32[]{:S(2)}, u32[]{:S(2)}) %collective-permute-start.3) | collective-permute-done | bytes 262176 | tf_op jit(solution)/shard_map/ppermute | solution.py:29
  39.4 3.5 %collective-permute-start.5 = (bf16[128,512]{1,0:T(8,128)(2,1)S(1)}, bf16[128,512]{1,0:T(8,128)(2,1)S(1)}, u32[]{:S(2)}, u32[]{:S(2)}) collective-permute-start(bf16[128,512]{1,0:T(8,128)(2,1)S(1)} %slice_bitcast_fusion), channel_id=1, source_target_pairs={{0,128},{128,0},{256,384},{384,256},{1,129},{129,1},{257,385},{385... | collective-permute-start | bytes 393224 | tf_op jit(solution)/shard_map/ppermute | solution.py:29
  42.9 0.0 collective-permute-done.2.in_ref
  42.9 6.3 %all-to-all-done.1.own_ref = bf16[4,320,512]{2,1,0:T(8,128)(2,1)S(1)} async-done(((bf16[4,320,512]{2,1,0:T(8,128)(2,1)}), bf16[4,320,512]{2,1,0:T(8,128)(2,1)S(1)}, u32[]{:S(2)}, u32[]{:S(2)}) %all-to-all-start.1) | async-done | bytes 1310752 | tf_op jit(solution)/shard_map/all_to_all | solution.py:255
  49.2 5.2 %collective-permute-start.6 = (bf16[4,320,512]{2,1,0:T(8,128)(2,1)S(1)}, bf16[4,320,512]{2,1,0:T(8,128)(2,1)S(1)}, u32[]{:S(2)}, u32[]{:S(2)}) collective-permute-start(bf16[4,320,512]{2,1,0:T(8,128)(2,1)S(1)} %all-to-all-done.1.own_ref), channel_id=1, source_target_pairs={{0,16},{16,0},{1,17},{17,1},{2,18},{18,2},{3,19},{19,3},{4,20},{20... | collective-permute-start | bytes 3932168 | tf_op jit(solution)/shard_map/ppermute | solution.py:29
  54.4 0.0 collective-permute-done.4.first_ref
  54.4 0.0 collective-permute-done.5.second_ref
  54.5 1.4 %shard_map.109 = (bf16[4,128,512]{2,1,0:T(8,128)(2,1)S(1)}, f32[4,128,128]{2,1,0:T(8,128)S(1)}, f32[16,512]{1,0:T(8,128)S(1)}) custom-call(s32[3]{0:T(128)S(1)} %pad_add_fusion.place_ref, bf16[4,320,512]{2,1,0:T(8,128)(2,1)S(1)} %all-to-all-done.1.own_ref, bf16[2,128,512]{2,1,0:T(8,128)(2,1)S(1)} %get-tuple-element.16.cot_ref, ...), custom_call_target="tpu_custom_call" | custom-call | flops 536870912 | bytes 3145728 | tf_op jit(solution)/shard_map/pallas_call | solution.py:258
  55.9 1.2 %collective-permute-done.6.other_ref = bf16[4,320,512]{2,1,0:T(8,128)(2,1)S(1)} collective-permute-done((bf16[4,320,512]{2,1,0:T(8,128)(2,1)S(1)}, bf16[4,320,512]{2,1,0:T(8,128)(2,1)S(1)}, u32[]{:S(2)}, u32[]{:S(2)}) %collective-permute-start.6) | collective-permute-done | bytes 1310752 | tf_op jit(solution)/shard_map/ppermute | solution.py:29
  57.1 2.3 %shard_map.110 = (bf16[4,128,1152]{2,1,0:T(8,128)(2,1)}, f32[16,512]{1,0:T(8,128)S(1)}) custom-call(s32[3]{0:T(128)S(1)} %pad_add_fusion.place_ref, bf16[4,128,512]{2,1,0:T(8,128)(2,1)S(1)} %get-tuple-element.20.done_ref, f32[4,128,128]{2,1,0:T(8,128)S(1)} %get-tuple-element.21.terms_ref, f32[16,512]{1,0:T(8,128)S(1)} %get-tuple-element.22.own_right_ref, ...), custom_call_target="tpu_custom_call" | custom-call | flops 536870912 | bytes 5242880 | tf_op jit(solution)/shard_map/pallas_call | solution.py:265
  59.3 0.0 copy-start
  59.3 10.1 %all-to-all-start.2 = ((bf16[64,8,1152]{2,1,0:T(8,128)(2,1)}), bf16[64,8,1152]{2,1,0:T(8,128)(2,1)S(1)}, u32[]{:S(2)}, u32[]{:S(2)}) async-start(bf16[64,8,1152]{2,1,0:T(8,128)(2,1)} %bitcast.4), calls=%async_computation.2 | async-start | bytes 2359296 | tf_op jit(solution)/shard_map/all_to_all | solution.py:274
  69.4 4.0 %collective-permute-start.7 = (bf16[16,512]{1,0:T(8,128)(2,1)S(1)}, bf16[16,512]{1,0:T(8,128)(2,1)S(1)}, u32[]{:S(2)}, u32[]{:S(2)}) collective-permute-start(bf16[16,512]{1,0:T(8,128)(2,1)S(1)} %convert_element_type.16), channel_id=1, source_target_pairs={{0,128},{128,0},{256,384},{384,256},{1,129},{129,1},{257,385},{385... | collective-permute-start | bytes 49160 | tf_op jit(solution)/shard_map/ppermute | solution.py:29
  73.4 5.4 %collective-permute-start.8 = (bf16[16,512]{1,0:T(8,128)(2,1)S(1)}, bf16[16,512]{1,0:T(8,128)(2,1)S(1)}, u32[]{:S(2)}, u32[]{:S(2)}) collective-permute-start(bf16[16,512]{1,0:T(8,128)(2,1)S(1)} %convert_element_type.16), channel_id=1, source_target_pairs={{0,256},{128,384},{256,0},{384,128},{1,257},{129,385},{257,1},{385... | collective-permute-start | bytes 49160 | tf_op jit(solution)/shard_map/ppermute | solution.py:29
  78.9 2.0 %collective-permute-start.9 = (bf16[16,512]{1,0:T(8,128)(2,1)S(1)}, bf16[16,512]{1,0:T(8,128)(2,1)S(1)}, u32[]{:S(2)}, u32[]{:S(2)}) collective-permute-start(bf16[16,512]{1,0:T(8,128)(2,1)S(1)} %convert_element_type.16), channel_id=1, source_target_pairs={{0,384},{128,256},{256,128},{384,0},{1,385},{129,257},{257,129},{3... | collective-permute-start | bytes 49160 | tf_op jit(solution)/shard_map/ppermute | solution.py:29
  80.8 0.9 collective-permute-done.7
  81.7 20.5 %collective-permute-done.8 = bf16[16,512]{1,0:T(8,128)(2,1)S(1)} collective-permute-done((bf16[16,512]{1,0:T(8,128)(2,1)S(1)}, bf16[16,512]{1,0:T(8,128)(2,1)S(1)}, u32[]{:S(2)}, u32[]{:S(2)}) %collective-permute-start.8) | collective-permute-done | bytes 16416 | tf_op jit(solution)/shard_map/ppermute | solution.py:29
  102.2 0.0 collective-permute-done.9
  102.2 0.6 add_multiply_fusion
  102.8 0.0 all-to-all-done.2.back_ref
  102.8 0.0 copy-done
  102.8 1.5 %shard_map.111 = (bf16[8,8192]{1,0:T(8,128)(2,1)}, f32[16,16]{1,0:T(8,128)}, f32[1,16]{1,0:T(1,128)}) custom-call(s32[3]{0:T(128)S(1)} %pad_add_fusion.place_ref, bf16[64,8,1152]{2,1,0:T(8,128)(2,1)S(1)} %all-to-all-done.2.back_ref, bf16[8,128]{1,0:T(8,128)(2,1)S(1)} %get-tuple-element.19.refs_1_.scaled_ref, bf16[16,8192]{1,0:T(8,128)(2,1)S(1)} %bitcast.12, ...), custom_call_target="tpu_custom_call" | custom-call | flops 2097152 | bytes 2097152 | tf_op jit(solution)/shard_map/pallas_call | solution.py:278
  (8 shorter events, 0.1 us)
Async XLA Ops:
  0.6 26.9 %copy-start.1 = (bf16[256,512]{1,0:T(8,128)(2,1)S(1)}, bf16[256,512]{1,0:T(8,128)(2,1)}, u32[]{:S(2)}) copy-start(bf16[256,512]{1,0:T(8,128)(2,1)} %weight_any.1) | copy-start | bytes 786436
  0.6 26.9 %copy-start.2 = (bf16[8,8192]{1,0:T(8,128)(2,1)S(1)}, bf16[8,8192]{1,0:T(8,128)(2,1)}, u32[]{:S(2)}) copy-start(bf16[8,8192]{1,0:T(8,128)(2,1)} %inputs_ref.1) | copy-start | bytes 393220
  0.7 5.5 %copy-start.3 = (bf16[16,512]{1,0:T(8,128)(2,1)S(1)}, bf16[16,512]{1,0:T(8,128)(2,1)}, u32[]{:S(2)}) copy-start(bf16[16,512]{1,0:T(8,128)(2,1)} %right_ref.1) | copy-start | bytes 49156
  0.7 26.9 %copy-start.4 = (f32[16]{0:T(128)S(1)}, f32[16]{0:T(128)}, u32[]{:S(2)}) copy-start(f32[16]{0:T(128)} %singular_ref.1) | copy-start | bytes 196
  0.7 26.9 %copy-start.5 = (s32[16]{0:T(128)S(1)}, s32[16]{0:T(128)}, u32[]{:S(2)}) copy-start(s32[16]{0:T(128)} %keep_ref.1) | copy-start | bytes 196
  2.6 12.9 %collective-permute-start = (bf16[256,512]{1,0:T(8,128)(2,1)S(1)}, bf16[256,512]{1,0:T(8,128)(2,1)S(1)}, u32[]{:S(2)}, u32[]{:S(2)}) collective-permute-start(bf16[256,512]{1,0:T(8,128)(2,1)S(1)} %pad_maximum_fusion.mixed_ref), channel_id=1, source_target_pairs={{0,1},{1,0},{2,3},{3,2},{4,5},{5,4},{6,7},{7,6},{8,9},{9,8},{10,11... | collective-permute-start | bytes 786440 | tf_op jit(solution)/shard_map/ppermute | solution.py:29
  7.0 20.5 %all-to-all-start = ((f32[16,8,128]{2,1,0:T(8,128)}), f32[16,8,128]{2,1,0:T(8,128)S(1)}, u32[]{:S(2)}, u32[]{:S(2)}) async-start(f32[16,8,128]{2,1,0:T(8,128)} %shard_map.102.sent_ref), calls=%async_computation | async-start | bytes 131072 | tf_op jit(solution)/shard_map/all_to_all | solution.py:233
  15.6 18.1 %collective-permute-start.1 = (bf16[128,512]{1,0:T(8,128)(2,1)S(1)}, bf16[128,512]{1,0:T(8,128)(2,1)S(1)}, u32[]{:S(2)}, u32[]{:S(2)}) collective-permute-start(bf16[128,512]{1,0:T(8,128)(2,1)S(1)} %get-tuple-element.18), channel_id=1, source_target_pairs={{0,128},{128,0},{256,384},{384,256},{1,129},{129,1},{257,385},{385... | collective-permute-start | bytes 393224 | tf_op jit(solution)/shard_map/ppermute | solution.py:29
  21.4 18.0 %collective-permute-start.3 = (bf16[2,128,512]{2,1,0:T(8,128)(2,1)S(1)}, bf16[2,128,512]{2,1,0:T(8,128)(2,1)S(1)}, u32[]{:S(2)}, u32[]{:S(2)}) collective-permute-start(bf16[2,128,512]{2,1,0:T(8,128)(2,1)S(1)} %get-tuple-element.16.cot_ref), channel_id=1, source_target_pairs={{0,384},{128,256},{256,128},{384,0},{1,385},{129,257},{257,129},{3... | collective-permute-start | bytes 786440 | tf_op jit(solution)/shard_map/ppermute | solution.py:29
  29.6 19.6 %all-to-all-start.1 = ((bf16[4,320,512]{2,1,0:T(8,128)(2,1)}), bf16[4,320,512]{2,1,0:T(8,128)(2,1)S(1)}, u32[]{:S(2)}, u32[]{:S(2)}) async-start(bf16[4,320,512]{2,1,0:T(8,128)(2,1)} %get-tuple-element.17), calls=%async_computation.1 | async-start | bytes 2621440 | tf_op jit(solution)/shard_map/all_to_all | solution.py:255
  33.7 20.7 %collective-permute-start.4 = (bf16[128,512]{1,0:T(8,128)(2,1)S(1)}, bf16[128,512]{1,0:T(8,128)(2,1)S(1)}, u32[]{:S(2)}, u32[]{:S(2)}) collective-permute-start(bf16[128,512]{1,0:T(8,128)(2,1)S(1)} %shard_map.105.in_ref), channel_id=1, source_target_pairs={{0,384},{128,256},{256,128},{384,0},{1,385},{129,257},{257,129},{3... | collective-permute-start | bytes 393224 | tf_op jit(solution)/shard_map/ppermute | solution.py:29
  35.6 7.3 %collective-permute-start.2 = (bf16[128,512]{1,0:T(8,128)(2,1)S(1)}, bf16[128,512]{1,0:T(8,128)(2,1)S(1)}, u32[]{:S(2)}, u32[]{:S(2)}) collective-permute-start(bf16[128,512]{1,0:T(8,128)(2,1)S(1)} %shard_map.106.after_ref.first_ref), channel_id=1, source_target_pairs={{0,1},{1,0},{2,3},{3,2},{4,5},{5,4},{6,7},{7,6},{8,9},{9,8},{10,11... | collective-permute-start | bytes 393224 | tf_op jit(solution)/shard_map/ppermute | solution.py:29
  39.4 15.0 %collective-permute-start.5 = (bf16[128,512]{1,0:T(8,128)(2,1)S(1)}, bf16[128,512]{1,0:T(8,128)(2,1)S(1)}, u32[]{:S(2)}, u32[]{:S(2)}) collective-permute-start(bf16[128,512]{1,0:T(8,128)(2,1)S(1)} %slice_bitcast_fusion), channel_id=1, source_target_pairs={{0,128},{128,0},{256,384},{384,256},{1,129},{129,1},{257,385},{385... | collective-permute-start | bytes 393224 | tf_op jit(solution)/shard_map/ppermute | solution.py:29
  49.2 7.8 %collective-permute-start.6 = (bf16[4,320,512]{2,1,0:T(8,128)(2,1)S(1)}, bf16[4,320,512]{2,1,0:T(8,128)(2,1)S(1)}, u32[]{:S(2)}, u32[]{:S(2)}) collective-permute-start(bf16[4,320,512]{2,1,0:T(8,128)(2,1)S(1)} %all-to-all-done.1.own_ref), channel_id=1, source_target_pairs={{0,16},{16,0},{1,17},{17,1},{2,18},{18,2},{3,19},{19,3},{4,20},{20... | collective-permute-start | bytes 3932168 | tf_op jit(solution)/shard_map/ppermute | solution.py:29
  59.3 43.5 %copy-start = (bf16[8192,16]{0,1:T(8,128)(2,1)S(1)}, bf16[8192,16]{0,1:T(8,128)(2,1)}, u32[]{:S(2)}) copy-start(bf16[8192,16]{0,1:T(8,128)(2,1)} %param.10) | copy-start | bytes 786436
  59.3 43.5 %all-to-all-start.2 = ((bf16[64,8,1152]{2,1,0:T(8,128)(2,1)}), bf16[64,8,1152]{2,1,0:T(8,128)(2,1)S(1)}, u32[]{:S(2)}, u32[]{:S(2)}) async-start(bf16[64,8,1152]{2,1,0:T(8,128)(2,1)} %bitcast.4), calls=%async_computation.2 | async-start | bytes 2359296 | tf_op jit(solution)/shard_map/all_to_all | solution.py:274
  69.4 12.3 %collective-permute-start.7 = (bf16[16,512]{1,0:T(8,128)(2,1)S(1)}, bf16[16,512]{1,0:T(8,128)(2,1)S(1)}, u32[]{:S(2)}, u32[]{:S(2)}) collective-permute-start(bf16[16,512]{1,0:T(8,128)(2,1)S(1)} %convert_element_type.16), channel_id=1, source_target_pairs={{0,128},{128,0},{256,384},{384,256},{1,129},{129,1},{257,385},{385... | collective-permute-start | bytes 49160 | tf_op jit(solution)/shard_map/ppermute | solution.py:29
  73.4 28.7 %collective-permute-start.8 = (bf16[16,512]{1,0:T(8,128)(2,1)S(1)}, bf16[16,512]{1,0:T(8,128)(2,1)S(1)}, u32[]{:S(2)}, u32[]{:S(2)}) collective-permute-start(bf16[16,512]{1,0:T(8,128)(2,1)S(1)} %convert_element_type.16), channel_id=1, source_target_pairs={{0,256},{128,384},{256,0},{384,128},{1,257},{129,385},{257,1},{385... | collective-permute-start | bytes 49160 | tf_op jit(solution)/shard_map/ppermute | solution.py:29
  78.9 23.3 %collective-permute-start.9 = (bf16[16,512]{1,0:T(8,128)(2,1)S(1)}, bf16[16,512]{1,0:T(8,128)(2,1)S(1)}, u32[]{:S(2)}, u32[]{:S(2)}) collective-permute-start(bf16[16,512]{1,0:T(8,128)(2,1)S(1)} %convert_element_type.16), channel_id=1, source_target_pairs={{0,384},{128,256},{256,128},{384,0},{1,385},{129,257},{257,129},{3... | collective-permute-start | bytes 49160 | tf_op jit(solution)/shard_map/ppermute | solution.py:29
